TPU v7x, 32 devices: a whole 2x2x4 slice. The times are simulated.
32 devices in a mesh: seq: 2 (over x), tensor: 4 (over z), dp: 4 (over y, core).
Axes of the slice: x: 2, y: 2, z: 4, core: 2. Of those that a mesh axis runs over, the one named last changes fastest.
Arguments:
- span_act: bfloat16 [2048, 8192], P(('seq', 'dp'), 'tensor'), may hold values from -6 to 6
- q_weight: bfloat16 [8192, 4096], P(('seq', 'dp'), 'tensor'), may hold values from -0.0625 to 0.0625
- out_grad: bfloat16 [2048, 4096], P(('seq', 'dp'), 'tensor'), may hold values from -6 to 6
- neighbour_kv: bfloat16 [64, 2, 256, 4096], P(('seq', 'dp'), None, None, 'tensor'), may hold values from -210 to 210
- neighbour_ids: int32 [64, 256], P(('seq', 'dp')), may hold values from 0 to 255999, as said below
- owner: int32 [32], replicated, may hold values from 0 to 1, as said below
Outputs:
- act_grad: bfloat16 [2048, 8192], P(('seq', 'dp'), 'tensor')
- weight_grad: float32 [8192, 4096], P(('seq', 'dp'), 'tensor')
- kv_grad: bfloat16 [64, 2, 256, 4096], P(('seq', 'dp'), None, None, 'tensor')
Inputs may be any that keep to these rules, and one draw needn't show every extreme that they name: owner[c] is the owner's index along seq within span c's own dp group. Of the 4 spans of one home block at most 4 name the same owner, and in each dp group some owner is named by 4 spans of every home block. `neighbour_ids`: each of the 2 neighbours of a slot takes 128 consecutive positions; its ids are positive on a leading run of 32 to 128 positions and 0 (padding) after it. Slots that no span names are never read.
All inputs are finite; a program needn't handle non-finite values.
Results may differ from a plain program's by a relative error of at most 0.022.
The roundings to bfloat16 on the way count: a program that leaves them out, or rounds other values in their place, can miss the bound.
Values may be sent and summed in bfloat16 or wider, within the bound.
No kernel may reach another device: no remote copies, remote signals or barrier semaphores. Data moves between devices by JAX's collectives and lax.ppermute only.
A program may use at most 128 MiB of HBM per device.

v0:
```python
import jax
import jax.numpy as jnp
from jax import lax
from jax.sharding import PartitionSpec as P

HD = 128
SPAN = 64
KEYS = 256


def attend_back(queries, grads, pair_kv, live):
    slots, rows, width = queries.shape
    heads = width // HD
    scale = HD ** (-0.5)
    query_heads = queries.reshape(slots, rows, heads, HD)
    grad_heads = grads.reshape(slots, rows, heads, HD)
    key_heads = pair_kv[:, 0].reshape(slots, -1, heads, HD)
    value_heads = pair_kv[:, 1].reshape(slots, -1, heads, HD)
    scores = (
        jnp.einsum("bqhd,bkhd->bhqk", query_heads, key_heads, preferred_element_type=jnp.float32)
        * scale
    )
    scores = jnp.where(live[:, None, None, :], scores, -1e30)
    top = jnp.max(scores, axis=-1, keepdims=True)
    expo = jnp.exp(scores - top)
    probs = expo / jnp.sum(expo, axis=-1, keepdims=True)
    value_grad = jnp.einsum(
        "bhqk,bqhd->bkhd",
        probs.astype(jnp.bfloat16),
        grad_heads,
        preferred_element_type=jnp.float32,
    )
    prob_grad = jnp.einsum(
        "bqhd,bkhd->bhqk", grad_heads, value_heads, preferred_element_type=jnp.float32
    )
    center = jnp.sum(probs * prob_grad, axis=-1, keepdims=True)
    score_grad = (probs * (prob_grad - center) * scale).astype(jnp.bfloat16)
    query_grad = jnp.einsum(
        "bhqk,bkhd->bqhd", score_grad, key_heads, preferred_element_type=jnp.float32
    )
    key_grad = jnp.einsum(
        "bhqk,bqhd->bkhd", score_grad, query_heads, preferred_element_type=jnp.float32
    )
    both = jnp.stack([key_grad.astype(jnp.bfloat16), value_grad.astype(jnp.bfloat16)], axis=1)
    return (
        query_grad.astype(jnp.bfloat16).reshape(slots, rows, width),
        both.reshape(slots, 2, -1, width),
    )


def on_device(span_act, q_weight, out_grad, neighbour_kv, neighbour_ids, owner):
    tok_rows = out_grad.shape[0]
    width = out_grad.shape[1]
    seq_count = lax.axis_size("seq")
    dp_count = lax.axis_size("dp")
    spans_dev = tok_rows // SPAN
    capacity = neighbour_kv.shape[0]
    pairs = capacity // seq_count
    block = lax.axis_index("seq") * dp_count + lax.axis_index("dp")
    whole = lax.all_gather(span_act, "tensor", axis=1, tiled=True)
    weights = lax.all_gather(q_weight, ("seq", "dp"), axis=0, tiled=True)
    queries = jnp.dot(whole, weights, preferred_element_type=jnp.float32).astype(jnp.bfloat16)
    mine = lax.dynamic_slice_in_dim(owner, block * spans_dev, spans_dev)
    position = jnp.arange(spans_dev)
    same = mine[:, None] == mine[None, :]
    before = position[None, :] < position[:, None]
    rank = jnp.sum(same & before, axis=1)
    target = mine * pairs + rank
    select = (jnp.arange(capacity)[:, None] == target[None, :]).astype(jnp.bfloat16)
    q_spans = queries.reshape(spans_dev, SPAN, width)
    g_spans = out_grad.reshape(spans_dev, SPAN, width)
    kv_recv, ids_recv = (
        lax.all_to_all(
            neighbour_kv.reshape(seq_count, pairs, 2, KEYS, width),
            "seq",
            split_axis=0,
            concat_axis=0,
            tiled=True,
        ),
        lax.all_to_all(
            neighbour_ids.reshape(seq_count, pairs, KEYS),
            "seq",
            split_axis=0,
            concat_axis=0,
            tiled=True,
        ),
    )
    flat_kv = kv_recv.reshape(capacity, 2 * KEYS * width)
    span_kv = jnp.einsum("sc,sf->cf", select, flat_kv, preferred_element_type=jnp.float32).astype(
        jnp.bfloat16
    )
    live_recv = (ids_recv.reshape(capacity, KEYS) != 0).astype(jnp.int32)
    span_live = jnp.sum(select.astype(jnp.int32)[:, :, None] * live_recv[:, None, :], axis=0) > 0
    query_grad, span_kv_grad = attend_back(
        q_spans, g_spans, span_kv.reshape(spans_dev, 2, KEYS, width), span_live
    )
    slot_kv_grad = jnp.einsum(
        "sc,cf->sf",
        select,
        span_kv_grad.reshape(spans_dev, 2 * KEYS * width),
        preferred_element_type=jnp.float32,
    ).astype(jnp.bfloat16)
    kv_grad = lax.all_to_all(
        slot_kv_grad.reshape(seq_count, pairs, 2, KEYS, width),
        "seq",
        split_axis=0,
        concat_axis=0,
        tiled=True,
    ).reshape(capacity, 2, KEYS, width)
    flat_grad = query_grad.reshape(tok_rows, width)
    partial_act = lax.dot_general(
        flat_grad, weights, (((1,), (1,)), ((), ())), preferred_element_type=jnp.float32
    )
    act_grad = lax.psum_scatter(
        partial_act.astype(jnp.bfloat16), "tensor", scatter_dimension=1, tiled=True
    )
    weight_grad = lax.psum_scatter(
        lax.dot_general(
            whole, flat_grad, (((0,), (0,)), ((), ())), preferred_element_type=jnp.float32
        ).astype(jnp.bfloat16),
        ("seq", "dp"),
        scatter_dimension=0,
        tiled=True,
    ).astype(jnp.float32)
    return (act_grad, weight_grad, kv_grad)


def solution(mesh):
    in_specs = (
        P(("seq", "dp"), "tensor"),
        P(("seq", "dp"), "tensor"),
        P(("seq", "dp"), "tensor"),
        P(("seq", "dp"), None, None, "tensor"),
        P(("seq", "dp"), None),
        P(),
    )
    out_specs = (
        P(("seq", "dp"), "tensor"),
        P(("seq", "dp"), "tensor"),
        P(("seq", "dp"), None, None, "tensor"),
    )
    return jax.shard_map(
        on_device, mesh=mesh, in_specs=in_specs, out_specs=out_specs, check_vma=False
    )
```

profile of v0, /device:TPU:0, one launch (start us, length us, event | category | flops | bytes accessed | tf_op | source)
XLA Modules:
  0.0 471.3 jit_solution(9219405413316166558)
XLA Ops:
  7.2 0.0 copy-start.4
  7.2 0.0 all-gather.3.cloned.1.call-start
  7.2 0.7 all-gather.3.cloned.1.call-update
  7.9 0.0 all-gather.5.cloned.1.call-start
  8.0 0.7 all-gather.5.cloned.1.call-update
  8.7 0.0 copy-done.4
  8.7 7.8 %all_to_all.15 = s32[2,4,256]{2,1,0:T(4,128)S(1)} all-to-all(s32[2,4,256]{2,1,0:T(4,128)S(1)} %reshape.65), channel_id=1, replica_groups=mesh['seq'=2,'tensor'=4,'dp'=4] {'seq'}, dimensions={0} | all-to-all | bytes 16384 | tf_op jit(solution)/shard_map/all_to_all | solution.py:80
  16.5 7.5 %all-to-all-start = ((bf16[2,4,2,256,1024]{4,3,2,1,0:T(8,128)(2,1)}), bf16[2,4,2,256,1024]{4,3,2,1,0:T(8,128)(2,1)}, u32[]{:S(2)}, u32[]{:S(2)}) async-start(bf16[2,4,2,256,1024]{4,3,2,1,0:T(8,128)(2,1)} %bitcast.77), calls=%async_computation | async-start | bytes 16777216 | tf_op jit(solution)/shard_map/all_to_all | solution.py:73
  24.0 0.0 reduce-scatter.5.cloned.1.call-start
  24.1 0.0 copy-done.3
  24.1 0.1 copy.49
  24.2 0.1 dynamic_slice.3
  24.3 0.2 convert_reduce_fusion
  24.5 0.1 multiply_add_fusion
  24.5 0.1 fusion.27
  24.6 0.1 multiply_reduce_fusion
  24.7 102.4 %all-to-all-done = bf16[2,4,2,256,1024]{4,3,2,1,0:T(8,128)(2,1)} async-done(((bf16[2,4,2,256,1024]{4,3,2,1,0:T(8,128)(2,1)}), bf16[2,4,2,256,1024]{4,3,2,1,0:T(8,128)(2,1)}, u32[]{:S(2)}, u32[]{:S(2)}) %all-to-all-start) | async-done | bytes 8388640 | tf_op jit(solution)/shard_map/all_to_all | solution.py:73
  127.1 10.6 %reshape.63 = bf16[8,524288]{1,0:T(8,128)(2,1)} reshape(bf16[2,4,2,256,1024]{4,3,2,1,0:T(8,128)(2,1)} %all-to-all-done) | data formatting | bytes 16777216 | tf_op jit(solution)/shard_map/reshape | solution.py:88
  137.7 5.8 %convolution_convert_fusion.1 = bf16[4,524288]{1,0:T(4,128)(2,1)S(1)} fusion(bf16[8,524288]{1,0:T(8,128)(2,1)} %reshape.63, s32[4]{0:T(128)S(1)} %multiply_add_fusion), kind=kOutput, calls=%fused_computation.3 | convolution fusion | flops 35651616 | bytes 12582928 | tf_op jit(solution)/shard_map/sc,sf->cf/dot_general | solution.py:89
  143.5 1.4 copy.47
  144.9 1.8 fusion.36
  146.6 2.7 copy.45
  149.3 2.8 copy.46
  152.2 1.8 fusion.20
  154.0 38.8 %all-gather.5.cloned.1.call-done = bf16[8192,1024]{1,0:T(8,128)(2,1)} async-done(((bf16[1024,1024]{1,0:T(8,128)(2,1)}), bf16[8192,1024]{1,0:T(8,128)(2,1)}) %all-gather.5.cloned.1.call-update) | async-done | bytes 16777232 | tf_op jit(solution)/shard_map/all_gather | solution.py:61
  192.8 11.7 %fusion.9 = bf16[32,8,8,128]{3,1,2,0:T(8,128)(2,1)S(1)} fusion(bf16[256,8192]{1,0:T(8,128)(2,1)} %all-gather.3.cloned.1.call-done, bf16[8192,1024]{1,0:T(8,128)(2,1)} %all-gather.5.cloned.1.call-done), kind=kOutput, calls=%fused_computation.22 | convolution fusion | flops 4295229440 | bytes 21495808 | tf_op jit(solution)/shard_map/dot_general | solution.py:62
  204.5 0.1 copy.48
  204.6 0.4 fusion.23
  205.0 0.4 copy-done.1
  205.4 1.8 fusion.37
  207.2 16.1 %fusion.8 = bf16[4,64,8,128]{3,1,2,0:T(8,128)(2,1)} fusion(bf16[4,256,8,128]{1,3,2,0:T(8,128)(2,1)} %bitcast.78, f32[4,8,256,64]{2,3,1,0:T(8,128)} %fusion.20, f32[4,8,64,256]{3,2,1,0:T(8,128)} %get-tuple-element.15, f32[4,8,64]{2,1,0:T(8,128)S(1)} %get-tuple-element.14), kind=kOutput, calls=%fused_computation.21 | convolution fusion | flops 138152192 | bytes 6823936 | tf_op jit(solution)/shard_map/bhqk,bkhd->bqhd/dot_general | solution.py:38
  223.2 1.4 copy.35
  224.6 10.3 %convert_bitcast_fusion = bf16[8192,1024]{0,1:T(8,128)(2,1)} fusion(bf16[256,8192]{1,0:T(8,128)(2,1)} %all-gather.3.cloned.1.call-done, bf16[32,8,8,128]{3,2,1,0:T(8,128)(2,1)S(1)} %bitcast.81), kind=kOutput, calls=%fused_computation.4 | convolution fusion | flops 4303355904 | bytes 21495808 | tf_op jit(solution)/shard_map/dot_general | solution.py:118
  235.0 0.0 reduce-scatter.5.cloned.1.call-update
  235.0 0.0 reduce-scatter.3.cloned.1.call-start
  235.0 10.2 %convolution_convert_fusion.2 = bf16[256,8192]{1,0:T(8,128)(2,1)} fusion(bf16[8192,1024]{1,0:T(8,128)(2,1)} %all-gather.5.cloned.1.call-done, bf16[32,8,8,128]{3,2,1,0:T(8,128)(2,1)S(1)} %bitcast.82), kind=kOutput, calls=%fused_computation.5 | convolution fusion | flops 4297064448 | bytes 21495808 | tf_op jit(solution)/shard_map/dot_general | solution.py:111
  245.2 0.0 reduce-scatter.3.cloned.1.call-update
  245.2 1.1 copy-done.2
  246.3 18.0 %convert_bitcast_fusion.2 = bf16[4,1,256,8,128]{2,4,3,0,1:T(8,128)(2,1)} fusion(f32[4,8,256,64]{2,3,1,0:T(8,128)} %fusion.20, bf16[4,64,8,128]{3,2,1,0:T(8,128)(2,1)S(1)} %bitcast.86, f32[4,8,64,256]{3,2,1,0:T(8,128)} %get-tuple-element.15, f32[4,8,64]{2,1,0:T(8,128)S(1)} %get-tuple-element.14), kind=kOutput, calls=%fused_computation.15 | convolution fusion | flops 138938624 | bytes 6823936 | tf_op jit(solution)/shard_map/bhqk,bqhd->bkhd/dot_general | solution.py:41
  264.3 5.3 %convert_bitcast_fusion.1 = bf16[4,1,256,8,128]{2,4,3,0,1:T(8,128)(2,1)} fusion(bf16[4,64,8,128]{3,2,1,0:T(8,128)(2,1)S(1)} %bitcast.84, f32[4,8,64]{2,1,0:T(8,128)S(1)} %get-tuple-element.14, f32[4,8,64,256]{3,2,1,0:T(8,128)S(1)} %fusion.23, pred[4,256]{1,0:T(4,128)(4,1)S(1)} %broadcast_compare_fusion), kind=kOutput, calls=%fused_computation.14 | convolution fusion | flops 137890048 | bytes 4727808 | tf_op jit(solution)/shard_map/bhqk,bqhd->bkhd/dot_general | solution.py:27
  269.6 5.2 %pad_maximum_fusion = bf16[4,2,256,8,128]{2,4,3,0,1:T(8,128)(2,1)} fusion(bf16[4,1,256,8,128]{2,4,3,0,1:T(8,128)(2,1)} %convert_bitcast_fusion.1, bf16[4,1,256,8,128]{2,4,3,0,1:T(8,128)(2,1)} %convert_bitcast_fusion.2), kind=kLoop, calls=%fused_computation.8 | loop fusion | flops 2097152 | bytes 8388608 | tf_op jit(solution)/shard_map/stack | solution.py:44
  274.8 7.6 %copy.39 = bf16[4,2,256,8,128]{4,3,2,1,0:T(8,128)(2,1)} copy(bf16[4,2,256,8,128]{2,4,3,0,1:T(8,128)(2,1)} %pad_maximum_fusion) | data formatting | bytes 8388608 | tf_op jit(solution)/shard_map/stack | solution.py:44
  282.5 9.0 %convolution_convert_fusion = bf16[8,524288]{1,0:T(8,128)(2,1)} fusion(bf16[1,4,4096,128]{3,2,1,0:T(8,128)(2,1)} %bitcast.75, s32[4]{0:T(128)S(1)} %multiply_add_fusion), kind=kOutput, calls=%fused_computation.2 | convolution fusion | flops 37748768 | bytes 12582928 | tf_op jit(solution)/shard_map/sc,cf->sf/dot_general | solution.py:97
  291.5 11.5 %copy.52 = bf16[1,8,512,1024]{3,2,1,0:T(8,128)(2,1)} copy(bf16[1,8,512,1024]{3,1,2,0:T(8,128)(2,1)} %bitcast.71) | data formatting | bytes 16777216
  302.9 127.7 %all_to_all.16 = bf16[2,4,2,256,1024]{4,3,2,1,0:T(8,128)(2,1)} all-to-all(bf16[2,4,2,256,1024]{4,3,2,1,0:T(8,128)(2,1)} %bitcast.73), channel_id=1, replica_groups=mesh['seq'=2,'tensor'=4,'dp'=4] {'seq'}, dimensions={0} | all-to-all | bytes 16777216 | tf_op jit(solution)/shard_map/all_to_all | solution.py:103
  430.6 4.1 copy.40
  434.8 21.5 %reduce-scatter.3.cloned.1.call-done = bf16[256,2048]{1,0:T(8,128)(2,1)} async-done(((bf16[256,8192]{1,0:T(8,128)(2,1)}), bf16[256,2048]{1,0:T(8,128)(2,1)}) %reduce-scatter.3.cloned.1.call-update) | async-done | bytes 1048592 | tf_op jit(solution)/shard_map/reduce_scatter | solution.py:114
  456.2 8.1 %copy.74 = bf16[8,2,256,1024]{3,2,1,0:T(8,128)(2,1)} copy(bf16[8,2,256,1024]{3,2,1,0:T(8,128)(2,1)} %bitcast.72) | data formatting | bytes 16777216
  (13 shorter events, 0.0 us)
Async XLA Ops:
  7.2 1.5 copy-start.4
  7.2 146.8 %all-gather.3.cloned.1.call-start = ((), (), s32[]{:S(2)}) async-start(), calls=%async_computation.5 | async-start | bytes 5242880 | tf_op jit(solution)/shard_map/all_gather | solution.py:60
  7.9 184.9 %all-gather.5.cloned.1.call-start = ((), (), s32[]{:S(2)}) async-start(), calls=%async_computation.6 | async-start | bytes 18874368 | tf_op jit(solution)/shard_map/all_gather | solution.py:61
  16.5 7.6 %copy-start.3 = (bf16[256,1024]{1,0:T(8,128)(2,1)S(1)}, bf16[256,1024]{1,0:T(8,128)(2,1)}, u32[]{:S(2)}) copy-start(bf16[256,1024]{1,0:T(8,128)(2,1)} %param.8) | copy-start | bytes 1572868
  16.5 7.7 %copy-start.5 = (s32[32]{0:T(128)S(1)}, s32[32]{0:T(128)}, u32[]{:S(2)}) copy-start(s32[32]{0:T(128)} %param.11) | copy-start | bytes 388
  16.5 110.6 %all-to-all-start = ((bf16[2,4,2,256,1024]{4,3,2,1,0:T(8,128)(2,1)}), bf16[2,4,2,256,1024]{4,3,2,1,0:T(8,128)(2,1)}, u32[]{:S(2)}, u32[]{:S(2)}) async-start(bf16[2,4,2,256,1024]{4,3,2,1,0:T(8,128)(2,1)} %bitcast.77), calls=%async_computation | async-start | bytes 16777216 | tf_op jit(solution)/shard_map/all_to_all | solution.py:73
  24.0 406.6 %reduce-scatter.5.cloned.1.call-start = ((), (), s32[]{:S(2)}) async-start(), calls=%async_computation.8 | async-start | bytes 18874368 | tf_op jit(solution)/shard_map/reduce_scatter | solution.py:117
  192.8 11.8 %copy-start = (bf16[4,1,256,1024]{2,3,0,1:T(8,128)(2,1)S(1)}, bf16[4,1,256,1024]{2,3,0,1:T(8,128)(2,1)}, u32[]{:S(2)}) copy-start(bf16[4,1,256,1024]{2,3,0,1:T(8,128)(2,1)} %copy.45) | copy-start | bytes 6291460
  204.6 0.8 copy-start.1
  235.0 221.3 %reduce-scatter.3.cloned.1.call-start = ((), (), s32[]{:S(2)}) async-start(), calls=%async_computation.7 | async-start | bytes 5242880 | tf_op jit(solution)/shard_map/reduce_scatter | solution.py:114
  245.2 1.1 copy-start.2
Sparse Core Ops, SparseCore 0:
  9.6 83.4 all-gather.2
  95.0 97.7 all-gather.4
  235.1 141.5 reduce-scatter.4
  379.4 76.7 reduce-scatter.2
where the time goes:
time: 479 us; the launch traced here: 471 us
  waiting for transfers between devices  164 us (34%)
  blocking collectives  136 us (28%)
  matrix products  88.5 us (18%)
  local copies, waits for them, and re-layouts  53.8 us (11%)
  between operations  14.3 us (3%)
  starting transfers between devices  7.65 us (2%)
  other arithmetic  7.44 us (2%)
    all_to_all x1, blocking collectives, on_device(): lax.all_to_all(slot_kv_grad.reshape(seq_count, pairs, 2, KEYS, width), 's...  128 us
    all_to_all x1, waiting for transfers between devices, on_device(): lax.all_to_all(neighbour_kv.reshape(seq_count, pairs, 2, KEYS, width), 's...  102 us
    all_gather x1, waiting for transfers between devices, on_device(): weights = lax.all_gather(q_weight, ('seq', 'dp'), axis=0, tiled=True)  38.8 us
    unnamed x20, local copies, waits for them, and re-layouts  32.3 us
    reduce_scatter x1, waiting for transfers between devices, on_device(): lax.psum_scatter(partial_act.astype(jnp.bfloat16), 'tensor', scatter_dime...  21.5 us
    dot_general x1, matrix products, attend_back(): jnp.einsum('bhqk,bqhd->bkhd', score_grad, query_heads, preferred_element_...  18 us
    dot_general x1, matrix products, attend_back(): jnp.einsum('bhqk,bkhd->bqhd', score_grad, key_heads, preferred_element_ty...  16.1 us
    dot_general x1, matrix products, on_device(): jnp.dot(whole, weights, preferred_element_type=jnp.float32)  11.7 us
  transfers between devices with their start and end apart: 5, of which 3 were waited for; matrix products, arithmetic and copies ran while one was open for 21% of the time, Pallas kernels for 0%

commit v1 on v0

v1 whole, which is shorter than its diff:
```python
import functools

import jax
import jax.numpy as jnp
from jax import lax
from jax.experimental import pallas as pl
from jax.experimental.pallas import tpu as pltpu
from jax.sharding import PartitionSpec as P

HD = 128
SPAN = 64
KEYS = 256
F32 = jnp.float32
BF16 = jnp.bfloat16


def dot(a, b, contract):
    return lax.dot_general(a, b, (contract, ((), ())), preferred_element_type=F32)


def shift(value, axis, step=1):
    if axis == "seq":
        size = lax.axis_size("seq")
        return lax.ppermute(value, "seq", [(i, (i + step) % size) for i in range(size)])
    size = lax.axis_size("dp")
    return lax.ppermute(value, "dp", [(i, (i + 2 * step) % size) for i in range(size)])


def swap(value):
    return lax.ppermute(value, "dp", [(i, i ^ 1) for i in range(lax.axis_size("dp"))])


def ring_gather(block, axis, size):
    blocks = [block]
    for _ in range(size - 1):
        blocks.append(shift(blocks[-1], axis))
    return blocks


def ring_reduce(blocks, axis):
    total = blocks[-1] if len(blocks) > 1 else blocks[0]
    size = len(blocks)
    for k in range(size - 1, 0, -1):
        total = shift(total.astype(BF16), axis, -1).astype(F32) + blocks[k - 1]
    return total


def attend_kernel(index_ref, named_ref, q_ref, g_ref, kv_ref, live_ref, *rest):
    dq_ref, grad_ref = rest[-2:]
    named = named_ref[pl.program_id(0)]
    heads = q_ref.shape[-1] // HD
    scale = HD ** (-0.5)

    @pl.when(named == 0)
    def _():
        dq_ref[...] = jnp.zeros_like(dq_ref)
        grad_ref[...] = jnp.zeros_like(grad_ref)

    @pl.when(named != 0)
    def _():
        live = live_ref[0] > 0.5
        zero = jnp.zeros((SPAN, HD), BF16)

        def diagonal(ref, start):
            one = ref[0, :, start:start + HD]
            two = ref[0, :, start + HD:start + 2 * HD]
            return jnp.concatenate(
                [jnp.concatenate([one, zero], axis=1), jnp.concatenate([zero, two], axis=1)], axis=0
            )

        for pair in range(heads // 2):
            start = pair * 2 * HD
            columns = slice(start, start + 2 * HD)
            q_two = diagonal(q_ref, start)
            g_two = diagonal(g_ref, start)
            keys = kv_ref[0, 0, :, columns]
            values = kv_ref[0, 1, :, columns]
            scores = jnp.where(live, dot(keys, q_two, ((1,), (1,))) * scale, -1e30)
            top = jnp.max(scores, axis=0, keepdims=True)
            expo = jnp.exp(scores - top)
            probs = expo * (1.0 / jnp.sum(expo, axis=0, keepdims=True))
            grad_ref[0, 1, :, columns] = dot(probs.astype(BF16), g_two, ((1,), (0,))).astype(BF16)
            prob_grad = dot(values, g_two, ((1,), (1,)))
            center = jnp.sum(probs * prob_grad, axis=0, keepdims=True)
            score_grad = (probs * (prob_grad - center) * scale).astype(BF16)
            grad_ref[0, 0, :, columns] = dot(score_grad, q_two, ((1,), (0,))).astype(BF16)
            both = dot(score_grad, keys, ((0,), (0,)))
            dq_ref[0, :, columns] = jnp.concatenate(
                [both[:SPAN, :HD], both[SPAN:, HD:]], axis=1
            ).astype(BF16)


def attend(index, named, queries, grads, kv, live, source, pairs, before):
    capacity, _, keys, width = kv.shape
    table = jnp.concatenate([index, jnp.reshape(source * pairs, (1,))]).astype(jnp.int32)
    span_block = pl.BlockSpec((1, SPAN, width), lambda r, t, n: (t[r], 0, 0))
    kv_block = pl.BlockSpec((1, 2, keys, width), lambda r, t, n: (t[pairs] + r, 0, 0, 0))
    live_block = pl.BlockSpec((1, keys, HD), lambda r, t, n: (t[pairs] + r, 0, 0))
    in_specs = [span_block, span_block, kv_block, live_block]
    operands = [table, named.astype(jnp.int32), queries, grads, kv, live]
    aliases = {}
    if before is not None:
        in_specs.append(pl.BlockSpec(memory_space=pl.ANY))
        operands.append(before)
        aliases = {len(operands) - 1: 1}
    heads = width // HD
    return pl.pallas_call(
        attend_kernel,
        grid_spec=pltpu.PrefetchScalarGridSpec(
            num_scalar_prefetch=2,
            grid=(pairs,),
            in_specs=in_specs,
            out_specs=[span_block, kv_block],
        ),
        out_shape=[
            jax.ShapeDtypeStruct(queries.shape, BF16),
            jax.ShapeDtypeStruct(kv.shape, BF16),
        ],
        input_output_aliases=aliases,
        compiler_params=pltpu.CompilerParams(vmem_limit_bytes=32 * 1024 * 1024),
        cost_estimate=pl.CostEstimate(
            flops=pairs * heads * 5 * 2 * SPAN * keys * HD * 4,
            bytes_accessed=pairs * 4 * keys * width * 2,
            transcendentals=pairs * heads * SPAN * keys,
        ),
    )(*operands)


def on_device(span_act, q_weight, out_grad, neighbour_kv, neighbour_ids, owner):
    rows, width = out_grad.shape
    depth = q_weight.shape[0]
    seq_count = lax.axis_size("seq")
    dp_count = lax.axis_size("dp")
    tensor_count = lax.axis_size("tensor")
    couples = dp_count // 2
    seq_at = lax.axis_index("seq")
    dp_at = lax.axis_index("dp")
    core = dp_at % 2
    spans = rows // SPAN
    capacity = neighbour_kv.shape[0]
    pairs = capacity // seq_count
    per = span_act.shape[1] // depth // 2

    act = span_act.reshape(rows, per, 2, depth)
    act_mine = lax.dynamic_index_in_dim(act, core, 2, keepdims=False).reshape(rows, per * depth)
    act_other = lax.dynamic_index_in_dim(act, 1 - core, 2, keepdims=False).reshape(rows, per * depth)
    act_both = jnp.concatenate([act_mine, swap(act_other)], axis=0)
    acts = lax.all_gather(act_both, "tensor", axis=0)

    cut = depth // 2
    seq_first = [
        ring_gather(block, "dp", couples) for block in ring_gather(q_weight[:cut], "seq", seq_count)
    ]
    dp_first = [
        ring_gather(block, "seq", seq_count) for block in ring_gather(q_weight[cut:], "dp", couples)
    ]

    def block_at(i, j):
        block = ((seq_at - i) % seq_count) * dp_count + ((dp_at // 2 - j) % couples) * 2
        return block // (2 * per), (block % (2 * per)) // 2

    def act_block(i, j):
        at, inner = block_at(i, j)
        return lax.dynamic_slice(acts, (at, 0, inner * depth), (1, 2 * rows, depth))[0]

    places = [(i, j) for i in range(seq_count) for j in range(couples)]
    partial = jnp.zeros((2 * rows, width), F32)
    for i, j in places:
        block = act_block(i, j)
        partial = partial + dot(block[:, :cut], seq_first[i][j], ((1,), (0,)))
        partial = partial + dot(block[:, cut:], dp_first[j][i], ((1,), (0,)))
    queries = (partial[:rows] + swap(partial[rows:])).astype(BF16)

    groups = owner.reshape(seq_count, dp_count, spans)
    groups = lax.dynamic_index_in_dim(groups, dp_at, 1, keepdims=False)

    def order(group, target):
        names = (group == target).astype(jnp.int32)
        count = jnp.sum(names)
        place = jnp.where(
            names == 1, jnp.cumsum(names) - 1, count + jnp.cumsum(1 - names) - 1
        )
        at = jnp.arange(spans)
        index = jnp.sum(jnp.where(place[None, :] == at[:, None], at[None, :], 0), axis=1)
        return index[:pairs], (at < count)[:pairs]

    whole_blocks = pairs == spans
    live = jnp.broadcast_to(
        (neighbour_ids != 0).astype(F32)[:, :, None], (capacity, KEYS, HD)
    )
    mine = lax.dynamic_index_in_dim(groups, seq_at, 0, keepdims=False)

    def to_owner(value, step):
        value = value.reshape(spans, SPAN, width)
        if not whole_blocks:
            index, _ = order(mine, (seq_at + step) % seq_count)
            value = jnp.take(value, index, axis=0)
        return shift(value, "seq", step) if step else value

    kv_grad = None
    query_grad = jnp.zeros((spans, SPAN, width), BF16)
    for step in range(seq_count):
        source = (seq_at - step) % seq_count
        group = lax.dynamic_index_in_dim(groups, source, 0, keepdims=False)
        index, named = order(group, seq_at)
        if not whole_blocks:
            index = jnp.arange(pairs)
        back, kv_grad = attend(
            index,
            named,
            to_owner(queries, step),
            to_owner(out_grad, step),
            neighbour_kv,
            live,
            source,
            pairs,
            kv_grad,
        )
        if step:
            back = shift(back, "seq", -step)
        if not whole_blocks:
            index, named = order(mine, (seq_at + step) % seq_count)
            hit = (index[:, None] == jnp.arange(spans)[None, :]) & named[:, None]
            back = jnp.sum(
                jnp.where(hit[:, :, None, None], back[:, None], jnp.zeros((), BF16)), axis=0
            )
        query_grad = query_grad + back
    flat_grad = query_grad.reshape(rows, width)
    both_grad = jnp.concatenate([flat_grad, swap(flat_grad)], axis=0)

    act_parts = jnp.zeros((tensor_count, 2 * rows, per * depth), BF16)
    for i, j in places:
        at, inner = block_at(i, j)
        weights = jnp.concatenate([seq_first[i][j], dp_first[j][i]], axis=0)
        part = dot(both_grad, weights, ((1,), (1,))).astype(BF16)
        act_parts = lax.dynamic_update_slice(act_parts, part[None], (at, 0, inner * depth))
    act_sum = lax.psum_scatter(act_parts, "tensor", scatter_dimension=0, tiled=False)
    kept = act_sum[:rows].reshape(rows, per, depth)
    arrived = swap(act_sum[rows:]).reshape(rows, per, depth)
    even = jnp.where(core == 0, kept, arrived)
    odd = jnp.where(core == 0, arrived, kept)
    act_grad = jnp.stack([even, odd], axis=2).reshape(rows, span_act.shape[1])

    products = {}
    for i, j in reversed(places):
        products[i, j] = dot(act_block(i, j), both_grad, ((0,), (0,)))
    upper = ring_reduce(
        [
            ring_reduce([products[i, j][:cut] for j in range(couples)], "dp")
            for i in range(seq_count)
        ],
        "seq",
    )
    lower = ring_reduce(
        [
            ring_reduce([products[i, j][cut:] for i in range(seq_count)], "seq")
            for j in range(couples)
        ],
        "dp",
    )
    weight_grad = jnp.concatenate([upper, lower], axis=0)
    return (act_grad, weight_grad, kv_grad)


def solution(mesh):
    in_specs = (
        P(("seq", "dp"), "tensor"),
        P(("seq", "dp"), "tensor"),
        P(("seq", "dp"), "tensor"),
        P(("seq", "dp"), None, None, "tensor"),
        P(("seq", "dp"), None),
        P(),
    )
    out_specs = (
        P(("seq", "dp"), "tensor"),
        P(("seq", "dp"), "tensor"),
        P(("seq", "dp"), None, None, "tensor"),
    )
    return jax.shard_map(
        on_device, mesh=mesh, in_specs=in_specs, out_specs=out_specs, check_vma=False
    )
```

time: 479 us -> 274 us (0.57); the launches traced: 471 us -> 273 us
  blocking collectives: 136 us -> 0 us
  matrix products: 88.5 us -> 35.5 us
  local copies, waits for them, and re-layouts: 53.8 us -> 26 us
  starting transfers between devices: 7.65 us -> 27 us
  waiting for transfers between devices: 164 us -> 146 us
  other arithmetic: 7.44 us -> 17.5 us
  Pallas kernels: 0 us -> 6.05 us
    all_to_all x2 -> x0, blocking collectives: 136 us -> none  [the longest x1 128 us: on_device(): lax.all_to_all(slot_kv_grad.reshape(seq_count, pairs, 2, KEYS, width), 's...]
    all_to_all x1 -> x0, waiting for transfers between devices: 102 us -> none  [on_device(): lax.all_to_all(neighbour_kv.reshape(seq_count, pairs, 2, KEYS, width), 's...]
    ppermute x0 -> x19, waiting for transfers between devices: none -> 57.3 us  [the longest x9 55.2 us: shift(): lax.ppermute(value, 'seq', [(i, (i + step) % size) for i in range(size)])]
    dot_general x10 -> x16, matrix products: 88.5 us -> 35.5 us  [dot(): lax.dot_general(a, b, (contract, ((), ())), preferred_element_type=F32)]
    ppermute x0 -> x19, starting transfers between devices: none -> 26.9 us  [the longest x9 18.1 us: shift(): lax.ppermute(value, 'seq', [(i, (i + step) % size) for i in range(size)])]
    unnamed x20 -> x40, local copies, waits for them, and re-layouts: 32.3 us -> 11.1 us
    reduce_scatter x2 -> x1, waiting for transfers between devices: 21.5 us -> 37.7 us  [on_device(): lax.psum_scatter(act_parts, 'tensor', scatter_dimension=0, tiled=False)]
    all_gather x2 -> x1, waiting for transfers between devices: 38.8 us -> 51.3 us  [on_device(): acts = lax.all_gather(act_both, 'tensor', axis=0)]
  transfers between devices with their start and end apart: 5 -> 21, of which waited for: 3 -> 8; matrix products, arithmetic and copies ran while one was open for 21% -> 18% of each run, Pallas kernels for 0% -> 1%
where the time goes in v1:
time: 274 us; the launch traced here: 273 us
  waiting for transfers between devices  146 us (53%)
  matrix products  35.5 us (13%)
  starting transfers between devices  27 us (10%)
  local copies, waits for them, and re-layouts  26 us (9%)
  other arithmetic  17.5 us (6%)
  between operations  14.5 us (5%)
  Pallas kernels  6.05 us (2%)
    ppermute x9, waiting for transfers between devices, shift(): lax.ppermute(value, 'seq', [(i, (i + step) % size) for i in range(size)])  55.2 us
    all_gather x1, waiting for transfers between devices, on_device(): acts = lax.all_gather(act_both, 'tensor', axis=0)  51.3 us
    reduce_scatter x1, waiting for transfers between devices, on_device(): lax.psum_scatter(act_parts, 'tensor', scatter_dimension=0, tiled=False)  37.7 us
    dot_general x16, matrix products, dot(): lax.dot_general(a, b, (contract, ((), ())), preferred_element_type=F32)  35.5 us
    ppermute x9, starting transfers between devices, shift(): lax.ppermute(value, 'seq', [(i, (i + step) % size) for i in range(size)])  18.1 us
    unnamed x40, local copies, waits for them, and re-layouts  11.1 us
    ppermute x6, starting transfers between devices, shift(): lax.ppermute(value, 'dp', [(i, (i + 2 * step) % size) for i in range(size)])  8.05 us
    pallas_call x2, Pallas kernels, attend(): pl.pallas_call(attend_kernel, grid_spec=pltpu.PrefetchScalarGridSpec(num_...  6.05 us
  transfers between devices with their start and end apart: 21, of which 8 were waited for; matrix products, arithmetic and copies ran while one was open for 18% of the time, Pallas kernels for 1%

profile of v1, /device:TPU:0, one launch (start us, length us, event | category | flops | bytes accessed | tf_op | source)
XLA Modules:
  0.0 272.8 jit_solution(17537278445759475246)
XLA Ops:
  7.2 1.5 copy.16
  10.3 1.4 copy.17
  12.0 2.1 pad_maximum_fusion.1
  14.2 1.5 fusion.75
  15.7 2.9 %collective-permute-start.3 = (bf16[512,1024]{1,0:T(8,128)(2,1)}, bf16[512,1024]{1,0:T(8,128)(2,1)}, u32[]{:S(2)}, u32[]{:S(2)}) collective-permute-start(bf16[512,1024]{1,0:T(8,128)(2,1)} %get-tuple-element.30), channel_id=1, source_target_pairs={{0,16},{16,0},{1,17},{17,1},{2,18},{18,2},{3,19},{19,3},{4,20},{20... | collective-permute-start | bytes 3145736 | tf_op jit(solution)/shard_map/ppermute | solution.py:24
  18.5 1.5 collective-permute-start.2
  20.6 2.0 collective-permute-start.9
  23.3 19.4 %collective-permute-done.3 = bf16[512,1024]{1,0:T(8,128)(2,1)} collective-permute-done((bf16[512,1024]{1,0:T(8,128)(2,1)}, bf16[512,1024]{1,0:T(8,128)(2,1)}, u32[]{:S(2)}, u32[]{:S(2)}) %collective-permute-start.3) | collective-permute-done | bytes 1048608 | tf_op jit(solution)/shard_map/ppermute | solution.py:24
  42.8 2.1 collective-permute-start.5
  44.9 1.5 collective-permute-start.6
  46.4 51.3 %all-gather.3.cloned.1.call-done = bf16[2048,1024]{1,0:T(8,128)(2,1)} async-done(((bf16[512,1024]{1,0:T(8,128)(2,1)}), bf16[2048,1024]{1,0:T(8,128)(2,1)}) %all-gather.3.cloned.1.call-update) | async-done | bytes 4194320 | tf_op jit(solution)/shard_map/all_gather | solution.py:148
  97.6 2.9 %dynamic-slice_bitcast_fusion.3 = (bf16[512,1024]{1,0:T(8,128)(2,1)S(1)}, bf16[512,1024]{1,0:T(8,128)(2,1)S(1)}, bf16[512,1024]{1,0:T(8,128)(2,1)S(1)}, bf16[512,1024]{1,0:T(8,128)(2,1)S(1)}) fusion(bf16[4,512,1024]{2,1,0:T(8,128)(2,1)} %bitcast.86, s32[]{:T(128)S(6)} %select_n.244, s32[]{:T(128)S(6)} %select_n.252, s32[]{:T(128)S(6)} %select_n.250, ...), kind=kLoop, calls=%fused_computation.45 | loop fusion | bytes 8388624 | tf_op jit(solution)/shard_map/squeeze | solution.py:164
  102.0 1.9 fusion.54
  104.0 1.9 fusion.56
  105.9 1.9 fusion.58
  107.9 1.9 fusion.52
  109.8 1.9 fusion.50
  111.8 2.4 add_add_fusion
  114.2 1.3 copy-done.8
  120.0 1.7 fusion.45
  121.7 1.6 collective-permute-start.8
  123.7 3.4 %copy-done = bf16[8,2,256,1024]{3,2,1,0:T(8,128)(2,1)S(1)} copy-done((bf16[8,2,256,1024]{3,2,1,0:T(8,128)(2,1)S(1)}, bf16[8,2,256,1024]{3,2,1,0:T(8,128)(2,1)}, u32[]{:S(2)}) %copy-start) | copy-done | bytes 8388632
  127.1 3.0 %shard_map.85 = (bf16[4,64,1024]{2,1,0:T(8,128)(2,1)S(1)}, bf16[8,2,256,1024]{3,2,1,0:T(8,128)(2,1)}) custom-call(s32[5]{0:T(128)S(1)} %pad_add_fusion.index_ref, s32[4]{0:T(128)S(1)} %compare_convert_fusion.3.named_ref, bf16[4,64,1024]{2,1,0:T(8,128)(2,1)S(1)} %bitcast.74, bf16[4,64,1024]{2,1,0:T(8,128)(2,1)S(1)} %bitcast.76, ...), custom_call_target="tpu_custom_call" | custom-call | flops 2684354560 | bytes 8388608 | tf_op jit(solution)/shard_map/pallas_call | solution.py:107
  130.1 6.0 %collective-permute-done.8.q_ref = bf16[4,64,1024]{2,1,0:T(8,128)(2,1)S(1)} collective-permute-done((bf16[4,64,1024]{2,1,0:T(8,128)(2,1)S(1)}, bf16[4,64,1024]{2,1,0:T(8,128)(2,1)S(1)}, u32[]{:S(2)}, u32[]{:S(2)}) %collective-permute-start.8) | collective-permute-done | bytes 524320 | tf_op jit(solution)/shard_map/ppermute | solution.py:24
  136.1 3.4 %copy-done.1 = bf16[8,2,256,1024]{3,2,1,0:T(8,128)(2,1)S(1)} copy-done((bf16[8,2,256,1024]{3,2,1,0:T(8,128)(2,1)S(1)}, bf16[8,2,256,1024]{3,2,1,0:T(8,128)(2,1)}, u32[]{:S(2)}) %copy-start.1) | copy-done | bytes 8388632
  139.5 3.0 %shard_map.86 = (bf16[4,64,1024]{2,1,0:T(8,128)(2,1)S(1)}, bf16[8,2,256,1024]{3,2,1,0:T(8,128)(2,1)}) custom-call(s32[5]{0:T(128)S(1)} %pad_add_fusion.1.index_ref, s32[4]{0:T(128)S(1)} %compare_convert_fusion.1.named_ref, bf16[4,64,1024]{2,1,0:T(8,128)(2,1)S(1)} %collective-permute-done.8.q_ref, ...), custom_call_target="tpu_custom_call", output_to_operand_aliasing={{1}: (6, {})} | custom-call | flops 2684354560 | bytes 8388608 | tf_op jit(solution)/shard_map/pallas_call | solution.py:107
  142.5 7.7 %collective-permute-start.10 = (bf16[4,64,1024]{2,1,0:T(8,128)(2,1)S(1)}, bf16[4,64,1024]{2,1,0:T(8,128)(2,1)S(1)}, u32[]{:S(2)}, u32[]{:S(2)}) collective-permute-start(bf16[4,64,1024]{2,1,0:T(8,128)(2,1)S(1)} %get-tuple-element.9), channel_id=1, source_target_pairs={{0,16},{16,0},{1,17},{17,1},{2,18},{18,2},{3,19},{19,3},{4,20},{20... | collective-permute-start | bytes 1572872 | tf_op jit(solution)/shard_map/ppermute | solution.py:24
  150.3 12.8 %collective-permute-done.10 = bf16[4,64,1024]{2,1,0:T(8,128)(2,1)S(1)} collective-permute-done((bf16[4,64,1024]{2,1,0:T(8,128)(2,1)S(1)}, bf16[4,64,1024]{2,1,0:T(8,128)(2,1)S(1)}, u32[]{:S(2)}, u32[]{:S(2)}) %collective-permute-start.10) | collective-permute-done | bytes 524320 | tf_op jit(solution)/shard_map/ppermute | solution.py:24
  163.4 1.8 collective-permute-done.11
  165.2 2.5 broadcast_in_dim.45
  167.8 2.3 fusion.26
  170.0 3.8 %fusion.30 = bf16[4,512,1024]{2,1,0:T(8,128)(2,1)} fusion(bf16[4,512,1024]{2,1,0:T(8,128)(2,1)} %fusion.26, s32[]{:T(128)S(6)} %select_n.247, bf16[512,1024]{1,0:T(8,128)(2,1)} %collective-permute-done.2, bf16[512,1024]{1,0:T(8,128)(2,1)} %collective-permute-done.1, bf16[256,1024]{1,0:T(8,128)(2,1)S(1)} %collective-permute-done.11, ...), kind=kOutput, calls=%fused_computation.32 | convolution fusion | flops 1080557568 | bytes 4194308 | tf_op jit(solution)/shard_map/dot_general | solution.py:18
  173.8 3.8 %fusion.36 = bf16[4,512,1024]{2,1,0:T(8,128)(2,1)} fusion(bf16[4,512,1024]{2,1,0:T(8,128)(2,1)} %fusion.30, s32[]{:T(128)S(6)} %select_n.250, bf16[512,1024]{1,0:T(8,128)(2,1)} %collective-permute-done.4, bf16[512,1024]{1,0:T(8,128)(2,1)} %collective-permute-done.3, bf16[256,1024]{1,0:T(8,128)(2,1)S(1)} %collective-permute-done.11, ...), kind=kOutput, calls=%fused_computation.34 | convolution fusion | flops 1080557568 | bytes 4194308 | tf_op jit(solution)/shard_map/dot_general | solution.py:18
  177.6 3.8 %fusion.42 = bf16[4,512,1024]{2,1,0:T(8,128)(2,1)} fusion(bf16[4,512,1024]{2,1,0:T(8,128)(2,1)} %fusion.36, s32[]{:T(128)S(6)} %select_n.252, bf16[512,1024]{1,0:T(8,128)(2,1)} %collective-permute-done.6, bf16[512,1024]{1,0:T(8,128)(2,1)} %collective-permute-done.5, bf16[256,1024]{1,0:T(8,128)(2,1)S(1)} %collective-permute-done.11, ...), kind=kOutput, calls=%fused_computation.36 | convolution fusion | flops 1080557568 | bytes 4194308 | tf_op jit(solution)/shard_map/dot_general | solution.py:18
  181.5 2.5 convolution_convert_fusion
  184.6 1.9 collective-permute-start.13
  186.5 1.3 fusion.71
  189.3 1.3 fusion.70
  191.8 1.5 collective-permute-start.15
  193.3 17.0 %collective-permute-done.16 = bf16[512,1024]{1,0:T(8,128)(2,1)S(1)} collective-permute-done((bf16[512,1024]{1,0:T(8,128)(2,1)S(1)}, bf16[512,1024]{1,0:T(8,128)(2,1)S(1)}, u32[]{:S(2)}, u32[]{:S(2)}) %collective-permute-start.16) | collective-permute-done | bytes 1048608 | tf_op jit(solution)/shard_map/ppermute | solution.py:24
  210.3 1.4 fusion.1
  212.2 1.3 fusion.3
  213.5 1.7 collective-permute-start.14
  215.2 3.2 %fusion.69 = f32[1024,1024]{1,0:T(8,128)} fusion(bf16[512,1024]{1,0:T(8,128)(2,1)S(1)} %get-tuple-element.23, bf16[256,1024]{1,0:T(8,128)(2,1)S(1)} %copy-done.14, bf16[256,1024]{1,0:T(8,128)(2,1)S(1)} %bitcast.85), kind=kOutput, calls=%fused_computation.90 | convolution fusion | flops 1075838976 | bytes 6291456 | tf_op jit(solution)/shard_map/dot_general | solution.py:18
  218.4 37.7 %reduce-scatter.2.cloned.1.call-done = bf16[1,512,1024]{2,1,0:T(8,128)(2,1)} async-done(((bf16[4,512,1024]{2,1,0:T(8,128)(2,1)}), bf16[1,512,1024]{2,1,0:T(8,128)(2,1)}) %reduce-scatter.2.cloned.1.call-update) | async-done | bytes 1048592 | tf_op jit(solution)/shard_map/reduce_scatter | solution.py:237
  257.3 4.2 %fusion.2 = (f32[512,1024]{1,0:T(8,128)S(1)}, f32[512,1024]{1,0:T(8,128)S(1)}) fusion(f32[1024,1024]{1,0:T(8,128)} %fusion.69, bf16[512,1024]{1,0:T(8,128)(2,1)S(1)} %collective-permute-done.15, bf16[512,1024]{1,0:T(8,128)(2,1)} %collective-permute-done.14, bf16[512,1024]{1,0:T(8,128)(2,1)} %collective-permute-done.18, ...), kind=kLoop, calls=%fused_computation.7 | loop fusion | flops 4194304 | bytes 12582912 | tf_op jit(solution)/shard_map/add | solution.py:44
  261.5 2.3 pad_maximum_fusion
  264.6 1.4 copy.20
  (92 shorter events, 15.7 us)
Async XLA Ops:
  7.2 90.5 %all-gather.3.cloned.1.call-start = ((), (), s32[]{:S(2)}) async-start(), calls=%async_computation.2 | async-start | bytes 5242880 | tf_op jit(solution)/shard_map/all_gather | solution.py:148
  9.8 2.2 collective-permute-start
  10.3 3.8 %copy-start.5 = (bf16[1024,1024]{1,0:T(8,128)(2,1)S(1)}, bf16[1024,1024]{1,0:T(8,128)(2,1)}, u32[]{:S(2)}) copy-start(bf16[1024,1024]{1,0:T(8,128)(2,1)} %param.7) | copy-start | bytes 6291460
  14.1 6.5 %copy-start.2 = (bf16[256,1024]{1,0:T(8,128)(2,1)S(1)}, bf16[256,1024]{1,0:T(8,128)(2,1)}, u32[]{:S(2)}) copy-start(bf16[256,1024]{1,0:T(8,128)(2,1)} %param.8) | copy-start | bytes 1572868
  14.1 8.5 %copy-start.18 = (s32[32]{0:T(128)S(1)}, s32[32]{0:T(128)}, u32[]{:S(2)}) copy-start(s32[32]{0:T(128)} %param.11) | copy-start | bytes 388
  14.1 242.0 %reduce-scatter.2.cloned.1.call-start = ((), (), s32[]{:S(2)}) async-start(), calls=%async_computation.1 | async-start | bytes 5242880 | tf_op jit(solution)/shard_map/reduce_scatter | solution.py:237
  15.7 27.1 %collective-permute-start.3 = (bf16[512,1024]{1,0:T(8,128)(2,1)}, bf16[512,1024]{1,0:T(8,128)(2,1)}, u32[]{:S(2)}, u32[]{:S(2)}) collective-permute-start(bf16[512,1024]{1,0:T(8,128)(2,1)} %get-tuple-element.30), channel_id=1, source_target_pairs={{0,16},{16,0},{1,17},{17,1},{2,18},{18,2},{3,19},{19,3},{4,20},{20... | collective-permute-start | bytes 3145736 | tf_op jit(solution)/shard_map/ppermute | solution.py:24
  18.5 26.4 %collective-permute-start.2 = (bf16[512,1024]{1,0:T(8,128)(2,1)}, bf16[512,1024]{1,0:T(8,128)(2,1)}, u32[]{:S(2)}, u32[]{:S(2)}) collective-permute-start(bf16[512,1024]{1,0:T(8,128)(2,1)} %get-tuple-element.29), channel_id=1, source_target_pairs={{0,2},{1,3},{2,0},{3,1},{4,6},{5,7},{6,4},{7,5},{8,10},{9,11},{10,... | collective-permute-start | bytes 3145736 | tf_op jit(solution)/shard_map/ppermute | solution.py:26
  20.0 85.9 %collective-permute-start.1 = (bf16[512,1024]{1,0:T(8,128)(2,1)}, bf16[512,1024]{1,0:T(8,128)(2,1)}, u32[]{:S(2)}, u32[]{:S(2)}) collective-permute-start(bf16[512,1024]{1,0:T(8,128)(2,1)} %get-tuple-element.30), channel_id=1, source_target_pairs={{0,2},{1,3},{2,0},{3,1},{4,6},{5,7},{6,4},{7,5},{8,10},{9,11},{10,... | collective-permute-start | bytes 3145736 | tf_op jit(solution)/shard_map/ppermute | solution.py:26
  20.6 87.3 %collective-permute-start.4 = (bf16[512,1024]{1,0:T(8,128)(2,1)}, bf16[512,1024]{1,0:T(8,128)(2,1)}, u32[]{:S(2)}, u32[]{:S(2)}) collective-permute-start(bf16[512,1024]{1,0:T(8,128)(2,1)} %get-tuple-element.29), channel_id=1, source_target_pairs={{0,16},{16,0},{1,17},{17,1},{2,18},{18,2},{3,19},{19,3},{4,20},{20... | collective-permute-start | bytes 3145736 | tf_op jit(solution)/shard_map/ppermute | solution.py:24
  20.6 109.5 %collective-permute-start.9 = (bf16[4,64,1024]{2,1,0:T(8,128)(2,1)S(1)}, bf16[4,64,1024]{2,1,0:T(8,128)(2,1)S(1)}, u32[]{:S(2)}, u32[]{:S(2)}) collective-permute-start(bf16[4,64,1024]{2,1,0:T(8,128)(2,1)S(1)} %bitcast.75), channel_id=1, source_target_pairs={{0,16},{16,0},{1,17},{17,1},{2,18},{18,2},{3,19},{19,3},{4,20},{20... | collective-permute-start | bytes 1572872 | tf_op jit(solution)/shard_map/ppermute | solution.py:24
  42.8 67.1 %collective-permute-start.5 = (bf16[512,1024]{1,0:T(8,128)(2,1)}, bf16[512,1024]{1,0:T(8,128)(2,1)}, u32[]{:S(2)}, u32[]{:S(2)}) collective-permute-start(bf16[512,1024]{1,0:T(8,128)(2,1)} %collective-permute-done.3), channel_id=1, source_target_pairs={{0,2},{1,3},{2,0},{3,1},{4,6},{5,7},{6,4},{7,5},{8,10},{9,11},{10,... | collective-permute-start | bytes 3145736 | tf_op jit(solution)/shard_map/ppermute | solution.py:26
  44.9 66.9 %collective-permute-start.6 = (bf16[512,1024]{1,0:T(8,128)(2,1)}, bf16[512,1024]{1,0:T(8,128)(2,1)}, u32[]{:S(2)}, u32[]{:S(2)}) collective-permute-start(bf16[512,1024]{1,0:T(8,128)(2,1)} %collective-permute-done.2), channel_id=1, source_target_pairs={{0,16},{16,0},{1,17},{17,1},{2,18},{18,2},{3,19},{19,3},{4,20},{20... | collective-permute-start | bytes 3145736 | tf_op jit(solution)/shard_map/ppermute | solution.py:24
  97.6 2.9 %copy-start.6 = (bf16[1024,1024]{1,0:T(8,128)(2,1)S(1)}, bf16[1024,1024]{1,0:T(8,128)(2,1)}, u32[]{:S(2)}) copy-start(bf16[1024,1024]{1,0:T(8,128)(2,1)} %param.7) | copy-start | bytes 6291460
  100.6 7.3 %copy-start.3 = (bf16[512,1024]{1,0:T(8,128)(2,1)}, bf16[512,1024]{1,0:T(8,128)(2,1)S(1)}, u32[]{:S(2)}) copy-start(bf16[512,1024]{1,0:T(8,128)(2,1)S(1)} %get-tuple-element.25) | copy-start | bytes 3145732
  100.6 11.2 %copy-start.15 = (bf16[512,1024]{1,0:T(8,128)(2,1)}, bf16[512,1024]{1,0:T(8,128)(2,1)S(1)}, u32[]{:S(2)}) copy-start(bf16[512,1024]{1,0:T(8,128)(2,1)S(1)} %get-tuple-element.24) | copy-start | bytes 3145732
  114.2 1.3 copy-start.8
  115.5 7.8 %copy-start.17 = (s32[8,256]{1,0:T(8,128)S(1)}, s32[8,256]{1,0:T(8,128)}, u32[]{:S(2)}) copy-start(s32[8,256]{1,0:T(8,128)} %param.10) | copy-start | bytes 24580
  116.6 3.5 %collective-permute-start.7 = (f32[256,1024]{1,0:T(8,128)}, f32[256,1024]{1,0:T(8,128)}, u32[]{:S(2)}, u32[]{:S(2)}) collective-permute-start(f32[256,1024]{1,0:T(8,128)} %slice.107), channel_id=1, source_target_pairs={{0,1},{1,0},{2,3},{3,2},{4,5},{5,4},{6,7},{7,6},{8,9},{9,8},{10,11... | collective-permute-start | bytes 3145736 | tf_op jit(solution)/shard_map/ppermute | solution.py:30
  121.7 14.4 %collective-permute-start.8 = (bf16[4,64,1024]{2,1,0:T(8,128)(2,1)S(1)}, bf16[4,64,1024]{2,1,0:T(8,128)(2,1)S(1)}, u32[]{:S(2)}, u32[]{:S(2)}) collective-permute-start(bf16[4,64,1024]{2,1,0:T(8,128)(2,1)S(1)} %bitcast.73), channel_id=1, source_target_pairs={{0,16},{16,0},{1,17},{17,1},{2,18},{18,2},{3,19},{19,3},{4,20},{20... | collective-permute-start | bytes 1572872 | tf_op jit(solution)/shard_map/ppermute | solution.py:24
  123.7 3.4 %copy-start = (bf16[8,2,256,1024]{3,2,1,0:T(8,128)(2,1)S(1)}, bf16[8,2,256,1024]{3,2,1,0:T(8,128)(2,1)}, u32[]{:S(2)}) copy-start(bf16[8,2,256,1024]{3,2,1,0:T(8,128)(2,1)} %kv_ref.3) | copy-start | bytes 25165828
  136.1 3.4 %copy-start.1 = (bf16[8,2,256,1024]{3,2,1,0:T(8,128)(2,1)S(1)}, bf16[8,2,256,1024]{3,2,1,0:T(8,128)(2,1)}, u32[]{:S(2)}) copy-start(bf16[8,2,256,1024]{3,2,1,0:T(8,128)(2,1)} %kv_ref.3) | copy-start | bytes 25165828
  142.5 20.5 %collective-permute-start.10 = (bf16[4,64,1024]{2,1,0:T(8,128)(2,1)S(1)}, bf16[4,64,1024]{2,1,0:T(8,128)(2,1)S(1)}, u32[]{:S(2)}, u32[]{:S(2)}) collective-permute-start(bf16[4,64,1024]{2,1,0:T(8,128)(2,1)S(1)} %get-tuple-element.9), channel_id=1, source_target_pairs={{0,16},{16,0},{1,17},{17,1},{2,18},{18,2},{3,19},{19,3},{4,20},{20... | collective-permute-start | bytes 1572872 | tf_op jit(solution)/shard_map/ppermute | solution.py:24
  163.2 18.2 %copy-start.9 = (bf16[4,64,1024]{2,1,0:T(8,128)(2,1)}, bf16[4,64,1024]{2,1,0:T(8,128)(2,1)S(1)}, u32[]{:S(2)}) copy-start(bf16[4,64,1024]{2,1,0:T(8,128)(2,1)S(1)} %add.267) | copy-start | bytes 1572868
  163.2 4.5 %copy-start.7 = (bf16[1024,1024]{1,0:T(8,128)(2,1)S(1)}, bf16[1024,1024]{1,0:T(8,128)(2,1)}, u32[]{:S(2)}) copy-start(bf16[1024,1024]{1,0:T(8,128)(2,1)} %param.7) | copy-start | bytes 6291460
  163.2 2.0 collective-permute-start.11
  165.2 16.2 %copy-start.12 = (bf16[256,1024]{1,0:T(8,128)(2,1)}, bf16[256,1024]{1,0:T(8,128)(2,1)S(1)}, u32[]{:S(2)}) copy-start(bf16[256,1024]{1,0:T(8,128)(2,1)S(1)} %collective-permute-done.11) | copy-start | bytes 1572868
  184.0 2.5 copy-start.4
  184.0 2.5 copy-start.10
  184.0 2.5 copy-start.13
  184.2 26.1 %collective-permute-start.16 = (bf16[512,1024]{1,0:T(8,128)(2,1)S(1)}, bf16[512,1024]{1,0:T(8,128)(2,1)S(1)}, u32[]{:S(2)}, u32[]{:S(2)}) collective-permute-start(bf16[512,1024]{1,0:T(8,128)(2,1)S(1)} %get-tuple-element.28), channel_id=1, source_target_pairs={{0,16},{16,0},{1,17},{17,1},{2,18},{18,2},{3,19},{19,3},{4,20},{20... | collective-permute-start | bytes 3145736 | tf_op jit(solution)/shard_map/ppermute | solution.py:24
  184.6 27.6 %collective-permute-start.13 = (bf16[512,1024]{1,0:T(8,128)(2,1)S(1)}, bf16[512,1024]{1,0:T(8,128)(2,1)S(1)}, u32[]{:S(2)}, u32[]{:S(2)}) collective-permute-start(bf16[512,1024]{1,0:T(8,128)(2,1)S(1)} %get-tuple-element.27), channel_id=1, source_target_pairs={{0,2},{1,3},{2,0},{3,1},{4,6},{5,7},{6,4},{7,5},{8,10},{9,11},{10,... | collective-permute-start | bytes 3145736 | tf_op jit(solution)/shard_map/ppermute | solution.py:26
  189.0 68.3 %collective-permute-start.18 = (bf16[512,1024]{1,0:T(8,128)(2,1)}, bf16[512,1024]{1,0:T(8,128)(2,1)}, u32[]{:S(2)}, u32[]{:S(2)}) collective-permute-start(bf16[512,1024]{1,0:T(8,128)(2,1)} %slice.163), channel_id=1, source_target_pairs={{0,16},{16,0},{1,17},{17,1},{2,18},{18,2},{3,19},{19,3},{4,20},{20... | collective-permute-start | bytes 3145736 | tf_op jit(solution)/shard_map/ppermute | solution.py:24
  191.8 65.5 %collective-permute-start.15 = (bf16[512,1024]{1,0:T(8,128)(2,1)}, bf16[512,1024]{1,0:T(8,128)(2,1)S(1)}, u32[]{:S(2)}, u32[]{:S(2)}) collective-permute-start(bf16[512,1024]{1,0:T(8,128)(2,1)} %slice.164), channel_id=1, source_target_pairs={{0,2},{1,3},{2,0},{3,1},{4,6},{5,7},{6,4},{7,5},{8,10},{9,11},{10,... | collective-permute-start | bytes 3145736 | tf_op jit(solution)/shard_map/ppermute | solution.py:26
  211.6 3.6 %copy-start.11 = (bf16[4,64,1024]{2,1,0:T(8,128)(2,1)S(1)}, bf16[4,64,1024]{2,1,0:T(8,128)(2,1)}, u32[]{:S(2)}) copy-start(bf16[4,64,1024]{2,1,0:T(8,128)(2,1)} %copy-done.9) | copy-start | bytes 1572868
  211.6 3.6 %copy-start.14 = (bf16[256,1024]{1,0:T(8,128)(2,1)S(1)}, bf16[256,1024]{1,0:T(8,128)(2,1)}, u32[]{:S(2)}) copy-start(bf16[256,1024]{1,0:T(8,128)(2,1)} %copy-done.12) | copy-start | bytes 1572868
  211.6 45.7 %collective-permute-start.17 = (bf16[512,1024]{1,0:T(8,128)(2,1)}, bf16[512,1024]{1,0:T(8,128)(2,1)}, u32[]{:S(2)}, u32[]{:S(2)}) collective-permute-start(bf16[512,1024]{1,0:T(8,128)(2,1)} %fusion.1), channel_id=1, source_target_pairs={{0,2},{1,3},{2,0},{3,1},{4,6},{5,7},{6,4},{7,5},{8,10},{9,11},{10,... | collective-permute-start | bytes 3145736 | tf_op jit(solution)/shard_map/ppermute | solution.py:26
  213.5 43.8 %collective-permute-start.14 = (bf16[512,1024]{1,0:T(8,128)(2,1)}, bf16[512,1024]{1,0:T(8,128)(2,1)}, u32[]{:S(2)}, u32[]{:S(2)}) collective-permute-start(bf16[512,1024]{1,0:T(8,128)(2,1)} %fusion.3), channel_id=1, source_target_pairs={{0,16},{16,0},{1,17},{17,1},{2,18},{18,2},{3,19},{19,3},{4,20},{20... | collective-permute-start | bytes 3145736 | tf_op jit(solution)/shard_map/ppermute | solution.py:24
  257.2 6.6 %collective-permute-start.12 = (bf16[256,1024]{1,0:T(8,128)(2,1)S(1)}, bf16[256,1024]{1,0:T(8,128)(2,1)S(1)}, u32[]{:S(2)}, u32[]{:S(2)}) collective-permute-start(bf16[256,1024]{1,0:T(8,128)(2,1)S(1)} %slice_bitcast_fusion), channel_id=1, source_target_pairs={{0,1},{1,0},{2,3},{3,2},{4,5},{5,4},{6,7},{7,6},{8,9},{9,8},{10,11... | collective-permute-start | bytes 1572872 | tf_op jit(solution)/shard_map/ppermute | solution.py:30
  261.5 2.3 copy-start.16
Sparse Core Ops, SparseCore 0:
  14.2 83.3 all-gather.2
  181.6 74.5 reduce-scatter.1

commit v2 on v1

v2 whole, which is shorter than its diff:
```python
import functools

import jax
import jax.numpy as jnp
from jax import lax
from jax.experimental import pallas as pl
from jax.experimental.pallas import tpu as pltpu
from jax.sharding import PartitionSpec as P

HD = 128
SPAN = 64
KEYS = 256
F32 = jnp.float32
BF16 = jnp.bfloat16


def dot(a, b, contract):
    return lax.dot_general(a, b, (contract, ((), ())), preferred_element_type=F32)


def shift(value, axis, step=1):
    stride = 2 if axis == "dp" else 1
    size = lax.axis_size(axis)
    return lax.ppermute(value, axis, [(i, (i + step * stride) % size) for i in range(size)])


def swap(value):
    return lax.ppermute(value, "dp", [(i, i ^ 1) for i in range(lax.axis_size("dp"))])


def ring_gather(block, axis, size):
    blocks = [block]
    for _ in range(size - 1):
        blocks.append(shift(blocks[-1], axis))
    return blocks


def ring_reduce(blocks, axis):
    total = blocks[-1].astype(F32)
    for block in blocks[-2::-1]:
        total = shift(total.astype(BF16), axis, -1).astype(F32) + block.astype(F32)
    return total


def product_kernel(count, table_ref, *refs):
    blocks, weight_ref, out_ref = refs[:count], refs[count], refs[count + 1]
    tile = min(256, out_ref.shape[1])

    @pl.loop(0, out_ref.shape[1] // tile)
    def _(step):
        columns = pl.ds(pl.multiple_of(step * tile, tile), tile)
        total = None
        for k in range(count):
            part = dot(blocks[k][...], weight_ref[table_ref[k], :, columns], ((1,), (0,)))
            total = part if total is None else total + part
        out_ref[:, columns] = total


def product(blocks, weights, table):
    count, (rows, depth), width = len(blocks), blocks[0].shape, weights.shape[2]
    return pl.pallas_call(
        functools.partial(product_kernel, count),
        out_shape=jax.ShapeDtypeStruct((rows, width), F32),
        in_specs=[pl.BlockSpec(memory_space=pltpu.SMEM)]
        + [pl.BlockSpec(memory_space=pltpu.VMEM)] * (count + 1),
        out_specs=pl.BlockSpec(memory_space=pltpu.VMEM),
        compiler_params=pltpu.CompilerParams(vmem_limit_bytes=24 * 1024 * 1024),
        cost_estimate=pl.CostEstimate(
            flops=2 * rows * count * depth * width,
            bytes_accessed=2 * count * depth * (rows + width) + 4 * rows * width,
            transcendentals=0,
        ),
    )(table, *blocks, weights)


def attend_kernel(table_ref, q_ref, g_ref, kv_ref, live_ref, *rest):
    dq_ref, grad_ref = rest[-2:]
    count = pl.num_programs(0)
    named = table_ref[count + pl.program_id(0)]
    pairs = q_ref.shape[-1] // HD // 2
    scale = HD ** (-0.5)

    @pl.when(named == 0)
    def _():
        dq_ref[...] = jnp.zeros_like(dq_ref)
        grad_ref[...] = jnp.zeros_like(grad_ref)

    @pl.when(named != 0)
    def _():
        live = live_ref[0] > 0.5
        zero = jnp.zeros((SPAN, HD), BF16)

        def diagonal(ref, start):
            one = ref[0, :, start:start + HD]
            two = ref[0, :, start + HD:start + 2 * HD]
            return jnp.concatenate(
                [jnp.concatenate([one, zero], axis=1), jnp.concatenate([zero, two], axis=1)], axis=0
            )

        def first(pair):
            start = pair * 2 * HD
            columns = slice(start, start + 2 * HD)
            scores = dot(kv_ref[0, 0, :, columns], diagonal(q_ref, start), ((1,), (1,)))
            prob_grad = dot(kv_ref[0, 1, :, columns], diagonal(g_ref, start), ((1,), (1,)))
            return scores, prob_grad

        ahead = first(0)
        for pair in range(pairs):
            scores, prob_grad = ahead
            if pair + 1 < pairs:
                ahead = first(pair + 1)
            start = pair * 2 * HD
            columns = slice(start, start + 2 * HD)
            scores = jnp.where(live, scores * scale, -1e30)
            expo = jnp.exp(scores - jnp.max(scores, axis=0, keepdims=True))
            probs = expo * (1.0 / jnp.sum(expo, axis=0, keepdims=True))
            center = jnp.sum(probs * prob_grad, axis=0, keepdims=True)
            score_grad = (probs * (prob_grad - center) * scale).astype(BF16)
            value_grad = dot(probs.astype(BF16), diagonal(g_ref, start), ((1,), (0,)))
            key_grad = dot(score_grad, diagonal(q_ref, start), ((1,), (0,)))
            both = dot(score_grad, kv_ref[0, 0, :, columns], ((0,), (0,)))
            grad_ref[0, 1, :, columns] = value_grad.astype(BF16)
            grad_ref[0, 0, :, columns] = key_grad.astype(BF16)
            dq_ref[0, :, columns] = jnp.concatenate(
                [both[:SPAN, :HD], both[SPAN:, HD:]], axis=1
            ).astype(BF16)


def attend(slots, named, queries, grads, kv, live, before):
    count, _, width = queries.shape
    keys = kv.shape[2]
    heads = width // HD
    table = jnp.concatenate([slots, named]).astype(jnp.int32)
    span_block = pl.BlockSpec((1, SPAN, width), lambda r, t: (r, 0, 0))
    kv_block = pl.BlockSpec((1, 2, keys, width), lambda r, t: (t[r], 0, 0, 0))
    live_block = pl.BlockSpec((1, keys, HD), lambda r, t: (t[r], 0, 0))
    in_specs = [span_block, span_block, kv_block, live_block]
    operands = [table, queries, grads, kv, live]
    aliases = {}
    if before is not None:
        in_specs.append(pl.BlockSpec(memory_space=pl.ANY))
        operands.append(before)
        aliases = {len(operands) - 1: 1}
    return pl.pallas_call(
        attend_kernel,
        grid_spec=pltpu.PrefetchScalarGridSpec(
            num_scalar_prefetch=1,
            grid=(count,),
            in_specs=in_specs,
            out_specs=[span_block, kv_block],
        ),
        out_shape=[
            jax.ShapeDtypeStruct(queries.shape, BF16),
            jax.ShapeDtypeStruct(kv.shape, BF16),
        ],
        input_output_aliases=aliases,
        compiler_params=pltpu.CompilerParams(vmem_limit_bytes=40 * 1024 * 1024),
        cost_estimate=pl.CostEstimate(
            flops=count * heads * 5 * 2 * SPAN * keys * HD * 4,
            bytes_accessed=count * 4 * keys * width * 2,
            transcendentals=count * heads * SPAN * keys,
        ),
    )(*operands)


def on_device(span_act, q_weight, out_grad, neighbour_kv, neighbour_ids, owner):
    rows, width = out_grad.shape
    depth = q_weight.shape[0]
    seq_count = lax.axis_size("seq")
    dp_count = lax.axis_size("dp")
    tensor_count = lax.axis_size("tensor")
    couples = dp_count // 2
    seq_at = lax.axis_index("seq")
    dp_at = lax.axis_index("dp")
    tensor_at = lax.axis_index("tensor")
    core = dp_at % 2
    spans = rows // SPAN
    capacity = neighbour_kv.shape[0]
    pairs = capacity // seq_count
    whole_blocks = pairs == spans
    chunks = 2 if whole_blocks and spans % 2 == 0 else 1
    chunk_rows = rows // chunks
    per = span_act.shape[1] // depth // 2
    cut = depth // 2

    def chunk_of(value, chunk):
        return value[chunk * chunk_rows:(chunk + 1) * chunk_rows]

    def columns_of(which):
        return jnp.concatenate(
            [
                lax.dynamic_slice(span_act, (0, (2 * p + which) * depth), (rows, depth))
                for p in range(per)
            ],
            axis=1,
        )

    act_mine, act_other = columns_of(core), columns_of(1 - core)
    acts = []
    for chunk in range(chunks):
        both = jnp.concatenate(
            [chunk_of(act_mine, chunk), swap(chunk_of(act_other, chunk))], axis=0
        )
        acts.append(ring_gather(both, "tensor", tensor_count))
    depth_blocks = [(tensor_at - k) % tensor_count for k in range(tensor_count)]
    table = jnp.stack(depth_blocks).astype(jnp.int32)

    seq_first = [
        ring_gather(block, "dp", couples) for block in ring_gather(q_weight[:cut], "seq", seq_count)
    ]
    dp_first = [
        ring_gather(block, "seq", seq_count) for block in ring_gather(q_weight[cut:], "dp", couples)
    ]

    def block_at(i, j):
        block = ((seq_at - i) % seq_count) * dp_count + ((dp_at // 2 - j) % couples) * 2
        return block // (2 * per), (block % (2 * per)) // 2

    places = [(i, j) for i in range(seq_count) for j in range(couples)]
    weights = jnp.zeros((tensor_count, per * depth, width), BF16)
    for i, j in places:
        at, inner = block_at(i, j)
        for piece, start in ((seq_first[i][j], 0), (dp_first[j][i], cut)):
            weights = lax.dynamic_update_slice(weights, piece[None], (at, inner * depth + start, 0))

    groups = owner.reshape(seq_count, dp_count, spans)
    groups = lax.dynamic_index_in_dim(groups, dp_at, 1, keepdims=False)
    mine = lax.dynamic_index_in_dim(groups, seq_at, 0, keepdims=False)

    def order(group, target):
        names = group == target
        at = jnp.arange(spans)
        ahead = (names[None, :] & ~names[:, None]) | (
            (names[None, :] == names[:, None]) & (at[None, :] < at[:, None])
        )
        return jnp.sum(ahead.astype(jnp.int32), axis=1), names.astype(jnp.int32)

    def message(target):
        place, names = order(mine, target)
        hit = place[None, :] == jnp.arange(pairs)[:, None]
        return hit & (names[None, :] == 1)

    def to_owner(value, step):
        value = value.reshape(-1, SPAN, width)
        if not whole_blocks:
            hit = message((seq_at + step) % seq_count)
            value = jnp.sum(
                jnp.where(hit[:, :, None, None], value[None], jnp.zeros((), BF16)), axis=1
            )
        return shift(value, "seq", step) if step else value

    live = jnp.broadcast_to((neighbour_ids != 0).astype(F32)[:, :, None], (capacity, KEYS, HD))

    def slots_of(step):
        source = (seq_at - step) % seq_count
        group = lax.dynamic_index_in_dim(groups, source, 0, keepdims=False)
        place, names = order(group, seq_at)
        if not whole_blocks:
            place = jnp.arange(pairs)
            names = (place < jnp.sum(names)).astype(jnp.int32)
        return source * pairs + place, names

    sent_grads = [
        [to_owner(chunk_of(out_grad, chunk), step) for step in range(seq_count)]
        for chunk in range(chunks)
    ]

    sent_queries = []
    for chunk in range(chunks):
        partial = product(acts[chunk], weights, table)
        queries = (partial[:chunk_rows] + swap(partial[chunk_rows:])).astype(BF16)
        sent_queries.append([to_owner(queries, step) for step in range(seq_count)])

    kv_grad = None
    query_grads = [None] * chunks
    for step in range(seq_count):
        slots, names = slots_of(step)
        held = pairs // chunks
        for chunk in range(chunks):
            back, kv_grad = attend(
                slots[chunk * held:(chunk + 1) * held],
                names[chunk * held:(chunk + 1) * held],
                sent_queries[chunk][step],
                sent_grads[chunk][step],
                neighbour_kv,
                live,
                kv_grad,
            )
            if step:
                back = shift(back, "seq", -step)
            if not whole_blocks:
                hit = message((seq_at + step) % seq_count)
                back = jnp.sum(
                    jnp.where(hit[:, :, None, None], back[:, None], jnp.zeros((), BF16)), axis=0
                )
            back = back.reshape(chunk_rows, width)
            query_grads[chunk] = back if step == 0 else query_grads[chunk] + back
    both_grads = [jnp.concatenate([grad, swap(grad)], axis=0) for grad in query_grads]

    even, odd = [], []
    for chunk in range(chunks):
        parts = [None] * tensor_count
        for k in reversed(range(tensor_count)):
            block = lax.dynamic_index_in_dim(weights, depth_blocks[k], 0, keepdims=False)
            parts[k] = dot(both_grads[chunk], block, ((1,), (1,))).astype(BF16)
        total = ring_reduce(lax.optimization_barrier(parts), "tensor").astype(BF16)
        kept, arrived = total[:chunk_rows], swap(total[chunk_rows:])
        even.append(jnp.where(core == 0, kept, arrived))
        odd.append(jnp.where(core == 0, arrived, kept))
    even, odd = jnp.concatenate(even, axis=0), jnp.concatenate(odd, axis=0)
    act_grad = jnp.concatenate(
        [half[:, p * depth:(p + 1) * depth] for p in range(per) for half in (even, odd)], axis=1
    )

    act_whole = jnp.zeros((tensor_count, 2 * rows, per * depth), BF16)
    for chunk in range(chunks):
        for k in range(tensor_count):
            act_whole = lax.dynamic_update_slice(
                act_whole, acts[chunk][k][None], (depth_blocks[k], 2 * chunk * chunk_rows, 0)
            )
    grad_whole = jnp.concatenate(both_grads, axis=0)
    products = {}
    for i, j in reversed(places):
        at, inner = block_at(i, j)
        block = lax.dynamic_slice(act_whole, (at, 0, inner * depth), (1, 2 * rows, depth))[0]
        products[i, j] = dot(block, grad_whole, ((0,), (0,)))
        if (i, j) != (0, 0):
            products[i, j] = lax.optimization_barrier(products[i, j].astype(BF16))
    upper = ring_reduce(
        [
            ring_reduce([products[i, j][:cut] for j in range(couples)], "dp")
            for i in range(seq_count)
        ],
        "seq",
    )
    lower = ring_reduce(
        [
            ring_reduce([products[i, j][cut:] for i in range(seq_count)], "seq")
            for j in range(couples)
        ],
        "dp",
    )
    weight_grad = jnp.concatenate([upper, lower], axis=0)
    return (act_grad, weight_grad, kv_grad)


def solution(mesh):
    in_specs = (
        P(("seq", "dp"), "tensor"),
        P(("seq", "dp"), "tensor"),
        P(("seq", "dp"), "tensor"),
        P(("seq", "dp"), None, None, "tensor"),
        P(("seq", "dp"), None),
        P(),
    )
    out_specs = (
        P(("seq", "dp"), "tensor"),
        P(("seq", "dp"), "tensor"),
        P(("seq", "dp"), None, None, "tensor"),
    )
    return jax.shard_map(
        on_device, mesh=mesh, in_specs=in_specs, out_specs=out_specs, check_vma=False
    )
```

time: 274 us -> 241 us (0.88)
  waiting for transfers between devices: 146 us -> 120 us
  Pallas kernels: 6.05 us -> 28.1 us
  between operations: 14.5 us -> 1.23 us
  matrix products: 35.5 us -> 24 us
  other arithmetic: 17.5 us -> 7.68 us
  starting transfers between devices: 27 us -> 36.3 us
  local copies, waits for them, and re-layouts: 26 us -> 22.8 us
    ppermute x15 -> x30, waiting for transfers between devices: 55.2 us -> 119 us  [shift(): lax.ppermute(value, axis, [(i, (i + step * stride) % size) for i in range...]
    all_gather x1 -> x0, waiting for transfers between devices: 51.3 us -> none  [on_device(): acts = lax.all_gather(act_both, 'tensor', axis=0)]
    reduce_scatter x1 -> x0, waiting for transfers between devices: 37.7 us -> none  [on_device(): lax.psum_scatter(act_parts, 'tensor', scatter_dimension=0, tiled=False)]
    pallas_call x0 -> x2, Pallas kernels: none -> 13 us  [product(): pl.pallas_call(functools.partial(product_kernel, count), out_shape=jax.Sh...]
    dynamic_update_slice x0 -> x14, local copies, waits for them, and re-layouts: none -> 12.5 us  [the longest x8 12.2 us: on_device(): lax.dynamic_update_slice(weights, piece[None], (at, inner * depth + start...]
    dot_general x16 -> x12, matrix products: 35.5 us -> 24 us  [dot(): lax.dot_general(a, b, (contract, ((), ())), preferred_element_type=F32)]
    unnamed x40 -> x18, local copies, waits for them, and re-layouts: 11.1 us -> 0.38 us
    pallas_call x2 -> x4, Pallas kernels: 6.05 us -> 15.1 us  [attend(): pl.pallas_call(attend_kernel, grid_spec=pltpu.PrefetchScalarGridSpec(num_...]
  transfers between devices with their start and end apart: 21 -> 38, of which waited for: 8 -> 19; matrix products, arithmetic and copies ran while one was open for 18% -> 20% of each run, Pallas kernels for 1% -> 10%
where the time goes in v2:
time: 241 us; the launch traced here: 240 us
  waiting for transfers between devices  120 us (50%)
  starting transfers between devices  36.3 us (15%)
  Pallas kernels  28.1 us (12%)
  matrix products  24 us (10%)
  local copies, waits for them, and re-layouts  22.8 us (9%)
  other arithmetic  7.68 us (3%)
    ppermute x30, waiting for transfers between devices, shift(): lax.ppermute(value, axis, [(i, (i + step * stride) % size) for i in range...  119 us
    ppermute x30, starting transfers between devices, shift(): lax.ppermute(value, axis, [(i, (i + step * stride) % size) for i in range...  35 us
    dot_general x12, matrix products, dot(): lax.dot_general(a, b, (contract, ((), ())), preferred_element_type=F32)  24 us
    pallas_call x4, Pallas kernels, attend(): pl.pallas_call(attend_kernel, grid_spec=pltpu.PrefetchScalarGridSpec(num_...  15.1 us
    pallas_call x2, Pallas kernels, product(): pl.pallas_call(functools.partial(product_kernel, count), out_shape=jax.Sh...  13 us
    dynamic_update_slice x8, local copies, waits for them, and re-layouts, on_device(): lax.dynamic_update_slice(weights, piece[None], (at, inner * depth + start...  12.2 us
  transfers between devices with their start and end apart: 38, of which 19 were waited for; matrix products, arithmetic and copies ran while one was open for 20% of the time, Pallas kernels for 10%

profile of v2, /device:TPU:0, one launch (start us, length us, event | category | flops | bytes accessed | tf_op | source)
XLA Modules:
  0.0 240.5 jit_solution(8174686088479222675)
XLA Ops:
  0.7 3.1 %fusion.80 = (bf16[512,1024]{1,0:T(8,128)(2,1)}, bf16[512,1024]{1,0:T(8,128)(2,1)}) fusion(bf16[1024,1024]{1,0:T(8,128)(2,1)} %param.7), kind=kLoop, calls=%fused_computation.123 | loop fusion | bytes 4194304 | tf_op jit(solution)/shard_map/slice | solution.py:212
  3.8 3.0 %collective-permute-start.4 = (bf16[512,1024]{1,0:T(8,128)(2,1)}, bf16[512,1024]{1,0:T(8,128)(2,1)}, u32[]{:S(2)}, u32[]{:S(2)}) collective-permute-start(bf16[512,1024]{1,0:T(8,128)(2,1)} %get-tuple-element.44), channel_id=1, source_target_pairs={{0,2},{1,3},{2,0},{3,1},{4,6},{5,7},{6,4},{7,5},{8,10},{9,11},{10,... | collective-permute-start | bytes 3145736 | tf_op jit(solution)/shard_map/ppermute | solution.py:24
  6.8 1.5 collective-permute-start.6
  10.7 4.4 %broadcast_in_dim.72 = bf16[4,1024,1024]{2,1,0:T(8,128)(2,1)} broadcast(bf16[]{:T(256)} %constant.300.clone.1), dimensions={} | broadcast | bytes 8388610 | tf_op jit(solution)/shard_map/broadcast_in_dim | solution.py:220
  17.5 1.6 collective-permute-start.1
  19.2 1.6 collective-permute-start.14
  21.9 12.2 %collective-permute-done.1.refs_1_ = bf16[256,1024]{1,0:T(8,128)(2,1)S(1)} collective-permute-done((bf16[256,1024]{1,0:T(8,128)(2,1)S(1)}, bf16[256,1024]{1,0:T(8,128)(2,1)S(1)}, u32[]{:S(2)}, u32[]{:S(2)}) %collective-permute-start.1) | collective-permute-done | bytes 524320 | tf_op jit(solution)/shard_map/ppermute | solution.py:24
  34.5 10.0 %collective-permute-done.14.refs_1_ = bf16[256,1024]{1,0:T(8,128)(2,1)S(1)} collective-permute-done((bf16[256,1024]{1,0:T(8,128)(2,1)S(1)}, bf16[256,1024]{1,0:T(8,128)(2,1)S(1)}, u32[]{:S(2)}, u32[]{:S(2)}) %collective-permute-start.14) | collective-permute-done | bytes 524320 | tf_op jit(solution)/shard_map/ppermute | solution.py:24
  47.2 6.3 %collective-permute-done.5 = bf16[512,1024]{1,0:T(8,128)(2,1)} collective-permute-done((bf16[512,1024]{1,0:T(8,128)(2,1)}, bf16[512,1024]{1,0:T(8,128)(2,1)}, u32[]{:S(2)}, u32[]{:S(2)}) %collective-permute-start.5) | collective-permute-done | bytes 1048608 | tf_op jit(solution)/shard_map/ppermute | solution.py:24
  53.5 2.0 collective-permute-start.9
  55.6 2.3 bitcast_dynamic-update-slice_fusion.5
  57.9 2.3 bitcast_dynamic-update-slice_fusion.4
  60.1 2.3 bitcast_dynamic-update-slice_fusion.3
  63.6 7.0 %collective-permute-done.15.refs_2_ = bf16[256,1024]{1,0:T(8,128)(2,1)S(1)} collective-permute-done((bf16[256,1024]{1,0:T(8,128)(2,1)S(1)}, bf16[256,1024]{1,0:T(8,128)(2,1)S(1)}, u32[]{:S(2)}, u32[]{:S(2)}) %collective-permute-start.15) | collective-permute-done | bytes 524320 | tf_op jit(solution)/shard_map/ppermute | solution.py:24
  71.3 3.7 %collective-permute-done.8 = bf16[512,1024]{1,0:T(8,128)(2,1)S(1)} collective-permute-done((bf16[512,1024]{1,0:T(8,128)(2,1)}, bf16[512,1024]{1,0:T(8,128)(2,1)S(1)}, u32[]{:S(2)}, u32[]{:S(2)}) %collective-permute-start.8) | collective-permute-done | bytes 1048608 | tf_op jit(solution)/shard_map/ppermute | solution.py:24
  75.1 1.8 collective-permute-start.3
  77.9 4.9 %collective-permute-done.9 = bf16[512,1024]{1,0:T(8,128)(2,1)S(1)} collective-permute-done((bf16[512,1024]{1,0:T(8,128)(2,1)}, bf16[512,1024]{1,0:T(8,128)(2,1)S(1)}, u32[]{:S(2)}, u32[]{:S(2)}) %collective-permute-start.9) | collective-permute-done | bytes 1048608 | tf_op jit(solution)/shard_map/ppermute | solution.py:24
  84.0 12.5 %collective-permute-done.3.refs_3_ = bf16[256,1024]{1,0:T(8,128)(2,1)S(1)} collective-permute-done((bf16[256,1024]{1,0:T(8,128)(2,1)S(1)}, bf16[256,1024]{1,0:T(8,128)(2,1)S(1)}, u32[]{:S(2)}, u32[]{:S(2)}) %collective-permute-start.3) | collective-permute-done | bytes 524320 | tf_op jit(solution)/shard_map/ppermute | solution.py:24
  96.5 6.4 %shard_map.85 = f32[256,1024]{1,0:T(8,128)S(1)} custom-call(s32[4]{0:T(128)S(1)} %pad_add_fusion.1.table_ref, bf16[256,1024]{1,0:T(8,128)(2,1)S(1)} %pad_maximum_fusion.2.refs_0_, bf16[256,1024]{1,0:T(8,128)(2,1)S(1)} %collective-permute-done.1.refs_1_, bf16[256,1024]{1,0:T(8,128)(2,1)S(1)} %collective-permute-done.2.refs_2_, ...), custom_call_target="tpu_custom_call" | custom-call | flops 2147483648 | bytes 11534336 | tf_op jit(solution)/shard_map/pallas_call | solution.py:61
  103.1 6.6 %shard_map.87 = f32[256,1024]{1,0:T(8,128)S(1)} custom-call(s32[4]{0:T(128)S(1)} %pad_add_fusion.1.table_ref, bf16[256,1024]{1,0:T(8,128)(2,1)S(1)} %pad_maximum_fusion.3.refs_0_, bf16[256,1024]{1,0:T(8,128)(2,1)S(1)} %collective-permute-done.14.refs_1_, bf16[256,1024]{1,0:T(8,128)(2,1)S(1)} %collective-permute-done.15.refs_2_, ...), custom_call_target="tpu_custom_call" | custom-call | flops 2147483648 | bytes 11534336 | tf_op jit(solution)/shard_map/pallas_call | solution.py:61
  113.1 3.8 %shard_map.86 = (bf16[2,64,1024]{2,1,0:T(8,128)(2,1)S(1)}, bf16[8,2,256,1024]{3,2,1,0:T(8,128)(2,1)}) custom-call(s32[4]{0:T(128)S(1)} %pad_add_fusion.table_ref, bf16[2,64,1024]{2,1,0:T(8,128)(2,1)S(1)} %bitcast.103, bf16[2,64,1024]{2,1,0:T(8,128)(2,1)S(1)} %bitcast.105, bf16[8,2,256,1024]{3,2,1,0:T(8,128)(2,1)S(1)} %bitcast.97, ...), custom_call_target="tpu_custom_call" | custom-call | flops 1342177280 | bytes 4194304 | tf_op jit(solution)/shard_map/pallas_call | solution.py:144
  116.9 3.8 %shard_map.88 = (bf16[2,64,1024]{2,1,0:T(8,128)(2,1)S(1)}, bf16[8,2,256,1024]{3,2,1,0:T(8,128)(2,1)}) custom-call(s32[4]{0:T(128)S(1)} %pad_add_fusion.3.table_ref, bf16[2,64,1024]{2,1,0:T(8,128)(2,1)S(1)} %bitcast.99, bf16[2,64,1024]{2,1,0:T(8,128)(2,1)S(1)} %bitcast.101, bf16[8,2,256,1024]{3,2,1,0:T(8,128)(2,1)S(1)} %bitcast.97, ...), custom_call_target="tpu_custom_call", output_to_operand_aliasing={{1}: (5, {})} | custom-call | flops 1342177280 | bytes 4194304 | tf_op jit(solution)/shard_map/pallas_call | solution.py:144
  120.7 3.8 %shard_map.89 = (bf16[2,64,1024]{2,1,0:T(8,128)(2,1)S(1)}, bf16[8,2,256,1024]{3,2,1,0:T(8,128)(2,1)}) custom-call(s32[4]{0:T(128)S(1)} %pad_add_fusion.2.table_ref, bf16[2,64,1024]{2,1,0:T(8,128)(2,1)S(1)} %collective-permute-done.11.q_ref, bf16[2,64,1024]{2,1,0:T(8,128)(2,1)S(1)} %collective-permute-done.12.g_ref, ...), custom_call_target="tpu_custom_call", output_to_operand_aliasing={{1}: (5, {})} | custom-call | flops 1342177280 | bytes 4194304 | tf_op jit(solution)/shard_map/pallas_call | solution.py:144
  124.5 3.8 %shard_map.90 = (bf16[2,64,1024]{2,1,0:T(8,128)(2,1)S(1)}, bf16[8,2,256,1024]{3,2,1,0:T(8,128)(2,1)}) custom-call(s32[4]{0:T(128)S(1)} %pad_add_fusion.4.table_ref, bf16[2,64,1024]{2,1,0:T(8,128)(2,1)S(1)} %collective-permute-done.24.q_ref, bf16[2,64,1024]{2,1,0:T(8,128)(2,1)S(1)} %collective-permute-done.25.g_ref, ...), custom_call_target="tpu_custom_call", output_to_operand_aliasing={{1}: (5, {})} | custom-call | flops 1342177280 | bytes 4194304 | tf_op jit(solution)/shard_map/pallas_call | solution.py:144
  128.4 2.1 collective-permute-start.18
  130.5 7.1 %collective-permute-done.26 = bf16[2,64,1024]{2,1,0:T(8,128)(2,1)S(1)} collective-permute-done((bf16[2,64,1024]{2,1,0:T(8,128)(2,1)S(1)}, bf16[2,64,1024]{2,1,0:T(8,128)(2,1)S(1)}, u32[]{:S(2)}, u32[]{:S(2)}) %collective-permute-start.26) | collective-permute-done | bytes 262176 | tf_op jit(solution)/shard_map/ppermute | solution.py:24
  137.8 3.7 %collective-permute-done.18 = bf16[2,64,1024]{2,1,0:T(8,128)(2,1)S(1)} collective-permute-done((bf16[2,64,1024]{2,1,0:T(8,128)(2,1)S(1)}, bf16[2,64,1024]{2,1,0:T(8,128)(2,1)S(1)}, u32[]{:S(2)}, u32[]{:S(2)}) %collective-permute-start.18) | collective-permute-done | bytes 262176 | tf_op jit(solution)/shard_map/ppermute | solution.py:24
  141.6 2.4 fusion.29
  144.0 2.4 fusion.35
  146.4 2.4 fusion.41
  148.7 2.4 fusion.47
  151.4 2.3 fusion.26
  153.8 2.3 fusion.32
  156.1 2.3 fusion.38
  158.4 2.3 fusion.44
  163.5 1.7 collective-permute-start.35
  166.3 1.9 collective-permute-start.29
  168.2 9.1 %collective-permute-done.20 = bf16[256,1024]{1,0:T(8,128)(2,1)S(1)} collective-permute-done((bf16[256,1024]{1,0:T(8,128)(2,1)S(1)}, bf16[256,1024]{1,0:T(8,128)(2,1)S(1)}, u32[]{:S(2)}, u32[]{:S(2)}) %collective-permute-start.20) | collective-permute-done | bytes 524320 | tf_op jit(solution)/shard_map/ppermute | solution.py:24
  177.5 1.9 collective-permute-start.21
  183.4 5.2 %collective-permute-done.29 = bf16[256,1024]{1,0:T(8,128)(2,1)S(1)} collective-permute-done((bf16[256,1024]{1,0:T(8,128)(2,1)S(1)}, bf16[256,1024]{1,0:T(8,128)(2,1)S(1)}, u32[]{:S(2)}, u32[]{:S(2)}) %collective-permute-start.29) | collective-permute-done | bytes 524320 | tf_op jit(solution)/shard_map/ppermute | solution.py:24
  188.6 1.6 collective-permute-start.37
  190.4 9.0 %collective-permute-done.21 = bf16[256,1024]{1,0:T(8,128)(2,1)S(1)} collective-permute-done((bf16[256,1024]{1,0:T(8,128)(2,1)S(1)}, bf16[256,1024]{1,0:T(8,128)(2,1)S(1)}, u32[]{:S(2)}, u32[]{:S(2)}) %collective-permute-start.21) | collective-permute-done | bytes 524320 | tf_op jit(solution)/shard_map/ppermute | solution.py:24
  199.4 2.1 collective-permute-start.30
  202.5 1.6 collective-permute-start.33
  204.4 9.8 %collective-permute-done.30 = bf16[256,1024]{1,0:T(8,128)(2,1)S(1)} collective-permute-done((bf16[256,1024]{1,0:T(8,128)(2,1)S(1)}, bf16[256,1024]{1,0:T(8,128)(2,1)S(1)}, u32[]{:S(2)}, u32[]{:S(2)}) %collective-permute-start.30) | collective-permute-done | bytes 524320 | tf_op jit(solution)/shard_map/ppermute | solution.py:24
  215.5 8.7 %collective-permute-done.22 = bf16[256,1024]{1,0:T(8,128)(2,1)S(1)} collective-permute-done((bf16[256,1024]{1,0:T(8,128)(2,1)S(1)}, bf16[256,1024]{1,0:T(8,128)(2,1)S(1)}, u32[]{:S(2)}, u32[]{:S(2)}) %collective-permute-start.22) | collective-permute-done | bytes 524320 | tf_op jit(solution)/shard_map/ppermute | solution.py:24
  228.4 7.1 %collective-permute-done.33 = bf16[512,1024]{1,0:T(8,128)(2,1)S(1)} collective-permute-done((bf16[512,1024]{1,0:T(8,128)(2,1)S(1)}, bf16[512,1024]{1,0:T(8,128)(2,1)S(1)}, u32[]{:S(2)}, u32[]{:S(2)}) %collective-permute-start.33) | collective-permute-done | bytes 1048608 | tf_op jit(solution)/shard_map/ppermute | solution.py:24
  238.2 2.3 pad_maximum_fusion
  (130 shorter events, 34.9 us)
Async XLA Ops:
  0.6 8.1 %copy-start.1 = (bf16[256,2048]{1,0:T(8,128)(2,1)S(1)}, bf16[256,2048]{1,0:T(8,128)(2,1)}, u32[]{:S(2)}) copy-start(bf16[256,2048]{1,0:T(8,128)(2,1)} %param.6) | copy-start | bytes 3145732
  0.6 9.4 %copy-start.6 = (s32[32]{0:T(128)S(1)}, s32[32]{0:T(128)}, u32[]{:S(2)}) copy-start(s32[32]{0:T(128)} %param.11) | copy-start | bytes 388
  0.7 9.9 %copy-start.4 = (bf16[256,1024]{1,0:T(8,128)(2,1)S(1)}, bf16[256,1024]{1,0:T(8,128)(2,1)}, u32[]{:S(2)}) copy-start(bf16[256,1024]{1,0:T(8,128)(2,1)} %param.8) | copy-start | bytes 1572868
  0.7 9.9 %copy-start.5 = (s32[8,256]{1,0:T(8,128)S(1)}, s32[8,256]{1,0:T(8,128)}, u32[]{:S(2)}) copy-start(s32[8,256]{1,0:T(8,128)} %param.10) | copy-start | bytes 24580
  3.8 40.6 %collective-permute-start.4 = (bf16[512,1024]{1,0:T(8,128)(2,1)}, bf16[512,1024]{1,0:T(8,128)(2,1)}, u32[]{:S(2)}, u32[]{:S(2)}) collective-permute-start(bf16[512,1024]{1,0:T(8,128)(2,1)} %get-tuple-element.44), channel_id=1, source_target_pairs={{0,2},{1,3},{2,0},{3,1},{4,6},{5,7},{6,4},{7,5},{8,10},{9,11},{10,... | collective-permute-start | bytes 3145736 | tf_op jit(solution)/shard_map/ppermute | solution.py:24
  6.8 39.0 %collective-permute-start.6 = (bf16[512,1024]{1,0:T(8,128)(2,1)}, bf16[512,1024]{1,0:T(8,128)(2,1)}, u32[]{:S(2)}, u32[]{:S(2)}) collective-permute-start(bf16[512,1024]{1,0:T(8,128)(2,1)} %get-tuple-element.44), channel_id=1, source_target_pairs={{0,16},{16,0},{1,17},{17,1},{2,18},{18,2},{3,19},{19,3},{4,20},{20... | collective-permute-start | bytes 3145736 | tf_op jit(solution)/shard_map/ppermute | solution.py:24
  8.3 45.3 %collective-permute-start.5 = (bf16[512,1024]{1,0:T(8,128)(2,1)}, bf16[512,1024]{1,0:T(8,128)(2,1)}, u32[]{:S(2)}, u32[]{:S(2)}) collective-permute-start(bf16[512,1024]{1,0:T(8,128)(2,1)} %get-tuple-element.43), channel_id=1, source_target_pairs={{0,2},{1,3},{2,0},{3,1},{4,6},{5,7},{6,4},{7,5},{8,10},{9,11},{10,... | collective-permute-start | bytes 3145736 | tf_op jit(solution)/shard_map/ppermute | solution.py:24
  9.6 9.6 %collective-permute-start.13 = (bf16[128,1024]{1,0:T(8,128)(2,1)}, bf16[128,1024]{1,0:T(8,128)(2,1)S(1)}, u32[]{:S(2)}, u32[]{:S(2)}) collective-permute-start(bf16[128,1024]{1,0:T(8,128)(2,1)} %get-tuple-element.47), channel_id=1, source_target_pairs={{0,1},{1,0},{2,3},{3,2},{4,5},{5,4},{6,7},{7,6},{8,9},{9,8},{10,11... | collective-permute-start | bytes 786440 | tf_op jit(solution)/shard_map/ppermute | solution.py:28
  9.6 7.9 %collective-permute-start = (bf16[128,1024]{1,0:T(8,128)(2,1)S(1)}, bf16[128,1024]{1,0:T(8,128)(2,1)S(1)}, u32[]{:S(2)}, u32[]{:S(2)}) collective-permute-start(bf16[128,1024]{1,0:T(8,128)(2,1)S(1)} %get-tuple-element.46), channel_id=1, source_target_pairs={{0,1},{1,0},{2,3},{3,2},{4,5},{5,4},{6,7},{7,6},{8,9},{9,8},{10,11... | collective-permute-start | bytes 786440 | tf_op jit(solution)/shard_map/ppermute | solution.py:28
  10.7 4.4 %copy-start = (bf16[1024,1024]{1,0:T(8,128)(2,1)S(1)}, bf16[1024,1024]{1,0:T(8,128)(2,1)}, u32[]{:S(2)}) copy-start(bf16[1024,1024]{1,0:T(8,128)(2,1)} %param.7) | copy-start | bytes 6291460
  17.4 1.8 copy-start.2
  17.5 16.6 %collective-permute-start.1 = (bf16[256,1024]{1,0:T(8,128)(2,1)S(1)}, bf16[256,1024]{1,0:T(8,128)(2,1)S(1)}, u32[]{:S(2)}, u32[]{:S(2)}) collective-permute-start(bf16[256,1024]{1,0:T(8,128)(2,1)S(1)} %pad_maximum_fusion.2.refs_0_), channel_id=1, source_target_pairs={{0,4},{4,8},{8,12},{12,0},{1,5},{5,9},{9,13},{13,1},{2,6},{6,10},{... | collective-permute-start | bytes 1572872 | tf_op jit(solution)/shard_map/ppermute | solution.py:24
  19.2 25.2 %collective-permute-start.14 = (bf16[256,1024]{1,0:T(8,128)(2,1)S(1)}, bf16[256,1024]{1,0:T(8,128)(2,1)S(1)}, u32[]{:S(2)}, u32[]{:S(2)}) collective-permute-start(bf16[256,1024]{1,0:T(8,128)(2,1)S(1)} %pad_maximum_fusion.3.refs_0_), channel_id=1, source_target_pairs={{0,4},{4,8},{8,12},{12,0},{1,5},{5,9},{9,13},{13,1},{2,6},{6,10},{... | collective-permute-start | bytes 1572872 | tf_op jit(solution)/shard_map/ppermute | solution.py:24
  20.9 0.9 copy-start.3
  34.1 28.3 %collective-permute-start.7 = (bf16[512,1024]{1,0:T(8,128)(2,1)}, bf16[512,1024]{1,0:T(8,128)(2,1)S(1)}, u32[]{:S(2)}, u32[]{:S(2)}) collective-permute-start(bf16[512,1024]{1,0:T(8,128)(2,1)} %get-tuple-element.43), channel_id=1, source_target_pairs={{0,16},{16,0},{1,17},{17,1},{2,18},{18,2},{3,19},{19,3},{4,20},{20... | collective-permute-start | bytes 3145736 | tf_op jit(solution)/shard_map/ppermute | solution.py:24
  44.5 26.9 %collective-permute-start.2 = (bf16[256,1024]{1,0:T(8,128)(2,1)S(1)}, bf16[256,1024]{1,0:T(8,128)(2,1)S(1)}, u32[]{:S(2)}, u32[]{:S(2)}) collective-permute-start(bf16[256,1024]{1,0:T(8,128)(2,1)S(1)} %collective-permute-done.1.refs_1_), channel_id=1, source_target_pairs={{0,4},{4,8},{8,12},{12,0},{1,5},{5,9},{9,13},{13,1},{2,6},{6,10},{... | collective-permute-start | bytes 1572872 | tf_op jit(solution)/shard_map/ppermute | solution.py:24
  44.5 26.1 %collective-permute-start.15 = (bf16[256,1024]{1,0:T(8,128)(2,1)S(1)}, bf16[256,1024]{1,0:T(8,128)(2,1)S(1)}, u32[]{:S(2)}, u32[]{:S(2)}) collective-permute-start(bf16[256,1024]{1,0:T(8,128)(2,1)S(1)} %collective-permute-done.14.refs_1_), channel_id=1, source_target_pairs={{0,4},{4,8},{8,12},{12,0},{1,5},{5,9},{9,13},{13,1},{2,6},{6,10},{... | collective-permute-start | bytes 1572872 | tf_op jit(solution)/shard_map/ppermute | solution.py:24
  45.8 29.3 %collective-permute-start.8 = (bf16[512,1024]{1,0:T(8,128)(2,1)}, bf16[512,1024]{1,0:T(8,128)(2,1)S(1)}, u32[]{:S(2)}, u32[]{:S(2)}) collective-permute-start(bf16[512,1024]{1,0:T(8,128)(2,1)} %collective-permute-done.6), channel_id=1, source_target_pairs={{0,2},{1,3},{2,0},{3,1},{4,6},{5,7},{6,4},{7,5},{8,10},{9,11},{10,... | collective-permute-start | bytes 3145736 | tf_op jit(solution)/shard_map/ppermute | solution.py:24
  53.5 29.3 %collective-permute-start.9 = (bf16[512,1024]{1,0:T(8,128)(2,1)}, bf16[512,1024]{1,0:T(8,128)(2,1)S(1)}, u32[]{:S(2)}, u32[]{:S(2)}) collective-permute-start(bf16[512,1024]{1,0:T(8,128)(2,1)} %collective-permute-done.5), channel_id=1, source_target_pairs={{0,16},{16,0},{1,17},{17,1},{2,18},{18,2},{3,19},{19,3},{4,20},{20... | collective-permute-start | bytes 3145736 | tf_op jit(solution)/shard_map/ppermute | solution.py:24
  62.4 62.1 %collective-permute-start.25 = (bf16[2,64,1024]{2,1,0:T(8,128)(2,1)S(1)}, bf16[2,64,1024]{2,1,0:T(8,128)(2,1)S(1)}, u32[]{:S(2)}, u32[]{:S(2)}) collective-permute-start(bf16[2,64,1024]{2,1,0:T(8,128)(2,1)S(1)} %bitcast.100), channel_id=1, source_target_pairs={{0,16},{16,0},{1,17},{17,1},{2,18},{18,2},{3,19},{19,3},{4,20},{20... | collective-permute-start | bytes 786440 | tf_op jit(solution)/shard_map/ppermute | solution.py:24
  70.5 50.2 %collective-permute-start.12 = (bf16[2,64,1024]{2,1,0:T(8,128)(2,1)S(1)}, bf16[2,64,1024]{2,1,0:T(8,128)(2,1)S(1)}, u32[]{:S(2)}, u32[]{:S(2)}) collective-permute-start(bf16[2,64,1024]{2,1,0:T(8,128)(2,1)S(1)} %bitcast.104), channel_id=1, source_target_pairs={{0,16},{16,0},{1,17},{17,1},{2,18},{18,2},{3,19},{19,3},{4,20},{20... | collective-permute-start | bytes 786440 | tf_op jit(solution)/shard_map/ppermute | solution.py:24
  71.3 31.7 %collective-permute-start.16 = (bf16[256,1024]{1,0:T(8,128)(2,1)S(1)}, bf16[256,1024]{1,0:T(8,128)(2,1)S(1)}, u32[]{:S(2)}, u32[]{:S(2)}) collective-permute-start(bf16[256,1024]{1,0:T(8,128)(2,1)S(1)} %collective-permute-done.15.refs_2_), channel_id=1, source_target_pairs={{0,4},{4,8},{8,12},{12,0},{1,5},{5,9},{9,13},{13,1},{2,6},{6,10},{... | collective-permute-start | bytes 1572872 | tf_op jit(solution)/shard_map/ppermute | solution.py:24
  75.1 21.4 %collective-permute-start.3 = (bf16[256,1024]{1,0:T(8,128)(2,1)S(1)}, bf16[256,1024]{1,0:T(8,128)(2,1)S(1)}, u32[]{:S(2)}, u32[]{:S(2)}) collective-permute-start(bf16[256,1024]{1,0:T(8,128)(2,1)S(1)} %collective-permute-done.2.refs_2_), channel_id=1, source_target_pairs={{0,4},{4,8},{8,12},{12,0},{1,5},{5,9},{9,13},{13,1},{2,6},{6,10},{... | collective-permute-start | bytes 1572872 | tf_op jit(solution)/shard_map/ppermute | solution.py:24
  102.9 10.2 %slice-start = ((s8[8388608]{0:T(1024)(128)(4,1)}), s8[4194304]{0:T(1024)(128)(4,1)S(1)}, s32[]{:S(2)}) async-start(s8[8388608]{0:T(1024)(128)(4,1)} %bitcast.96), calls=%async_computation | async-start | bytes 8388608
  103.0 10.2 %slice-start.1 = ((s8[8388608]{0:T(1024)(128)(4,1)}), s8[4194304]{0:T(1024)(128)(4,1)S(1)}, s32[]{:S(2)}) async-start(s8[8388608]{0:T(1024)(128)(4,1)} %bitcast.96), calls=%async_computation.1 | async-start | bytes 8388608
  103.0 7.2 %collective-permute-start.10 = (f32[128,1024]{1,0:T(8,128)S(1)}, f32[128,1024]{1,0:T(8,128)S(1)}, u32[]{:S(2)}, u32[]{:S(2)}) collective-permute-start(f32[128,1024]{1,0:T(8,128)S(1)} %slice.131), channel_id=1, source_target_pairs={{0,1},{1,0},{2,3},{3,2},{4,5},{5,4},{6,7},{7,6},{8,9},{9,8},{10,11... | collective-permute-start | bytes 1572872 | tf_op jit(solution)/shard_map/ppermute | solution.py:28
  109.7 2.0 collective-permute-start.17
  110.2 10.5 %collective-permute-start.11 = (bf16[2,64,1024]{2,1,0:T(8,128)(2,1)S(1)}, bf16[2,64,1024]{2,1,0:T(8,128)(2,1)S(1)}, u32[]{:S(2)}, u32[]{:S(2)}) collective-permute-start(bf16[2,64,1024]{2,1,0:T(8,128)(2,1)S(1)} %bitcast.102), channel_id=1, source_target_pairs={{0,16},{16,0},{1,17},{17,1},{2,18},{18,2},{3,19},{19,3},{4,20},{20... | collective-permute-start | bytes 786440 | tf_op jit(solution)/shard_map/ppermute | solution.py:24
  111.7 12.8 %collective-permute-start.24 = (bf16[2,64,1024]{2,1,0:T(8,128)(2,1)S(1)}, bf16[2,64,1024]{2,1,0:T(8,128)(2,1)S(1)}, u32[]{:S(2)}, u32[]{:S(2)}) collective-permute-start(bf16[2,64,1024]{2,1,0:T(8,128)(2,1)S(1)} %bitcast.98), channel_id=1, source_target_pairs={{0,16},{16,0},{1,17},{17,1},{2,18},{18,2},{3,19},{19,3},{4,20},{20... | collective-permute-start | bytes 786440 | tf_op jit(solution)/shard_map/ppermute | solution.py:24
  128.3 9.2 %collective-permute-start.26 = (bf16[2,64,1024]{2,1,0:T(8,128)(2,1)S(1)}, bf16[2,64,1024]{2,1,0:T(8,128)(2,1)S(1)}, u32[]{:S(2)}, u32[]{:S(2)}) collective-permute-start(bf16[2,64,1024]{2,1,0:T(8,128)(2,1)S(1)} %get-tuple-element.29), channel_id=1, source_target_pairs={{0,16},{16,0},{1,17},{17,1},{2,18},{18,2},{3,19},{19,3},{4,20},{20... | collective-permute-start | bytes 786440 | tf_op jit(solution)/shard_map/ppermute | solution.py:24
  128.4 13.1 %collective-permute-start.18 = (bf16[2,64,1024]{2,1,0:T(8,128)(2,1)S(1)}, bf16[2,64,1024]{2,1,0:T(8,128)(2,1)S(1)}, u32[]{:S(2)}, u32[]{:S(2)}) collective-permute-start(bf16[2,64,1024]{2,1,0:T(8,128)(2,1)S(1)} %get-tuple-element.22), channel_id=1, source_target_pairs={{0,16},{16,0},{1,17},{17,1},{2,18},{18,2},{3,19},{19,3},{4,20},{20... | collective-permute-start | bytes 786440 | tf_op jit(solution)/shard_map/ppermute | solution.py:24
  137.6 4.0 %collective-permute-start.27 = (bf16[128,1024]{1,0:T(8,128)(2,1)S(1)}, bf16[128,1024]{1,0:T(8,128)(2,1)S(1)}, u32[]{:S(2)}, u32[]{:S(2)}) collective-permute-start(bf16[128,1024]{1,0:T(8,128)(2,1)S(1)} %bitcast.106), channel_id=1, source_target_pairs={{0,1},{1,0},{2,3},{3,2},{4,5},{5,4},{6,7},{7,6},{8,9},{9,8},{10,11... | collective-permute-start | bytes 786440 | tf_op jit(solution)/shard_map/ppermute | solution.py:28
  141.5 9.9 %collective-permute-start.19 = (bf16[128,1024]{1,0:T(8,128)(2,1)S(1)}, bf16[128,1024]{1,0:T(8,128)(2,1)S(1)}, u32[]{:S(2)}, u32[]{:S(2)}) collective-permute-start(bf16[128,1024]{1,0:T(8,128)(2,1)S(1)} %bitcast.115), channel_id=1, source_target_pairs={{0,1},{1,0},{2,3},{3,2},{4,5},{5,4},{6,7},{7,6},{8,9},{9,8},{10,11... | collective-permute-start | bytes 786440 | tf_op jit(solution)/shard_map/ppermute | solution.py:28
  151.1 15.0 %collective-permute-start.28 = (bf16[256,1024]{1,0:T(8,128)(2,1)S(1)}, bf16[256,1024]{1,0:T(8,128)(2,1)S(1)}, u32[]{:S(2)}, u32[]{:S(2)}) collective-permute-start(bf16[256,1024]{1,0:T(8,128)(2,1)S(1)} %fusion.47), channel_id=1, source_target_pairs={{0,12},{4,0},{8,4},{12,8},{1,13},{5,1},{9,5},{13,9},{2,14},{6,2},{... | collective-permute-start | bytes 1572872 | tf_op jit(solution)/shard_map/ppermute | solution.py:24
  160.8 16.5 %collective-permute-start.20 = (bf16[256,1024]{1,0:T(8,128)(2,1)S(1)}, bf16[256,1024]{1,0:T(8,128)(2,1)S(1)}, u32[]{:S(2)}, u32[]{:S(2)}) collective-permute-start(bf16[256,1024]{1,0:T(8,128)(2,1)S(1)} %fusion.44), channel_id=1, source_target_pairs={{0,12},{4,0},{8,4},{12,8},{1,13},{5,1},{9,5},{13,9},{2,14},{6,2},{... | collective-permute-start | bytes 1572872 | tf_op jit(solution)/shard_map/ppermute | solution.py:24
  162.4 39.3 %collective-permute-start.32 = (bf16[512,1024]{1,0:T(8,128)(2,1)S(1)}, bf16[512,1024]{1,0:T(8,128)(2,1)S(1)}, u32[]{:S(2)}, u32[]{:S(2)}) collective-permute-start(bf16[512,1024]{1,0:T(8,128)(2,1)S(1)} %get-tuple-element.41), channel_id=1, source_target_pairs={{0,2},{1,3},{2,0},{3,1},{4,6},{5,7},{6,4},{7,5},{8,10},{9,11},{10,... | collective-permute-start | bytes 3145736 | tf_op jit(solution)/shard_map/ppermute | solution.py:24
  163.5 39.0 %collective-permute-start.35 = (bf16[512,1024]{1,0:T(8,128)(2,1)S(1)}, bf16[512,1024]{1,0:T(8,128)(2,1)S(1)}, u32[]{:S(2)}, u32[]{:S(2)}) collective-permute-start(bf16[512,1024]{1,0:T(8,128)(2,1)S(1)} %get-tuple-element.42), channel_id=1, source_target_pairs={{0,16},{16,0},{1,17},{17,1},{2,18},{18,2},{3,19},{19,3},{4,20},{20... | collective-permute-start | bytes 3145736 | tf_op jit(solution)/shard_map/ppermute | solution.py:24
  166.3 22.3 %collective-permute-start.29 = (bf16[256,1024]{1,0:T(8,128)(2,1)S(1)}, bf16[256,1024]{1,0:T(8,128)(2,1)S(1)}, u32[]{:S(2)}, u32[]{:S(2)}) collective-permute-start(bf16[256,1024]{1,0:T(8,128)(2,1)S(1)} %add_convert_fusion.4), channel_id=1, source_target_pairs={{0,12},{4,0},{8,4},{12,8},{1,13},{5,1},{9,5},{13,9},{2,14},{6,2},{... | collective-permute-start | bytes 1572872 | tf_op jit(solution)/shard_map/ppermute | solution.py:24
  177.5 21.9 %collective-permute-start.21 = (bf16[256,1024]{1,0:T(8,128)(2,1)S(1)}, bf16[256,1024]{1,0:T(8,128)(2,1)S(1)}, u32[]{:S(2)}, u32[]{:S(2)}) collective-permute-start(bf16[256,1024]{1,0:T(8,128)(2,1)S(1)} %add_convert_fusion.7), channel_id=1, source_target_pairs={{0,12},{4,0},{8,4},{12,8},{1,13},{5,1},{9,5},{13,9},{2,14},{6,2},{... | collective-permute-start | bytes 1572872 | tf_op jit(solution)/shard_map/ppermute | solution.py:24
  180.9 47.5 %collective-permute-start.34 = (bf16[512,1024]{1,0:T(8,128)(2,1)S(1)}, bf16[512,1024]{1,0:T(8,128)(2,1)S(1)}, u32[]{:S(2)}, u32[]{:S(2)}) collective-permute-start(bf16[512,1024]{1,0:T(8,128)(2,1)S(1)} %slice.140), channel_id=1, source_target_pairs={{0,2},{1,3},{2,0},{3,1},{4,6},{5,7},{6,4},{7,5},{8,10},{9,11},{10,... | collective-permute-start | bytes 3145736 | tf_op jit(solution)/shard_map/ppermute | solution.py:24
  188.6 39.8 %collective-permute-start.37 = (bf16[512,1024]{1,0:T(8,128)(2,1)S(1)}, bf16[512,1024]{1,0:T(8,128)(2,1)S(1)}, u32[]{:S(2)}, u32[]{:S(2)}) collective-permute-start(bf16[512,1024]{1,0:T(8,128)(2,1)S(1)} %slice.144), channel_id=1, source_target_pairs={{0,16},{16,0},{1,17},{17,1},{2,18},{18,2},{3,19},{19,3},{4,20},{20... | collective-permute-start | bytes 3145736 | tf_op jit(solution)/shard_map/ppermute | solution.py:24
  199.4 14.8 %collective-permute-start.30 = (bf16[256,1024]{1,0:T(8,128)(2,1)S(1)}, bf16[256,1024]{1,0:T(8,128)(2,1)S(1)}, u32[]{:S(2)}, u32[]{:S(2)}) collective-permute-start(bf16[256,1024]{1,0:T(8,128)(2,1)S(1)} %add_convert_fusion.3), channel_id=1, source_target_pairs={{0,12},{4,0},{8,4},{12,8},{1,13},{5,1},{9,5},{13,9},{2,14},{6,2},{... | collective-permute-start | bytes 1572872 | tf_op jit(solution)/shard_map/ppermute | solution.py:24
  201.7 22.5 %collective-permute-start.22 = (bf16[256,1024]{1,0:T(8,128)(2,1)S(1)}, bf16[256,1024]{1,0:T(8,128)(2,1)S(1)}, u32[]{:S(2)}, u32[]{:S(2)}) collective-permute-start(bf16[256,1024]{1,0:T(8,128)(2,1)S(1)} %add_convert_fusion.6), channel_id=1, source_target_pairs={{0,12},{4,0},{8,4},{12,8},{1,13},{5,1},{9,5},{13,9},{2,14},{6,2},{... | collective-permute-start | bytes 1572872 | tf_op jit(solution)/shard_map/ppermute | solution.py:24
  202.5 33.0 %collective-permute-start.33 = (bf16[512,1024]{1,0:T(8,128)(2,1)S(1)}, bf16[512,1024]{1,0:T(8,128)(2,1)S(1)}, u32[]{:S(2)}, u32[]{:S(2)}) collective-permute-start(bf16[512,1024]{1,0:T(8,128)(2,1)S(1)} %add_convert_fusion.1), channel_id=1, source_target_pairs={{0,16},{16,0},{1,17},{17,1},{2,18},{18,2},{3,19},{19,3},{4,20},{20... | collective-permute-start | bytes 3145736 | tf_op jit(solution)/shard_map/ppermute | solution.py:24
  214.2 22.6 %collective-permute-start.36 = (bf16[512,1024]{1,0:T(8,128)(2,1)S(1)}, bf16[512,1024]{1,0:T(8,128)(2,1)S(1)}, u32[]{:S(2)}, u32[]{:S(2)}) collective-permute-start(bf16[512,1024]{1,0:T(8,128)(2,1)S(1)} %add_convert_fusion), channel_id=1, source_target_pairs={{0,2},{1,3},{2,0},{3,1},{4,6},{5,7},{6,4},{7,5},{8,10},{9,11},{10,... | collective-permute-start | bytes 3145736 | tf_op jit(solution)/shard_map/ppermute | solution.py:24
  224.2 1.5 collective-permute-start.31
  225.7 1.5 collective-permute-start.23

commit v3 on v2

v3 whole, which is shorter than its diff:
```python
import functools

import jax
import jax.numpy as jnp
from jax import lax
from jax.experimental import pallas as pl
from jax.experimental.pallas import tpu as pltpu
from jax.sharding import PartitionSpec as P

HD = 128
SPAN = 64
KEYS = 256
F32 = jnp.float32
BF16 = jnp.bfloat16


def dot(a, b, contract):
    return lax.dot_general(a, b, (contract, ((), ())), preferred_element_type=F32)


def shift(value, axis, step=1):
    stride = 2 if axis == "dp" else 1
    size = lax.axis_size(axis)
    return lax.ppermute(value, axis, [(i, (i + step * stride) % size) for i in range(size)])


def swap(value):
    return lax.ppermute(value, "dp", [(i, i ^ 1) for i in range(lax.axis_size("dp"))])


def shift_swap(value, step):
    tensor_count, dp_count = lax.axis_size("tensor"), lax.axis_size("dp")
    pairs = [
        (t * dp_count + d, (t + step) % tensor_count * dp_count + (d ^ 1))
        for t in range(tensor_count)
        for d in range(dp_count)
    ]
    return lax.ppermute(value, ("tensor", "dp"), pairs)


def after(value, *others):
    return lax.optimization_barrier((value, *others))[0]


def reaches(size, far_up):
    up = size // 2 if far_up else (size - 1) // 2
    return up, size - 1 - up


def gather_rings(streams, axis, size):
    held = [[block] + [None] * (size - 1) for block, _, _ in streams]
    for m in range(1, size // 2 + 1):
        came = {}
        for s, (_, far_up, hop) in enumerate(streams):
            for sign, count in zip((1, -1), reaches(size, far_up)):
                if m <= count:
                    first = hop is not None and m == 1
                    block = held[s][(sign * (m - 1)) % size]
                    came[s, (sign * m) % size] = hop(sign) if first else shift(block, axis, sign)
        for (s, k), block in zip(came, lax.optimization_barrier(tuple(came.values()))):
            held[s][k] = block
    return held


def reduce_rings(streams, axis):
    size = len(streams[0][0])
    found = [[blocks[0]] for blocks, _ in streams]
    came = {}
    for m in range(1, size // 2 + 1):
        sent = {}
        for s, (blocks, far_up) in enumerate(streams):
            for sign, count in zip((1, -1), reaches(size, far_up)):
                if m <= count:
                    block = blocks[(-sign * (count - m + 1)) % size]
                    if m > 1:
                        block = came[s, sign].astype(F32) + block.astype(F32)
                    sent[s, sign] = shift(block.astype(BF16), axis, sign)
        came = dict(zip(sent, lax.optimization_barrier(tuple(sent.values()))))
        for (s, sign), block in came.items():
            if m == reaches(size, streams[s][1])[0 if sign == 1 else 1]:
                found[s].append(block)
    return found


def total(values):
    return functools.reduce(lambda a, b: a + b, [value.astype(F32) for value in values])


def product_kernel(count, start, table_ref, *refs):
    blocks, weight_ref, out_ref = refs[:count], refs[count], refs[count + 1]
    tile = min(256, out_ref.shape[1])
    for at in range(0, out_ref.shape[1], tile):
        total = None
        for k in range(count):
            weight = weight_ref[table_ref[k], :, start + at:start + at + tile]
            part = dot(blocks[k][...], weight, ((1,), (0,)))
            total = part if total is None else total + part
        out_ref[:, at:at + tile] = total


def product(blocks, weights, table, start, width):
    count, (rows, depth) = len(blocks), blocks[0].shape
    return pl.pallas_call(
        functools.partial(product_kernel, count, start),
        out_shape=jax.ShapeDtypeStruct((rows, width), F32),
        in_specs=[pl.BlockSpec(memory_space=pltpu.SMEM)]
        + [pl.BlockSpec(memory_space=pltpu.VMEM)] * (count + 1),
        out_specs=pl.BlockSpec(memory_space=pltpu.VMEM),
        compiler_params=pltpu.CompilerParams(vmem_limit_bytes=32 * 1024 * 1024),
        cost_estimate=pl.CostEstimate(
            flops=2 * rows * count * depth * width,
            bytes_accessed=2 * count * depth * (rows + width) + 4 * rows * width,
            transcendentals=0,
        ),
    )(table, *blocks, weights)


def attend_kernel(table_ref, q_ref, g_ref, kv_ref, live_ref, *rest):
    dq_ref, grad_ref = rest[-2:]
    count = pl.num_programs(0)
    named = table_ref[count + pl.program_id(0)]
    pairs = q_ref.shape[-1] // HD // 2
    scale = HD ** (-0.5)

    @pl.when(named == 0)
    def _():
        dq_ref[...] = jnp.zeros_like(dq_ref)
        grad_ref[...] = jnp.zeros_like(grad_ref)

    @pl.when(named != 0)
    def _():
        live = live_ref[0] > 0.5
        zero = jnp.zeros((SPAN, HD), BF16)

        def diagonal(ref, start):
            one = ref[0, :, start:start + HD]
            two = ref[0, :, start + HD:start + 2 * HD]
            return jnp.concatenate(
                [jnp.concatenate([one, zero], axis=1), jnp.concatenate([zero, two], axis=1)], axis=0
            )

        def first(pair):
            start = pair * 2 * HD
            columns = slice(start, start + 2 * HD)
            scores = dot(kv_ref[0, 0, :, columns], diagonal(q_ref, start), ((1,), (1,)))
            prob_grad = dot(kv_ref[0, 1, :, columns], diagonal(g_ref, start), ((1,), (1,)))
            return scores, prob_grad

        ahead = first(0)
        for pair in range(pairs):
            scores, prob_grad = ahead
            if pair + 1 < pairs:
                ahead = first(pair + 1)
            start = pair * 2 * HD
            columns = slice(start, start + 2 * HD)
            scores = jnp.where(live, scores * scale, -1e30)
            expo = jnp.exp(scores - jnp.max(scores, axis=0, keepdims=True))
            probs = expo * (1.0 / jnp.sum(expo, axis=0, keepdims=True))
            center = jnp.sum(probs * prob_grad, axis=0, keepdims=True)
            score_grad = (probs * (prob_grad - center) * scale).astype(BF16)
            value_grad = dot(probs.astype(BF16), diagonal(g_ref, start), ((1,), (0,)))
            key_grad = dot(score_grad, diagonal(q_ref, start), ((1,), (0,)))
            both = dot(score_grad, kv_ref[0, 0, :, columns], ((0,), (0,)))
            grad_ref[0, 1, :, columns] = value_grad.astype(BF16)
            grad_ref[0, 0, :, columns] = key_grad.astype(BF16)
            dq_ref[0, :, columns] = jnp.concatenate(
                [both[:SPAN, :HD], both[SPAN:, HD:]], axis=1
            ).astype(BF16)


def attend(slots, named, queries, grads, kv, live, part, before):
    count, _, width = queries.shape
    keys = kv.shape[2]
    heads = width // HD
    table = jnp.concatenate([slots, named]).astype(jnp.int32)
    span_block = pl.BlockSpec((1, SPAN, width), lambda r, t: (r, 0, 0))
    part_block = pl.BlockSpec((1, SPAN, width), lambda r, t: (r, 0, part))
    kv_block = pl.BlockSpec((1, 2, keys, width), lambda r, t: (t[r], 0, 0, part))
    live_block = pl.BlockSpec((1, keys, HD), lambda r, t: (t[r], 0, 0))
    in_specs = [span_block, part_block, kv_block, live_block]
    operands = [table, queries, grads, kv, live]
    aliases = {}
    if before is not None:
        in_specs.append(pl.BlockSpec(memory_space=pl.ANY))
        operands.append(before)
        aliases = {len(operands) - 1: 1}
    return pl.pallas_call(
        attend_kernel,
        grid_spec=pltpu.PrefetchScalarGridSpec(
            num_scalar_prefetch=1,
            grid=(count,),
            in_specs=in_specs,
            out_specs=[span_block, kv_block],
        ),
        out_shape=[
            jax.ShapeDtypeStruct(queries.shape, BF16),
            jax.ShapeDtypeStruct(kv.shape, BF16),
        ],
        input_output_aliases=aliases,
        compiler_params=pltpu.CompilerParams(vmem_limit_bytes=40 * 1024 * 1024),
        cost_estimate=pl.CostEstimate(
            flops=count * heads * 5 * 2 * SPAN * keys * HD * 4,
            bytes_accessed=count * 4 * keys * width * 2,
            transcendentals=count * heads * SPAN * keys,
        ),
    )(*operands)


def on_device(span_act, q_weight, out_grad, neighbour_kv, neighbour_ids, owner):
    rows, width = out_grad.shape
    depth = q_weight.shape[0]
    seq_count = lax.axis_size("seq")
    dp_count = lax.axis_size("dp")
    tensor_count = lax.axis_size("tensor")
    couples = dp_count // 2
    seq_at = lax.axis_index("seq")
    dp_at = lax.axis_index("dp")
    tensor_at = lax.axis_index("tensor")
    core = dp_at % 2
    spans = rows // SPAN
    capacity = neighbour_kv.shape[0]
    pairs = capacity // seq_count
    whole_blocks = pairs == spans
    per = span_act.shape[1] // depth // 2
    half = width // 2

    along_seq = gather_rings([(q_weight, True, None)], "seq", seq_count)[0]
    along_dp = gather_rings([(q_weight, True, None)], "dp", couples)[0]
    along_seq, along_dp = lax.optimization_barrier((along_seq, along_dp))

    def columns_of(which):
        return jnp.concatenate(
            [
                lax.dynamic_slice(span_act, (0, (2 * p + which) * depth), (rows, depth))
                for p in range(per)
            ],
            axis=1,
        )

    act_mine, act_other = columns_of(core), columns_of(1 - core)
    own_other = swap(act_other)
    acts_mine, acts_other = gather_rings(
        [(act_mine, True, None), (own_other, False, functools.partial(shift_swap, act_other))],
        "tensor",
        tensor_count,
    )
    acts = [jnp.concatenate(both, axis=0) for both in zip(acts_mine, acts_other)]
    depth_blocks = [(tensor_at - k) % tensor_count for k in range(tensor_count)]
    table = jnp.stack(depth_blocks).astype(jnp.int32)

    cut = width * 5 // 8 // HD * HD
    corner_left = gather_rings(
        [(block[:, :cut], True, None) for block in along_seq[1:]], "dp", couples
    )
    corner_right = gather_rings(
        [(block[:, cut:], True, None) for block in along_dp[1:]], "seq", seq_count
    )

    def block_at(i, j):
        block = ((seq_at - i) % seq_count) * dp_count + ((dp_at // 2 - j) % couples) * 2
        return block // (2 * per), (block % (2 * per)) // 2

    places = [(i, j) for i in range(seq_count) for j in range(couples)]
    zero = after(jnp.zeros((), BF16), own_other)
    weights = jnp.broadcast_to(zero, (tensor_count, per * depth, width))
    for i, j in places:
        at, inner = block_at(i, j)
        if j == 0:
            pieces = [(along_seq[i], 0)]
        elif i == 0:
            pieces = [(along_dp[j], 0)]
        else:
            pieces = [(corner_left[i - 1][j], 0), (corner_right[j - 1][i], cut)]
        for piece, start in pieces:
            weights = lax.dynamic_update_slice(weights, piece[None], (at, inner * depth, start))

    groups = owner.reshape(seq_count, dp_count, spans)
    groups = lax.dynamic_index_in_dim(groups, dp_at, 1, keepdims=False)
    mine = lax.dynamic_index_in_dim(groups, seq_at, 0, keepdims=False)

    def order(group, target):
        names = group == target
        at = jnp.arange(spans)
        ahead = (names[None, :] & ~names[:, None]) | (
            (names[None, :] == names[:, None]) & (at[None, :] < at[:, None])
        )
        return jnp.sum(ahead.astype(jnp.int32), axis=1), names.astype(jnp.int32)

    def message(target):
        place, names = order(mine, target)
        hit = place[None, :] == jnp.arange(pairs)[:, None]
        return hit & (names[None, :] == 1)

    def to_owner(value, step):
        value = value.reshape(spans, SPAN, -1)
        if not whole_blocks:
            hit = message((seq_at + step) % seq_count)
            value = jnp.sum(
                jnp.where(hit[:, :, None, None], value[None], jnp.zeros((), BF16)), axis=1
            )
        return shift(value, "seq", step) if step else value

    def from_owner(value, step):
        value = shift(value, "seq", -step) if step else value
        if not whole_blocks:
            hit = message((seq_at + step) % seq_count)
            value = jnp.sum(
                jnp.where(hit[:, :, None, None], value[:, None], jnp.zeros((), BF16)), axis=0
            )
        return value.reshape(rows, -1)

    def slots_of(step):
        source = (seq_at - step) % seq_count
        group = lax.dynamic_index_in_dim(groups, source, 0, keepdims=False)
        place, names = order(group, seq_at)
        if not whole_blocks:
            place = jnp.arange(pairs)
            names = (place < jnp.sum(names)).astype(jnp.int32)
        return source * pairs + place, names

    live = jnp.broadcast_to((neighbour_ids != 0).astype(F32)[:, :, None], (capacity, KEYS, HD))
    slots = [slots_of(step) for step in range(seq_count)]
    grads = [to_owner(out_grad, step) for step in range(seq_count)]

    table = after(table, *grads)
    queries = []
    for part in range(2):
        partial = product(acts, weights, table, part * half, half)
        queries.append((partial[:rows] + swap(partial[rows:])).astype(BF16))
    asked = [[to_owner(value, step) for step in range(seq_count)] for value in queries]

    kv_grad = None
    both_grads, products = [], []
    for part in range(2):
        answers = []
        for step in range(seq_count):
            answer, kv_grad = attend(
                *slots[step], asked[part][step], grads[step], neighbour_kv, live, part, kv_grad
            )
            answers.append(from_owner(answer, step))
        if part:
            answers[-1] = after(answers[-1], products[0][places[-1]])
        grad = sum(answers[1:], answers[0])
        both_grads.append(jnp.concatenate([grad, swap(grad)], axis=0))
        if part == 0:
            act_whole = jnp.broadcast_to(zero, (tensor_count, 2 * rows, per * depth))
            for k in range(tensor_count):
                act_whole = lax.dynamic_update_slice(
                    act_whole, acts[k][None], (depth_blocks[k], 0, 0)
                )

        found = {}
        for i, j in reversed(places):
            at, inner = block_at(i, j)
            block = lax.dynamic_slice(act_whole, (at, 0, inner * depth), (1, 2 * rows, depth))[0]
            found[i, j] = dot(block, both_grads[part], ((0,), (0,)))
            if (i, j) != (0, 0):
                found[i, j] = lax.optimization_barrier(found[i, j].astype(BF16))
        products.append(found)

    both_grad = jnp.concatenate(both_grads, axis=1)
    parts = [None] * tensor_count
    for k in sorted(range(tensor_count), key=lambda k: -min(k, tensor_count - k)):
        block = lax.dynamic_index_in_dim(weights, depth_blocks[k], 0, keepdims=False)
        part = dot(both_grad, block, ((1,), (1,))).astype(BF16)
        parts[k] = lax.optimization_barrier(part)
    mine_parts, other_parts = reduce_rings(
        [([part[:rows] for part in parts], True), ([part[rows:] for part in parts], False)],
        "tensor",
    )
    arrived = swap(total(other_parts).astype(BF16))
    kept = total(mine_parts).astype(BF16)
    even = jnp.where(core == 0, kept, arrived)
    odd = jnp.where(core == 0, arrived, kept)
    act_grad = jnp.concatenate(
        [value[:, p * depth:(p + 1) * depth] for p in range(per) for value in (even, odd)], axis=1
    )

    left = reduce_rings(
        [([products[0][i, j] for j in range(couples)], True) for i in range(seq_count)], "dp"
    )
    right = reduce_rings(
        [([products[1][i, j] for i in range(seq_count)], True) for j in range(couples)], "seq"
    )
    left, right = lax.optimization_barrier((left, right))
    left = reduce_rings([([total(values) for values in left], True)], "seq")[0]
    right = reduce_rings([([total(values) for values in right], True)], "dp")[0]
    left, right = total(left), total(right)
    weight_grad = jnp.concatenate([left, right], axis=1)
    return (act_grad, weight_grad, kv_grad)


def solution(mesh):
    in_specs = (
        P(("seq", "dp"), "tensor"),
        P(("seq", "dp"), "tensor"),
        P(("seq", "dp"), "tensor"),
        P(("seq", "dp"), None, None, "tensor"),
        P(("seq", "dp"), None),
        P(),
    )
    out_specs = (
        P(("seq", "dp"), "tensor"),
        P(("seq", "dp"), "tensor"),
        P(("seq", "dp"), None, None, "tensor"),
    )
    return jax.shard_map(
        on_device, mesh=mesh, in_specs=in_specs, out_specs=out_specs, check_vma=False
    )
```

time: 241 us -> 260 us (1.079)
  waiting for transfers between devices: 120 us -> 137 us
  Pallas kernels: 28.1 us -> 16.1 us
  other arithmetic: 7.68 us -> 16.1 us
  starting transfers between devices: 36.3 us -> 42.3 us
    ppermute x0 -> x2, waiting for transfers between devices: none -> 9.8 us  [shift_swap(): return lax.ppermute(value, ('tensor', 'dp'), pairs)]
    pallas_call x2, Pallas kernels: 13 us -> 5.74 us  [product(): pl.pallas_call(functools.partial(product_kernel, count, start), out_shape...]
    ppermute x30 -> x25, waiting for transfers between devices: 119 us -> 125 us  [shift(): lax.ppermute(value, axis, [(i, (i + step * stride) % size) for i in range...]
    ppermute x30 -> x25, starting transfers between devices: 35 us -> 41.5 us  [shift(): lax.ppermute(value, axis, [(i, (i + step * stride) % size) for i in range...]
    unnamed x18 -> x41, local copies, waits for them, and re-layouts: 0.38 us -> 5.81 us
    dynamic_update_slice x14 -> x8, local copies, waits for them, and re-layouts: 12.5 us -> 7.61 us  [the longest x5 4.49 us: on_device(): lax.dynamic_update_slice(weights, piece[None], (at, inner * depth, start))]
    pallas_call x4, Pallas kernels: 15.1 us -> 10.3 us  [attend(): pl.pallas_call(attend_kernel, grid_spec=pltpu.PrefetchScalarGridSpec(num_...]
  transfers between devices with their start and end apart: 38 -> 33, of which waited for: 19 -> 17; matrix products, arithmetic and copies ran while one was open for 20% -> 20% of each run, Pallas kernels for 10% -> 5%
where the time goes in v3:
time: 260 us; the launch traced here: 259 us
  waiting for transfers between devices  137 us (53%)
  starting transfers between devices  42.3 us (16%)
  matrix products  22.9 us (9%)
  local copies, waits for them, and re-layouts  22.7 us (9%)
  other arithmetic  16.1 us (6%)
  Pallas kernels  16.1 us (6%)
    ppermute x25, waiting for transfers between devices, shift(): lax.ppermute(value, axis, [(i, (i + step * stride) % size) for i in range...  125 us
    ppermute x25, starting transfers between devices, shift(): lax.ppermute(value, axis, [(i, (i + step * stride) % size) for i in range...  41.5 us
    dot_general x12, matrix products, dot(): lax.dot_general(a, b, (contract, ((), ())), preferred_element_type=F32)  22.9 us
    pallas_call x4, Pallas kernels, attend(): pl.pallas_call(attend_kernel, grid_spec=pltpu.PrefetchScalarGridSpec(num_...  10.3 us
    ppermute x2, waiting for transfers between devices, shift_swap(): return lax.ppermute(value, ('tensor', 'dp'), pairs)  9.8 us
    unnamed x41, local copies, waits for them, and re-layouts  5.81 us
    pallas_call x2, Pallas kernels, product(): pl.pallas_call(functools.partial(product_kernel, count, start), out_shape...  5.74 us
  transfers between devices with their start and end apart: 33, of which 17 were waited for; matrix products, arithmetic and copies ran while one was open for 20% of the time, Pallas kernels for 5%

profile of v3, /device:TPU:0, one launch (start us, length us, event | category | flops | bytes accessed | tf_op | source)
XLA Modules:
  0.0 258.6 jit_solution(14035272333805853756)
XLA Ops:
  0.7 3.0 %collective-permute-start.8 = (bf16[1024,1024]{1,0:T(8,128)(2,1)}, bf16[1024,1024]{1,0:T(8,128)(2,1)}, u32[]{:S(2)}, u32[]{:S(2)}) collective-permute-start(bf16[1024,1024]{1,0:T(8,128)(2,1)} %param.7), channel_id=1, source_target_pairs={{0,16},{16,0},{1,17},{17,1},{2,18},{18,2},{3,19},{19,3},{4,20},{20... | collective-permute-start | bytes 6291464 | tf_op jit(solution)/shard_map/ppermute | solution.py:24
  8.1 2.2 collective-permute-start.3
  10.7 12.7 %collective-permute-done.2 = bf16[256,1024]{1,0:T(8,128)(2,1)} collective-permute-done((bf16[256,1024]{1,0:T(8,128)(2,1)S(1)}, bf16[256,1024]{1,0:T(8,128)(2,1)}, u32[]{:S(2)}, u32[]{:S(2)}) %collective-permute-start.2) | collective-permute-done | bytes 524320 | tf_op jit(solution)/shard_map/ppermute | solution.py:24
  23.4 19.1 %collective-permute-done.3 = bf16[256,1024]{1,0:T(8,128)(2,1)S(1)} collective-permute-done((bf16[256,1024]{1,0:T(8,128)(2,1)S(1)}, bf16[256,1024]{1,0:T(8,128)(2,1)S(1)}, u32[]{:S(2)}, u32[]{:S(2)}) %collective-permute-start.3) | collective-permute-done | bytes 524320 | tf_op jit(solution)/shard_map/ppermute | solution.py:24
  44.3 9.6 %collective-permute-done.5 = bf16[256,1024]{1,0:T(8,128)(2,1)} collective-permute-done((bf16[256,1024]{1,0:T(8,128)(2,1)S(1)}, bf16[256,1024]{1,0:T(8,128)(2,1)}, u32[]{:S(2)}, u32[]{:S(2)}) %collective-permute-start.5) | collective-permute-done | bytes 524320 | tf_op jit(solution)/shard_map/ppermute | solution.py:38
  53.9 1.8 collective-permute-start.6
  55.8 2.0 collective-permute-start.7
  63.2 7.6 %collective-permute-done.6 = bf16[256,1024]{1,0:T(8,128)(2,1)S(1)} collective-permute-done((bf16[256,1024]{1,0:T(8,128)(2,1)}, bf16[256,1024]{1,0:T(8,128)(2,1)S(1)}, u32[]{:S(2)}, u32[]{:S(2)}) %collective-permute-start.6) | collective-permute-done | bytes 524320 | tf_op jit(solution)/shard_map/ppermute | solution.py:24
  70.8 10.1 %collective-permute-done.7 = bf16[256,1024]{1,0:T(8,128)(2,1)S(1)} collective-permute-done((bf16[256,1024]{1,0:T(8,128)(2,1)}, bf16[256,1024]{1,0:T(8,128)(2,1)S(1)}, u32[]{:S(2)}, u32[]{:S(2)}) %collective-permute-start.7) | collective-permute-done | bytes 524320 | tf_op jit(solution)/shard_map/ppermute | solution.py:24
  84.2 1.9 bitcast_dynamic-update-slice_fusion.1
  86.1 1.9 bitcast_dynamic-update-slice_fusion
  87.9 12.9 %collective-permute-done.11 = bf16[1024,384]{1,0:T(8,128)(2,1)S(1)} collective-permute-done((bf16[1024,384]{1,0:T(8,128)(2,1)S(1)}, bf16[1024,384]{1,0:T(8,128)(2,1)S(1)}, u32[]{:S(2)}, u32[]{:S(2)}) %collective-permute-start.11) | collective-permute-done | bytes 786464 | tf_op jit(solution)/shard_map/ppermute | solution.py:24
  101.3 2.9 %shard_map.85 = f32[512,512]{1,0:T(8,128)S(1)} custom-call(s32[4]{0:T(128)S(1)} %pad_add_fusion.1.table_ref, bf16[512,1024]{1,0:T(8,128)(2,1)S(1)} %pad_maximum_fusion.1.refs_0_, bf16[512,1024]{1,0:T(8,128)(2,1)S(1)} %get-tuple-element.93.refs_1_, bf16[512,1024]{1,0:T(8,128)(2,1)S(1)} %constant_dynamic-update-slice_fusion.2.refs_2_, ...), custom_call_target="tpu_custom_call" | custom-call | flops 2147483648 | bytes 9437184 | tf_op jit(solution)/shard_map/pallas_call | solution.py:103
  104.8 2.5 broadcast_in_dim.58
  107.3 2.2 bitcast_dynamic-update-slice_fusion.7
  109.5 3.4 %copy-done.1 = bf16[4,1024,1024]{2,1,0:T(8,128)(2,1)S(1)} copy-done((bf16[4,1024,1024]{2,1,0:T(8,128)(2,1)S(1)}, bf16[4,1024,1024]{2,1,0:T(8,128)(2,1)}, u32[]{:S(2)}) %copy-start.1) | copy-done | bytes 8388632
  112.9 2.9 %shard_map.88 = f32[512,512]{1,0:T(8,128)S(1)} custom-call(s32[4]{0:T(128)S(1)} %pad_add_fusion.1.table_ref, bf16[512,1024]{1,0:T(8,128)(2,1)S(1)} %pad_maximum_fusion.1.refs_0_, bf16[512,1024]{1,0:T(8,128)(2,1)S(1)} %get-tuple-element.93.refs_1_, bf16[512,1024]{1,0:T(8,128)(2,1)S(1)} %constant_dynamic-update-slice_fusion.2.refs_2_, ...), custom_call_target="tpu_custom_call" | custom-call | flops 2147483648 | bytes 9437184 | tf_op jit(solution)/shard_map/pallas_call | solution.py:103
  118.1 1.7 collective-permute-start.17
  120.2 2.6 shard_map.86
  122.7 4.0 %collective-permute-done.13.q_ref = bf16[4,64,512]{2,1,0:T(8,128)(2,1)S(1)} collective-permute-done((bf16[4,64,512]{2,1,0:T(8,128)(2,1)S(1)}, bf16[4,64,512]{2,1,0:T(8,128)(2,1)S(1)}, u32[]{:S(2)}, u32[]{:S(2)}) %collective-permute-start.13) | collective-permute-done | bytes 262176 | tf_op jit(solution)/shard_map/ppermute | solution.py:24
  126.8 2.6 shard_map.87
  129.3 2.1 collective-permute-start.14
  132.5 2.6 shard_map.89
  135.1 2.6 shard_map.90
  137.7 3.4 %collective-permute-start.18 = (bf16[4,64,512]{2,1,0:T(8,128)(2,1)S(1)}, bf16[4,64,512]{2,1,0:T(8,128)(2,1)S(1)}, u32[]{:S(2)}, u32[]{:S(2)}) collective-permute-start(bf16[4,64,512]{2,1,0:T(8,128)(2,1)S(1)} %get-tuple-element.58), channel_id=1, source_target_pairs={{0,16},{16,0},{1,17},{17,1},{2,18},{18,2},{3,19},{19,3},{4,20},{20... | collective-permute-start | bytes 786440 | tf_op jit(solution)/shard_map/ppermute | solution.py:24
  142.8 2.0 convolution_convert_fusion.5
  148.9 2.5 collective-permute-start.20
  156.3 3.3 %collective-permute-start.23 = (bf16[256,1024]{1,0:T(8,128)(2,1)S(1)}, bf16[256,1024]{1,0:T(8,128)(2,1)S(1)}, u32[]{:S(2)}, u32[]{:S(2)}) collective-permute-start(bf16[256,1024]{1,0:T(8,128)(2,1)S(1)} %get-tuple-element.85), channel_id=1, source_target_pairs={{0,12},{4,0},{8,4},{12,8},{1,13},{5,1},{9,5},{13,9},{2,14},{6,2},{... | collective-permute-start | bytes 1572872 | tf_op jit(solution)/shard_map/ppermute | solution.py:24
  159.6 2.0 convolution_convert_fusion.4
  162.2 2.0 fusion.30
  164.2 2.0 convolution_convert_fusion.2
  166.2 2.0 convolution_convert_fusion.1
  169.7 7.4 %collective-permute-done.21 = bf16[256,1024]{1,0:T(8,128)(2,1)} collective-permute-done((bf16[256,1024]{1,0:T(8,128)(2,1)S(1)}, bf16[256,1024]{1,0:T(8,128)(2,1)}, u32[]{:S(2)}, u32[]{:S(2)}) %collective-permute-start.21) | collective-permute-done | bytes 524320 | tf_op jit(solution)/shard_map/ppermute | solution.py:24
  177.2 1.7 collective-permute-start.29
  178.9 9.4 %collective-permute-done.22 = bf16[256,1024]{1,0:T(8,128)(2,1)S(1)} collective-permute-done((bf16[256,1024]{1,0:T(8,128)(2,1)S(1)}, bf16[256,1024]{1,0:T(8,128)(2,1)S(1)}, u32[]{:S(2)}, u32[]{:S(2)}) %collective-permute-start.22) | collective-permute-done | bytes 524320 | tf_op jit(solution)/shard_map/ppermute | solution.py:24
  188.3 1.7 collective-permute-start.30
  190.0 8.6 %collective-permute-done.23 = bf16[256,1024]{1,0:T(8,128)(2,1)S(1)} collective-permute-done((bf16[256,1024]{1,0:T(8,128)(2,1)S(1)}, bf16[256,1024]{1,0:T(8,128)(2,1)S(1)}, u32[]{:S(2)}, u32[]{:S(2)}) %collective-permute-start.23) | collective-permute-done | bytes 524320 | tf_op jit(solution)/shard_map/ppermute | solution.py:24
  199.6 3.3 %collective-permute-start.25 = (bf16[256,1024]{1,0:T(8,128)(2,1)S(1)}, bf16[256,1024]{1,0:T(8,128)(2,1)S(1)}, u32[]{:S(2)}, u32[]{:S(2)}) collective-permute-start(bf16[256,1024]{1,0:T(8,128)(2,1)S(1)} %add_convert_fusion.4), channel_id=1, source_target_pairs={{0,12},{4,0},{8,4},{12,8},{1,13},{5,1},{9,5},{13,9},{2,14},{6,2},{... | collective-permute-start | bytes 1572872 | tf_op jit(solution)/shard_map/ppermute | solution.py:24
  202.9 2.0 convolution_convert_fusion.3
  206.3 2.4 convolution_convert_fusion
  208.7 3.3 %fusion.28 = f32[1024,512]{1,0:T(8,128)} fusion(bf16[4,512,1024]{2,1,0:T(8,128)(2,1)} %bitcast_dynamic-update-slice_fusion.4, s32[]{:T(128)S(6)} %select_n.256, bf16[256,512]{1,0:T(8,128)(2,1)S(1)} %collective-permute-done.19, bf16[256,512]{1,0:T(8,128)(2,1)S(1)} %bitcast_add_fusion), kind=kOutput, calls=%fused_computation.38 | convolution fusion | flops 537919488 | bytes 3670020 | tf_op jit(solution)/shard_map/dot_general | solution.py:18
  212.0 3.5 %collective-permute-done.24 = bf16[256,1024]{1,0:T(8,128)(2,1)S(1)} collective-permute-done((bf16[256,1024]{1,0:T(8,128)(2,1)S(1)}, bf16[256,1024]{1,0:T(8,128)(2,1)S(1)}, u32[]{:S(2)}, u32[]{:S(2)}) %collective-permute-start.24) | collective-permute-done | bytes 524320 | tf_op jit(solution)/shard_map/ppermute | solution.py:24
  215.5 9.0 %collective-permute-done.25 = bf16[256,1024]{1,0:T(8,128)(2,1)S(1)} collective-permute-done((bf16[256,1024]{1,0:T(8,128)(2,1)S(1)}, bf16[256,1024]{1,0:T(8,128)(2,1)S(1)}, u32[]{:S(2)}, u32[]{:S(2)}) %collective-permute-start.25) | collective-permute-done | bytes 524320 | tf_op jit(solution)/shard_map/ppermute | solution.py:24
  227.8 1.8 collective-permute-start.31
  229.6 2.1 broadcast_select_fusion.1
  232.7 20.1 %collective-permute-done.32 = bf16[1024,512]{1,0:T(8,128)(2,1)} collective-permute-done((bf16[1024,512]{1,0:T(8,128)(2,1)}, bf16[1024,512]{1,0:T(8,128)(2,1)}, u32[]{:S(2)}, u32[]{:S(2)}) %collective-permute-start.32) | collective-permute-done | bytes 1048608 | tf_op jit(solution)/shard_map/ppermute | solution.py:24
  252.8 1.7 convert_add_fusion
  256.2 2.4 pad_maximum_fusion
  (127 shorter events, 40.9 us)
Async XLA Ops:
  0.6 9.7 %copy-start.14 = (s32[32]{0:T(128)S(1)}, s32[32]{0:T(128)}, u32[]{:S(2)}) copy-start(s32[32]{0:T(128)} %param.11) | copy-start | bytes 388
  0.6 22.8 %copy-start.13 = (s32[8,256]{1,0:T(8,128)S(1)}, s32[8,256]{1,0:T(8,128)}, u32[]{:S(2)}) copy-start(s32[8,256]{1,0:T(8,128)} %param.10) | copy-start | bytes 24580
  0.7 43.1 %copy-start.2 = (bf16[256,1024]{1,0:T(8,128)(2,1)S(1)}, bf16[256,1024]{1,0:T(8,128)(2,1)}, u32[]{:S(2)}) copy-start(bf16[256,1024]{1,0:T(8,128)(2,1)} %param.8) | copy-start | bytes 1572868
  0.7 55.1 %collective-permute-start.8 = (bf16[1024,1024]{1,0:T(8,128)(2,1)}, bf16[1024,1024]{1,0:T(8,128)(2,1)}, u32[]{:S(2)}, u32[]{:S(2)}) collective-permute-start(bf16[1024,1024]{1,0:T(8,128)(2,1)} %param.7), channel_id=1, source_target_pairs={{0,16},{16,0},{1,17},{17,1},{2,18},{18,2},{3,19},{19,3},{4,20},{20... | collective-permute-start | bytes 6291464 | tf_op jit(solution)/shard_map/ppermute | solution.py:24
  3.7 56.4 %collective-permute-start.9 = (bf16[1024,1024]{1,0:T(8,128)(2,1)}, bf16[1024,1024]{1,0:T(8,128)(2,1)}, u32[]{:S(2)}, u32[]{:S(2)}) collective-permute-start(bf16[1024,1024]{1,0:T(8,128)(2,1)} %param.7), channel_id=1, source_target_pairs={{0,2},{1,3},{2,0},{3,1},{4,6},{5,7},{6,4},{7,5},{8,10},{9,11},{10,... | collective-permute-start | bytes 6291464 | tf_op jit(solution)/shard_map/ppermute | solution.py:24
  6.5 16.9 %collective-permute-start.2 = (bf16[256,1024]{1,0:T(8,128)(2,1)S(1)}, bf16[256,1024]{1,0:T(8,128)(2,1)}, u32[]{:S(2)}, u32[]{:S(2)}) collective-permute-start(bf16[256,1024]{1,0:T(8,128)(2,1)S(1)} %get-tuple-element.87), channel_id=1, source_target_pairs={{0,4},{4,8},{8,12},{12,0},{1,5},{5,9},{9,13},{13,1},{2,6},{6,10},{... | collective-permute-start | bytes 1572872 | tf_op jit(solution)/shard_map/ppermute | solution.py:24
  8.1 34.4 %collective-permute-start.3 = (bf16[256,1024]{1,0:T(8,128)(2,1)S(1)}, bf16[256,1024]{1,0:T(8,128)(2,1)S(1)}, u32[]{:S(2)}, u32[]{:S(2)}) collective-permute-start(bf16[256,1024]{1,0:T(8,128)(2,1)S(1)} %get-tuple-element.87), channel_id=1, source_target_pairs={{0,12},{4,0},{8,4},{12,8},{1,13},{5,1},{9,5},{13,9},{2,14},{6,2},{... | collective-permute-start | bytes 1572872 | tf_op jit(solution)/shard_map/ppermute | solution.py:24
  10.3 32.7 %collective-permute-start.4 = (bf16[256,1024]{1,0:T(8,128)(2,1)S(1)}, bf16[256,1024]{1,0:T(8,128)(2,1)S(1)}, u32[]{:S(2)}, u32[]{:S(2)}) collective-permute-start(bf16[256,1024]{1,0:T(8,128)(2,1)S(1)} %get-tuple-element.88), channel_id=1, source_target_pairs={{0,5},{1,4},{2,7},{3,6},{4,9},{5,8},{6,11},{7,10},{8,13},{9,12},{1... | collective-permute-start | bytes 1572872 | tf_op jit(solution)/shard_map/ppermute | solution.py:38
  23.3 30.6 %collective-permute-start.5 = (bf16[256,1024]{1,0:T(8,128)(2,1)S(1)}, bf16[256,1024]{1,0:T(8,128)(2,1)}, u32[]{:S(2)}, u32[]{:S(2)}) collective-permute-start(bf16[256,1024]{1,0:T(8,128)(2,1)S(1)} %get-tuple-element.88), channel_id=1, source_target_pairs={{0,13},{1,12},{2,15},{3,14},{4,1},{5,0},{6,3},{7,2},{8,5},{9,4},{1... | collective-permute-start | bytes 1572872 | tf_op jit(solution)/shard_map/ppermute | solution.py:38
  42.5 19.6 %collective-permute-start.1 = (bf16[256,1024]{1,0:T(8,128)(2,1)S(1)}, bf16[256,1024]{1,0:T(8,128)(2,1)}, u32[]{:S(2)}, u32[]{:S(2)}) collective-permute-start(bf16[256,1024]{1,0:T(8,128)(2,1)S(1)} %get-tuple-element.88), channel_id=1, source_target_pairs={{0,1},{1,0},{2,3},{3,2},{4,5},{5,4},{6,7},{7,6},{8,9},{9,8},{10,11... | collective-permute-start | bytes 1572872 | tf_op jit(solution)/shard_map/ppermute | solution.py:28
  43.8 15.1 %copy-start.11 = (bf16[256,1024]{1,0:T(8,128)(2,1)S(1)}, bf16[256,1024]{1,0:T(8,128)(2,1)}, u32[]{:S(2)}) copy-start(bf16[256,1024]{1,0:T(8,128)(2,1)} %copy-done.10) | copy-start | bytes 1572868
  43.8 19.4 %collective-permute-start = (bf16[4,64,1024]{2,1,0:T(8,128)(2,1)S(1)}, bf16[4,64,1024]{2,1,0:T(8,128)(2,1)S(1)}, u32[]{:S(2)}, u32[]{:S(2)}) collective-permute-start(bf16[4,64,1024]{2,1,0:T(8,128)(2,1)S(1)} %bitcast.79), channel_id=1, source_target_pairs={{0,16},{16,0},{1,17},{17,1},{2,18},{18,2},{3,19},{19,3},{4,20},{20... | collective-permute-start | bytes 1572872 | tf_op jit(solution)/shard_map/ppermute | solution.py:24
  53.9 16.9 %collective-permute-start.6 = (bf16[256,1024]{1,0:T(8,128)(2,1)}, bf16[256,1024]{1,0:T(8,128)(2,1)S(1)}, u32[]{:S(2)}, u32[]{:S(2)}) collective-permute-start(bf16[256,1024]{1,0:T(8,128)(2,1)} %collective-permute-done.2), channel_id=1, source_target_pairs={{0,4},{4,8},{8,12},{12,0},{1,5},{5,9},{9,13},{13,1},{2,6},{6,10},{... | collective-permute-start | bytes 1572872 | tf_op jit(solution)/shard_map/ppermute | solution.py:24
  55.8 25.1 %collective-permute-start.7 = (bf16[256,1024]{1,0:T(8,128)(2,1)}, bf16[256,1024]{1,0:T(8,128)(2,1)S(1)}, u32[]{:S(2)}, u32[]{:S(2)}) collective-permute-start(bf16[256,1024]{1,0:T(8,128)(2,1)} %collective-permute-done.5), channel_id=1, source_target_pairs={{0,12},{4,0},{8,4},{12,8},{1,13},{5,1},{9,5},{13,9},{2,14},{6,2},{... | collective-permute-start | bytes 1572872 | tf_op jit(solution)/shard_map/ppermute | solution.py:24
  61.5 39.3 %collective-permute-start.10 = (bf16[1024,640]{1,0:T(8,128)(2,1)S(1)}, bf16[1024,640]{1,0:T(8,128)(2,1)S(1)}, u32[]{:S(2)}, u32[]{:S(2)}) collective-permute-start(bf16[1024,640]{1,0:T(8,128)(2,1)S(1)} %slice.42), channel_id=1, source_target_pairs={{0,2},{1,3},{2,0},{3,1},{4,6},{5,7},{6,4},{7,5},{8,10},{9,11},{10,... | collective-permute-start | bytes 3932168 | tf_op jit(solution)/shard_map/ppermute | solution.py:24
  82.2 18.6 %collective-permute-start.11 = (bf16[1024,384]{1,0:T(8,128)(2,1)S(1)}, bf16[1024,384]{1,0:T(8,128)(2,1)S(1)}, u32[]{:S(2)}, u32[]{:S(2)}) collective-permute-start(bf16[1024,384]{1,0:T(8,128)(2,1)S(1)} %slice.43), channel_id=1, source_target_pairs={{0,16},{16,0},{1,17},{17,1},{2,18},{18,2},{3,19},{19,3},{4,20},{20... | collective-permute-start | bytes 2359304 | tf_op jit(solution)/shard_map/ppermute | solution.py:24
  104.7 12.8 %collective-permute-start.12 = (f32[256,512]{1,0:T(8,128)S(1)}, f32[256,512]{1,0:T(8,128)S(1)}, u32[]{:S(2)}, u32[]{:S(2)}) collective-permute-start(f32[256,512]{1,0:T(8,128)S(1)} %slice.57), channel_id=1, source_target_pairs={{0,1},{1,0},{2,3},{3,2},{4,5},{5,4},{6,7},{7,6},{8,9},{9,8},{10,11... | collective-permute-start | bytes 1572872 | tf_op jit(solution)/shard_map/ppermute | solution.py:28
  107.3 12.8 %slice-start = ((s8[8388608]{0:T(1024)(128)(4,1)}), s8[4194304]{0:T(1024)(128)(4,1)S(1)}, s32[]{:S(2)}) async-start(s8[8388608]{0:T(1024)(128)(4,1)} %bitcast.75), calls=%async_computation | async-start | bytes 8388608
  109.5 3.4 %copy-start.1 = (bf16[4,1024,1024]{2,1,0:T(8,128)(2,1)S(1)}, bf16[4,1024,1024]{2,1,0:T(8,128)(2,1)}, u32[]{:S(2)}) copy-start(bf16[4,1024,1024]{2,1,0:T(8,128)(2,1)} %copy-done) | copy-start | bytes 25165828
  112.9 7.2 %slice-start.1 = ((s8[8388608]{0:T(1024)(128)(4,1)}), s8[4194304]{0:T(1024)(128)(4,1)S(1)}, s32[]{:S(2)}) async-start(s8[8388608]{0:T(1024)(128)(4,1)} %bitcast.75), calls=%async_computation.1 | async-start | bytes 8388608
  115.8 2.2 collective-permute-start.16
  117.5 9.2 %collective-permute-start.13 = (bf16[4,64,512]{2,1,0:T(8,128)(2,1)S(1)}, bf16[4,64,512]{2,1,0:T(8,128)(2,1)S(1)}, u32[]{:S(2)}, u32[]{:S(2)}) collective-permute-start(bf16[4,64,512]{2,1,0:T(8,128)(2,1)S(1)} %bitcast.84), channel_id=1, source_target_pairs={{0,16},{16,0},{1,17},{17,1},{2,18},{18,2},{3,19},{19,3},{4,20},{20... | collective-permute-start | bytes 786440 | tf_op jit(solution)/shard_map/ppermute | solution.py:24
  118.1 17.0 %collective-permute-start.17 = (bf16[4,64,512]{2,1,0:T(8,128)(2,1)S(1)}, bf16[4,64,512]{2,1,0:T(8,128)(2,1)S(1)}, u32[]{:S(2)}, u32[]{:S(2)}) collective-permute-start(bf16[4,64,512]{2,1,0:T(8,128)(2,1)S(1)} %bitcast.82), channel_id=1, source_target_pairs={{0,16},{16,0},{1,17},{17,1},{2,18},{18,2},{3,19},{19,3},{4,20},{20... | collective-permute-start | bytes 786440 | tf_op jit(solution)/shard_map/ppermute | solution.py:24
  129.3 11.8 %collective-permute-start.14 = (bf16[4,64,512]{2,1,0:T(8,128)(2,1)S(1)}, bf16[4,64,512]{2,1,0:T(8,128)(2,1)S(1)}, u32[]{:S(2)}, u32[]{:S(2)}) collective-permute-start(bf16[4,64,512]{2,1,0:T(8,128)(2,1)S(1)} %get-tuple-element.54), channel_id=1, source_target_pairs={{0,16},{16,0},{1,17},{17,1},{2,18},{18,2},{3,19},{19,3},{4,20},{20... | collective-permute-start | bytes 786440 | tf_op jit(solution)/shard_map/ppermute | solution.py:24
  132.5 15.0 %slice-start.2 = ((s8[8388608]{0:T(1024)(128)(4,1)}), s8[4194304]{0:T(1024)(128)(4,1)S(1)}, s32[]{:S(2)}) async-start(s8[8388608]{0:T(1024)(128)(4,1)} %bitcast.77), calls=%async_computation.2 | async-start | bytes 8388608
  135.1 12.4 %slice-start.3 = ((s8[8388608]{0:T(1024)(128)(4,1)}), s8[4194304]{0:T(1024)(128)(4,1)S(1)}, s32[]{:S(2)}) async-start(s8[8388608]{0:T(1024)(128)(4,1)} %bitcast.77), calls=%async_computation.3 | async-start | bytes 8388608
  137.7 8.1 %collective-permute-start.18 = (bf16[4,64,512]{2,1,0:T(8,128)(2,1)S(1)}, bf16[4,64,512]{2,1,0:T(8,128)(2,1)S(1)}, u32[]{:S(2)}, u32[]{:S(2)}) collective-permute-start(bf16[4,64,512]{2,1,0:T(8,128)(2,1)S(1)} %get-tuple-element.58), channel_id=1, source_target_pairs={{0,16},{16,0},{1,17},{17,1},{2,18},{18,2},{3,19},{19,3},{4,20},{20... | collective-permute-start | bytes 786440 | tf_op jit(solution)/shard_map/ppermute | solution.py:24
  141.2 1.6 collective-permute-start.15
  145.9 1.6 collective-permute-start.19
  148.9 19.2 %collective-permute-start.20 = (bf16[256,1024]{1,0:T(8,128)(2,1)S(1)}, bf16[256,1024]{1,0:T(8,128)(2,1)S(1)}, u32[]{:S(2)}, u32[]{:S(2)}) collective-permute-start(bf16[256,1024]{1,0:T(8,128)(2,1)S(1)} %get-tuple-element.86), channel_id=1, source_target_pairs={{0,4},{4,8},{8,12},{12,0},{1,5},{5,9},{9,13},{13,1},{2,6},{6,10},{... | collective-permute-start | bytes 1572872 | tf_op jit(solution)/shard_map/ppermute | solution.py:24
  152.8 24.4 %collective-permute-start.21 = (bf16[256,1024]{1,0:T(8,128)(2,1)S(1)}, bf16[256,1024]{1,0:T(8,128)(2,1)}, u32[]{:S(2)}, u32[]{:S(2)}) collective-permute-start(bf16[256,1024]{1,0:T(8,128)(2,1)S(1)} %slice.62), channel_id=1, source_target_pairs={{0,12},{4,0},{8,4},{12,8},{1,13},{5,1},{9,5},{13,9},{2,14},{6,2},{... | collective-permute-start | bytes 1572872 | tf_op jit(solution)/shard_map/ppermute | solution.py:24
  155.7 32.5 %collective-permute-start.22 = (bf16[256,1024]{1,0:T(8,128)(2,1)S(1)}, bf16[256,1024]{1,0:T(8,128)(2,1)S(1)}, u32[]{:S(2)}, u32[]{:S(2)}) collective-permute-start(bf16[256,1024]{1,0:T(8,128)(2,1)S(1)} %slice.63), channel_id=1, source_target_pairs={{0,4},{4,8},{8,12},{12,0},{1,5},{5,9},{9,13},{13,1},{2,6},{6,10},{... | collective-permute-start | bytes 1572872 | tf_op jit(solution)/shard_map/ppermute | solution.py:24
  156.3 42.3 %collective-permute-start.23 = (bf16[256,1024]{1,0:T(8,128)(2,1)S(1)}, bf16[256,1024]{1,0:T(8,128)(2,1)S(1)}, u32[]{:S(2)}, u32[]{:S(2)}) collective-permute-start(bf16[256,1024]{1,0:T(8,128)(2,1)S(1)} %get-tuple-element.85), channel_id=1, source_target_pairs={{0,12},{4,0},{8,4},{12,8},{1,13},{5,1},{9,5},{13,9},{2,14},{6,2},{... | collective-permute-start | bytes 1572872 | tf_op jit(solution)/shard_map/ppermute | solution.py:24
  161.6 38.0 %collective-permute-start.27 = (bf16[1024,512]{1,0:T(8,128)(2,1)S(1)}, bf16[1024,512]{1,0:T(8,128)(2,1)S(1)}, u32[]{:S(2)}, u32[]{:S(2)}) collective-permute-start(bf16[1024,512]{1,0:T(8,128)(2,1)S(1)} %convolution_convert_fusion.4), channel_id=1, source_target_pairs={{0,2},{1,3},{2,0},{3,1},{4,6},{5,7},{6,4},{7,5},{8,10},{9,11},{10,... | collective-permute-start | bytes 3145736 | tf_op jit(solution)/shard_map/ppermute | solution.py:24
  168.2 43.8 %collective-permute-start.28 = (bf16[1024,512]{1,0:T(8,128)(2,1)S(1)}, bf16[1024,512]{1,0:T(8,128)(2,1)S(1)}, u32[]{:S(2)}, u32[]{:S(2)}) collective-permute-start(bf16[1024,512]{1,0:T(8,128)(2,1)S(1)} %convolution_convert_fusion.5), channel_id=1, source_target_pairs={{0,2},{1,3},{2,0},{3,1},{4,6},{5,7},{6,4},{7,5},{8,10},{9,11},{10,... | collective-permute-start | bytes 3145736 | tf_op jit(solution)/shard_map/ppermute | solution.py:24
  177.2 48.5 %collective-permute-start.29 = (bf16[1024,512]{1,0:T(8,128)(2,1)S(1)}, bf16[1024,512]{1,0:T(8,128)(2,1)S(1)}, u32[]{:S(2)}, u32[]{:S(2)}) collective-permute-start(bf16[1024,512]{1,0:T(8,128)(2,1)S(1)} %convolution_convert_fusion.2), channel_id=1, source_target_pairs={{0,16},{16,0},{1,17},{17,1},{2,18},{18,2},{3,19},{19,3},{4,20},{20... | collective-permute-start | bytes 3145736 | tf_op jit(solution)/shard_map/ppermute | solution.py:24
  188.3 37.4 %collective-permute-start.30 = (bf16[1024,512]{1,0:T(8,128)(2,1)S(1)}, bf16[1024,512]{1,0:T(8,128)(2,1)S(1)}, u32[]{:S(2)}, u32[]{:S(2)}) collective-permute-start(bf16[1024,512]{1,0:T(8,128)(2,1)S(1)} %convolution_convert_fusion.1), channel_id=1, source_target_pairs={{0,16},{16,0},{1,17},{17,1},{2,18},{18,2},{3,19},{19,3},{4,20},{20... | collective-permute-start | bytes 3145736 | tf_op jit(solution)/shard_map/ppermute | solution.py:24
  198.8 16.7 %collective-permute-start.24 = (bf16[256,1024]{1,0:T(8,128)(2,1)S(1)}, bf16[256,1024]{1,0:T(8,128)(2,1)S(1)}, u32[]{:S(2)}, u32[]{:S(2)}) collective-permute-start(bf16[256,1024]{1,0:T(8,128)(2,1)S(1)} %add_convert_fusion.5), channel_id=1, source_target_pairs={{0,4},{4,8},{8,12},{12,0},{1,5},{5,9},{9,13},{13,1},{2,6},{6,10},{... | collective-permute-start | bytes 1572872 | tf_op jit(solution)/shard_map/ppermute | solution.py:24
  199.6 6.6 %copy-start.5 = (bf16[1024,512]{1,0:T(8,128)(2,1)}, bf16[1024,512]{1,0:T(8,128)(2,1)S(1)}, u32[]{:S(2)}) copy-start(bf16[1024,512]{1,0:T(8,128)(2,1)S(1)} %collective-permute-done.27) | copy-start | bytes 3145732
  199.6 24.9 %collective-permute-start.25 = (bf16[256,1024]{1,0:T(8,128)(2,1)S(1)}, bf16[256,1024]{1,0:T(8,128)(2,1)S(1)}, u32[]{:S(2)}, u32[]{:S(2)}) collective-permute-start(bf16[256,1024]{1,0:T(8,128)(2,1)S(1)} %add_convert_fusion.4), channel_id=1, source_target_pairs={{0,12},{4,0},{8,4},{12,8},{1,13},{5,1},{9,5},{13,9},{2,14},{6,2},{... | collective-permute-start | bytes 1572872 | tf_op jit(solution)/shard_map/ppermute | solution.py:24
  206.3 20.7 %copy-start.9 = (bf16[512,1024]{1,0:T(8,128)(2,1)}, bf16[512,1024]{1,0:T(8,128)(2,1)S(1)}, u32[]{:S(2)}) copy-start(bf16[512,1024]{1,0:T(8,128)(2,1)S(1)} %fusion.12) | copy-start | bytes 3145732
  215.5 12.3 %copy-start.12 = (bf16[256,1024]{1,0:T(8,128)(2,1)}, bf16[256,1024]{1,0:T(8,128)(2,1)S(1)}, u32[]{:S(2)}) copy-start(bf16[256,1024]{1,0:T(8,128)(2,1)S(1)} %collective-permute-done.24) | copy-start | bytes 1572868
  225.6 4.0 %collective-permute-start.26 = (bf16[256,1024]{1,0:T(8,128)(2,1)}, bf16[256,1024]{1,0:T(8,128)(2,1)}, u32[]{:S(2)}, u32[]{:S(2)}) collective-permute-start(bf16[256,1024]{1,0:T(8,128)(2,1)} %add_convert_fusion.2), channel_id=1, source_target_pairs={{0,1},{1,0},{2,3},{3,2},{4,5},{5,4},{6,7},{7,6},{8,9},{9,8},{10,11... | collective-permute-start | bytes 1572872 | tf_op jit(solution)/shard_map/ppermute | solution.py:28
  227.0 25.9 %collective-permute-start.32 = (bf16[1024,512]{1,0:T(8,128)(2,1)}, bf16[1024,512]{1,0:T(8,128)(2,1)}, u32[]{:S(2)}, u32[]{:S(2)}) collective-permute-start(bf16[1024,512]{1,0:T(8,128)(2,1)} %add_convert_fusion), channel_id=1, source_target_pairs={{0,2},{1,3},{2,0},{3,1},{4,6},{5,7},{6,4},{7,5},{8,10},{9,11},{10,... | collective-permute-start | bytes 3145736 | tf_op jit(solution)/shard_map/ppermute | solution.py:24
  227.8 26.8 %collective-permute-start.31 = (bf16[1024,512]{1,0:T(8,128)(2,1)S(1)}, bf16[1024,512]{1,0:T(8,128)(2,1)}, u32[]{:S(2)}, u32[]{:S(2)}) collective-permute-start(bf16[1024,512]{1,0:T(8,128)(2,1)S(1)} %add_convert_fusion.1), channel_id=1, source_target_pairs={{0,16},{16,0},{1,17},{17,1},{2,18},{18,2},{3,19},{19,3},{4,20},{20... | collective-permute-start | bytes 3145736 | tf_op jit(solution)/shard_map/ppermute | solution.py:24
  229.6 23.3 %copy-start.3 = (f32[1024,512]{1,0:T(8,128)S(1)}, f32[1024,512]{1,0:T(8,128)}, u32[]{:S(2)}) copy-start(f32[1024,512]{1,0:T(8,128)} %fusion.28) | copy-start | bytes 6291460
  229.6 23.3 %copy-start.8 = (bf16[1024,512]{1,0:T(8,128)(2,1)S(1)}, bf16[1024,512]{1,0:T(8,128)(2,1)}, u32[]{:S(2)}) copy-start(bf16[1024,512]{1,0:T(8,128)(2,1)} %copy-done.7) | copy-start | bytes 3145732
  232.7 21.8 %copy-start.6 = (bf16[1024,512]{1,0:T(8,128)(2,1)S(1)}, bf16[1024,512]{1,0:T(8,128)(2,1)}, u32[]{:S(2)}) copy-start(bf16[1024,512]{1,0:T(8,128)(2,1)} %copy-done.5) | copy-start | bytes 3145732
  (4 other events, 7.9 us)

commit v4 on v3

--- a/solution.py
+++ b/solution.py
@@ -28,16 +28,6 @@
     return lax.ppermute(value, "dp", [(i, i ^ 1) for i in range(lax.axis_size("dp"))])
 
 
-def shift_swap(value, step):
-    tensor_count, dp_count = lax.axis_size("tensor"), lax.axis_size("dp")
-    pairs = [
-        (t * dp_count + d, (t + step) % tensor_count * dp_count + (d ^ 1))
-        for t in range(tensor_count)
-        for d in range(dp_count)
-    ]
-    return lax.ppermute(value, ("tensor", "dp"), pairs)
-
-
 def after(value, *others):
     return lax.optimization_barrier((value, *others))[0]
 
@@ -47,19 +37,16 @@
     return up, size - 1 - up
 
 
-def gather_rings(streams, axis, size):
-    held = [[block] + [None] * (size - 1) for block, _, _ in streams]
-    for m in range(1, size // 2 + 1):
+def gather_ring(block, axis, size, rounds=None):
+    blocks = [block] + [None] * (size - 1)
+    for m in range(1, (size // 2 if rounds is None else rounds) + 1):
         came = {}
-        for s, (_, far_up, hop) in enumerate(streams):
-            for sign, count in zip((1, -1), reaches(size, far_up)):
-                if m <= count:
-                    first = hop is not None and m == 1
-                    block = held[s][(sign * (m - 1)) % size]
-                    came[s, (sign * m) % size] = hop(sign) if first else shift(block, axis, sign)
-        for (s, k), block in zip(came, lax.optimization_barrier(tuple(came.values()))):
-            held[s][k] = block
-    return held
+        for sign, count in zip((1, -1), reaches(size, True)):
+            if m <= count:
+                came[(sign * m) % size] = shift(blocks[(sign * (m - 1)) % size], axis, sign)
+        for k, value in zip(came, lax.optimization_barrier(tuple(came.values()))):
+            blocks[k] = value
+    return blocks
 
 
 def reduce_rings(streams, axis):
@@ -223,10 +210,7 @@
     whole_blocks = pairs == spans
     per = span_act.shape[1] // depth // 2
     half = width // 2
-
-    along_seq = gather_rings([(q_weight, True, None)], "seq", seq_count)[0]
-    along_dp = gather_rings([(q_weight, True, None)], "dp", couples)[0]
-    along_seq, along_dp = lax.optimization_barrier((along_seq, along_dp))
+    opposite = tensor_count // 2
 
     def columns_of(which):
         return jnp.concatenate(
@@ -237,32 +221,37 @@
             axis=1,
         )
 
-    act_mine, act_other = columns_of(core), columns_of(1 - core)
-    own_other = swap(act_other)
-    acts_mine, acts_other = gather_rings(
-        [(act_mine, True, None), (own_other, False, functools.partial(shift_swap, act_other))],
-        "tensor",
-        tensor_count,
-    )
-    acts = [jnp.concatenate(both, axis=0) for both in zip(acts_mine, acts_other)]
+    act_both = jnp.concatenate([columns_of(core), swap(columns_of(1 - core))], axis=0)
+
+    acts = gather_ring(act_both, "tensor", tensor_count, opposite - 1)
+    near = [act for act in acts if act is not None]
+    along_seq = gather_ring(q_weight, "seq", seq_count)
+    along_dp = gather_ring(q_weight, "dp", couples)
+    near, along_seq, along_dp, grad_out = lax.optimization_barrier(
+        (near, along_seq, along_dp, out_grad)
+    )
+
+    acts = near[:opposite] + [None] + near[opposite:]
+    acts[opposite] = jnp.concatenate(
+        [
+            shift(acts[opposite - 1][:rows], "tensor", 1),
+            shift(acts[opposite + 1][rows:], "tensor", -1),
+        ],
+        axis=0,
+    )
     depth_blocks = [(tensor_at - k) % tensor_count for k in range(tensor_count)]
     table = jnp.stack(depth_blocks).astype(jnp.int32)
 
     cut = width * 5 // 8 // HD * HD
-    corner_left = gather_rings(
-        [(block[:, :cut], True, None) for block in along_seq[1:]], "dp", couples
-    )
-    corner_right = gather_rings(
-        [(block[:, cut:], True, None) for block in along_dp[1:]], "seq", seq_count
-    )
+    corner_left = [gather_ring(block[:, :cut], "dp", couples) for block in along_seq[1:]]
+    corner_right = [gather_ring(block[:, cut:], "seq", seq_count) for block in along_dp[1:]]
 
     def block_at(i, j):
         block = ((seq_at - i) % seq_count) * dp_count + ((dp_at // 2 - j) % couples) * 2
         return block // (2 * per), (block % (2 * per)) // 2
 
     places = [(i, j) for i in range(seq_count) for j in range(couples)]
-    zero = after(jnp.zeros((), BF16), own_other)
-    weights = jnp.broadcast_to(zero, (tensor_count, per * depth, width))
+    weights = jnp.zeros((tensor_count, per * depth, width), BF16)
     for i, j in places:
         at, inner = block_at(i, j)
         if j == 0:
@@ -320,7 +309,7 @@
 
     live = jnp.broadcast_to((neighbour_ids != 0).astype(F32)[:, :, None], (capacity, KEYS, HD))
     slots = [slots_of(step) for step in range(seq_count)]
-    grads = [to_owner(out_grad, step) for step in range(seq_count)]
+    grads = [to_owner(grad_out, step) for step in range(seq_count)]
 
     table = after(table, *grads)
     queries = []
@@ -329,8 +318,20 @@
         queries.append((partial[:rows] + swap(partial[rows:])).astype(BF16))
     asked = [[to_owner(value, step) for step in range(seq_count)] for value in queries]
 
+    stacked = jnp.stack(after(acts, queries[1]))
+
+    def act_block(i, j):
+        at, inner = block_at(i, j)
+        k = (tensor_at - at) % tensor_count
+        return lax.dynamic_slice(stacked, (k, 0, inner * depth), (1, 2 * rows, depth))[0]
+
+    def weight_product(i, j, grad):
+        found = dot(act_block(i, j), grad, ((0,), (0,)))
+        return lax.optimization_barrier(found.astype(BF16))
+
     kv_grad = None
-    both_grads, products = [], []
+    both_grads, corners = [], []
+    corner_places = [(i, j) for i in range(1, seq_count) for j in range(1, couples)]
     for part in range(2):
         answers = []
         for step in range(seq_count):
@@ -339,54 +340,67 @@
             )
             answers.append(from_owner(answer, step))
         if part:
-            answers[-1] = after(answers[-1], products[0][places[-1]])
+            answers[-1] = after(answers[-1], corners[0][corner_places[-1]])
         grad = sum(answers[1:], answers[0])
         both_grads.append(jnp.concatenate([grad, swap(grad)], axis=0))
-        if part == 0:
-            act_whole = jnp.broadcast_to(zero, (tensor_count, 2 * rows, per * depth))
-            for k in range(tensor_count):
-                act_whole = lax.dynamic_update_slice(
-                    act_whole, acts[k][None], (depth_blocks[k], 0, 0)
-                )
-
-        found = {}
-        for i, j in reversed(places):
-            at, inner = block_at(i, j)
-            block = lax.dynamic_slice(act_whole, (at, 0, inner * depth), (1, 2 * rows, depth))[0]
-            found[i, j] = dot(block, both_grads[part], ((0,), (0,)))
-            if (i, j) != (0, 0):
-                found[i, j] = lax.optimization_barrier(found[i, j].astype(BF16))
-        products.append(found)
-
+        corners.append({at: weight_product(*at, both_grads[part]) for at in corner_places[::-1]})
     both_grad = jnp.concatenate(both_grads, axis=1)
-    parts = [None] * tensor_count
-    for k in sorted(range(tensor_count), key=lambda k: -min(k, tensor_count - k)):
+
+    both_grad = after(both_grad, corners[1][corner_places[-1]])
+
+    def act_product(k):
         block = lax.dynamic_index_in_dim(weights, depth_blocks[k], 0, keepdims=False)
-        part = dot(both_grad, block, ((1,), (1,))).astype(BF16)
-        parts[k] = lax.optimization_barrier(part)
-    mine_parts, other_parts = reduce_rings(
-        [([part[:rows] for part in parts], True), ([part[rows:] for part in parts], False)],
-        "tensor",
-    )
-    arrived = swap(total(other_parts).astype(BF16))
-    kept = total(mine_parts).astype(BF16)
+        return lax.optimization_barrier(dot(both_grad, block, ((1,), (1,))).astype(BF16))
+
+    far = act_product(opposite)
+    up, down = shift(far[:rows], "tensor", 1), shift(far[rows:], "tensor", -1)
+
+    left = [
+        reduce_rings([([None] + [corners[0][i, j] for j in range(1, couples)], True)], "dp")[0][1:]
+        for i in range(1, seq_count)
+    ]
+    right = [
+        reduce_rings([([None] + [corners[1][i, j] for i in range(1, seq_count)], True)], "seq")[0][1:]
+        for j in range(1, couples)
+    ]
+    act_parts = {k: act_product(k) for k in range(tensor_count) if k != opposite}
+    beside_seq = [weight_product(i, 0, both_grad) for i in range(1, seq_count)]
+    beside_dp = [weight_product(0, j, both_grad) for j in range(1, couples)]
+    up, down, left, right, act_parts, beside_seq, beside_dp = lax.optimization_barrier(
+        (up, down, left, right, act_parts, beside_seq, beside_dp)
+    )
+
+    for m in range(opposite - 1, 0, -1):
+        block = act_parts[tensor_count - m]
+        if up.shape[0] == rows:
+            up = jnp.concatenate([total([block[:rows], up]).astype(BF16), block[rows:]], axis=0)
+        else:
+            up = total([block, up]).astype(BF16)
+        block = act_parts[m]
+        if down.shape[0] == rows:
+            down = jnp.concatenate([block[:rows], total([block[rows:], down]).astype(BF16)], axis=0)
+        else:
+            down = total([block, down]).astype(BF16)
+        up, down = shift(up, "tensor", 1), shift(down, "tensor", -1)
+    beside_seq = [
+        jnp.concatenate([total([block[:, :half]] + came).astype(BF16), block[:, half:]], axis=1)
+        for block, came in zip(beside_seq, left)
+    ]
+    beside_dp = [
+        jnp.concatenate([block[:, :half], total([block[:, half:]] + came).astype(BF16)], axis=1)
+        for block, came in zip(beside_dp, right)
+    ]
+    from_seq = reduce_rings([([None] + beside_seq, True)], "seq")[0][1:]
+    from_dp = reduce_rings([([None] + beside_dp, True)], "dp")[0][1:]
+
+    act_sum = total([act_parts[0], up, down])
+    kept, arrived = act_sum[:rows].astype(BF16), swap(act_sum[rows:].astype(BF16))
     even = jnp.where(core == 0, kept, arrived)
     odd = jnp.where(core == 0, arrived, kept)
     act_grad = jnp.concatenate(
         [value[:, p * depth:(p + 1) * depth] for p in range(per) for value in (even, odd)], axis=1
     )
-
-    left = reduce_rings(
-        [([products[0][i, j] for j in range(couples)], True) for i in range(seq_count)], "dp"
-    )
-    right = reduce_rings(
-        [([products[1][i, j] for i in range(seq_count)], True) for j in range(couples)], "seq"
-    )
-    left, right = lax.optimization_barrier((left, right))
-    left = reduce_rings([([total(values) for values in left], True)], "seq")[0]
-    right = reduce_rings([([total(values) for values in right], True)], "dp")[0]
-    left, right = total(left), total(right)
-    weight_grad = jnp.concatenate([left, right], axis=1)
+    weight_grad = total([weight_product(0, 0, both_grad)] + from_seq + from_dp)
     return (act_grad, weight_grad, kv_grad)
 
 

time: 260 us -> 230 us (0.88)
  starting transfers between devices: 42.3 us -> 28.1 us
  waiting for transfers between devices: 137 us -> 123 us
  Pallas kernels: 16.1 us -> 24.1 us
  matrix products: 22.9 us -> 16.9 us
    ppermute x25 -> x21, starting transfers between devices: 41.5 us -> 27.5 us  [shift(): lax.ppermute(value, axis, [(i, (i + step * stride) % size) for i in range...]
    ppermute x2 -> x0, waiting for transfers between devices: 9.8 us -> none  [shift_swap(): return lax.ppermute(value, ('tensor', 'dp'), pairs)]
    pallas_call x4, Pallas kernels: 10.3 us -> 18.3 us  [attend(): pl.pallas_call(attend_kernel, grid_spec=pltpu.PrefetchScalarGridSpec(num_...]
    ppermute x25 -> x21, waiting for transfers between devices: 125 us -> 119 us  [shift(): lax.ppermute(value, axis, [(i, (i + step * stride) % size) for i in range...]
    dot_general x12 -> x9, matrix products: 22.9 us -> 16.9 us  [dot(): lax.dot_general(a, b, (contract, ((), ())), preferred_element_type=F32)]
    unnamed x41 -> x49, local copies, waits for them, and re-layouts: 5.81 us -> 9.02 us
    dynamic_update_slice x3 -> x0, local copies, waits for them, and re-layouts: 3.12 us -> none  [on_device(): lax.dynamic_update_slice(act_whole, acts[k][None], (depth_blocks[k], 0, 0))]
  transfers between devices with their start and end apart: 33 -> 27, of which waited for: 17 -> 17; matrix products, arithmetic and copies ran while one was open for 20% -> 16% of each run, Pallas kernels for 5% -> 9%
where the time goes in v4:
time: 230 us; the launch traced here: 229 us
  waiting for transfers between devices  123 us (53%)
  starting transfers between devices  28.1 us (12%)
  Pallas kernels  24.1 us (10%)
  local copies, waits for them, and re-layouts  20.6 us (9%)
  matrix products  16.9 us (7%)
  other arithmetic  14.9 us (6%)
    ppermute x21, waiting for transfers between devices, shift(): lax.ppermute(value, axis, [(i, (i + step * stride) % size) for i in range...  119 us
    ppermute x21, starting transfers between devices, shift(): lax.ppermute(value, axis, [(i, (i + step * stride) % size) for i in range...  27.5 us
    pallas_call x4, Pallas kernels, attend(): pl.pallas_call(attend_kernel, grid_spec=pltpu.PrefetchScalarGridSpec(num_...  18.3 us
    dot_general x9, matrix products, dot(): lax.dot_general(a, b, (contract, ((), ())), preferred_element_type=F32)  16.9 us
    unnamed x49, local copies, waits for them, and re-layouts  9.02 us
    pallas_call x2, Pallas kernels, product(): pl.pallas_call(functools.partial(product_kernel, count, start), out_shape...  5.81 us
    add x1, other arithmetic, total(): a + b  4.99 us
  transfers between devices with their start and end apart: 27, of which 17 were waited for; matrix products, arithmetic and copies ran while one was open for 16% of the time, Pallas kernels for 9%

profile of v4, /device:TPU:0, one launch (start us, length us, event | category | flops | bytes accessed | tf_op | source)
XLA Modules:
  0.0 229.1 jit_solution(3674260166644945994)
XLA Ops:
  0.6 3.0 %collective-permute-start.3 = (bf16[1024,1024]{1,0:T(8,128)(2,1)}, bf16[1024,1024]{1,0:T(8,128)(2,1)}, u32[]{:S(2)}, u32[]{:S(2)}) collective-permute-start(bf16[1024,1024]{1,0:T(8,128)(2,1)} %param.7), channel_id=1, source_target_pairs={{0,16},{16,0},{1,17},{17,1},{2,18},{18,2},{3,19},{19,3},{4,20},{20... | collective-permute-start | bytes 6291464 | tf_op jit(solution)/shard_map/ppermute | solution.py:24
  3.6 1.5 collective-permute-start.4
  6.5 1.9 collective-permute-done
  8.5 1.6 collective-permute-start.1
  10.1 2.2 collective-permute-start.2
  12.8 23.5 %collective-permute-done.1.refs_1_ = bf16[512,1024]{1,0:T(8,128)(2,1)S(1)} collective-permute-done((bf16[512,1024]{1,0:T(8,128)(2,1)S(1)}, bf16[512,1024]{1,0:T(8,128)(2,1)S(1)}, u32[]{:S(2)}, u32[]{:S(2)}) %collective-permute-start.1) | collective-permute-done | bytes 1048608 | tf_op jit(solution)/shard_map/ppermute | solution.py:24
  36.4 21.1 %collective-permute-done.2.refs_3_ = bf16[512,1024]{1,0:T(8,128)(2,1)S(1)} collective-permute-done((bf16[512,1024]{1,0:T(8,128)(2,1)S(1)}, bf16[512,1024]{1,0:T(8,128)(2,1)S(1)}, u32[]{:S(2)}, u32[]{:S(2)}) %collective-permute-start.2) | collective-permute-done | bytes 1048608 | tf_op jit(solution)/shard_map/ppermute | solution.py:24
  57.5 1.8 slice.64
  61.8 2.7 %collective-permute-start.7 = (bf16[256,1024]{1,0:T(8,128)(2,1)S(1)}, bf16[256,1024]{1,0:T(8,128)(2,1)S(1)}, u32[]{:S(2)}, u32[]{:S(2)}) collective-permute-start(bf16[256,1024]{1,0:T(8,128)(2,1)S(1)} %slice.63), channel_id=1, source_target_pairs={{0,12},{4,0},{8,4},{12,8},{1,13},{5,1},{9,5},{13,9},{2,14},{6,2},{... | collective-permute-start | bytes 1572872 | tf_op jit(solution)/shard_map/ppermute | solution.py:24
  65.8 1.6 collective-permute-start.9
  68.7 1.9 bitcast_dynamic-update-slice_fusion.1
  70.6 1.9 bitcast_dynamic-update-slice_fusion
  72.4 2.4 %collective-permute-done.5.g_ref = bf16[4,64,1024]{2,1,0:T(8,128)(2,1)S(1)} collective-permute-done((bf16[4,64,1024]{2,1,0:T(8,128)(2,1)S(1)}, bf16[4,64,1024]{2,1,0:T(8,128)(2,1)S(1)}, u32[]{:S(2)}, u32[]{:S(2)}) %collective-permute-start.5) | collective-permute-done | bytes 524320 | tf_op jit(solution)/shard_map/ppermute | solution.py:24
  74.9 2.4 %collective-permute-done.6 = bf16[256,1024]{1,0:T(8,128)(2,1)S(1)} collective-permute-done((bf16[256,1024]{1,0:T(8,128)(2,1)S(1)}, bf16[256,1024]{1,0:T(8,128)(2,1)S(1)}, u32[]{:S(2)}, u32[]{:S(2)}) %collective-permute-start.6) | collective-permute-done | bytes 524320 | tf_op jit(solution)/shard_map/ppermute | solution.py:24
  77.3 8.8 %collective-permute-done.7 = bf16[256,1024]{1,0:T(8,128)(2,1)S(1)} collective-permute-done((bf16[256,1024]{1,0:T(8,128)(2,1)S(1)}, bf16[256,1024]{1,0:T(8,128)(2,1)S(1)}, u32[]{:S(2)}, u32[]{:S(2)}) %collective-permute-start.7) | collective-permute-done | bytes 524320 | tf_op jit(solution)/shard_map/ppermute | solution.py:24
  86.2 3.7 %collective-permute-done.9 = bf16[1024,384]{1,0:T(8,128)(2,1)S(1)} collective-permute-done((bf16[1024,384]{1,0:T(8,128)(2,1)S(1)}, bf16[1024,384]{1,0:T(8,128)(2,1)S(1)}, u32[]{:S(2)}, u32[]{:S(2)}) %collective-permute-start.9) | collective-permute-done | bytes 786464 | tf_op jit(solution)/shard_map/ppermute | solution.py:24
  90.4 2.9 %shard_map.85 = f32[512,512]{1,0:T(8,128)S(1)} custom-call(s32[4]{0:T(128)S(1)} %pad_add_fusion.1.table_ref, bf16[512,1024]{1,0:T(8,128)(2,1)S(1)} %pad_maximum_fusion.3.refs_0_, bf16[512,1024]{1,0:T(8,128)(2,1)S(1)} %collective-permute-done.1.refs_1_, bf16[512,1024]{1,0:T(8,128)(2,1)S(1)} %constant_dynamic-update-slice_fusion.refs_2_, ...), custom_call_target="tpu_custom_call" | custom-call | flops 2147483648 | bytes 9437184 | tf_op jit(solution)/shard_map/pallas_call | solution.py:90
  93.7 2.9 %shard_map.88 = f32[512,512]{1,0:T(8,128)S(1)} custom-call(s32[4]{0:T(128)S(1)} %pad_add_fusion.1.table_ref, bf16[512,1024]{1,0:T(8,128)(2,1)S(1)} %pad_maximum_fusion.3.refs_0_, bf16[512,1024]{1,0:T(8,128)(2,1)S(1)} %collective-permute-done.1.refs_1_, bf16[512,1024]{1,0:T(8,128)(2,1)S(1)} %constant_dynamic-update-slice_fusion.refs_2_, ...), custom_call_target="tpu_custom_call" | custom-call | flops 2147483648 | bytes 9437184 | tf_op jit(solution)/shard_map/pallas_call | solution.py:90
  99.8 4.3 %shard_map.86 = (bf16[4,64,512]{2,1,0:T(8,128)(2,1)S(1)}, bf16[8,2,256,1024]{3,2,1,0:T(8,128)(2,1)}) custom-call(s32[8]{0:T(128)S(1)} %pad_add_fusion.table_ref, bf16[4,64,512]{2,1,0:T(8,128)(2,1)S(1)} %bitcast.86, bf16[4,64,1024]{2,1,0:T(8,128)(2,1)S(1)} %bitcast.81, bf16[8,2,256,1024]{3,2,1,0:T(8,128)(2,1)S(1)} %bitcast.73, ...), custom_call_target="tpu_custom_call" | custom-call | flops 1342177280 | bytes 4194304 | tf_op jit(solution)/shard_map/pallas_call | solution.py:174
  104.1 2.3 %collective-permute-done.11.q_ref = bf16[4,64,512]{2,1,0:T(8,128)(2,1)S(1)} collective-permute-done((bf16[4,64,512]{2,1,0:T(8,128)(2,1)S(1)}, bf16[4,64,512]{2,1,0:T(8,128)(2,1)S(1)}, u32[]{:S(2)}, u32[]{:S(2)}) %collective-permute-start.11) | collective-permute-done | bytes 262176 | tf_op jit(solution)/shard_map/ppermute | solution.py:24
  106.4 4.4 %shard_map.87 = (bf16[4,64,512]{2,1,0:T(8,128)(2,1)}, bf16[8,2,256,1024]{3,2,1,0:T(8,128)(2,1)}) custom-call(s32[8]{0:T(128)S(1)} %pad_add_fusion.2.table_ref, bf16[4,64,512]{2,1,0:T(8,128)(2,1)S(1)} %collective-permute-done.11.q_ref, bf16[4,64,1024]{2,1,0:T(8,128)(2,1)S(1)} %collective-permute-done.5.g_ref, ...), custom_call_target="tpu_custom_call", output_to_operand_aliasing={{1}: (5, {})} | custom-call | flops 1342177280 | bytes 4194304 | tf_op jit(solution)/shard_map/pallas_call | solution.py:174
  110.7 3.4 %copy-done = bf16[8,2,256,1024]{3,2,1,0:T(8,128)(2,1)S(1)} copy-done((bf16[8,2,256,1024]{3,2,1,0:T(8,128)(2,1)S(1)}, bf16[8,2,256,1024]{3,2,1,0:T(8,128)(2,1)}, u32[]{:S(2)}) %copy-start) | copy-done | bytes 8388632
  115.2 4.3 %shard_map.89 = (bf16[4,64,512]{2,1,0:T(8,128)(2,1)S(1)}, bf16[8,2,256,1024]{3,2,1,0:T(8,128)(2,1)}) custom-call(s32[8]{0:T(128)S(1)} %pad_add_fusion.table_ref, bf16[4,64,512]{2,1,0:T(8,128)(2,1)S(1)} %bitcast.84, bf16[4,64,1024]{2,1,0:T(8,128)(2,1)S(1)} %bitcast.82, bf16[8,2,256,1024]{3,2,1,0:T(8,128)(2,1)S(1)} %copy-done, ...), custom_call_target="tpu_custom_call", output_to_operand_aliasing={{1}: (5, {})} | custom-call | flops 1342177280 | bytes 4194304 | tf_op jit(solution)/shard_map/pallas_call | solution.py:174
  119.5 3.4 %copy-done.1 = bf16[8,2,256,1024]{3,2,1,0:T(8,128)(2,1)S(1)} copy-done((bf16[8,2,256,1024]{3,2,1,0:T(8,128)(2,1)S(1)}, bf16[8,2,256,1024]{3,2,1,0:T(8,128)(2,1)}, u32[]{:S(2)}) %copy-start.1) | copy-done | bytes 8388632
  122.8 5.3 %shard_map.90 = (bf16[4,64,512]{2,1,0:T(8,128)(2,1)S(1)}, bf16[8,2,256,1024]{3,2,1,0:T(8,128)(2,1)}) custom-call(s32[8]{0:T(128)S(1)} %pad_add_fusion.2.table_ref, bf16[4,64,512]{2,1,0:T(8,128)(2,1)} %collective-permute-done.15.q_ref, bf16[4,64,1024]{2,1,0:T(8,128)(2,1)S(1)} %copy-done.11, ...), custom_call_target="tpu_custom_call", output_to_operand_aliasing={{1}: (5, {})} | custom-call | flops 1342177280 | bytes 4194304 | tf_op jit(solution)/shard_map/pallas_call | solution.py:174
  131.6 3.5 %collective-permute-done.16 = bf16[4,64,512]{2,1,0:T(8,128)(2,1)S(1)} collective-permute-done((bf16[4,64,512]{2,1,0:T(8,128)(2,1)S(1)}, bf16[4,64,512]{2,1,0:T(8,128)(2,1)S(1)}, u32[]{:S(2)}, u32[]{:S(2)}) %collective-permute-start.16) | collective-permute-done | bytes 262176 | tf_op jit(solution)/shard_map/ppermute | solution.py:24
  135.3 1.6 collective-permute-start.20
  136.9 2.0 convolution_convert_fusion.3
  139.4 3.3 %fusion.12 = bf16[512,1024]{1,0:T(8,128)(2,1)S(1)} fusion(bf16[512,1024]{1,0:T(8,128)(2,1)S(1)} %maximum_maximum_fusion, bf16[4,1024,1024]{2,1,0:T(8,128)(2,1)} %copy-done.2, s32[]{:T(128)S(6)} %select_n.258), kind=kOutput, calls=%fused_computation.25 | convolution fusion | flops 1074266112 | bytes 4194308 | tf_op jit(solution)/shard_map/dot_general | solution.py:18
  142.8 1.8 collective-permute-start.18
  144.5 2.1 collective-permute-start.19
  146.7 2.9 %fusion.15 = bf16[512,1024]{1,0:T(8,128)(2,1)S(1)} fusion(bf16[512,1024]{1,0:T(8,128)(2,1)S(1)} %maximum_maximum_fusion, bf16[4,1024,1024]{2,1,0:T(8,128)(2,1)} %copy-done.2, s32[]{:T(128)S(6)} %select_n.259), kind=kOutput, calls=%fused_computation.26 | convolution fusion | flops 1074266112 | bytes 4194308 | tf_op jit(solution)/shard_map/dot_general | solution.py:18
  149.6 1.3 fusion.18
  150.9 1.3 fusion.21
  153.1 1.3 convolution_convert_fusion.2
  154.4 1.3 convolution_convert_fusion.1
  155.7 5.1 %collective-permute-done.20 = bf16[1024,512]{1,0:T(8,128)(2,1)S(1)} collective-permute-done((bf16[1024,512]{1,0:T(8,128)(2,1)S(1)}, bf16[1024,512]{1,0:T(8,128)(2,1)S(1)}, u32[]{:S(2)}, u32[]{:S(2)}) %collective-permute-start.20) | collective-permute-done | bytes 1048608 | tf_op jit(solution)/shard_map/ppermute | solution.py:24
  160.8 3.3 %collective-permute-done.21 = bf16[1024,512]{1,0:T(8,128)(2,1)S(1)} collective-permute-done((bf16[1024,512]{1,0:T(8,128)(2,1)S(1)}, bf16[1024,512]{1,0:T(8,128)(2,1)S(1)}, u32[]{:S(2)}, u32[]{:S(2)}) %collective-permute-start.21) | collective-permute-done | bytes 1048608 | tf_op jit(solution)/shard_map/ppermute | solution.py:24
  164.1 5.1 %collective-permute-done.19 = bf16[256,1024]{1,0:T(8,128)(2,1)S(1)} collective-permute-done((bf16[256,1024]{1,0:T(8,128)(2,1)S(1)}, bf16[256,1024]{1,0:T(8,128)(2,1)S(1)}, u32[]{:S(2)}, u32[]{:S(2)}) %collective-permute-start.19) | collective-permute-done | bytes 524320 | tf_op jit(solution)/shard_map/ppermute | solution.py:24
  169.5 2.1 collective-permute-start.23
  172.5 1.6 pad_maximum_fusion.2
  174.1 1.4 collective-permute-start.26
  176.0 1.6 pad_maximum_fusion.1
  177.7 1.7 collective-permute-start.25
  179.4 17.1 %collective-permute-done.23 = bf16[512,1024]{1,0:T(8,128)(2,1)S(1)} collective-permute-done((bf16[512,1024]{1,0:T(8,128)(2,1)S(1)}, bf16[512,1024]{1,0:T(8,128)(2,1)S(1)}, u32[]{:S(2)}, u32[]{:S(2)}) %collective-permute-start.23) | collective-permute-done | bytes 1048608 | tf_op jit(solution)/shard_map/ppermute | solution.py:24
  196.5 20.1 %collective-permute-done.22 = bf16[512,1024]{1,0:T(8,128)(2,1)S(1)} collective-permute-done((bf16[512,1024]{1,0:T(8,128)(2,1)S(1)}, bf16[512,1024]{1,0:T(8,128)(2,1)S(1)}, u32[]{:S(2)}, u32[]{:S(2)}) %collective-permute-start.22) | collective-permute-done | bytes 1048608 | tf_op jit(solution)/shard_map/ppermute | solution.py:24
  218.1 2.8 %convolution_convert_fusion = bf16[1024,1024]{1,0:T(8,128)(2,1)S(1)} fusion(bf16[512,1024]{1,0:T(8,128)(2,1)} %copy-done.17, bf16[4,512,1024]{2,1,0:T(8,128)(2,1)} %copy-done.14, s32[]{:T(128)S(6)} %select_n.269), kind=kOutput, calls=%fused_computation.22 | convolution fusion | flops 1074790400 | bytes 4194308 | tf_op jit(solution)/shard_map/dot_general | solution.py:18
  224.1 5.0 %convert_add_fusion = f32[1024,1024]{1,0:T(8,128)} fusion(bf16[1024,1024]{1,0:T(8,128)(2,1)S(1)} %collective-permute-done.26, bf16[1024,1024]{1,0:T(8,128)(2,1)} %collective-permute-done.25, bf16[1024,1024]{1,0:T(8,128)(2,1)S(1)} %convolution_convert_fusion), kind=kLoop, calls=%fused_computation.1 | loop fusion | flops 5242880 | bytes 10485760 | tf_op jit(solution)/shard_map/add | solution.py:73
  (123 shorter events, 23.2 us)
Async XLA Ops:
  0.6 56.9 %collective-permute-start.3 = (bf16[1024,1024]{1,0:T(8,128)(2,1)}, bf16[1024,1024]{1,0:T(8,128)(2,1)}, u32[]{:S(2)}, u32[]{:S(2)}) collective-permute-start(bf16[1024,1024]{1,0:T(8,128)(2,1)} %param.7), channel_id=1, source_target_pairs={{0,16},{16,0},{1,17},{17,1},{2,18},{18,2},{3,19},{19,3},{4,20},{20... | collective-permute-start | bytes 6291464 | tf_op jit(solution)/shard_map/ppermute | solution.py:24
  3.6 53.9 %collective-permute-start.4 = (bf16[1024,1024]{1,0:T(8,128)(2,1)}, bf16[1024,1024]{1,0:T(8,128)(2,1)}, u32[]{:S(2)}, u32[]{:S(2)}) collective-permute-start(bf16[1024,1024]{1,0:T(8,128)(2,1)} %param.7), channel_id=1, source_target_pairs={{0,2},{1,3},{2,0},{3,1},{4,6},{5,7},{6,4},{7,5},{8,10},{9,11},{10,... | collective-permute-start | bytes 6291464 | tf_op jit(solution)/shard_map/ppermute | solution.py:24
  5.2 7.2 %copy-start.19 = (s32[32]{0:T(128)S(1)}, s32[32]{0:T(128)}, u32[]{:S(2)}) copy-start(s32[32]{0:T(128)} %param.11) | copy-start | bytes 388
  6.4 2.0 collective-permute-start
  8.5 27.9 %collective-permute-start.1 = (bf16[512,1024]{1,0:T(8,128)(2,1)S(1)}, bf16[512,1024]{1,0:T(8,128)(2,1)S(1)}, u32[]{:S(2)}, u32[]{:S(2)}) collective-permute-start(bf16[512,1024]{1,0:T(8,128)(2,1)S(1)} %pad_maximum_fusion.3.refs_0_), channel_id=1, source_target_pairs={{0,4},{4,8},{8,12},{12,0},{1,5},{5,9},{9,13},{13,1},{2,6},{6,10},{... | collective-permute-start | bytes 3145736 | tf_op jit(solution)/shard_map/ppermute | solution.py:24
  10.1 47.4 %collective-permute-start.2 = (bf16[512,1024]{1,0:T(8,128)(2,1)S(1)}, bf16[512,1024]{1,0:T(8,128)(2,1)S(1)}, u32[]{:S(2)}, u32[]{:S(2)}) collective-permute-start(bf16[512,1024]{1,0:T(8,128)(2,1)S(1)} %pad_maximum_fusion.3.refs_0_), channel_id=1, source_target_pairs={{0,12},{4,0},{8,4},{12,8},{1,13},{5,1},{9,5},{13,9},{2,14},{6,2},{... | collective-permute-start | bytes 3145736 | tf_op jit(solution)/shard_map/ppermute | solution.py:24
  12.6 47.4 %copy-start.8 = (bf16[256,1024]{1,0:T(8,128)(2,1)S(1)}, bf16[256,1024]{1,0:T(8,128)(2,1)}, u32[]{:S(2)}) copy-start(bf16[256,1024]{1,0:T(8,128)(2,1)} %param.8) | copy-start | bytes 1572868
  57.5 4.3 %copy-start.3 = (bf16[512,1024]{1,0:T(8,128)(2,1)}, bf16[512,1024]{1,0:T(8,128)(2,1)S(1)}, u32[]{:S(2)}) copy-start(bf16[512,1024]{1,0:T(8,128)(2,1)S(1)} %collective-permute-done.2.refs_3_) | copy-start | bytes 3145732
  59.3 30.5 %collective-permute-start.8 = (bf16[1024,640]{1,0:T(8,128)(2,1)S(1)}, bf16[1024,640]{1,0:T(8,128)(2,1)S(1)}, u32[]{:S(2)}, u32[]{:S(2)}) collective-permute-start(bf16[1024,640]{1,0:T(8,128)(2,1)S(1)} %slice.64), channel_id=1, source_target_pairs={{0,2},{1,3},{2,0},{3,1},{4,6},{5,7},{6,4},{7,5},{8,10},{9,11},{10,... | collective-permute-start | bytes 3932168 | tf_op jit(solution)/shard_map/ppermute | solution.py:24
  60.0 14.9 %collective-permute-start.5 = (bf16[4,64,1024]{2,1,0:T(8,128)(2,1)S(1)}, bf16[4,64,1024]{2,1,0:T(8,128)(2,1)S(1)}, u32[]{:S(2)}, u32[]{:S(2)}) collective-permute-start(bf16[4,64,1024]{2,1,0:T(8,128)(2,1)S(1)} %bitcast.80), channel_id=1, source_target_pairs={{0,16},{16,0},{1,17},{17,1},{2,18},{18,2},{3,19},{19,3},{4,20},{20... | collective-permute-start | bytes 1572872 | tf_op jit(solution)/shard_map/ppermute | solution.py:24
  60.6 16.7 %collective-permute-start.6 = (bf16[256,1024]{1,0:T(8,128)(2,1)S(1)}, bf16[256,1024]{1,0:T(8,128)(2,1)S(1)}, u32[]{:S(2)}, u32[]{:S(2)}) collective-permute-start(bf16[256,1024]{1,0:T(8,128)(2,1)S(1)} %slice.62), channel_id=1, source_target_pairs={{0,4},{4,8},{8,12},{12,0},{1,5},{5,9},{9,13},{13,1},{2,6},{6,10},{... | collective-permute-start | bytes 1572872 | tf_op jit(solution)/shard_map/ppermute | solution.py:24
  61.8 24.3 %collective-permute-start.7 = (bf16[256,1024]{1,0:T(8,128)(2,1)S(1)}, bf16[256,1024]{1,0:T(8,128)(2,1)S(1)}, u32[]{:S(2)}, u32[]{:S(2)}) collective-permute-start(bf16[256,1024]{1,0:T(8,128)(2,1)S(1)} %slice.63), channel_id=1, source_target_pairs={{0,12},{4,0},{8,4},{12,8},{1,13},{5,1},{9,5},{13,9},{2,14},{6,2},{... | collective-permute-start | bytes 1572872 | tf_op jit(solution)/shard_map/ppermute | solution.py:24
  65.8 24.1 %collective-permute-start.9 = (bf16[1024,384]{1,0:T(8,128)(2,1)S(1)}, bf16[1024,384]{1,0:T(8,128)(2,1)S(1)}, u32[]{:S(2)}, u32[]{:S(2)}) collective-permute-start(bf16[1024,384]{1,0:T(8,128)(2,1)S(1)} %slice.65), channel_id=1, source_target_pairs={{0,16},{16,0},{1,17},{17,1},{2,18},{18,2},{3,19},{19,3},{4,20},{20... | collective-permute-start | bytes 2359304 | tf_op jit(solution)/shard_map/ppermute | solution.py:24
  74.9 31.5 %copy-start.10 = (bf16[4,64,1024]{2,1,0:T(8,128)(2,1)}, bf16[4,64,1024]{2,1,0:T(8,128)(2,1)S(1)}, u32[]{:S(2)}) copy-start(bf16[4,64,1024]{2,1,0:T(8,128)(2,1)S(1)} %collective-permute-done.5.g_ref) | copy-start | bytes 1572868
  86.1 7.3 %copy-start.6 = (bf16[512,1024]{1,0:T(8,128)(2,1)}, bf16[512,1024]{1,0:T(8,128)(2,1)S(1)}, u32[]{:S(2)}) copy-start(bf16[512,1024]{1,0:T(8,128)(2,1)S(1)} %constant_dynamic-update-slice_fusion.refs_2_) | copy-start | bytes 3145732
  86.1 4.2 %copy-start.4 = (bf16[512,1024]{1,0:T(8,128)(2,1)S(1)}, bf16[512,1024]{1,0:T(8,128)(2,1)}, u32[]{:S(2)}) copy-start(bf16[512,1024]{1,0:T(8,128)(2,1)} %copy-done.3) | copy-start | bytes 3145732
  90.4 3.3 %copy-start.2 = (bf16[4,1024,1024]{2,1,0:T(8,128)(2,1)}, bf16[4,1024,1024]{2,1,0:T(8,128)(2,1)S(1)}, u32[]{:S(2)}) copy-start(bf16[4,1024,1024]{2,1,0:T(8,128)(2,1)S(1)} %bitcast_dynamic-update-slice_fusion.4.refs_4_) | copy-start | bytes 25165828
  93.3 6.5 %slice-start = ((s8[8388608]{0:T(1024)(128)(4,1)}), s8[4194304]{0:T(1024)(128)(4,1)S(1)}, s32[]{:S(2)}) async-start(s8[8388608]{0:T(1024)(128)(4,1)} %bitcast.72), calls=%async_computation | async-start | bytes 8388608
  93.3 3.7 %copy-start.18 = (s32[8,256]{1,0:T(8,128)S(1)}, s32[8,256]{1,0:T(8,128)}, u32[]{:S(2)}) copy-start(s32[8,256]{1,0:T(8,128)} %param.10) | copy-start | bytes 24580
  93.3 6.4 %slice-start.1 = ((s8[8388608]{0:T(1024)(128)(4,1)}), s8[4194304]{0:T(1024)(128)(4,1)S(1)}, s32[]{:S(2)}) async-start(s8[8388608]{0:T(1024)(128)(4,1)} %bitcast.72), calls=%async_computation.1 | async-start | bytes 8388608
  93.4 3.7 %collective-permute-start.10 = (f32[256,512]{1,0:T(8,128)S(1)}, f32[256,512]{1,0:T(8,128)S(1)}, u32[]{:S(2)}, u32[]{:S(2)}) collective-permute-start(f32[256,512]{1,0:T(8,128)S(1)} %slice.83), channel_id=1, source_target_pairs={{0,1},{1,0},{2,3},{3,2},{4,5},{5,4},{6,7},{7,6},{8,9},{9,8},{10,11... | collective-permute-start | bytes 1572872 | tf_op jit(solution)/shard_map/ppermute | solution.py:28
  96.6 2.0 collective-permute-start.14
  97.1 9.2 %collective-permute-start.11 = (bf16[4,64,512]{2,1,0:T(8,128)(2,1)S(1)}, bf16[4,64,512]{2,1,0:T(8,128)(2,1)S(1)}, u32[]{:S(2)}, u32[]{:S(2)}) collective-permute-start(bf16[4,64,512]{2,1,0:T(8,128)(2,1)S(1)} %bitcast.85), channel_id=1, source_target_pairs={{0,16},{16,0},{1,17},{17,1},{2,18},{18,2},{3,19},{19,3},{4,20},{20... | collective-permute-start | bytes 786440 | tf_op jit(solution)/shard_map/ppermute | solution.py:24
  98.7 20.8 %collective-permute-start.15 = (bf16[4,64,512]{2,1,0:T(8,128)(2,1)S(1)}, bf16[4,64,512]{2,1,0:T(8,128)(2,1)}, u32[]{:S(2)}, u32[]{:S(2)}) collective-permute-start(bf16[4,64,512]{2,1,0:T(8,128)(2,1)S(1)} %bitcast.83), channel_id=1, source_target_pairs={{0,16},{16,0},{1,17},{17,1},{2,18},{18,2},{3,19},{19,3},{4,20},{20... | collective-permute-start | bytes 786440 | tf_op jit(solution)/shard_map/ppermute | solution.py:24
  104.1 6.7 %copy-start.12 = (bf16[4,64,512]{2,1,0:T(8,128)(2,1)}, bf16[4,64,512]{2,1,0:T(8,128)(2,1)S(1)}, u32[]{:S(2)}) copy-start(bf16[4,64,512]{2,1,0:T(8,128)(2,1)S(1)} %get-tuple-element.46) | copy-start | bytes 786436
  110.7 17.5 %collective-permute-start.12 = (bf16[4,64,512]{2,1,0:T(8,128)(2,1)}, bf16[4,64,512]{2,1,0:T(8,128)(2,1)}, u32[]{:S(2)}, u32[]{:S(2)}) collective-permute-start(bf16[4,64,512]{2,1,0:T(8,128)(2,1)} %get-tuple-element.48), channel_id=1, source_target_pairs={{0,16},{16,0},{1,17},{17,1},{2,18},{18,2},{3,19},{19,3},{4,20},{20... | collective-permute-start | bytes 786440 | tf_op jit(solution)/shard_map/ppermute | solution.py:24
  110.7 3.4 %copy-start = (bf16[8,2,256,1024]{3,2,1,0:T(8,128)(2,1)S(1)}, bf16[8,2,256,1024]{3,2,1,0:T(8,128)(2,1)}, u32[]{:S(2)}) copy-start(bf16[8,2,256,1024]{3,2,1,0:T(8,128)(2,1)} %kv_ref.7) | copy-start | bytes 25165828
  115.2 4.3 %copy-start.11 = (bf16[4,64,1024]{2,1,0:T(8,128)(2,1)S(1)}, bf16[4,64,1024]{2,1,0:T(8,128)(2,1)}, u32[]{:S(2)}) copy-start(bf16[4,64,1024]{2,1,0:T(8,128)(2,1)} %copy-done.10) | copy-start | bytes 1572868
  119.5 3.4 %copy-start.1 = (bf16[8,2,256,1024]{3,2,1,0:T(8,128)(2,1)S(1)}, bf16[8,2,256,1024]{3,2,1,0:T(8,128)(2,1)}, u32[]{:S(2)}) copy-start(bf16[8,2,256,1024]{3,2,1,0:T(8,128)(2,1)} %kv_ref.7) | copy-start | bytes 25165828
  122.8 5.4 %copy-start.13 = (bf16[4,64,512]{2,1,0:T(8,128)(2,1)S(1)}, bf16[4,64,512]{2,1,0:T(8,128)(2,1)}, u32[]{:S(2)}) copy-start(bf16[4,64,512]{2,1,0:T(8,128)(2,1)} %copy-done.12) | copy-start | bytes 786436
  122.8 6.5 %copy-start.5 = (bf16[512,1024]{1,0:T(8,128)(2,1)S(1)}, bf16[512,1024]{1,0:T(8,128)(2,1)}, u32[]{:S(2)}) copy-start(bf16[512,1024]{1,0:T(8,128)(2,1)} %copy-done.3) | copy-start | bytes 3145732
  122.8 6.5 %copy-start.7 = (bf16[512,1024]{1,0:T(8,128)(2,1)S(1)}, bf16[512,1024]{1,0:T(8,128)(2,1)}, u32[]{:S(2)}) copy-start(bf16[512,1024]{1,0:T(8,128)(2,1)} %copy-done.6) | copy-start | bytes 3145732
  128.2 6.9 %collective-permute-start.16 = (bf16[4,64,512]{2,1,0:T(8,128)(2,1)S(1)}, bf16[4,64,512]{2,1,0:T(8,128)(2,1)S(1)}, u32[]{:S(2)}, u32[]{:S(2)}) collective-permute-start(bf16[4,64,512]{2,1,0:T(8,128)(2,1)S(1)} %get-tuple-element.52), channel_id=1, source_target_pairs={{0,16},{16,0},{1,17},{17,1},{2,18},{18,2},{3,19},{19,3},{4,20},{20... | collective-permute-start | bytes 786440 | tf_op jit(solution)/shard_map/ppermute | solution.py:24
  129.2 1.6 collective-permute-start.13
  129.9 5.2 %copy-start.14 = (bf16[4,512,1024]{2,1,0:T(8,128)(2,1)}, bf16[4,512,1024]{2,1,0:T(8,128)(2,1)S(1)}, u32[]{:S(2)}) copy-start(bf16[4,512,1024]{2,1,0:T(8,128)(2,1)S(1)} %pad_maximum_fusion) | copy-start | bytes 12582916
  135.1 1.7 collective-permute-start.17
  135.3 25.5 %collective-permute-start.20 = (bf16[1024,512]{1,0:T(8,128)(2,1)S(1)}, bf16[1024,512]{1,0:T(8,128)(2,1)S(1)}, u32[]{:S(2)}, u32[]{:S(2)}) collective-permute-start(bf16[1024,512]{1,0:T(8,128)(2,1)S(1)} %convolution_convert_fusion.4), channel_id=1, source_target_pairs={{0,2},{1,3},{2,0},{3,1},{4,6},{5,7},{6,4},{7,5},{8,10},{9,11},{10,... | collective-permute-start | bytes 3145736 | tf_op jit(solution)/shard_map/ppermute | solution.py:24
  138.9 25.2 %collective-permute-start.21 = (bf16[1024,512]{1,0:T(8,128)(2,1)S(1)}, bf16[1024,512]{1,0:T(8,128)(2,1)S(1)}, u32[]{:S(2)}, u32[]{:S(2)}) collective-permute-start(bf16[1024,512]{1,0:T(8,128)(2,1)S(1)} %convolution_convert_fusion.3), channel_id=1, source_target_pairs={{0,16},{16,0},{1,17},{17,1},{2,18},{18,2},{3,19},{19,3},{4,20},{20... | collective-permute-start | bytes 3145736 | tf_op jit(solution)/shard_map/ppermute | solution.py:24
  139.4 15.0 %copy-start.17 = (bf16[512,1024]{1,0:T(8,128)(2,1)}, bf16[512,1024]{1,0:T(8,128)(2,1)S(1)}, u32[]{:S(2)}) copy-start(bf16[512,1024]{1,0:T(8,128)(2,1)S(1)} %maximum_maximum_fusion) | copy-start | bytes 3145732
  139.4 10.2 %slice-start.2 = ((s8[8388608]{0:T(1024)(128)(4,1)}), s8[4194304]{0:T(1024)(128)(4,1)S(1)}, s32[]{:S(2)}) async-start(s8[8388608]{0:T(1024)(128)(4,1)} %bitcast.74), calls=%async_computation.2 | async-start | bytes 8388608
  142.7 6.9 %slice-start.3 = ((s8[8388608]{0:T(1024)(128)(4,1)}), s8[4194304]{0:T(1024)(128)(4,1)S(1)}, s32[]{:S(2)}) async-start(s8[8388608]{0:T(1024)(128)(4,1)} %bitcast.74), calls=%async_computation.3 | async-start | bytes 8388608
  142.8 21.3 %collective-permute-start.18 = (bf16[256,1024]{1,0:T(8,128)(2,1)S(1)}, bf16[256,1024]{1,0:T(8,128)(2,1)S(1)}, u32[]{:S(2)}, u32[]{:S(2)}) collective-permute-start(bf16[256,1024]{1,0:T(8,128)(2,1)S(1)} %get-tuple-element.76), channel_id=1, source_target_pairs={{0,4},{4,8},{8,12},{12,0},{1,5},{5,9},{9,13},{13,1},{2,6},{6,10},{... | collective-permute-start | bytes 1572872 | tf_op jit(solution)/shard_map/ppermute | solution.py:24
  144.5 24.6 %collective-permute-start.19 = (bf16[256,1024]{1,0:T(8,128)(2,1)S(1)}, bf16[256,1024]{1,0:T(8,128)(2,1)S(1)}, u32[]{:S(2)}, u32[]{:S(2)}) collective-permute-start(bf16[256,1024]{1,0:T(8,128)(2,1)S(1)} %get-tuple-element.75), channel_id=1, source_target_pairs={{0,12},{4,0},{8,4},{12,8},{1,13},{5,1},{9,5},{13,9},{2,14},{6,2},{... | collective-permute-start | bytes 1572872 | tf_op jit(solution)/shard_map/ppermute | solution.py:24
  169.5 27.1 %collective-permute-start.23 = (bf16[512,1024]{1,0:T(8,128)(2,1)S(1)}, bf16[512,1024]{1,0:T(8,128)(2,1)S(1)}, u32[]{:S(2)}, u32[]{:S(2)}) collective-permute-start(bf16[512,1024]{1,0:T(8,128)(2,1)S(1)} %pad_maximum_fusion.5), channel_id=1, source_target_pairs={{0,12},{4,0},{8,4},{12,8},{1,13},{5,1},{9,5},{13,9},{2,14},{6,2},{... | collective-permute-start | bytes 3145736 | tf_op jit(solution)/shard_map/ppermute | solution.py:24
  171.9 44.7 %collective-permute-start.22 = (bf16[512,1024]{1,0:T(8,128)(2,1)S(1)}, bf16[512,1024]{1,0:T(8,128)(2,1)S(1)}, u32[]{:S(2)}, u32[]{:S(2)}) collective-permute-start(bf16[512,1024]{1,0:T(8,128)(2,1)S(1)} %pad_maximum_fusion.4), channel_id=1, source_target_pairs={{0,4},{4,8},{8,12},{12,0},{1,5},{5,9},{9,13},{13,1},{2,6},{6,10},{... | collective-permute-start | bytes 3145736 | tf_op jit(solution)/shard_map/ppermute | solution.py:24
  174.1 49.0 %collective-permute-start.26 = (bf16[1024,1024]{1,0:T(8,128)(2,1)}, bf16[1024,1024]{1,0:T(8,128)(2,1)S(1)}, u32[]{:S(2)}, u32[]{:S(2)}) collective-permute-start(bf16[1024,1024]{1,0:T(8,128)(2,1)} %pad_maximum_fusion.2), channel_id=1, source_target_pairs={{0,2},{1,3},{2,0},{3,1},{4,6},{5,7},{6,4},{7,5},{8,10},{9,11},{10,... | collective-permute-start | bytes 6291464 | tf_op jit(solution)/shard_map/ppermute | solution.py:24
  177.7 46.5 %collective-permute-start.25 = (bf16[1024,1024]{1,0:T(8,128)(2,1)}, bf16[1024,1024]{1,0:T(8,128)(2,1)}, u32[]{:S(2)}, u32[]{:S(2)}) collective-permute-start(bf16[1024,1024]{1,0:T(8,128)(2,1)} %pad_maximum_fusion.1), channel_id=1, source_target_pairs={{0,16},{16,0},{1,17},{17,1},{2,18},{18,2},{3,19},{19,3},{4,20},{20... | collective-permute-start | bytes 6291464 | tf_op jit(solution)/shard_map/ppermute | solution.py:24
  218.1 2.8 %collective-permute-start.24 = (bf16[256,1024]{1,0:T(8,128)(2,1)}, bf16[256,1024]{1,0:T(8,128)(2,1)}, u32[]{:S(2)}, u32[]{:S(2)}) collective-permute-start(bf16[256,1024]{1,0:T(8,128)(2,1)} %slice.89), channel_id=1, source_target_pairs={{0,1},{1,0},{2,3},{3,2},{4,5},{5,4},{6,7},{7,6},{8,9},{9,8},{10,11... | collective-permute-start | bytes 1572872 | tf_op jit(solution)/shard_map/ppermute | solution.py:28
  (3 other events, 5.9 us)

commit v5 on v4

--- a/solution.py
+++ b/solution.py
@@ -93,7 +93,7 @@
         in_specs=[pl.BlockSpec(memory_space=pltpu.SMEM)]
         + [pl.BlockSpec(memory_space=pltpu.VMEM)] * (count + 1),
         out_specs=pl.BlockSpec(memory_space=pltpu.VMEM),
-        compiler_params=pltpu.CompilerParams(vmem_limit_bytes=32 * 1024 * 1024),
+        compiler_params=pltpu.CompilerParams(vmem_limit_bytes=16 * 1024 * 1024),
         cost_estimate=pl.CostEstimate(
             flops=2 * rows * count * depth * width,
             bytes_accessed=2 * count * depth * (rows + width) + 4 * rows * width,
@@ -102,57 +102,97 @@
     )(table, *blocks, weights)
 
 
-def attend_kernel(table_ref, q_ref, g_ref, kv_ref, live_ref, *rest):
-    dq_ref, grad_ref = rest[-2:]
-    count = pl.num_programs(0)
-    named = table_ref[count + pl.program_id(0)]
+def attend_block(q_ref, g_ref, kv_ref, live_ref, dq_ref, grad_ref):
     pairs = q_ref.shape[-1] // HD // 2
     scale = HD ** (-0.5)
-
-    @pl.when(named == 0)
-    def _():
-        dq_ref[...] = jnp.zeros_like(dq_ref)
-        grad_ref[...] = jnp.zeros_like(grad_ref)
-
-    @pl.when(named != 0)
-    def _():
-        live = live_ref[0] > 0.5
-        zero = jnp.zeros((SPAN, HD), BF16)
-
-        def diagonal(ref, start):
-            one = ref[0, :, start:start + HD]
-            two = ref[0, :, start + HD:start + 2 * HD]
-            return jnp.concatenate(
-                [jnp.concatenate([one, zero], axis=1), jnp.concatenate([zero, two], axis=1)], axis=0
+    live = live_ref[...] > 0.5
+    zero = jnp.zeros((SPAN, HD), BF16)
+
+    def diagonal(ref, start):
+        one = ref[:, start:start + HD]
+        two = ref[:, start + HD:start + 2 * HD]
+        return jnp.concatenate(
+            [jnp.concatenate([one, zero], axis=1), jnp.concatenate([zero, two], axis=1)], axis=0
+        )
+
+    def first(pair):
+        start = pair * 2 * HD
+        columns = slice(start, start + 2 * HD)
+        scores = dot(kv_ref[0, :, columns], diagonal(q_ref, start), ((1,), (1,)))
+        prob_grad = dot(kv_ref[1, :, columns], diagonal(g_ref, start), ((1,), (1,)))
+        return scores, prob_grad
+
+    ahead = first(0)
+    for pair in range(pairs):
+        scores, prob_grad = ahead
+        if pair + 1 < pairs:
+            ahead = first(pair + 1)
+        start = pair * 2 * HD
+        columns = slice(start, start + 2 * HD)
+        scores = jnp.where(live, scores * scale, -1e30)
+        expo = jnp.exp(scores - jnp.max(scores, axis=0, keepdims=True))
+        probs = expo * (1.0 / jnp.sum(expo, axis=0, keepdims=True))
+        center = jnp.sum(probs * prob_grad, axis=0, keepdims=True)
+        score_grad = (probs * (prob_grad - center) * scale).astype(BF16)
+        value_grad = dot(probs.astype(BF16), diagonal(g_ref, start), ((1,), (0,)))
+        key_grad = dot(score_grad, diagonal(q_ref, start), ((1,), (0,)))
+        both = dot(score_grad, kv_ref[0, :, columns], ((0,), (0,)))
+        grad_ref[1, :, columns] = value_grad.astype(BF16)
+        grad_ref[0, :, columns] = key_grad.astype(BF16)
+        dq_ref[:, columns] = jnp.concatenate([both[:SPAN, :HD], both[SPAN:, HD:]], axis=1).astype(
+            BF16
+        )
+
+
+def attend_kernel(part, table_ref, q_ref, g_ref, live_ref, kv_ref, *rest):
+    dq_ref, grad_ref, kv_buf, grad_buf, in_sem, out_sem = rest[-6:]
+    count, _, width = q_ref.shape
+    columns = pl.ds(part * width, width)
+
+    def copy_in(r):
+        source = kv_ref.at[table_ref[r], :, :, columns]
+        return pltpu.make_async_copy(source, kv_buf.at[r % 2], in_sem.at[r % 2])
+
+    def copy_out(r):
+        target = grad_ref.at[table_ref[r], :, :, columns]
+        return pltpu.make_async_copy(grad_buf.at[r % 2], target, out_sem.at[r % 2])
+
+    copy_in(0).start()
+
+    @pl.loop(0, count)
+    def _(r):
+        @pl.when(r + 1 < count)
+        def _():
+            copy_in(r + 1).start()
+
+        copy_in(r).wait()
+
+        @pl.when(r >= 2)
+        def _():
+            copy_out(r - 2).wait()
+
+        slot = r % 2
+
+        @pl.when(table_ref[count + r] == 0)
+        def _():
+            dq_ref[r] = jnp.zeros(dq_ref.shape[1:], BF16)
+            grad_buf[slot] = jnp.zeros(grad_buf.shape[1:], BF16)
+
+        @pl.when(table_ref[count + r] != 0)
+        def _():
+            attend_block(
+                q_ref.at[r],
+                g_ref.at[r, :, columns],
+                kv_buf.at[slot],
+                live_ref.at[table_ref[r]],
+                dq_ref.at[r],
+                grad_buf.at[slot],
             )
 
-        def first(pair):
-            start = pair * 2 * HD
-            columns = slice(start, start + 2 * HD)
-            scores = dot(kv_ref[0, 0, :, columns], diagonal(q_ref, start), ((1,), (1,)))
-            prob_grad = dot(kv_ref[0, 1, :, columns], diagonal(g_ref, start), ((1,), (1,)))
-            return scores, prob_grad
-
-        ahead = first(0)
-        for pair in range(pairs):
-            scores, prob_grad = ahead
-            if pair + 1 < pairs:
-                ahead = first(pair + 1)
-            start = pair * 2 * HD
-            columns = slice(start, start + 2 * HD)
-            scores = jnp.where(live, scores * scale, -1e30)
-            expo = jnp.exp(scores - jnp.max(scores, axis=0, keepdims=True))
-            probs = expo * (1.0 / jnp.sum(expo, axis=0, keepdims=True))
-            center = jnp.sum(probs * prob_grad, axis=0, keepdims=True)
-            score_grad = (probs * (prob_grad - center) * scale).astype(BF16)
-            value_grad = dot(probs.astype(BF16), diagonal(g_ref, start), ((1,), (0,)))
-            key_grad = dot(score_grad, diagonal(q_ref, start), ((1,), (0,)))
-            both = dot(score_grad, kv_ref[0, 0, :, columns], ((0,), (0,)))
-            grad_ref[0, 1, :, columns] = value_grad.astype(BF16)
-            grad_ref[0, 0, :, columns] = key_grad.astype(BF16)
-            dq_ref[0, :, columns] = jnp.concatenate(
-                [both[:SPAN, :HD], both[SPAN:, HD:]], axis=1
-            ).astype(BF16)
+        copy_out(r).start()
+
+    for r in range(max(0, count - 2), count):
+        copy_out(r).wait()
 
 
 def attend(slots, named, queries, grads, kv, live, part, before):
@@ -160,37 +200,64 @@
     keys = kv.shape[2]
     heads = width // HD
     table = jnp.concatenate([slots, named]).astype(jnp.int32)
-    span_block = pl.BlockSpec((1, SPAN, width), lambda r, t: (r, 0, 0))
-    part_block = pl.BlockSpec((1, SPAN, width), lambda r, t: (r, 0, part))
-    kv_block = pl.BlockSpec((1, 2, keys, width), lambda r, t: (t[r], 0, 0, part))
-    live_block = pl.BlockSpec((1, keys, HD), lambda r, t: (t[r], 0, 0))
-    in_specs = [span_block, part_block, kv_block, live_block]
-    operands = [table, queries, grads, kv, live]
+    inside = pl.BlockSpec(memory_space=pltpu.VMEM)
+    outside = pl.BlockSpec(memory_space=pltpu.HBM)
+    in_specs = [pl.BlockSpec(memory_space=pltpu.SMEM), inside, inside, inside, outside]
+    operands = [table, queries, grads, live, kv]
     aliases = {}
     if before is not None:
-        in_specs.append(pl.BlockSpec(memory_space=pl.ANY))
+        in_specs.append(outside)
         operands.append(before)
         aliases = {len(operands) - 1: 1}
     return pl.pallas_call(
-        attend_kernel,
-        grid_spec=pltpu.PrefetchScalarGridSpec(
-            num_scalar_prefetch=1,
-            grid=(count,),
-            in_specs=in_specs,
-            out_specs=[span_block, kv_block],
-        ),
+        functools.partial(attend_kernel, part),
+        in_specs=in_specs,
+        out_specs=[inside, outside],
         out_shape=[
             jax.ShapeDtypeStruct(queries.shape, BF16),
             jax.ShapeDtypeStruct(kv.shape, BF16),
         ],
+        scratch_shapes=[
+            pltpu.VMEM((2, 2, keys, width), BF16),
+            pltpu.VMEM((2, 2, keys, width), BF16),
+            pltpu.SemaphoreType.DMA((2,)),
+            pltpu.SemaphoreType.DMA((2,)),
+        ],
         input_output_aliases=aliases,
-        compiler_params=pltpu.CompilerParams(vmem_limit_bytes=40 * 1024 * 1024),
+        compiler_params=pltpu.CompilerParams(vmem_limit_bytes=16 * 1024 * 1024),
         cost_estimate=pl.CostEstimate(
             flops=count * heads * 5 * 2 * SPAN * keys * HD * 4,
             bytes_accessed=count * 4 * keys * width * 2,
             transcendentals=count * heads * SPAN * keys,
         ),
     )(*operands)
+
+
+def assemble_kernel(depth, core_ref, own_ref, up_ref, down_ref, arrived_ref, out_ref):
+    kept = own_ref[...].astype(F32) + up_ref[...].astype(F32) + down_ref[...].astype(F32)
+    kept = kept.astype(BF16)
+    for p in range(kept.shape[1] // depth):
+        columns = slice(p * depth, (p + 1) * depth)
+        mine, other = 2 * p + core_ref[0], 2 * p + 1 - core_ref[0]
+        out_ref[:, pl.ds(pl.multiple_of(mine * depth, depth), depth)] = kept[:, columns]
+        out_ref[:, pl.ds(pl.multiple_of(other * depth, depth), depth)] = arrived_ref[:, columns]
+
+
+def assemble(core, own, up, down, arrived, depth):
+    rows, columns = arrived.shape
+    tile = min(64, rows)
+    block = pl.BlockSpec((tile, columns), lambda r: (r, 0))
+    return pl.pallas_call(
+        functools.partial(assemble_kernel, depth),
+        grid=(rows // tile,),
+        in_specs=[pl.BlockSpec(memory_space=pltpu.SMEM)] + [block] * 4,
+        out_specs=pl.BlockSpec((tile, 2 * columns), lambda r: (r, 0)),
+        out_shape=jax.ShapeDtypeStruct((rows, 2 * columns), BF16),
+        compiler_params=pltpu.CompilerParams(vmem_limit_bytes=16 * 1024 * 1024),
+        cost_estimate=pl.CostEstimate(
+            flops=2 * rows * columns, bytes_accessed=12 * rows * columns, transcendentals=0
+        ),
+    )(jnp.reshape(core, (1,)).astype(jnp.int32), own, up, down, arrived)
 
 
 def on_device(span_act, q_weight, out_grad, neighbour_kv, neighbour_ids, owner):
@@ -221,30 +288,29 @@
             axis=1,
         )
 
-    act_both = jnp.concatenate([columns_of(core), swap(columns_of(1 - core))], axis=0)
-
+    act_mine, act_other = columns_of(core), columns_of(1 - core)
+    act_both = jnp.concatenate([act_mine, swap(act_other)], axis=0)
+
+    q_weight = after(q_weight, act_other)
     acts = gather_ring(act_both, "tensor", tensor_count, opposite - 1)
-    near = [act for act in acts if act is not None]
     along_seq = gather_ring(q_weight, "seq", seq_count)
     along_dp = gather_ring(q_weight, "dp", couples)
-    near, along_seq, along_dp, grad_out = lax.optimization_barrier(
-        (near, along_seq, along_dp, out_grad)
-    )
-
-    acts = near[:opposite] + [None] + near[opposite:]
+
+    cut = width * 5 // 8 // HD * HD
+    left_from = [block[:, :cut] for block in along_seq[1:]]
+    right_from = [block[:, cut:] for block in along_dp[1:]]
+    left_from, right_from, grad_out = lax.optimization_barrier((left_from, right_from, out_grad))
+    corner_left = [gather_ring(block, "dp", couples) for block in left_from]
+    corner_right = [gather_ring(block, "seq", seq_count) for block in right_from]
     acts[opposite] = jnp.concatenate(
         [
             shift(acts[opposite - 1][:rows], "tensor", 1),
-            shift(acts[opposite + 1][rows:], "tensor", -1),
+            shift(after(acts[opposite + 1][rows:], grad_out), "tensor", -1),
         ],
         axis=0,
     )
     depth_blocks = [(tensor_at - k) % tensor_count for k in range(tensor_count)]
     table = jnp.stack(depth_blocks).astype(jnp.int32)
-
-    cut = width * 5 // 8 // HD * HD
-    corner_left = [gather_ring(block[:, :cut], "dp", couples) for block in along_seq[1:]]
-    corner_right = [gather_ring(block[:, cut:], "seq", seq_count) for block in along_dp[1:]]
 
     def block_at(i, j):
         block = ((seq_at - i) % seq_count) * dp_count + ((dp_at // 2 - j) % couples) * 2
@@ -343,10 +409,9 @@
             answers[-1] = after(answers[-1], corners[0][corner_places[-1]])
         grad = sum(answers[1:], answers[0])
         both_grads.append(jnp.concatenate([grad, swap(grad)], axis=0))
-        corners.append({at: weight_product(*at, both_grads[part]) for at in corner_places[::-1]})
+        if part == 0:
+            corners.append({at: weight_product(*at, both_grads[0]) for at in corner_places[::-1]})
     both_grad = jnp.concatenate(both_grads, axis=1)
-
-    both_grad = after(both_grad, corners[1][corner_places[-1]])
 
     def act_product(k):
         block = lax.dynamic_index_in_dim(weights, depth_blocks[k], 0, keepdims=False)
@@ -355,6 +420,8 @@
     far = act_product(opposite)
     up, down = shift(far[:rows], "tensor", 1), shift(far[rows:], "tensor", -1)
 
+    late_grad = after(both_grads[1], far)
+    corners.append({at: weight_product(*at, late_grad) for at in corner_places[::-1]})
     left = [
         reduce_rings([([None] + [corners[0][i, j] for j in range(1, couples)], True)], "dp")[0][1:]
         for i in range(1, seq_count)
@@ -364,43 +431,41 @@
         for j in range(1, couples)
     ]
     act_parts = {k: act_product(k) for k in range(tensor_count) if k != opposite}
+    own = weight_product(0, 0, both_grad)
     beside_seq = [weight_product(i, 0, both_grad) for i in range(1, seq_count)]
     beside_dp = [weight_product(0, j, both_grad) for j in range(1, couples)]
-    up, down, left, right, act_parts, beside_seq, beside_dp = lax.optimization_barrier(
-        (up, down, left, right, act_parts, beside_seq, beside_dp)
+    up, down, left, right, act_parts, own, beside_seq, beside_dp = lax.optimization_barrier(
+        (up, down, left, right, act_parts, own, beside_seq, beside_dp)
     )
 
+    beside_seq = [
+        lax.dynamic_update_slice(block, total([block[:, :half]] + came).astype(BF16), (0, 0))
+        for block, came in zip(beside_seq, left)
+    ]
+    from_seq = reduce_rings([([None] + beside_seq, True)], "seq")[0][1:]
     for m in range(opposite - 1, 0, -1):
         block = act_parts[tensor_count - m]
         if up.shape[0] == rows:
-            up = jnp.concatenate([total([block[:rows], up]).astype(BF16), block[rows:]], axis=0)
+            up = lax.dynamic_update_slice(block, total([block[:rows], up]).astype(BF16), (0, 0))
         else:
             up = total([block, up]).astype(BF16)
         block = act_parts[m]
         if down.shape[0] == rows:
-            down = jnp.concatenate([block[:rows], total([block[rows:], down]).astype(BF16)], axis=0)
+            down = lax.dynamic_update_slice(
+                block, total([block[rows:], down]).astype(BF16), (rows, 0)
+            )
         else:
             down = total([block, down]).astype(BF16)
         up, down = shift(up, "tensor", 1), shift(down, "tensor", -1)
-    beside_seq = [
-        jnp.concatenate([total([block[:, :half]] + came).astype(BF16), block[:, half:]], axis=1)
-        for block, came in zip(beside_seq, left)
-    ]
     beside_dp = [
-        jnp.concatenate([block[:, :half], total([block[:, half:]] + came).astype(BF16)], axis=1)
+        lax.dynamic_update_slice(block, total([block[:, half:]] + came).astype(BF16), (0, half))
         for block, came in zip(beside_dp, right)
     ]
-    from_seq = reduce_rings([([None] + beside_seq, True)], "seq")[0][1:]
     from_dp = reduce_rings([([None] + beside_dp, True)], "dp")[0][1:]
 
-    act_sum = total([act_parts[0], up, down])
-    kept, arrived = act_sum[:rows].astype(BF16), swap(act_sum[rows:].astype(BF16))
-    even = jnp.where(core == 0, kept, arrived)
-    odd = jnp.where(core == 0, arrived, kept)
-    act_grad = jnp.concatenate(
-        [value[:, p * depth:(p + 1) * depth] for p in range(per) for value in (even, odd)], axis=1
-    )
-    weight_grad = total([weight_product(0, 0, both_grad)] + from_seq + from_dp)
+    arrived = swap(total([part[rows:] for part in (act_parts[0], up, down)]).astype(BF16))
+    act_grad = assemble(core, act_parts[0], up, down, arrived, depth)
+    weight_grad = total([own] + from_seq + from_dp)
     return (act_grad, weight_grad, kv_grad)
 
 

time: 230 us -> 226 us (0.983)
  other arithmetic: 14.9 us -> 7.77 us
  waiting for transfers between devices: 123 us -> 129 us
  starting transfers between devices: 28.1 us -> 33.6 us
  Pallas kernels: 24.1 us -> 19.1 us
  matrix products: 16.9 us -> 14.2 us
    ppermute x21, starting transfers between devices: 27.5 us -> 33 us  [shift(): lax.ppermute(value, axis, [(i, (i + step * stride) % size) for i in range...]
    pallas_call x4 -> x5, Pallas kernels: 18.3 us -> 13.3 us  [the longest x4 11.7 us: attend(): pl.pallas_call(functools.partial(attend_kernel, part), in_specs=in_specs,...]
    concatenate x7 -> x2, other arithmetic: 4.63 us -> 0.1 us  [the longest x1 0.07 us: on_device(): act_both = jnp.concatenate([act_mine, swap(act_other)], axis=0)]
    ppermute x6, waiting for transfers between devices: 3.64 us -> 6.89 us  [swap(): lax.ppermute(value, 'dp', [(i, i ^ 1) for i in range(lax.axis_size('dp'))])]
    ppermute x21, waiting for transfers between devices: 119 us -> 122 us  [shift(): lax.ppermute(value, axis, [(i, (i + step * stride) % size) for i in range...]
    dot_general x9, matrix products: 16.9 us -> 14.2 us  [dot(): lax.dot_general(a, b, (contract, ((), ())), preferred_element_type=F32)]
    unnamed x49 -> x47, local copies, waits for them, and re-layouts: 9.02 us -> 8.14 us
  transfers between devices with their start and end apart: 27 -> 27, of which waited for: 17 -> 15; matrix products, arithmetic and copies ran while one was open for 16% -> 13% of each run, Pallas kernels for 9% -> 7%
where the time goes in v5:
time: 226 us; the launch traced here: 225 us
  waiting for transfers between devices  129 us (57%)
  starting transfers between devices  33.6 us (15%)
  local copies, waits for them, and re-layouts  19.9 us (9%)
  Pallas kernels  19.1 us (8%)
  matrix products  14.2 us (6%)
  other arithmetic  7.77 us (3%)
    ppermute x21, waiting for transfers between devices, shift(): lax.ppermute(value, axis, [(i, (i + step * stride) % size) for i in range...  122 us
    ppermute x21, starting transfers between devices, shift(): lax.ppermute(value, axis, [(i, (i + step * stride) % size) for i in range...  33 us
    dot_general x9, matrix products, dot(): lax.dot_general(a, b, (contract, ((), ())), preferred_element_type=F32)  14.2 us
    pallas_call x4, Pallas kernels, attend(): pl.pallas_call(functools.partial(attend_kernel, part), in_specs=in_specs,...  11.7 us
    unnamed x47, local copies, waits for them, and re-layouts  8.14 us
    ppermute x6, waiting for transfers between devices, swap(): lax.ppermute(value, 'dp', [(i, i ^ 1) for i in range(lax.axis_size('dp'))])  6.89 us
    dynamic_update_slice x5, local copies, waits for them, and re-layouts, on_device(): lax.dynamic_update_slice(weights, piece[None], (at, inner * depth, start))  6.07 us
    pallas_call x2, Pallas kernels, product(): pl.pallas_call(functools.partial(product_kernel, count, start), out_shape...  5.81 us
  transfers between devices with their start and end apart: 27, of which 15 were waited for; matrix products, arithmetic and copies ran while one was open for 13% of the time, Pallas kernels for 7%

profile of v5, /device:TPU:0, one launch (start us, length us, event | category | flops | bytes accessed | tf_op | source)
XLA Modules:
  0.0 225.1 jit_solution(12825657010844597392)
XLA Ops:
  0.7 1.3 constant_dynamic-slice_fusion.1
  1.9 3.0 %collective-permute-start = (bf16[1024,1024]{1,0:T(8,128)(2,1)}, bf16[1024,1024]{1,0:T(8,128)(2,1)}, u32[]{:S(2)}, u32[]{:S(2)}) collective-permute-start(bf16[1024,1024]{1,0:T(8,128)(2,1)} %param.7), channel_id=1, source_target_pairs={{0,16},{16,0},{1,17},{17,1},{2,18},{18,2},{3,19},{19,3},{4,20},{20... | collective-permute-start | bytes 6291464 | tf_op jit(solution)/shard_map/ppermute | solution.py:24
  4.9 1.5 collective-permute-start.1
  6.5 1.9 collective-permute-done.3
  8.4 1.6 collective-permute-start.4
  10.1 2.2 collective-permute-start.5
  13.8 1.9 bitcast_dynamic-update-slice_fusion.2
  15.7 35.2 %collective-permute-done = bf16[1024,1024]{1,0:T(8,128)(2,1)} collective-permute-done((bf16[1024,1024]{1,0:T(8,128)(2,1)}, bf16[1024,1024]{1,0:T(8,128)(2,1)}, u32[]{:S(2)}, u32[]{:S(2)}) %collective-permute-start) | collective-permute-done | bytes 2097184 | tf_op jit(solution)/shard_map/ppermute | solution.py:24
  50.9 1.4 slice.68
  52.4 1.3 slice.69
  53.6 1.8 collective-permute-start.8
  55.6 1.9 collective-permute-done.5.refs_3_
  57.5 1.2 collective-permute-start.6
  59.3 1.5 collective-permute-start.2
  60.8 2.7 %collective-permute-start.7 = (bf16[256,1024]{1,0:T(8,128)(2,1)S(1)}, bf16[256,1024]{1,0:T(8,128)(2,1)S(1)}, u32[]{:S(2)}, u32[]{:S(2)}) collective-permute-start(bf16[256,1024]{1,0:T(8,128)(2,1)S(1)} %slice.54), channel_id=1, source_target_pairs={{0,12},{4,0},{8,4},{12,8},{1,13},{5,1},{9,5},{13,9},{2,14},{6,2},{... | collective-permute-start | bytes 1572872 | tf_op jit(solution)/shard_map/ppermute | solution.py:24
  63.5 1.9 bitcast_dynamic-update-slice_fusion.1
  65.4 8.9 %collective-permute-done.6 = bf16[256,1024]{1,0:T(8,128)(2,1)S(1)} collective-permute-done((bf16[256,1024]{1,0:T(8,128)(2,1)S(1)}, bf16[256,1024]{1,0:T(8,128)(2,1)S(1)}, u32[]{:S(2)}, u32[]{:S(2)}) %collective-permute-start.6) | collective-permute-done | bytes 524320 | tf_op jit(solution)/shard_map/ppermute | solution.py:24
  74.3 1.9 bitcast_dynamic-update-slice_fusion
  76.2 13.0 %collective-permute-done.2.g_ref = bf16[4,64,1024]{2,1,0:T(8,128)(2,1)S(1)} collective-permute-done((bf16[4,64,1024]{2,1,0:T(8,128)(2,1)S(1)}, bf16[4,64,1024]{2,1,0:T(8,128)(2,1)S(1)}, u32[]{:S(2)}, u32[]{:S(2)}) %collective-permute-start.2) | collective-permute-done | bytes 524320 | tf_op jit(solution)/shard_map/ppermute | solution.py:24
  89.8 2.9 %shard_map.85 = f32[512,512]{1,0:T(8,128)S(1)} custom-call(s32[4]{0:T(128)S(1)} %pad_add_fusion.1.table_ref, bf16[512,1024]{1,0:T(8,128)(2,1)S(1)} %pad_maximum_fusion.1.refs_0_, bf16[512,1024]{1,0:T(8,128)(2,1)S(1)} %collective-permute-done.4.refs_1_, bf16[512,1024]{1,0:T(8,128)(2,1)S(1)} %constant_dynamic-update-slice_fusion.refs_2_, ...), custom_call_target="tpu_custom_call" | custom-call | flops 2147483648 | bytes 9437184 | tf_op jit(solution)/shard_map/pallas_call | solution.py:90
  93.1 2.9 %shard_map.88 = f32[512,512]{1,0:T(8,128)S(1)} custom-call(s32[4]{0:T(128)S(1)} %pad_add_fusion.1.table_ref, bf16[512,1024]{1,0:T(8,128)(2,1)S(1)} %pad_maximum_fusion.1.refs_0_, bf16[512,1024]{1,0:T(8,128)(2,1)S(1)} %collective-permute-done.4.refs_1_, bf16[512,1024]{1,0:T(8,128)(2,1)S(1)} %constant_dynamic-update-slice_fusion.refs_2_, ...), custom_call_target="tpu_custom_call" | custom-call | flops 2147483648 | bytes 9437184 | tf_op jit(solution)/shard_map/pallas_call | solution.py:90
  99.2 2.6 %shard_map.86 = (bf16[4,64,512]{2,1,0:T(8,128)(2,1)S(1)}, bf16[8,2,256,1024]{3,2,1,0:T(8,128)(2,1)}) custom-call(s32[8]{0:T(128)S(1)} %pad_add_fusion.table_ref, bf16[4,64,512]{2,1,0:T(8,128)(2,1)S(1)} %bitcast.81, bf16[4,64,1024]{2,1,0:T(8,128)(2,1)S(1)} %bitcast.76, f32[8,256,128]{2,1,0:T(8,128)S(1)} %broadcast_in_dim.20.live_ref, ...), custom_call_target="tpu_custom_call" | custom-call | flops 1342177280 | bytes 4194304 | tf_op jit(solution)/shard_map/pallas_call | solution.py:212
  101.8 4.0 %collective-permute-done.11.q_ref = bf16[4,64,512]{2,1,0:T(8,128)(2,1)S(1)} collective-permute-done((bf16[4,64,512]{2,1,0:T(8,128)(2,1)S(1)}, bf16[4,64,512]{2,1,0:T(8,128)(2,1)S(1)}, u32[]{:S(2)}, u32[]{:S(2)}) %collective-permute-start.11) | collective-permute-done | bytes 262176 | tf_op jit(solution)/shard_map/ppermute | solution.py:24
  105.8 3.3 %shard_map.87 = (bf16[4,64,512]{2,1,0:T(8,128)(2,1)}, bf16[8,2,256,1024]{3,2,1,0:T(8,128)(2,1)}) custom-call(s32[8]{0:T(128)S(1)} %pad_add_fusion.2.table_ref, bf16[4,64,512]{2,1,0:T(8,128)(2,1)S(1)} %collective-permute-done.11.q_ref, bf16[4,64,1024]{2,1,0:T(8,128)(2,1)S(1)} %collective-permute-done.2.g_ref, ...), custom_call_target="tpu_custom_call", output_to_operand_aliasing={{1}: (5, {})} | custom-call | flops 1342177280 | bytes 4194304 | tf_op jit(solution)/shard_map/pallas_call | solution.py:212
  109.1 2.4 %collective-permute-start.12 = (bf16[4,64,512]{2,1,0:T(8,128)(2,1)}, bf16[4,64,512]{2,1,0:T(8,128)(2,1)}, u32[]{:S(2)}, u32[]{:S(2)}) collective-permute-start(bf16[4,64,512]{2,1,0:T(8,128)(2,1)} %get-tuple-element.45), channel_id=1, source_target_pairs={{0,16},{16,0},{1,17},{17,1},{2,18},{18,2},{3,19},{19,3},{4,20},{20... | collective-permute-start | bytes 786440 | tf_op jit(solution)/shard_map/ppermute | solution.py:24
  111.5 3.4 %copy-done = bf16[8,2,256,1024]{3,2,1,0:T(8,128)(2,1)S(1)} copy-done((bf16[8,2,256,1024]{3,2,1,0:T(8,128)(2,1)S(1)}, bf16[8,2,256,1024]{3,2,1,0:T(8,128)(2,1)}, u32[]{:S(2)}) %copy-start) | copy-done | bytes 8388632
  116.0 2.6 %shard_map.89 = (bf16[4,64,512]{2,1,0:T(8,128)(2,1)S(1)}, bf16[8,2,256,1024]{3,2,1,0:T(8,128)(2,1)}) custom-call(s32[8]{0:T(128)S(1)} %pad_add_fusion.table_ref, bf16[4,64,512]{2,1,0:T(8,128)(2,1)S(1)} %bitcast.79, bf16[4,64,1024]{2,1,0:T(8,128)(2,1)S(1)} %bitcast.77, f32[8,256,128]{2,1,0:T(8,128)S(1)} %broadcast_in_dim.20.live_ref, ...), custom_call_target="tpu_custom_call", output_to_operand_aliasing={{1}: (5, {})} | custom-call | flops 1342177280 | bytes 4194304 | tf_op jit(solution)/shard_map/pallas_call | solution.py:212
  118.6 3.4 %copy-done.1 = bf16[8,2,256,1024]{3,2,1,0:T(8,128)(2,1)S(1)} copy-done((bf16[8,2,256,1024]{3,2,1,0:T(8,128)(2,1)S(1)}, bf16[8,2,256,1024]{3,2,1,0:T(8,128)(2,1)}, u32[]{:S(2)}) %copy-start.1) | copy-done | bytes 8388632
  122.0 3.2 %shard_map.90 = (bf16[4,64,512]{2,1,0:T(8,128)(2,1)S(1)}, bf16[8,2,256,1024]{3,2,1,0:T(8,128)(2,1)}) custom-call(s32[8]{0:T(128)S(1)} %pad_add_fusion.2.table_ref, bf16[4,64,512]{2,1,0:T(8,128)(2,1)} %collective-permute-done.15.q_ref, bf16[4,64,1024]{2,1,0:T(8,128)(2,1)S(1)} %copy-done.10, ...), custom_call_target="tpu_custom_call", output_to_operand_aliasing={{1}: (5, {})} | custom-call | flops 1342177280 | bytes 4194304 | tf_op jit(solution)/shard_map/pallas_call | solution.py:212
  125.2 3.7 %collective-permute-start.16 = (bf16[4,64,512]{2,1,0:T(8,128)(2,1)S(1)}, bf16[4,64,512]{2,1,0:T(8,128)(2,1)S(1)}, u32[]{:S(2)}, u32[]{:S(2)}) collective-permute-start(bf16[4,64,512]{2,1,0:T(8,128)(2,1)S(1)} %get-tuple-element.49), channel_id=1, source_target_pairs={{0,16},{16,0},{1,17},{17,1},{2,18},{18,2},{3,19},{19,3},{4,20},{20... | collective-permute-start | bytes 786440 | tf_op jit(solution)/shard_map/ppermute | solution.py:24
  132.2 3.0 %collective-permute-done.16 = bf16[4,64,512]{2,1,0:T(8,128)(2,1)S(1)} collective-permute-done((bf16[4,64,512]{2,1,0:T(8,128)(2,1)S(1)}, bf16[4,64,512]{2,1,0:T(8,128)(2,1)S(1)}, u32[]{:S(2)}, u32[]{:S(2)}) %collective-permute-start.16) | collective-permute-done | bytes 262176 | tf_op jit(solution)/shard_map/ppermute | solution.py:24
  135.6 1.3 collective-permute-done.17
  136.9 3.1 %fusion.12 = bf16[512,1024]{1,0:T(8,128)(2,1)S(1)} fusion(bf16[4,1024,1024]{2,1,0:T(8,128)(2,1)} %copy-done.2, s32[]{:T(128)S(6)} %select_n.245, bf16[256,512]{1,0:T(8,128)(2,1)S(1)} %collective-permute-done.17, bf16[256,512]{1,0:T(8,128)(2,1)S(1)} %bitcast_add_fusion, bf16[256,512]{1,0:T(8,128)(2,1)} %copy-done.17, bf16[256,512]{1,0:T(8,128)(2,1)S(1)} %bitcast.84), kind=kOutput, calls=%fused_computation.22 | convolution fusion | flops 1078460416 | bytes 4194308 | tf_op jit(solution)/shard_map/dot_general | solution.py:18
  140.5 3.5 %collective-permute-start.19 = (bf16[256,1024]{1,0:T(8,128)(2,1)S(1)}, bf16[256,1024]{1,0:T(8,128)(2,1)S(1)}, u32[]{:S(2)}, u32[]{:S(2)}) collective-permute-start(bf16[256,1024]{1,0:T(8,128)(2,1)S(1)} %get-tuple-element.71), channel_id=1, source_target_pairs={{0,12},{4,0},{8,4},{12,8},{1,13},{5,1},{9,5},{13,9},{2,14},{6,2},{... | collective-permute-start | bytes 1572872 | tf_op jit(solution)/shard_map/ppermute | solution.py:24
  145.1 3.0 %fusion.15.own_ref = bf16[512,1024]{1,0:T(8,128)(2,1)S(1)} fusion(bf16[4,1024,1024]{2,1,0:T(8,128)(2,1)} %copy-done.2, s32[]{:T(128)S(6)} %select_n.246, bf16[256,512]{1,0:T(8,128)(2,1)S(1)} %collective-permute-done.17, bf16[256,512]{1,0:T(8,128)(2,1)S(1)} %bitcast_add_fusion, bf16[256,512]{1,0:T(8,128)(2,1)S(1)} %copy-done.18, ...), kind=kOutput, calls=%fused_computation.23 | convolution fusion | flops 1078460416 | bytes 4194308 | tf_op jit(solution)/shard_map/dot_general | solution.py:18
  148.2 1.3 fusion.18
  149.5 1.3 fusion.21
  150.9 1.3 convolution_convert_fusion.2
  152.2 1.3 convolution_convert_fusion.1
  153.5 1.3 convolution_convert_fusion
  154.8 6.1 %collective-permute-done.20 = bf16[1024,512]{1,0:T(8,128)(2,1)S(1)} collective-permute-done((bf16[1024,512]{1,0:T(8,128)(2,1)S(1)}, bf16[1024,512]{1,0:T(8,128)(2,1)S(1)}, u32[]{:S(2)}, u32[]{:S(2)}) %collective-permute-start.20) | collective-permute-done | bytes 1048608 | tf_op jit(solution)/shard_map/ppermute | solution.py:24
  160.9 8.5 %collective-permute-done.21 = bf16[1024,512]{1,0:T(8,128)(2,1)S(1)} collective-permute-done((bf16[1024,512]{1,0:T(8,128)(2,1)S(1)}, bf16[1024,512]{1,0:T(8,128)(2,1)S(1)}, u32[]{:S(2)}, u32[]{:S(2)}) %collective-permute-start.21) | collective-permute-done | bytes 1048608 | tf_op jit(solution)/shard_map/ppermute | solution.py:24
  172.5 3.9 %collective-permute-start.23 = (bf16[512,1024]{1,0:T(8,128)(2,1)S(1)}, bf16[512,1024]{1,0:T(8,128)(2,1)S(1)}, u32[]{:S(2)}, u32[]{:S(2)}) collective-permute-start(bf16[512,1024]{1,0:T(8,128)(2,1)S(1)} %fusion.37), channel_id=1, source_target_pairs={{0,12},{4,0},{8,4},{12,8},{1,13},{5,1},{9,5},{13,9},{2,14},{6,2},{... | collective-permute-start | bytes 3145736 | tf_op jit(solution)/shard_map/ppermute | solution.py:24
  176.3 21.4 %collective-permute-done.22.up_ref = bf16[512,1024]{1,0:T(8,128)(2,1)S(1)} collective-permute-done((bf16[512,1024]{1,0:T(8,128)(2,1)S(1)}, bf16[512,1024]{1,0:T(8,128)(2,1)S(1)}, u32[]{:S(2)}, u32[]{:S(2)}) %collective-permute-start.22) | collective-permute-done | bytes 1048608 | tf_op jit(solution)/shard_map/ppermute | solution.py:24
  197.7 20.2 %collective-permute-done.23.down_ref = bf16[512,1024]{1,0:T(8,128)(2,1)S(1)} collective-permute-done((bf16[512,1024]{1,0:T(8,128)(2,1)S(1)}, bf16[512,1024]{1,0:T(8,128)(2,1)S(1)}, u32[]{:S(2)}, u32[]{:S(2)}) %collective-permute-start.23) | collective-permute-done | bytes 1048608 | tf_op jit(solution)/shard_map/ppermute | solution.py:24
  218.2 1.9 collective-permute-done.24.arrived_ref
  220.1 1.6 shard_map.91
  221.7 3.4 %convert_add_fusion = f32[1024,1024]{1,0:T(8,128)} fusion(bf16[1024,1024]{1,0:T(8,128)(2,1)S(1)} %collective-permute-done.26, bf16[1024,1024]{1,0:T(8,128)(2,1)S(1)} %collective-permute-done.25, bf16[1024,1024]{1,0:T(8,128)(2,1)S(1)} %convolution_convert_fusion.2), kind=kLoop, calls=%fused_computation.1 | loop fusion | flops 5242880 | bytes 10485760 | tf_op jit(solution)/shard_map/add | solution.py:73
  (111 shorter events, 15.8 us)
Async XLA Ops:
  0.7 11.7 %copy-start.16 = (s32[32]{0:T(128)S(1)}, s32[32]{0:T(128)}, u32[]{:S(2)}) copy-start(s32[32]{0:T(128)} %param.11) | copy-start | bytes 388
  1.9 49.0 %collective-permute-start = (bf16[1024,1024]{1,0:T(8,128)(2,1)}, bf16[1024,1024]{1,0:T(8,128)(2,1)}, u32[]{:S(2)}, u32[]{:S(2)}) collective-permute-start(bf16[1024,1024]{1,0:T(8,128)(2,1)} %param.7), channel_id=1, source_target_pairs={{0,16},{16,0},{1,17},{17,1},{2,18},{18,2},{3,19},{19,3},{4,20},{20... | collective-permute-start | bytes 6291464 | tf_op jit(solution)/shard_map/ppermute | solution.py:24
  4.9 47.4 %collective-permute-start.1 = (bf16[1024,1024]{1,0:T(8,128)(2,1)}, bf16[1024,1024]{1,0:T(8,128)(2,1)}, u32[]{:S(2)}, u32[]{:S(2)}) collective-permute-start(bf16[1024,1024]{1,0:T(8,128)(2,1)} %param.7), channel_id=1, source_target_pairs={{0,2},{1,3},{2,0},{3,1},{4,6},{5,7},{6,4},{7,5},{8,10},{9,11},{10,... | collective-permute-start | bytes 6291464 | tf_op jit(solution)/shard_map/ppermute | solution.py:24
  6.5 1.9 collective-permute-start.3
  8.4 47.2 %collective-permute-start.4 = (bf16[512,1024]{1,0:T(8,128)(2,1)S(1)}, bf16[512,1024]{1,0:T(8,128)(2,1)S(1)}, u32[]{:S(2)}, u32[]{:S(2)}) collective-permute-start(bf16[512,1024]{1,0:T(8,128)(2,1)S(1)} %pad_maximum_fusion.1.refs_0_), channel_id=1, source_target_pairs={{0,4},{4,8},{8,12},{12,0},{1,5},{5,9},{9,13},{13,1},{2,6},{6,10},{... | collective-permute-start | bytes 3145736 | tf_op jit(solution)/shard_map/ppermute | solution.py:24
  10.1 47.4 %collective-permute-start.5 = (bf16[512,1024]{1,0:T(8,128)(2,1)S(1)}, bf16[512,1024]{1,0:T(8,128)(2,1)S(1)}, u32[]{:S(2)}, u32[]{:S(2)}) collective-permute-start(bf16[512,1024]{1,0:T(8,128)(2,1)S(1)} %pad_maximum_fusion.1.refs_0_), channel_id=1, source_target_pairs={{0,12},{4,0},{8,4},{12,8},{1,13},{5,1},{9,5},{13,9},{2,14},{6,2},{... | collective-permute-start | bytes 3145736 | tf_op jit(solution)/shard_map/ppermute | solution.py:24
  52.3 7.0 %copy-start.7 = (bf16[256,1024]{1,0:T(8,128)(2,1)S(1)}, bf16[256,1024]{1,0:T(8,128)(2,1)}, u32[]{:S(2)}) copy-start(bf16[256,1024]{1,0:T(8,128)(2,1)} %param.8) | copy-start | bytes 1572868
  53.6 35.7 %collective-permute-start.8 = (bf16[1024,640]{1,0:T(8,128)(2,1)S(1)}, bf16[1024,640]{1,0:T(8,128)(2,1)S(1)}, u32[]{:S(2)}, u32[]{:S(2)}) collective-permute-start(bf16[1024,640]{1,0:T(8,128)(2,1)S(1)} %slice.68), channel_id=1, source_target_pairs={{0,2},{1,3},{2,0},{3,1},{4,6},{5,7},{6,4},{7,5},{8,10},{9,11},{10,... | collective-permute-start | bytes 3932168 | tf_op jit(solution)/shard_map/ppermute | solution.py:24
  57.5 35.4 %copy-start.3 = (bf16[512,1024]{1,0:T(8,128)(2,1)}, bf16[512,1024]{1,0:T(8,128)(2,1)S(1)}, u32[]{:S(2)}) copy-start(bf16[512,1024]{1,0:T(8,128)(2,1)S(1)} %collective-permute-done.5.refs_3_) | copy-start | bytes 3145732
  57.5 16.8 %collective-permute-start.6 = (bf16[256,1024]{1,0:T(8,128)(2,1)S(1)}, bf16[256,1024]{1,0:T(8,128)(2,1)S(1)}, u32[]{:S(2)}, u32[]{:S(2)}) collective-permute-start(bf16[256,1024]{1,0:T(8,128)(2,1)S(1)} %slice.53), channel_id=1, source_target_pairs={{0,4},{4,8},{8,12},{12,0},{1,5},{5,9},{9,13},{13,1},{2,6},{6,10},{... | collective-permute-start | bytes 1572872 | tf_op jit(solution)/shard_map/ppermute | solution.py:24
  58.7 30.5 %collective-permute-start.9 = (bf16[1024,384]{1,0:T(8,128)(2,1)S(1)}, bf16[1024,384]{1,0:T(8,128)(2,1)S(1)}, u32[]{:S(2)}, u32[]{:S(2)}) collective-permute-start(bf16[1024,384]{1,0:T(8,128)(2,1)S(1)} %slice.69), channel_id=1, source_target_pairs={{0,16},{16,0},{1,17},{17,1},{2,18},{18,2},{3,19},{19,3},{4,20},{20... | collective-permute-start | bytes 2359304 | tf_op jit(solution)/shard_map/ppermute | solution.py:24
  59.3 29.9 %collective-permute-start.2 = (bf16[4,64,1024]{2,1,0:T(8,128)(2,1)S(1)}, bf16[4,64,1024]{2,1,0:T(8,128)(2,1)S(1)}, u32[]{:S(2)}, u32[]{:S(2)}) collective-permute-start(bf16[4,64,1024]{2,1,0:T(8,128)(2,1)S(1)} %bitcast.75), channel_id=1, source_target_pairs={{0,16},{16,0},{1,17},{17,1},{2,18},{18,2},{3,19},{19,3},{4,20},{20... | collective-permute-start | bytes 1572872 | tf_op jit(solution)/shard_map/ppermute | solution.py:24
  60.8 28.4 %collective-permute-start.7 = (bf16[256,1024]{1,0:T(8,128)(2,1)S(1)}, bf16[256,1024]{1,0:T(8,128)(2,1)S(1)}, u32[]{:S(2)}, u32[]{:S(2)}) collective-permute-start(bf16[256,1024]{1,0:T(8,128)(2,1)S(1)} %slice.54), channel_id=1, source_target_pairs={{0,12},{4,0},{8,4},{12,8},{1,13},{5,1},{9,5},{13,9},{2,14},{6,2},{... | collective-permute-start | bytes 1572872 | tf_op jit(solution)/shard_map/ppermute | solution.py:24
  89.2 16.6 %copy-start.9 = (bf16[4,64,1024]{2,1,0:T(8,128)(2,1)}, bf16[4,64,1024]{2,1,0:T(8,128)(2,1)S(1)}, u32[]{:S(2)}) copy-start(bf16[4,64,1024]{2,1,0:T(8,128)(2,1)S(1)} %collective-permute-done.2.g_ref) | copy-start | bytes 1572868
  89.3 3.6 %copy-start.5 = (bf16[512,1024]{1,0:T(8,128)(2,1)}, bf16[512,1024]{1,0:T(8,128)(2,1)S(1)}, u32[]{:S(2)}) copy-start(bf16[512,1024]{1,0:T(8,128)(2,1)S(1)} %constant_dynamic-update-slice_fusion.refs_2_) | copy-start | bytes 3145732
  89.8 3.3 %copy-start.2 = (bf16[4,1024,1024]{2,1,0:T(8,128)(2,1)}, bf16[4,1024,1024]{2,1,0:T(8,128)(2,1)S(1)}, u32[]{:S(2)}) copy-start(bf16[4,1024,1024]{2,1,0:T(8,128)(2,1)S(1)} %bitcast_dynamic-update-slice_fusion.4.refs_4_) | copy-start | bytes 25165828
  92.7 6.5 %slice-start = ((s8[8388608]{0:T(1024)(128)(4,1)}), s8[4194304]{0:T(1024)(128)(4,1)S(1)}, s32[]{:S(2)}) async-start(s8[8388608]{0:T(1024)(128)(4,1)} %bitcast.67), calls=%async_computation | async-start | bytes 8388608
  92.8 3.7 %copy-start.15 = (s32[8,256]{1,0:T(8,128)S(1)}, s32[8,256]{1,0:T(8,128)}, u32[]{:S(2)}) copy-start(s32[8,256]{1,0:T(8,128)} %param.10) | copy-start | bytes 24580
  92.8 6.4 %slice-start.1 = ((s8[8388608]{0:T(1024)(128)(4,1)}), s8[4194304]{0:T(1024)(128)(4,1)S(1)}, s32[]{:S(2)}) async-start(s8[8388608]{0:T(1024)(128)(4,1)} %bitcast.67), calls=%async_computation.1 | async-start | bytes 8388608
  92.8 3.7 %collective-permute-start.10 = (f32[256,512]{1,0:T(8,128)S(1)}, f32[256,512]{1,0:T(8,128)S(1)}, u32[]{:S(2)}, u32[]{:S(2)}) collective-permute-start(f32[256,512]{1,0:T(8,128)S(1)} %slice.71), channel_id=1, source_target_pairs={{0,1},{1,0},{2,3},{3,2},{4,5},{5,4},{6,7},{7,6},{8,9},{9,8},{10,11... | collective-permute-start | bytes 1572872 | tf_op jit(solution)/shard_map/ppermute | solution.py:28
  96.1 2.0 collective-permute-start.14
  96.6 9.2 %collective-permute-start.11 = (bf16[4,64,512]{2,1,0:T(8,128)(2,1)S(1)}, bf16[4,64,512]{2,1,0:T(8,128)(2,1)S(1)}, u32[]{:S(2)}, u32[]{:S(2)}) collective-permute-start(bf16[4,64,512]{2,1,0:T(8,128)(2,1)S(1)} %bitcast.80), channel_id=1, source_target_pairs={{0,16},{16,0},{1,17},{17,1},{2,18},{18,2},{3,19},{19,3},{4,20},{20... | collective-permute-start | bytes 786440 | tf_op jit(solution)/shard_map/ppermute | solution.py:24
  98.1 20.4 %collective-permute-start.15 = (bf16[4,64,512]{2,1,0:T(8,128)(2,1)S(1)}, bf16[4,64,512]{2,1,0:T(8,128)(2,1)}, u32[]{:S(2)}, u32[]{:S(2)}) collective-permute-start(bf16[4,64,512]{2,1,0:T(8,128)(2,1)S(1)} %bitcast.78), channel_id=1, source_target_pairs={{0,16},{16,0},{1,17},{17,1},{2,18},{18,2},{3,19},{19,3},{4,20},{20... | collective-permute-start | bytes 786440 | tf_op jit(solution)/shard_map/ppermute | solution.py:24
  101.8 7.3 %copy-start.11 = (bf16[4,64,512]{2,1,0:T(8,128)(2,1)}, bf16[4,64,512]{2,1,0:T(8,128)(2,1)S(1)}, u32[]{:S(2)}) copy-start(bf16[4,64,512]{2,1,0:T(8,128)(2,1)S(1)} %get-tuple-element.43) | copy-start | bytes 786436
  109.1 19.7 %collective-permute-start.12 = (bf16[4,64,512]{2,1,0:T(8,128)(2,1)}, bf16[4,64,512]{2,1,0:T(8,128)(2,1)}, u32[]{:S(2)}, u32[]{:S(2)}) collective-permute-start(bf16[4,64,512]{2,1,0:T(8,128)(2,1)} %get-tuple-element.45), channel_id=1, source_target_pairs={{0,16},{16,0},{1,17},{17,1},{2,18},{18,2},{3,19},{19,3},{4,20},{20... | collective-permute-start | bytes 786440 | tf_op jit(solution)/shard_map/ppermute | solution.py:24
  111.5 3.4 %copy-start = (bf16[8,2,256,1024]{3,2,1,0:T(8,128)(2,1)S(1)}, bf16[8,2,256,1024]{3,2,1,0:T(8,128)(2,1)}, u32[]{:S(2)}) copy-start(bf16[8,2,256,1024]{3,2,1,0:T(8,128)(2,1)} %kv_ref.7) | copy-start | bytes 25165828
  118.6 3.4 %copy-start.1 = (bf16[8,2,256,1024]{3,2,1,0:T(8,128)(2,1)S(1)}, bf16[8,2,256,1024]{3,2,1,0:T(8,128)(2,1)}, u32[]{:S(2)}) copy-start(bf16[8,2,256,1024]{3,2,1,0:T(8,128)(2,1)} %kv_ref.7) | copy-start | bytes 25165828
  122.0 6.9 %copy-start.12 = (bf16[4,64,512]{2,1,0:T(8,128)(2,1)S(1)}, bf16[4,64,512]{2,1,0:T(8,128)(2,1)}, u32[]{:S(2)}) copy-start(bf16[4,64,512]{2,1,0:T(8,128)(2,1)} %copy-done.11) | copy-start | bytes 786436
  122.0 8.0 %copy-start.4 = (bf16[512,1024]{1,0:T(8,128)(2,1)S(1)}, bf16[512,1024]{1,0:T(8,128)(2,1)}, u32[]{:S(2)}) copy-start(bf16[512,1024]{1,0:T(8,128)(2,1)} %copy-done.3) | copy-start | bytes 3145732
  122.0 8.0 %copy-start.6 = (bf16[512,1024]{1,0:T(8,128)(2,1)S(1)}, bf16[512,1024]{1,0:T(8,128)(2,1)}, u32[]{:S(2)}) copy-start(bf16[512,1024]{1,0:T(8,128)(2,1)} %copy-done.5) | copy-start | bytes 3145732
  125.2 10.1 %collective-permute-start.16 = (bf16[4,64,512]{2,1,0:T(8,128)(2,1)S(1)}, bf16[4,64,512]{2,1,0:T(8,128)(2,1)S(1)}, u32[]{:S(2)}, u32[]{:S(2)}) collective-permute-start(bf16[4,64,512]{2,1,0:T(8,128)(2,1)S(1)} %get-tuple-element.49), channel_id=1, source_target_pairs={{0,16},{16,0},{1,17},{17,1},{2,18},{18,2},{3,19},{19,3},{4,20},{20... | collective-permute-start | bytes 786440 | tf_op jit(solution)/shard_map/ppermute | solution.py:24
  129.9 1.6 collective-permute-start.13
  130.5 4.7 %copy-start.13 = (bf16[4,512,1024]{2,1,0:T(8,128)(2,1)}, bf16[4,512,1024]{2,1,0:T(8,128)(2,1)S(1)}, u32[]{:S(2)}) copy-start(bf16[4,512,1024]{2,1,0:T(8,128)(2,1)S(1)} %pad_maximum_fusion) | copy-start | bytes 12582916
  131.5 3.8 %copy-start.17 = (bf16[256,512]{1,0:T(8,128)(2,1)}, bf16[256,512]{1,0:T(8,128)(2,1)S(1)}, u32[]{:S(2)}) copy-start(bf16[256,512]{1,0:T(8,128)(2,1)S(1)} %collective-permute-done.13) | copy-start | bytes 786436
  135.3 1.6 collective-permute-start.17
  135.5 25.5 %collective-permute-start.20 = (bf16[1024,512]{1,0:T(8,128)(2,1)S(1)}, bf16[1024,512]{1,0:T(8,128)(2,1)S(1)}, u32[]{:S(2)}, u32[]{:S(2)}) collective-permute-start(bf16[1024,512]{1,0:T(8,128)(2,1)S(1)} %convolution_convert_fusion.4), channel_id=1, source_target_pairs={{0,2},{1,3},{2,0},{3,1},{4,6},{5,7},{6,4},{7,5},{8,10},{9,11},{10,... | collective-permute-start | bytes 3145736 | tf_op jit(solution)/shard_map/ppermute | solution.py:24
  136.9 7.1 %copy-start.14 = (bf16[4,512,1024]{2,1,0:T(8,128)(2,1)S(1)}, bf16[4,512,1024]{2,1,0:T(8,128)(2,1)}, u32[]{:S(2)}) copy-start(bf16[4,512,1024]{2,1,0:T(8,128)(2,1)} %copy-done.13) | copy-start | bytes 12582916
  136.9 11.3 %slice-start.2 = ((s8[8388608]{0:T(1024)(128)(4,1)}), s8[4194304]{0:T(1024)(128)(4,1)S(1)}, s32[]{:S(2)}) async-start(s8[8388608]{0:T(1024)(128)(4,1)} %bitcast.69), calls=%async_computation.2 | async-start | bytes 8388608
  140.1 29.4 %collective-permute-start.18 = (bf16[256,1024]{1,0:T(8,128)(2,1)S(1)}, bf16[256,1024]{1,0:T(8,128)(2,1)S(1)}, u32[]{:S(2)}, u32[]{:S(2)}) collective-permute-start(bf16[256,1024]{1,0:T(8,128)(2,1)S(1)} %get-tuple-element.72), channel_id=1, source_target_pairs={{0,4},{4,8},{8,12},{12,0},{1,5},{5,9},{9,13},{13,1},{2,6},{6,10},{... | collective-permute-start | bytes 1572872 | tf_op jit(solution)/shard_map/ppermute | solution.py:24
  140.5 4.7 %copy-start.18 = (bf16[256,512]{1,0:T(8,128)(2,1)S(1)}, bf16[256,512]{1,0:T(8,128)(2,1)}, u32[]{:S(2)}) copy-start(bf16[256,512]{1,0:T(8,128)(2,1)} %copy-done.17) | copy-start | bytes 786436
  140.5 29.0 %collective-permute-start.19 = (bf16[256,1024]{1,0:T(8,128)(2,1)S(1)}, bf16[256,1024]{1,0:T(8,128)(2,1)S(1)}, u32[]{:S(2)}, u32[]{:S(2)}) collective-permute-start(bf16[256,1024]{1,0:T(8,128)(2,1)S(1)} %get-tuple-element.71), channel_id=1, source_target_pairs={{0,12},{4,0},{8,4},{12,8},{1,13},{5,1},{9,5},{13,9},{2,14},{6,2},{... | collective-permute-start | bytes 1572872 | tf_op jit(solution)/shard_map/ppermute | solution.py:24
  144.0 4.2 %slice-start.3 = ((s8[8388608]{0:T(1024)(128)(4,1)}), s8[4194304]{0:T(1024)(128)(4,1)S(1)}, s32[]{:S(2)}) async-start(s8[8388608]{0:T(1024)(128)(4,1)} %bitcast.69), calls=%async_computation.3 | async-start | bytes 8388608
  144.8 24.7 %collective-permute-start.21 = (bf16[1024,512]{1,0:T(8,128)(2,1)S(1)}, bf16[1024,512]{1,0:T(8,128)(2,1)S(1)}, u32[]{:S(2)}, u32[]{:S(2)}) collective-permute-start(bf16[1024,512]{1,0:T(8,128)(2,1)S(1)} %convolution_convert_fusion.3), channel_id=1, source_target_pairs={{0,16},{16,0},{1,17},{17,1},{2,18},{18,2},{3,19},{19,3},{4,20},{20... | collective-permute-start | bytes 3145736 | tf_op jit(solution)/shard_map/ppermute | solution.py:24
  169.7 28.0 %collective-permute-start.22 = (bf16[512,1024]{1,0:T(8,128)(2,1)S(1)}, bf16[512,1024]{1,0:T(8,128)(2,1)S(1)}, u32[]{:S(2)}, u32[]{:S(2)}) collective-permute-start(bf16[512,1024]{1,0:T(8,128)(2,1)S(1)} %fusion.36), channel_id=1, source_target_pairs={{0,4},{4,8},{8,12},{12,0},{1,5},{5,9},{9,13},{13,1},{2,6},{6,10},{... | collective-permute-start | bytes 3145736 | tf_op jit(solution)/shard_map/ppermute | solution.py:24
  170.4 51.3 %collective-permute-start.26 = (bf16[1024,1024]{1,0:T(8,128)(2,1)S(1)}, bf16[1024,1024]{1,0:T(8,128)(2,1)S(1)}, u32[]{:S(2)}, u32[]{:S(2)}) collective-permute-start(bf16[1024,1024]{1,0:T(8,128)(2,1)S(1)} %fusion.25), channel_id=1, source_target_pairs={{0,2},{1,3},{2,0},{3,1},{4,6},{5,7},{6,4},{7,5},{8,10},{9,11},{10,... | collective-permute-start | bytes 6291464 | tf_op jit(solution)/shard_map/ppermute | solution.py:24
  171.7 50.0 %collective-permute-start.25 = (bf16[1024,1024]{1,0:T(8,128)(2,1)S(1)}, bf16[1024,1024]{1,0:T(8,128)(2,1)S(1)}, u32[]{:S(2)}, u32[]{:S(2)}) collective-permute-start(bf16[1024,1024]{1,0:T(8,128)(2,1)S(1)} %fusion.24), channel_id=1, source_target_pairs={{0,16},{16,0},{1,17},{17,1},{2,18},{18,2},{3,19},{19,3},{4,20},{20... | collective-permute-start | bytes 6291464 | tf_op jit(solution)/shard_map/ppermute | solution.py:24
  172.5 45.4 %collective-permute-start.23 = (bf16[512,1024]{1,0:T(8,128)(2,1)S(1)}, bf16[512,1024]{1,0:T(8,128)(2,1)S(1)}, u32[]{:S(2)}, u32[]{:S(2)}) collective-permute-start(bf16[512,1024]{1,0:T(8,128)(2,1)S(1)} %fusion.37), channel_id=1, source_target_pairs={{0,12},{4,0},{8,4},{12,8},{1,13},{5,1},{9,5},{13,9},{2,14},{6,2},{... | collective-permute-start | bytes 3145736 | tf_op jit(solution)/shard_map/ppermute | solution.py:24
  218.1 2.0 collective-permute-start.24
  (2 other events, 3.7 us)

commit v6 on v5

--- a/solution.py
+++ b/solution.py
@@ -144,93 +144,68 @@
         )
 
 
-def attend_kernel(part, table_ref, q_ref, g_ref, live_ref, kv_ref, *rest):
-    dq_ref, grad_ref, kv_buf, grad_buf, in_sem, out_sem = rest[-6:]
-    count, _, width = q_ref.shape
-    columns = pl.ds(part * width, width)
-
-    def copy_in(r):
-        source = kv_ref.at[table_ref[r], :, :, columns]
-        return pltpu.make_async_copy(source, kv_buf.at[r % 2], in_sem.at[r % 2])
-
-    def copy_out(r):
-        target = grad_ref.at[table_ref[r], :, :, columns]
-        return pltpu.make_async_copy(grad_buf.at[r % 2], target, out_sem.at[r % 2])
-
-    copy_in(0).start()
-
-    @pl.loop(0, count)
-    def _(r):
-        @pl.when(r + 1 < count)
-        def _():
-            copy_in(r + 1).start()
-
-        copy_in(r).wait()
-
-        @pl.when(r >= 2)
-        def _():
-            copy_out(r - 2).wait()
-
-        slot = r % 2
-
-        @pl.when(table_ref[count + r] == 0)
-        def _():
-            dq_ref[r] = jnp.zeros(dq_ref.shape[1:], BF16)
-            grad_buf[slot] = jnp.zeros(grad_buf.shape[1:], BF16)
-
-        @pl.when(table_ref[count + r] != 0)
-        def _():
-            attend_block(
-                q_ref.at[r],
-                g_ref.at[r, :, columns],
-                kv_buf.at[slot],
-                live_ref.at[table_ref[r]],
-                dq_ref.at[r],
-                grad_buf.at[slot],
-            )
-
-        copy_out(r).start()
-
-    for r in range(max(0, count - 2), count):
-        copy_out(r).wait()
-
-
-def attend(slots, named, queries, grads, kv, live, part, before):
+def attend_kernel(table_ref, q_ref, g_ref, live_ref, kv_ref, dq_ref, grad_ref):
+    named = table_ref[pl.num_programs(0) + pl.program_id(0)]
+
+    @pl.when(named == 0)
+    def _():
+        dq_ref[...] = jnp.zeros_like(dq_ref)
+        grad_ref[...] = jnp.zeros_like(grad_ref)
+
+    @pl.when(named != 0)
+    def _():
+        refs = (q_ref, g_ref, kv_ref, live_ref, dq_ref, grad_ref)
+        attend_block(*(ref.at[0] for ref in refs))
+
+
+def attend(slots, named, queries, grads, live, part, state):
     count, _, width = queries.shape
-    keys = kv.shape[2]
+    keys = state.shape[2]
     heads = width // HD
     table = jnp.concatenate([slots, named]).astype(jnp.int32)
-    inside = pl.BlockSpec(memory_space=pltpu.VMEM)
-    outside = pl.BlockSpec(memory_space=pltpu.HBM)
-    in_specs = [pl.BlockSpec(memory_space=pltpu.SMEM), inside, inside, inside, outside]
-    operands = [table, queries, grads, live, kv]
-    aliases = {}
-    if before is not None:
-        in_specs.append(outside)
-        operands.append(before)
-        aliases = {len(operands) - 1: 1}
+    span_block = pl.BlockSpec((1, SPAN, width), lambda r, t: (r, 0, 0))
+    part_block = pl.BlockSpec((1, SPAN, width), lambda r, t: (r, 0, part))
+    live_block = pl.BlockSpec((1, keys, HD), lambda r, t: (t[r], 0, 0))
+    kv_block = pl.BlockSpec((1, 2, keys, width), lambda r, t: (t[r], 0, 0, part))
     return pl.pallas_call(
-        functools.partial(attend_kernel, part),
-        in_specs=in_specs,
-        out_specs=[inside, outside],
+        attend_kernel,
+        grid_spec=pltpu.PrefetchScalarGridSpec(
+            num_scalar_prefetch=1,
+            grid=(count,),
+            in_specs=[span_block, part_block, live_block, kv_block],
+            out_specs=[span_block, kv_block],
+        ),
         out_shape=[
             jax.ShapeDtypeStruct(queries.shape, BF16),
-            jax.ShapeDtypeStruct(kv.shape, BF16),
+            jax.ShapeDtypeStruct(state.shape, BF16),
         ],
-        scratch_shapes=[
-            pltpu.VMEM((2, 2, keys, width), BF16),
-            pltpu.VMEM((2, 2, keys, width), BF16),
-            pltpu.SemaphoreType.DMA((2,)),
-            pltpu.SemaphoreType.DMA((2,)),
-        ],
-        input_output_aliases=aliases,
-        compiler_params=pltpu.CompilerParams(vmem_limit_bytes=16 * 1024 * 1024),
+        input_output_aliases={4: 1},
+        compiler_params=pltpu.CompilerParams(vmem_limit_bytes=12 * 1024 * 1024),
         cost_estimate=pl.CostEstimate(
             flops=count * heads * 5 * 2 * SPAN * keys * HD * 4,
             bytes_accessed=count * 4 * keys * width * 2,
             transcendentals=count * heads * SPAN * keys,
         ),
-    )(*operands)
+    )(table, queries, grads, live, state)
+
+
+def copy_kernel(in_ref, out_ref, sem):
+    copy = pltpu.make_async_copy(in_ref, out_ref, sem)
+    copy.start()
+    copy.wait()
+
+
+def copied(value):
+    return pl.pallas_call(
+        copy_kernel,
+        in_specs=[pl.BlockSpec(memory_space=pltpu.HBM)],
+        out_specs=pl.BlockSpec(memory_space=pltpu.HBM),
+        out_shape=jax.ShapeDtypeStruct(value.shape, value.dtype),
+        scratch_shapes=[pltpu.SemaphoreType.DMA],
+        cost_estimate=pl.CostEstimate(
+            flops=0, bytes_accessed=2 * value.size * 2, transcendentals=0
+        ),
+    )(value)
 
 
 def assemble_kernel(depth, core_ref, own_ref, up_ref, down_ref, arrived_ref, out_ref):
@@ -279,36 +254,66 @@
     half = width // 2
     opposite = tensor_count // 2
 
-    def columns_of(which):
+    raw = gather_ring(span_act, "tensor", tensor_count, opposite - 1)
+    along_seq = gather_ring(q_weight, "seq", seq_count)
+    along_dp = gather_ring(q_weight, "dp", couples)
+
+    groups = owner.reshape(seq_count, dp_count, spans)
+    groups = lax.dynamic_index_in_dim(groups, dp_at, 1, keepdims=False)
+    mine = lax.dynamic_index_in_dim(groups, seq_at, 0, keepdims=False)
+
+    def order(group, target):
+        names = group == target
+        at = jnp.arange(spans)
+        ahead = (names[None, :] & ~names[:, None]) | (
+            (names[None, :] == names[:, None]) & (at[None, :] < at[:, None])
+        )
+        return jnp.sum(ahead.astype(jnp.int32), axis=1), names.astype(jnp.int32)
+
+    def message(target):
+        place, names = order(mine, target)
+        hit = place[None, :] == jnp.arange(pairs)[:, None]
+        return hit & (names[None, :] == 1)
+
+    def to_owner(value, step):
+        value = value.reshape(spans, SPAN, -1)
+        if not whole_blocks:
+            hit = message((seq_at + step) % seq_count)
+            value = jnp.sum(
+                jnp.where(hit[:, :, None, None], value[None], jnp.zeros((), BF16)), axis=1
+            )
+        return shift(value, "seq", step) if step else value
+
+    state = copied(neighbour_kv)
+    left_from = [block[:, :half] for block in along_seq[1:]]
+    right_from = [block[:, half:] for block in along_dp[1:]]
+    left_from, right_from, state = lax.optimization_barrier((left_from, right_from, state))
+    corner_left = [gather_ring(block, "dp", couples) for block in left_from]
+    corner_right = [gather_ring(block, "seq", seq_count) for block in right_from]
+    up_from, down_from = raw[opposite - 1][:rows // 2], raw[opposite + 1][rows // 2:]
+    up_from, down_from = lax.optimization_barrier((up_from, down_from, left_from, right_from))[:2]
+    raw[opposite] = jnp.concatenate(
+        [shift(up_from, "tensor", 1), shift(down_from, "tensor", -1)], axis=0
+    )
+    grad_out = after(out_grad, corner_right)
+    grads = [to_owner(grad_out, step) for step in range(seq_count)]
+
+    def columns_of(block, which):
         return jnp.concatenate(
             [
-                lax.dynamic_slice(span_act, (0, (2 * p + which) * depth), (rows, depth))
+                lax.dynamic_slice(block, (0, (2 * p + which) * depth), (block.shape[0], depth))
                 for p in range(per)
             ],
             axis=1,
         )
 
-    act_mine, act_other = columns_of(core), columns_of(1 - core)
-    act_both = jnp.concatenate([act_mine, swap(act_other)], axis=0)
-
-    q_weight = after(q_weight, act_other)
-    acts = gather_ring(act_both, "tensor", tensor_count, opposite - 1)
-    along_seq = gather_ring(q_weight, "seq", seq_count)
-    along_dp = gather_ring(q_weight, "dp", couples)
-
-    cut = width * 5 // 8 // HD * HD
-    left_from = [block[:, :cut] for block in along_seq[1:]]
-    right_from = [block[:, cut:] for block in along_dp[1:]]
-    left_from, right_from, grad_out = lax.optimization_barrier((left_from, right_from, out_grad))
-    corner_left = [gather_ring(block, "dp", couples) for block in left_from]
-    corner_right = [gather_ring(block, "seq", seq_count) for block in right_from]
-    acts[opposite] = jnp.concatenate(
-        [
-            shift(acts[opposite - 1][:rows], "tensor", 1),
-            shift(after(acts[opposite + 1][rows:], grad_out), "tensor", -1),
-        ],
-        axis=0,
-    )
+    near = [k for k in range(tensor_count) if k != opposite]
+    others = swap(jnp.concatenate([columns_of(raw[k], 1 - core) for k in near], axis=0))
+    others = {k: others[n * rows:(n + 1) * rows] for n, k in enumerate(near)}
+    others[opposite] = swap(after(columns_of(raw[opposite], 1 - core), others))
+    acts = [
+        jnp.concatenate([columns_of(raw[k], core), others[k]], axis=0) for k in range(tensor_count)
+    ]
     depth_blocks = [(tensor_at - k) % tensor_count for k in range(tensor_count)]
     table = jnp.stack(depth_blocks).astype(jnp.int32)
 
@@ -325,35 +330,9 @@
         elif i == 0:
             pieces = [(along_dp[j], 0)]
         else:
-            pieces = [(corner_left[i - 1][j], 0), (corner_right[j - 1][i], cut)]
+            pieces = [(corner_left[i - 1][j], 0), (corner_right[j - 1][i], half)]
         for piece, start in pieces:
             weights = lax.dynamic_update_slice(weights, piece[None], (at, inner * depth, start))
-
-    groups = owner.reshape(seq_count, dp_count, spans)
-    groups = lax.dynamic_index_in_dim(groups, dp_at, 1, keepdims=False)
-    mine = lax.dynamic_index_in_dim(groups, seq_at, 0, keepdims=False)
-
-    def order(group, target):
-        names = group == target
-        at = jnp.arange(spans)
-        ahead = (names[None, :] & ~names[:, None]) | (
-            (names[None, :] == names[:, None]) & (at[None, :] < at[:, None])
-        )
-        return jnp.sum(ahead.astype(jnp.int32), axis=1), names.astype(jnp.int32)
-
-    def message(target):
-        place, names = order(mine, target)
-        hit = place[None, :] == jnp.arange(pairs)[:, None]
-        return hit & (names[None, :] == 1)
-
-    def to_owner(value, step):
-        value = value.reshape(spans, SPAN, -1)
-        if not whole_blocks:
-            hit = message((seq_at + step) % seq_count)
-            value = jnp.sum(
-                jnp.where(hit[:, :, None, None], value[None], jnp.zeros((), BF16)), axis=1
-            )
-        return shift(value, "seq", step) if step else value
 
     def from_owner(value, step):
         value = shift(value, "seq", -step) if step else value
@@ -375,14 +354,16 @@
 
     live = jnp.broadcast_to((neighbour_ids != 0).astype(F32)[:, :, None], (capacity, KEYS, HD))
     slots = [slots_of(step) for step in range(seq_count)]
-    grads = [to_owner(grad_out, step) for step in range(seq_count)]
-
-    table = after(table, *grads)
+
     queries = []
     for part in range(2):
         partial = product(acts, weights, table, part * half, half)
-        queries.append((partial[:rows] + swap(partial[rows:])).astype(BF16))
+        arrived = swap(partial[rows:])
+        if part == 0:
+            partial = after(partial, grads)
+        queries.append((partial[:rows] + arrived).astype(BF16))
     asked = [[to_owner(value, step) for step in range(seq_count)] for value in queries]
+    asked[0][0] = after(asked[0][0], queries[1])
 
     stacked = jnp.stack(after(acts, queries[1]))
 
@@ -395,14 +376,13 @@
         found = dot(act_block(i, j), grad, ((0,), (0,)))
         return lax.optimization_barrier(found.astype(BF16))
 
-    kv_grad = None
     both_grads, corners = [], []
     corner_places = [(i, j) for i in range(1, seq_count) for j in range(1, couples)]
     for part in range(2):
         answers = []
         for step in range(seq_count):
-            answer, kv_grad = attend(
-                *slots[step], asked[part][step], grads[step], neighbour_kv, live, part, kv_grad
+            answer, state = attend(
+                *slots[step], asked[part][step], grads[step], live, part, state
             )
             answers.append(from_owner(answer, step))
         if part:
@@ -466,7 +446,7 @@
     arrived = swap(total([part[rows:] for part in (act_parts[0], up, down)]).astype(BF16))
     act_grad = assemble(core, act_parts[0], up, down, arrived, depth)
     weight_grad = total([own] + from_seq + from_dp)
-    return (act_grad, weight_grad, kv_grad)
+    return (act_grad, weight_grad, state)
 
 
 def solution(mesh):

time: 226 us -> 438 us (1.94)
  Pallas kernels: 19.1 us -> 280 us
  waiting for transfers between devices: 129 us -> 83 us
  local copies, waits for them, and re-layouts: 19.9 us -> 12.6 us
    pallas_call x4 -> x5, Pallas kernels: 11.7 us -> 273 us  [the longest x1 255 us: copied(): pl.pallas_call(copy_kernel, in_specs=[pl.BlockSpec(memory_space=pltpu.HBM...]
    ppermute x21, waiting for transfers between devices: 122 us -> 80.2 us  [shift(): lax.ppermute(value, axis, [(i, (i + step * stride) % size) for i in range...]
    unnamed x47 -> x41, local copies, waits for them, and re-layouts: 8.14 us -> 2.84 us
  transfers between devices with their start and end apart: 27 -> 28, of which waited for: 15 -> 11; matrix products, arithmetic and copies ran while one was open for 13% -> 6% of each run, Pallas kernels for 7% -> 64%
where the time goes in v6:
time: 438 us; the launch traced here: 437 us
  Pallas kernels  280 us (64%)
  waiting for transfers between devices  83 us (19%)
  starting transfers between devices  37.7 us (9%)
  matrix products  14.1 us (3%)
  local copies, waits for them, and re-layouts  12.6 us (3%)
  other arithmetic  8.12 us (2%)
    pallas_call x1, Pallas kernels, copied(): pl.pallas_call(copy_kernel, in_specs=[pl.BlockSpec(memory_space=pltpu.HBM...  255 us
    ppermute x21, waiting for transfers between devices, shift(): lax.ppermute(value, axis, [(i, (i + step * stride) % size) for i in range...  80.2 us
    ppermute x21, starting transfers between devices, shift(): lax.ppermute(value, axis, [(i, (i + step * stride) % size) for i in range...  36.8 us
    pallas_call x4, Pallas kernels, attend(): pl.pallas_call(attend_kernel, grid_spec=pltpu.PrefetchScalarGridSpec(num_...  17.7 us
    dot_general x9, matrix products, dot(): lax.dot_general(a, b, (contract, ((), ())), preferred_element_type=F32)  14.1 us
  transfers between devices with their start and end apart: 28, of which 11 were waited for; matrix products, arithmetic and copies ran while one was open for 6% of the time, Pallas kernels for 64%

profile of v6, /device:TPU:0, one launch (start us, length us, event | category | flops | bytes accessed | tf_op | source)
XLA Modules:
  0.0 437.3 jit_solution(5556917586675507271)
XLA Ops:
  0.6 3.0 collective-permute-start.3
  3.6 1.5 collective-permute-start.4
  5.2 1.6 collective-permute-start
  6.7 2.2 collective-permute-start.1
  9.0 255.2 %shard_map.85.kv_ref = bf16[8,2,256,1024]{3,2,1,0:T(8,128)(2,1)} custom-call(bf16[8,2,256,1024]{3,2,1,0:T(8,128)(2,1)} %in_ref.1), custom_call_target="tpu_custom_call" | custom-call | bytes 16777216 | tf_op jit(solution)/shard_map/pallas_call | solution.py:199
  264.8 1.3 constant_dynamic-slice_fusion.8
  266.1 1.5 constant_dynamic-slice_fusion.1
  267.8 1.1 broadcast_in_dim.14
  269.6 1.1 slice.63
  270.8 1.3 slice.83
  273.0 3.8 collective-permute-start.6
  276.8 1.9 bitcast_dynamic-update-slice_fusion.1
  279.0 10.7 %collective-permute-done.5 = bf16[128,2048]{1,0:T(8,128)(2,1)S(1)} collective-permute-done((bf16[128,2048]{1,0:T(8,128)(2,1)S(1)}, bf16[128,2048]{1,0:T(8,128)(2,1)S(1)}, u32[]{:S(2)}, u32[]{:S(2)}) %collective-permute-start.5) | collective-permute-done | bytes 524320 | tf_op jit(solution)/shard_map/ppermute | solution.py:24
  289.7 8.0 %collective-permute-done.6 = bf16[128,2048]{1,0:T(8,128)(2,1)S(1)} collective-permute-done((bf16[128,2048]{1,0:T(8,128)(2,1)S(1)}, bf16[128,2048]{1,0:T(8,128)(2,1)S(1)}, u32[]{:S(2)}, u32[]{:S(2)}) %collective-permute-start.6) | collective-permute-done | bytes 524320 | tf_op jit(solution)/shard_map/ppermute | solution.py:24
  299.2 1.6 collective-permute-start.10
  301.2 2.9 shard_map.86
  304.8 2.9 shard_map.87
  308.1 5.4 %collective-permute-done.10.g_ref = bf16[4,64,1024]{2,1,0:T(8,128)(2,1)S(1)} collective-permute-done((bf16[4,64,1024]{2,1,0:T(8,128)(2,1)S(1)}, bf16[4,64,1024]{2,1,0:T(8,128)(2,1)S(1)}, u32[]{:S(2)}, u32[]{:S(2)}) %collective-permute-start.10) | collective-permute-done | bytes 524320 | tf_op jit(solution)/shard_map/ppermute | solution.py:24
  313.6 1.6 collective-permute-start.13
  316.2 4.4 %shard_map.88 = (bf16[4,64,512]{2,1,0:T(8,128)(2,1)S(1)}, bf16[8,2,256,1024]{3,2,1,0:T(8,128)(2,1)}) custom-call(s32[8]{0:T(128)S(1)} %pad_add_fusion.table_ref, bf16[4,64,512]{2,1,0:T(8,128)(2,1)S(1)} %bitcast.79, bf16[4,64,1024]{2,1,0:T(8,128)(2,1)S(1)} %bitcast.74, f32[8,256,128]{2,1,0:T(8,128)S(1)} %broadcast_in_dim.20.live_ref, ...), custom_call_target="tpu_custom_call", output_to_operand_aliasing={{1}: (4, {})} | custom-call | flops 1342177280 | bytes 4194304 | tf_op jit(solution)/shard_map/pallas_call | solution.py:170
  320.6 2.3 collective-permute-done.13.q_ref
  322.9 4.4 %shard_map.89 = (bf16[4,64,512]{2,1,0:T(8,128)(2,1)}, bf16[8,2,256,1024]{3,2,1,0:T(8,128)(2,1)}) custom-call(s32[8]{0:T(128)S(1)} %pad_add_fusion.2.table_ref, bf16[4,64,512]{2,1,0:T(8,128)(2,1)S(1)} %collective-permute-done.13.q_ref, bf16[4,64,1024]{2,1,0:T(8,128)(2,1)S(1)} %collective-permute-done.10.g_ref, ...), custom_call_target="tpu_custom_call", output_to_operand_aliasing={{1}: (4, {})} | custom-call | flops 1342177280 | bytes 4194304 | tf_op jit(solution)/shard_map/pallas_call | solution.py:170
  327.3 2.9 collective-permute-start.14
  331.3 4.4 shard_map.90
  335.7 4.5 %shard_map.91 = (bf16[4,64,512]{2,1,0:T(8,128)(2,1)S(1)}, bf16[8,2,256,1024]{3,2,1,0:T(8,128)(2,1)}) custom-call(s32[8]{0:T(128)S(1)} %pad_add_fusion.2.table_ref, bf16[4,64,512]{2,1,0:T(8,128)(2,1)} %collective-permute-done.16.q_ref, bf16[4,64,1024]{2,1,0:T(8,128)(2,1)S(1)} %copy-done.8, ...), custom_call_target="tpu_custom_call", output_to_operand_aliasing={{1}: (4, {})} | custom-call | flops 1342177280 | bytes 4194304 | tf_op jit(solution)/shard_map/pallas_call | solution.py:170
  340.2 2.6 collective-permute-start.17
  346.2 1.3 collective-permute-done.17
  347.7 1.6 collective-permute-start.21
  349.3 3.1 fusion.12
  352.5 1.1 collective-permute-start.19
  353.7 2.8 collective-permute-start.20
  357.2 1.8 collective-permute-start.22
  359.0 2.9 fusion.15.own_ref
  361.9 1.3 fusion.18
  363.3 1.3 fusion.21
  364.6 1.3 convolution_convert_fusion.2
  365.9 1.3 convolution_convert_fusion.1
  367.3 1.3 convolution_convert_fusion
  368.6 4.6 %collective-permute-done.21 = bf16[1024,512]{1,0:T(8,128)(2,1)S(1)} collective-permute-done((bf16[1024,512]{1,0:T(8,128)(2,1)S(1)}, bf16[1024,512]{1,0:T(8,128)(2,1)S(1)}, u32[]{:S(2)}, u32[]{:S(2)}) %collective-permute-start.21) | collective-permute-done | bytes 1048608 | tf_op jit(solution)/shard_map/ppermute | solution.py:24
  373.2 8.6 %collective-permute-done.22 = bf16[1024,512]{1,0:T(8,128)(2,1)S(1)} collective-permute-done((bf16[1024,512]{1,0:T(8,128)(2,1)S(1)}, bf16[1024,512]{1,0:T(8,128)(2,1)S(1)}, u32[]{:S(2)}, u32[]{:S(2)}) %collective-permute-start.22) | collective-permute-done | bytes 1048608 | tf_op jit(solution)/shard_map/ppermute | solution.py:24
  382.8 1.5 collective-permute-start.27
  384.9 1.8 collective-permute-start.26
  387.0 3.9 collective-permute-start.24
  390.8 19.2 %collective-permute-done.23.up_ref = bf16[512,1024]{1,0:T(8,128)(2,1)S(1)} collective-permute-done((bf16[512,1024]{1,0:T(8,128)(2,1)S(1)}, bf16[512,1024]{1,0:T(8,128)(2,1)S(1)}, u32[]{:S(2)}, u32[]{:S(2)}) %collective-permute-start.23) | collective-permute-done | bytes 1048608 | tf_op jit(solution)/shard_map/ppermute | solution.py:24
  410.1 20.0 %collective-permute-done.24.down_ref = bf16[512,1024]{1,0:T(8,128)(2,1)S(1)} collective-permute-done((bf16[512,1024]{1,0:T(8,128)(2,1)S(1)}, bf16[512,1024]{1,0:T(8,128)(2,1)S(1)}, u32[]{:S(2)}, u32[]{:S(2)}) %collective-permute-start.24) | collective-permute-done | bytes 1048608 | tf_op jit(solution)/shard_map/ppermute | solution.py:24
  430.4 1.9 collective-permute-done.25.arrived_ref
  432.3 1.6 shard_map.92
  433.9 3.4 convert_add_fusion
  (114 shorter events, 14.1 us)
Async XLA Ops:
  0.6 270.0 %collective-permute-start.3 = (bf16[1024,1024]{1,0:T(8,128)(2,1)}, bf16[1024,1024]{1,0:T(8,128)(2,1)S(1)}, u32[]{:S(2)}, u32[]{:S(2)}) collective-permute-start(bf16[1024,1024]{1,0:T(8,128)(2,1)} %param.7), channel_id=1, source_target_pairs={{0,16},{16,0},{1,17},{17,1},{2,18},{18,2},{3,19},{19,3},{4,20},{20... | collective-permute-start | bytes 6291464 | tf_op jit(solution)/shard_map/ppermute | solution.py:24
  3.6 267.2 %collective-permute-start.4 = (bf16[1024,1024]{1,0:T(8,128)(2,1)}, bf16[1024,1024]{1,0:T(8,128)(2,1)}, u32[]{:S(2)}, u32[]{:S(2)}) collective-permute-start(bf16[1024,1024]{1,0:T(8,128)(2,1)} %param.7), channel_id=1, source_target_pairs={{0,2},{1,3},{2,0},{3,1},{4,6},{5,7},{6,4},{7,5},{8,10},{9,11},{10,... | collective-permute-start | bytes 6291464 | tf_op jit(solution)/shard_map/ppermute | solution.py:24
  5.2 260.9 %collective-permute-start = (bf16[256,2048]{1,0:T(8,128)(2,1)}, bf16[256,2048]{1,0:T(8,128)(2,1)S(1)}, u32[]{:S(2)}, u32[]{:S(2)}) collective-permute-start(bf16[256,2048]{1,0:T(8,128)(2,1)} %param.6), channel_id=1, source_target_pairs={{0,4},{4,8},{8,12},{12,0},{1,5},{5,9},{9,13},{13,1},{2,6},{6,10},{... | collective-permute-start | bytes 3145736 | tf_op jit(solution)/shard_map/ppermute | solution.py:24
  6.7 259.3 %collective-permute-start.1 = (bf16[256,2048]{1,0:T(8,128)(2,1)}, bf16[256,2048]{1,0:T(8,128)(2,1)}, u32[]{:S(2)}, u32[]{:S(2)}) collective-permute-start(bf16[256,2048]{1,0:T(8,128)(2,1)} %param.6), channel_id=1, source_target_pairs={{0,12},{4,0},{8,4},{12,8},{1,13},{5,1},{9,5},{13,9},{2,14},{6,2},{... | collective-permute-start | bytes 3145736 | tf_op jit(solution)/shard_map/ppermute | solution.py:24
  9.0 255.2 %copy-start.15 = (s32[32]{0:T(128)S(1)}, s32[32]{0:T(128)}, u32[]{:S(2)}) copy-start(s32[32]{0:T(128)} %param.11) | copy-start | bytes 388
  267.7 1.6 copy-start.13
  267.7 30.2 %collective-permute-start.2 = (bf16[768,1024]{1,0:T(8,128)(2,1)S(1)}, bf16[768,1024]{1,0:T(8,128)(2,1)S(1)}, u32[]{:S(2)}, u32[]{:S(2)}) collective-permute-start(bf16[768,1024]{1,0:T(8,128)(2,1)S(1)} %pad_maximum_fusion.1), channel_id=1, source_target_pairs={{0,1},{1,0},{2,3},{3,2},{4,5},{5,4},{6,7},{7,6},{8,9},{9,8},{10,11... | collective-permute-start | bytes 4718600 | tf_op jit(solution)/shard_map/ppermute | solution.py:28
  272.1 28.7 %collective-permute-start.8 = (bf16[1024,512]{1,0:T(8,128)(2,1)S(1)}, bf16[1024,512]{1,0:T(8,128)(2,1)S(1)}, u32[]{:S(2)}, u32[]{:S(2)}) collective-permute-start(bf16[1024,512]{1,0:T(8,128)(2,1)S(1)} %slice.82), channel_id=1, source_target_pairs={{0,2},{1,3},{2,0},{3,1},{4,6},{5,7},{6,4},{7,5},{8,10},{9,11},{10,... | collective-permute-start | bytes 3145736 | tf_op jit(solution)/shard_map/ppermute | solution.py:24
  272.7 25.7 %collective-permute-start.9 = (bf16[1024,512]{1,0:T(8,128)(2,1)S(1)}, bf16[1024,512]{1,0:T(8,128)(2,1)S(1)}, u32[]{:S(2)}, u32[]{:S(2)}) collective-permute-start(bf16[1024,512]{1,0:T(8,128)(2,1)S(1)} %slice.83), channel_id=1, source_target_pairs={{0,16},{16,0},{1,17},{17,1},{2,18},{18,2},{3,19},{19,3},{4,20},{20... | collective-permute-start | bytes 3145736 | tf_op jit(solution)/shard_map/ppermute | solution.py:24
  273.0 16.6 %collective-permute-start.5 = (bf16[128,2048]{1,0:T(8,128)(2,1)S(1)}, bf16[128,2048]{1,0:T(8,128)(2,1)S(1)}, u32[]{:S(2)}, u32[]{:S(2)}) collective-permute-start(bf16[128,2048]{1,0:T(8,128)(2,1)S(1)} %slice.62), channel_id=1, source_target_pairs={{0,4},{4,8},{8,12},{12,0},{1,5},{5,9},{9,13},{13,1},{2,6},{6,10},{... | collective-permute-start | bytes 1572872 | tf_op jit(solution)/shard_map/ppermute | solution.py:24
  273.0 24.7 %collective-permute-start.6 = (bf16[128,2048]{1,0:T(8,128)(2,1)S(1)}, bf16[128,2048]{1,0:T(8,128)(2,1)S(1)}, u32[]{:S(2)}, u32[]{:S(2)}) collective-permute-start(bf16[128,2048]{1,0:T(8,128)(2,1)S(1)} %slice.63), channel_id=1, source_target_pairs={{0,12},{4,0},{8,4},{12,8},{1,13},{5,1},{9,5},{13,9},{2,14},{6,2},{... | collective-permute-start | bytes 1572872 | tf_op jit(solution)/shard_map/ppermute | solution.py:24
  298.0 3.1 collective-permute-start.7
  298.1 1.0 copy-start.5
  298.3 6.1 %copy-start.1 = (bf16[512,1024]{1,0:T(8,128)(2,1)}, bf16[512,1024]{1,0:T(8,128)(2,1)S(1)}, u32[]{:S(2)}) copy-start(bf16[512,1024]{1,0:T(8,128)(2,1)S(1)} %pad_maximum_fusion.5.refs_3_) | copy-start | bytes 3145732
  299.2 14.3 %collective-permute-start.10 = (bf16[4,64,1024]{2,1,0:T(8,128)(2,1)S(1)}, bf16[4,64,1024]{2,1,0:T(8,128)(2,1)S(1)}, u32[]{:S(2)}, u32[]{:S(2)}) collective-permute-start(bf16[4,64,1024]{2,1,0:T(8,128)(2,1)S(1)} %bitcast.73), channel_id=1, source_target_pairs={{0,16},{16,0},{1,17},{17,1},{2,18},{18,2},{3,19},{19,3},{4,20},{20... | collective-permute-start | bytes 1572872 | tf_op jit(solution)/shard_map/ppermute | solution.py:24
  301.1 3.4 copy-start
  301.2 3.6 copy-start.3
  304.1 4.0 copy-start.14
  304.1 9.4 %collective-permute-start.11 = (f32[256,512]{1,0:T(8,128)S(1)}, f32[256,512]{1,0:T(8,128)S(1)}, u32[]{:S(2)}, u32[]{:S(2)}) collective-permute-start(f32[256,512]{1,0:T(8,128)S(1)} %slice.85), channel_id=1, source_target_pairs={{0,1},{1,0},{2,3},{3,2},{4,5},{5,4},{6,7},{7,6},{8,9},{9,8},{10,11... | collective-permute-start | bytes 1572872 | tf_op jit(solution)/shard_map/ppermute | solution.py:28
  307.7 7.5 %collective-permute-start.12 = (f32[256,512]{1,0:T(8,128)S(1)}, f32[256,512]{1,0:T(8,128)S(1)}, u32[]{:S(2)}, u32[]{:S(2)}) collective-permute-start(f32[256,512]{1,0:T(8,128)S(1)} %slice.87), channel_id=1, source_target_pairs={{0,1},{1,0},{2,3},{3,2},{4,5},{5,4},{6,7},{7,6},{8,9},{9,8},{10,11... | collective-permute-start | bytes 1572872 | tf_op jit(solution)/shard_map/ppermute | solution.py:28
  313.5 9.4 %copy-start.7 = (bf16[4,64,1024]{2,1,0:T(8,128)(2,1)}, bf16[4,64,1024]{2,1,0:T(8,128)(2,1)S(1)}, u32[]{:S(2)}) copy-start(bf16[4,64,1024]{2,1,0:T(8,128)(2,1)S(1)} %collective-permute-done.10.g_ref) | copy-start | bytes 1572868
  313.6 9.3 %collective-permute-start.13 = (bf16[4,64,512]{2,1,0:T(8,128)(2,1)S(1)}, bf16[4,64,512]{2,1,0:T(8,128)(2,1)S(1)}, u32[]{:S(2)}, u32[]{:S(2)}) collective-permute-start(bf16[4,64,512]{2,1,0:T(8,128)(2,1)S(1)} %bitcast.78), channel_id=1, source_target_pairs={{0,16},{16,0},{1,17},{17,1},{2,18},{18,2},{3,19},{19,3},{4,20},{20... | collective-permute-start | bytes 786440 | tf_op jit(solution)/shard_map/ppermute | solution.py:24
  315.4 20.3 %collective-permute-start.16 = (bf16[4,64,512]{2,1,0:T(8,128)(2,1)S(1)}, bf16[4,64,512]{2,1,0:T(8,128)(2,1)}, u32[]{:S(2)}, u32[]{:S(2)}) collective-permute-start(bf16[4,64,512]{2,1,0:T(8,128)(2,1)S(1)} %bitcast.76), channel_id=1, source_target_pairs={{0,16},{16,0},{1,17},{17,1},{2,18},{18,2},{3,19},{19,3},{4,20},{20... | collective-permute-start | bytes 786440 | tf_op jit(solution)/shard_map/ppermute | solution.py:24
  320.6 6.7 %copy-start.9 = (bf16[4,64,512]{2,1,0:T(8,128)(2,1)}, bf16[4,64,512]{2,1,0:T(8,128)(2,1)S(1)}, u32[]{:S(2)}) copy-start(bf16[4,64,512]{2,1,0:T(8,128)(2,1)S(1)} %get-tuple-element.49) | copy-start | bytes 786436
  327.3 15.5 %collective-permute-start.14 = (bf16[4,64,512]{2,1,0:T(8,128)(2,1)}, bf16[4,64,512]{2,1,0:T(8,128)(2,1)}, u32[]{:S(2)}, u32[]{:S(2)}) collective-permute-start(bf16[4,64,512]{2,1,0:T(8,128)(2,1)} %get-tuple-element.51), channel_id=1, source_target_pairs={{0,16},{16,0},{1,17},{17,1},{2,18},{18,2},{3,19},{19,3},{4,20},{20... | collective-permute-start | bytes 786440 | tf_op jit(solution)/shard_map/ppermute | solution.py:24
  330.2 1.0 copy-start.6
  331.3 4.4 %copy-start.8 = (bf16[4,64,1024]{2,1,0:T(8,128)(2,1)S(1)}, bf16[4,64,1024]{2,1,0:T(8,128)(2,1)}, u32[]{:S(2)}) copy-start(bf16[4,64,1024]{2,1,0:T(8,128)(2,1)} %copy-done.7) | copy-start | bytes 1572868
  335.6 7.2 %copy-start.10 = (bf16[4,64,512]{2,1,0:T(8,128)(2,1)S(1)}, bf16[4,64,512]{2,1,0:T(8,128)(2,1)}, u32[]{:S(2)}) copy-start(bf16[4,64,512]{2,1,0:T(8,128)(2,1)} %copy-done.9) | copy-start | bytes 786436
  335.6 8.3 %copy-start.2 = (bf16[512,1024]{1,0:T(8,128)(2,1)S(1)}, bf16[512,1024]{1,0:T(8,128)(2,1)}, u32[]{:S(2)}) copy-start(bf16[512,1024]{1,0:T(8,128)(2,1)} %copy-done.1) | copy-start | bytes 3145732
  335.7 8.3 %copy-start.4 = (bf16[512,1024]{1,0:T(8,128)(2,1)S(1)}, bf16[512,1024]{1,0:T(8,128)(2,1)}, u32[]{:S(2)}) copy-start(bf16[512,1024]{1,0:T(8,128)(2,1)} %copy-done.3) | copy-start | bytes 3145732
  340.2 7.3 %collective-permute-start.17 = (bf16[4,64,512]{2,1,0:T(8,128)(2,1)S(1)}, bf16[4,64,512]{2,1,0:T(8,128)(2,1)S(1)}, u32[]{:S(2)}, u32[]{:S(2)}) collective-permute-start(bf16[4,64,512]{2,1,0:T(8,128)(2,1)S(1)} %get-tuple-element.55), channel_id=1, source_target_pairs={{0,16},{16,0},{1,17},{17,1},{2,18},{18,2},{3,19},{19,3},{4,20},{20... | collective-permute-start | bytes 786440 | tf_op jit(solution)/shard_map/ppermute | solution.py:24
  343.9 1.6 collective-permute-start.15
  344.6 3.0 copy-start.11
  345.5 2.1 copy-start.16
  347.6 1.8 collective-permute-start.18
  347.7 25.5 %collective-permute-start.21 = (bf16[1024,512]{1,0:T(8,128)(2,1)S(1)}, bf16[1024,512]{1,0:T(8,128)(2,1)S(1)}, u32[]{:S(2)}, u32[]{:S(2)}) collective-permute-start(bf16[1024,512]{1,0:T(8,128)(2,1)S(1)} %convolution_convert_fusion.4), channel_id=1, source_target_pairs={{0,2},{1,3},{2,0},{3,1},{4,6},{5,7},{6,4},{7,5},{8,10},{9,11},{10,... | collective-permute-start | bytes 3145736 | tf_op jit(solution)/shard_map/ppermute | solution.py:24
  349.3 7.1 %copy-start.12 = (bf16[4,512,1024]{2,1,0:T(8,128)(2,1)S(1)}, bf16[4,512,1024]{2,1,0:T(8,128)(2,1)}, u32[]{:S(2)}) copy-start(bf16[4,512,1024]{2,1,0:T(8,128)(2,1)} %copy-done.11) | copy-start | bytes 12582916
  349.3 12.6 %slice-start = ((s8[8388608]{0:T(1024)(128)(4,1)}), s8[4194304]{0:T(1024)(128)(4,1)S(1)}, s32[]{:S(2)}) async-start(s8[8388608]{0:T(1024)(128)(4,1)} %bitcast.67), calls=%async_computation | async-start | bytes 8388608
  352.5 29.3 %collective-permute-start.19 = (bf16[256,1024]{1,0:T(8,128)(2,1)S(1)}, bf16[256,1024]{1,0:T(8,128)(2,1)S(1)}, u32[]{:S(2)}, u32[]{:S(2)}) collective-permute-start(bf16[256,1024]{1,0:T(8,128)(2,1)S(1)} %get-tuple-element.81), channel_id=1, source_target_pairs={{0,4},{4,8},{8,12},{12,0},{1,5},{5,9},{9,13},{13,1},{2,6},{6,10},{... | collective-permute-start | bytes 1572872 | tf_op jit(solution)/shard_map/ppermute | solution.py:24
  353.7 5.4 %copy-start.17 = (bf16[256,512]{1,0:T(8,128)(2,1)S(1)}, bf16[256,512]{1,0:T(8,128)(2,1)}, u32[]{:S(2)}) copy-start(bf16[256,512]{1,0:T(8,128)(2,1)} %copy-done.16) | copy-start | bytes 786436
  353.7 28.2 %collective-permute-start.20 = (bf16[256,1024]{1,0:T(8,128)(2,1)S(1)}, bf16[256,1024]{1,0:T(8,128)(2,1)S(1)}, u32[]{:S(2)}, u32[]{:S(2)}) collective-permute-start(bf16[256,1024]{1,0:T(8,128)(2,1)S(1)} %get-tuple-element.80), channel_id=1, source_target_pairs={{0,12},{4,0},{8,4},{12,8},{1,13},{5,1},{9,5},{13,9},{2,14},{6,2},{... | collective-permute-start | bytes 1572872 | tf_op jit(solution)/shard_map/ppermute | solution.py:24
  356.5 5.5 %slice-start.1 = ((s8[8388608]{0:T(1024)(128)(4,1)}), s8[4194304]{0:T(1024)(128)(4,1)S(1)}, s32[]{:S(2)}) async-start(s8[8388608]{0:T(1024)(128)(4,1)} %bitcast.67), calls=%async_computation.1 | async-start | bytes 8388608
  357.2 24.6 %collective-permute-start.22 = (bf16[1024,512]{1,0:T(8,128)(2,1)S(1)}, bf16[1024,512]{1,0:T(8,128)(2,1)S(1)}, u32[]{:S(2)}, u32[]{:S(2)}) collective-permute-start(bf16[1024,512]{1,0:T(8,128)(2,1)S(1)} %convolution_convert_fusion.3), channel_id=1, source_target_pairs={{0,16},{16,0},{1,17},{17,1},{2,18},{18,2},{3,19},{19,3},{4,20},{20... | collective-permute-start | bytes 3145736 | tf_op jit(solution)/shard_map/ppermute | solution.py:24
  382.1 28.0 %collective-permute-start.23 = (bf16[512,1024]{1,0:T(8,128)(2,1)S(1)}, bf16[512,1024]{1,0:T(8,128)(2,1)S(1)}, u32[]{:S(2)}, u32[]{:S(2)}) collective-permute-start(bf16[512,1024]{1,0:T(8,128)(2,1)S(1)} %fusion.36), channel_id=1, source_target_pairs={{0,4},{4,8},{8,12},{12,0},{1,5},{5,9},{9,13},{13,1},{2,6},{6,10},{... | collective-permute-start | bytes 3145736 | tf_op jit(solution)/shard_map/ppermute | solution.py:24
  382.8 51.1 %collective-permute-start.27 = (bf16[1024,1024]{1,0:T(8,128)(2,1)S(1)}, bf16[1024,1024]{1,0:T(8,128)(2,1)S(1)}, u32[]{:S(2)}, u32[]{:S(2)}) collective-permute-start(bf16[1024,1024]{1,0:T(8,128)(2,1)S(1)} %fusion.25), channel_id=1, source_target_pairs={{0,2},{1,3},{2,0},{3,1},{4,6},{5,7},{6,4},{7,5},{8,10},{9,11},{10,... | collective-permute-start | bytes 6291464 | tf_op jit(solution)/shard_map/ppermute | solution.py:24
  384.9 48.9 %collective-permute-start.26 = (bf16[1024,1024]{1,0:T(8,128)(2,1)S(1)}, bf16[1024,1024]{1,0:T(8,128)(2,1)S(1)}, u32[]{:S(2)}, u32[]{:S(2)}) collective-permute-start(bf16[1024,1024]{1,0:T(8,128)(2,1)S(1)} %fusion.24), channel_id=1, source_target_pairs={{0,16},{16,0},{1,17},{17,1},{2,18},{18,2},{3,19},{19,3},{4,20},{20... | collective-permute-start | bytes 6291464 | tf_op jit(solution)/shard_map/ppermute | solution.py:24
  387.0 43.0 %collective-permute-start.24 = (bf16[512,1024]{1,0:T(8,128)(2,1)S(1)}, bf16[512,1024]{1,0:T(8,128)(2,1)S(1)}, u32[]{:S(2)}, u32[]{:S(2)}) collective-permute-start(bf16[512,1024]{1,0:T(8,128)(2,1)S(1)} %fusion.37), channel_id=1, source_target_pairs={{0,12},{4,0},{8,4},{12,8},{1,13},{5,1},{9,5},{13,9},{2,14},{6,2},{... | collective-permute-start | bytes 3145736 | tf_op jit(solution)/shard_map/ppermute | solution.py:24
  430.3 2.0 collective-permute-start.25

commit v7 on v6

--- a/solution.py
+++ b/solution.py
@@ -144,7 +144,8 @@
         )
 
 
-def attend_kernel(table_ref, q_ref, g_ref, live_ref, kv_ref, dq_ref, grad_ref):
+def attend_kernel(table_ref, q_ref, g_ref, live_ref, kv_ref, *rest):
+    dq_ref, grad_ref = rest[-2:]
     named = table_ref[pl.num_programs(0) + pl.program_id(0)]
 
     @pl.when(named == 0)
@@ -158,54 +159,94 @@
         attend_block(*(ref.at[0] for ref in refs))
 
 
-def attend(slots, named, queries, grads, live, part, state):
+def attend(place, named, source, queries, grads, kv, live, part, before):
     count, _, width = queries.shape
-    keys = state.shape[2]
+    capacity, keys, _ = live.shape
     heads = width // HD
-    table = jnp.concatenate([slots, named]).astype(jnp.int32)
+    table = jnp.concatenate([place, named, source * count + place]).astype(jnp.int32)
     span_block = pl.BlockSpec((1, SPAN, width), lambda r, t: (r, 0, 0))
     part_block = pl.BlockSpec((1, SPAN, width), lambda r, t: (r, 0, part))
-    live_block = pl.BlockSpec((1, keys, HD), lambda r, t: (t[r], 0, 0))
-    kv_block = pl.BlockSpec((1, 2, keys, width), lambda r, t: (t[r], 0, 0, part))
+    live_block = pl.BlockSpec((1, keys, HD), lambda r, t: (t[2 * count + r], 0, 0))
+    kv_block = pl.BlockSpec((1, 2, keys, width), lambda r, t: (t[r], 0, 0, 0))
+    grad_block = pl.BlockSpec((1, 2, keys, width), lambda r, t: (t[2 * count + r], 0, 0, part))
+    in_specs = [span_block, part_block, live_block, kv_block]
+    operands = [table, queries, grads, live, kv]
+    aliases = {}
+    if before is not None:
+        in_specs.append(pl.BlockSpec(memory_space=pl.ANY))
+        operands.append(before)
+        aliases = {len(operands) - 1: 1}
     return pl.pallas_call(
         attend_kernel,
         grid_spec=pltpu.PrefetchScalarGridSpec(
             num_scalar_prefetch=1,
             grid=(count,),
-            in_specs=[span_block, part_block, live_block, kv_block],
-            out_specs=[span_block, kv_block],
+            in_specs=in_specs,
+            out_specs=[span_block, grad_block],
         ),
         out_shape=[
             jax.ShapeDtypeStruct(queries.shape, BF16),
-            jax.ShapeDtypeStruct(state.shape, BF16),
+            jax.ShapeDtypeStruct((capacity, 2, keys, 2 * width), BF16),
         ],
-        input_output_aliases={4: 1},
+        input_output_aliases=aliases,
         compiler_params=pltpu.CompilerParams(vmem_limit_bytes=12 * 1024 * 1024),
         cost_estimate=pl.CostEstimate(
             flops=count * heads * 5 * 2 * SPAN * keys * HD * 4,
             bytes_accessed=count * 4 * keys * width * 2,
             transcendentals=count * heads * SPAN * keys,
         ),
-    )(table, queries, grads, live, state)
-
-
-def copy_kernel(in_ref, out_ref, sem):
-    copy = pltpu.make_async_copy(in_ref, out_ref, sem)
-    copy.start()
-    copy.wait()
-
-
-def copied(value):
+    )(*operands)
+
+
+def stage_kernel(source_ref, kv_ref, left_ref, right_ref):
+    width = left_ref.shape[-1]
+    left_ref[...] = kv_ref[:, :, :, :width]
+    right_ref[...] = kv_ref[:, :, :, width:]
+
+
+def stage(kv, source, count):
+    _, _, keys, width = kv.shape
+    half_block = pl.BlockSpec((1, 2, keys, width // 2), lambda r, t: (r, 0, 0, 0))
+    half_shape = jax.ShapeDtypeStruct((count, 2, keys, width // 2), kv.dtype)
     return pl.pallas_call(
-        copy_kernel,
-        in_specs=[pl.BlockSpec(memory_space=pltpu.HBM)],
-        out_specs=pl.BlockSpec(memory_space=pltpu.HBM),
-        out_shape=jax.ShapeDtypeStruct(value.shape, value.dtype),
-        scratch_shapes=[pltpu.SemaphoreType.DMA],
+        stage_kernel,
+        grid_spec=pltpu.PrefetchScalarGridSpec(
+            num_scalar_prefetch=1,
+            grid=(count,),
+            in_specs=[
+                pl.BlockSpec((1, 2, keys, width), lambda r, t: (t[0] * count + r, 0, 0, 0))
+            ],
+            out_specs=[half_block, half_block],
+        ),
+        out_shape=[half_shape, half_shape],
+        compiler_params=pltpu.CompilerParams(vmem_limit_bytes=12 * 1024 * 1024),
         cost_estimate=pl.CostEstimate(
-            flops=0, bytes_accessed=2 * value.size * 2, transcendentals=0
-        ),
-    )(value)
+            flops=0, bytes_accessed=8 * count * keys * width, transcendentals=0
+        ),
+    )(jnp.reshape(source, (1,)).astype(jnp.int32), kv)
+
+
+def total_kernel(*refs):
+    refs[-1][...] = total([ref[...] for ref in refs[:-1]])
+
+
+def summed(values):
+    rows, columns = values[0].shape
+    tile = min(128, rows)
+    block = pl.BlockSpec((tile, columns), lambda r: (r, 0))
+    return pl.pallas_call(
+        total_kernel,
+        grid=(rows // tile,),
+        in_specs=[block] * len(values),
+        out_specs=block,
+        out_shape=jax.ShapeDtypeStruct((rows, columns), F32),
+        compiler_params=pltpu.CompilerParams(vmem_limit_bytes=16 * 1024 * 1024),
+        cost_estimate=pl.CostEstimate(
+            flops=len(values) * rows * columns,
+            bytes_accessed=(2 * len(values) + 4) * rows * columns,
+            transcendentals=0,
+        ),
+    )(*values)
 
 
 def assemble_kernel(depth, core_ref, own_ref, up_ref, down_ref, arrived_ref, out_ref):
@@ -284,20 +325,16 @@
             )
         return shift(value, "seq", step) if step else value
 
-    state = copied(neighbour_kv)
-    left_from = [block[:, :half] for block in along_seq[1:]]
-    right_from = [block[:, half:] for block in along_dp[1:]]
-    left_from, right_from, state = lax.optimization_barrier((left_from, right_from, state))
+    cut = width * 5 // 8 // HD * HD
+    sources = [(seq_at - step) % seq_count for step in range(seq_count)]
+    staged = [stage(neighbour_kv, source, pairs) for source in sources]
+    left_from = [block[:, :cut] for block in along_seq[1:]]
+    right_from = [block[:, cut:] for block in along_dp[1:]]
+    left_from, right_from, staged, grad_out = lax.optimization_barrier(
+        (left_from, right_from, staged, out_grad)
+    )
     corner_left = [gather_ring(block, "dp", couples) for block in left_from]
     corner_right = [gather_ring(block, "seq", seq_count) for block in right_from]
-    up_from, down_from = raw[opposite - 1][:rows // 2], raw[opposite + 1][rows // 2:]
-    up_from, down_from = lax.optimization_barrier((up_from, down_from, left_from, right_from))[:2]
-    raw[opposite] = jnp.concatenate(
-        [shift(up_from, "tensor", 1), shift(down_from, "tensor", -1)], axis=0
-    )
-    grad_out = after(out_grad, corner_right)
-    grads = [to_owner(grad_out, step) for step in range(seq_count)]
-
     def columns_of(block, which):
         return jnp.concatenate(
             [
@@ -309,13 +346,20 @@
 
     near = [k for k in range(tensor_count) if k != opposite]
     others = swap(jnp.concatenate([columns_of(raw[k], 1 - core) for k in near], axis=0))
+    up_from, down_from = raw[opposite - 1][:rows // 2], raw[opposite + 1][rows // 2:]
+    up_from, down_from = lax.optimization_barrier((up_from, down_from, left_from, right_from))[:2]
+    up = shift(up_from, "tensor", 1)
+    down_from, grad_out, others = lax.optimization_barrier((down_from, grad_out, others))
+    down = shift(down_from, "tensor", -1)
+    grads = [to_owner(grad_out, step) for step in range(seq_count)]
+    raw[opposite] = jnp.concatenate([up, down], axis=0)
     others = {k: others[n * rows:(n + 1) * rows] for n, k in enumerate(near)}
-    others[opposite] = swap(after(columns_of(raw[opposite], 1 - core), others))
+    others[opposite] = swap(columns_of(raw[opposite], 1 - core))
     acts = [
         jnp.concatenate([columns_of(raw[k], core), others[k]], axis=0) for k in range(tensor_count)
     ]
     depth_blocks = [(tensor_at - k) % tensor_count for k in range(tensor_count)]
-    table = jnp.stack(depth_blocks).astype(jnp.int32)
+    table = after(jnp.stack(depth_blocks).astype(jnp.int32), grads)
 
     def block_at(i, j):
         block = ((seq_at - i) % seq_count) * dp_count + ((dp_at // 2 - j) % couples) * 2
@@ -330,7 +374,7 @@
         elif i == 0:
             pieces = [(along_dp[j], 0)]
         else:
-            pieces = [(corner_left[i - 1][j], 0), (corner_right[j - 1][i], half)]
+            pieces = [(corner_left[i - 1][j], 0), (corner_right[j - 1][i], cut)]
         for piece, start in pieces:
             weights = lax.dynamic_update_slice(weights, piece[None], (at, inner * depth, start))
 
@@ -344,13 +388,12 @@
         return value.reshape(rows, -1)
 
     def slots_of(step):
-        source = (seq_at - step) % seq_count
-        group = lax.dynamic_index_in_dim(groups, source, 0, keepdims=False)
+        group = lax.dynamic_index_in_dim(groups, sources[step], 0, keepdims=False)
         place, names = order(group, seq_at)
         if not whole_blocks:
             place = jnp.arange(pairs)
             names = (place < jnp.sum(names)).astype(jnp.int32)
-        return source * pairs + place, names
+        return place, names, sources[step]
 
     live = jnp.broadcast_to((neighbour_ids != 0).astype(F32)[:, :, None], (capacity, KEYS, HD))
     slots = [slots_of(step) for step in range(seq_count)]
@@ -359,8 +402,6 @@
     for part in range(2):
         partial = product(acts, weights, table, part * half, half)
         arrived = swap(partial[rows:])
-        if part == 0:
-            partial = after(partial, grads)
         queries.append((partial[:rows] + arrived).astype(BF16))
     asked = [[to_owner(value, step) for step in range(seq_count)] for value in queries]
     asked[0][0] = after(asked[0][0], queries[1])
@@ -376,13 +417,20 @@
         found = dot(act_block(i, j), grad, ((0,), (0,)))
         return lax.optimization_barrier(found.astype(BF16))
 
+    kv_grad = None
     both_grads, corners = [], []
     corner_places = [(i, j) for i in range(1, seq_count) for j in range(1, couples)]
     for part in range(2):
         answers = []
         for step in range(seq_count):
-            answer, state = attend(
-                *slots[step], asked[part][step], grads[step], live, part, state
+            answer, kv_grad = attend(
+                *slots[step],
+                asked[part][step],
+                grads[step],
+                staged[step][part],
+                live,
+                part,
+                kv_grad,
             )
             answers.append(from_owner(answer, step))
         if part:
@@ -445,8 +493,8 @@
 
     arrived = swap(total([part[rows:] for part in (act_parts[0], up, down)]).astype(BF16))
     act_grad = assemble(core, act_parts[0], up, down, arrived, depth)
-    weight_grad = total([own] + from_seq + from_dp)
-    return (act_grad, weight_grad, state)
+    weight_grad = summed([own] + from_seq + from_dp)
+    return (act_grad, weight_grad, kv_grad)
 
 
 def solution(mesh):

time: 438 us -> 233 us (0.53)
  Pallas kernels: 280 us -> 23.3 us
  waiting for transfers between devices: 83 us -> 125 us
  local copies, waits for them, and re-layouts: 12.6 us -> 28 us
    pallas_call x1 -> x3, Pallas kernels: 255 us -> 4.37 us  [the longest x1 3.71 us: summed(): pl.pallas_call(total_kernel, grid=(rows // tile,), in_specs=[block] * len...]
    ppermute x21, waiting for transfers between devices: 80.2 us -> 122 us  [shift(): lax.ppermute(value, axis, [(i, (i + step * stride) % size) for i in range...]
    unnamed x41 -> x63, local copies, waits for them, and re-layouts: 2.84 us -> 14.4 us
    pallas_call x4, Pallas kernels: 17.7 us -> 11.5 us  [attend(): pl.pallas_call(attend_kernel, grid_spec=pltpu.PrefetchScalarGridSpec(num_...]
  transfers between devices with their start and end apart: 28 -> 28, of which waited for: 11 -> 17; matrix products, arithmetic and copies ran while one was open for 6% -> 14% of each run, Pallas kernels for 64% -> 7%
where the time goes in v7:
time: 233 us; the launch traced here: 232 us
  waiting for transfers between devices  125 us (54%)
  starting transfers between devices  35.6 us (15%)
  local copies, waits for them, and re-layouts  28 us (12%)
  Pallas kernels  23.3 us (10%)
  matrix products  12.5 us (5%)
  other arithmetic  6.04 us (3%)
    ppermute x21, waiting for transfers between devices, shift(): lax.ppermute(value, axis, [(i, (i + step * stride) % size) for i in range...  122 us
    ppermute x21, starting transfers between devices, shift(): lax.ppermute(value, axis, [(i, (i + step * stride) % size) for i in range...  35.2 us
    unnamed x63, local copies, waits for them, and re-layouts  14.4 us
    dot_general x9, matrix products, dot(): lax.dot_general(a, b, (contract, ((), ())), preferred_element_type=F32)  12.5 us
    pallas_call x4, Pallas kernels, attend(): pl.pallas_call(attend_kernel, grid_spec=pltpu.PrefetchScalarGridSpec(num_...  11.5 us
    pallas_call x2, Pallas kernels, product(): pl.pallas_call(functools.partial(product_kernel, count, start), out_shape...  5.81 us
  transfers between devices with their start and end apart: 28, of which 17 were waited for; matrix products, arithmetic and copies ran while one was open for 14% of the time, Pallas kernels for 7%

profile of v7, /device:TPU:0, one launch (start us, length us, event | category | flops | bytes accessed | tf_op | source)
XLA Modules:
  0.0 232.4 jit_solution(1850709690610334221)
XLA Ops:
  0.6 3.1 %collective-permute-start = (bf16[256,2048]{1,0:T(8,128)(2,1)}, bf16[256,2048]{1,0:T(8,128)(2,1)S(1)}, u32[]{:S(2)}, u32[]{:S(2)}) collective-permute-start(bf16[256,2048]{1,0:T(8,128)(2,1)} %param.6), channel_id=1, source_target_pairs={{0,4},{4,8},{8,12},{12,0},{1,5},{5,9},{9,13},{13,1},{2,6},{6,10},{... | collective-permute-start | bytes 3145736 | tf_op jit(solution)/shard_map/ppermute | solution.py:24
  3.7 2.1 collective-permute-start.1
  5.8 1.6 collective-permute-start.2
  7.4 1.5 collective-permute-start.3
  9.9 2.1 constant_dynamic-slice_fusion.5
  12.0 18.0 %collective-permute-done = bf16[256,2048]{1,0:T(8,128)(2,1)S(1)} collective-permute-done((bf16[256,2048]{1,0:T(8,128)(2,1)}, bf16[256,2048]{1,0:T(8,128)(2,1)S(1)}, u32[]{:S(2)}, u32[]{:S(2)}) %collective-permute-start) | collective-permute-done | bytes 1048608 | tf_op jit(solution)/shard_map/ppermute | solution.py:24
  30.0 21.1 %collective-permute-done.1 = bf16[256,2048]{1,0:T(8,128)(2,1)} collective-permute-done((bf16[256,2048]{1,0:T(8,128)(2,1)}, bf16[256,2048]{1,0:T(8,128)(2,1)}, u32[]{:S(2)}, u32[]{:S(2)}) %collective-permute-start.1) | collective-permute-done | bytes 1048608 | tf_op jit(solution)/shard_map/ppermute | solution.py:24
  51.1 2.4 %constant_dynamic-slice_fusion.1 = (bf16[256,1024]{1,0:T(8,128)(2,1)}, bf16[256,1024]{1,0:T(8,128)(2,1)S(1)}, bf16[256,1024]{1,0:T(8,128)(2,1)S(1)}, bf16[256,1024]{1,0:T(8,128)(2,1)}) fusion(bf16[256,2048]{1,0:T(8,128)(2,1)} %collective-permute-done.1, s32[]{:T(128)S(6)} %select_n.235, s32[]{:T(128)S(6)} %select_n.234, ...), kind=kLoop, calls=%fused_computation.72 | loop fusion | bytes 4194312 | tf_op jit(solution)/shard_map/dynamic_slice | solution.py:341
  54.8 3.4 %copy-done.1 = bf16[8,2,256,1024]{3,2,1,0:T(8,128)(2,1)S(1)} copy-done((bf16[8,2,256,1024]{3,2,1,0:T(8,128)(2,1)S(1)}, bf16[8,2,256,1024]{3,2,1,0:T(8,128)(2,1)}, u32[]{:S(2)}) %copy-start.1) | copy-done | bytes 8388632
  59.8 1.4 copy-done.12
  62.9 1.3 copy-done.18
  68.9 1.6 collective-permute-start.9
  70.5 1.5 collective-permute-start.10
  73.1 1.9 bitcast_dynamic-update-slice_fusion.1
  75.3 2.9 %collective-permute-start.7 = (bf16[128,2048]{1,0:T(8,128)(2,1)S(1)}, bf16[128,2048]{1,0:T(8,128)(2,1)S(1)}, u32[]{:S(2)}, u32[]{:S(2)}) collective-permute-start(bf16[128,2048]{1,0:T(8,128)(2,1)S(1)} %slice.61), channel_id=1, source_target_pairs={{0,12},{4,0},{8,4},{12,8},{1,13},{5,1},{9,5},{13,9},{2,14},{6,2},{... | collective-permute-start | bytes 1572872 | tf_op jit(solution)/shard_map/ppermute | solution.py:24
  78.2 1.5 fusion.59
  80.4 8.2 %collective-permute-done.6 = bf16[128,2048]{1,0:T(8,128)(2,1)S(1)} collective-permute-done((bf16[128,2048]{1,0:T(8,128)(2,1)S(1)}, bf16[128,2048]{1,0:T(8,128)(2,1)S(1)}, u32[]{:S(2)}, u32[]{:S(2)}) %collective-permute-start.6) | collective-permute-done | bytes 524320 | tf_op jit(solution)/shard_map/ppermute | solution.py:24
  88.9 2.0 collective-permute-done.10
  90.9 7.9 %collective-permute-done.7 = bf16[128,2048]{1,0:T(8,128)(2,1)S(1)} collective-permute-done((bf16[128,2048]{1,0:T(8,128)(2,1)S(1)}, bf16[128,2048]{1,0:T(8,128)(2,1)S(1)}, u32[]{:S(2)}, u32[]{:S(2)}) %collective-permute-start.7) | collective-permute-done | bytes 524320 | tf_op jit(solution)/shard_map/ppermute | solution.py:24
  99.0 2.4 %collective-permute-done.5.g_ref = bf16[4,64,1024]{2,1,0:T(8,128)(2,1)S(1)} collective-permute-done((bf16[4,64,1024]{2,1,0:T(8,128)(2,1)S(1)}, bf16[4,64,1024]{2,1,0:T(8,128)(2,1)S(1)}, u32[]{:S(2)}, u32[]{:S(2)}) %collective-permute-start.5) | collective-permute-done | bytes 524320 | tf_op jit(solution)/shard_map/ppermute | solution.py:24
  102.0 2.9 %shard_map.87 = f32[512,512]{1,0:T(8,128)S(1)} custom-call(s32[4]{0:T(128)S(1)} %pad_add_fusion.1.table_ref, bf16[512,1024]{1,0:T(8,128)(2,1)S(1)} %pad_maximum_fusion.2.refs_0_, bf16[512,1024]{1,0:T(8,128)(2,1)S(1)} %pad_maximum_fusion.3.refs_1_, bf16[512,1024]{1,0:T(8,128)(2,1)S(1)} %pad_maximum_fusion.4.refs_2_, ...), custom_call_target="tpu_custom_call" | custom-call | flops 2147483648 | bytes 9437184 | tf_op jit(solution)/shard_map/pallas_call | solution.py:90
  105.7 2.9 %shard_map.88 = f32[512,512]{1,0:T(8,128)S(1)} custom-call(s32[4]{0:T(128)S(1)} %pad_add_fusion.1.table_ref, bf16[512,1024]{1,0:T(8,128)(2,1)S(1)} %pad_maximum_fusion.2.refs_0_, bf16[512,1024]{1,0:T(8,128)(2,1)S(1)} %pad_maximum_fusion.3.refs_1_, bf16[512,1024]{1,0:T(8,128)(2,1)S(1)} %pad_maximum_fusion.4.refs_2_, ...), custom_call_target="tpu_custom_call" | custom-call | flops 2147483648 | bytes 9437184 | tf_op jit(solution)/shard_map/pallas_call | solution.py:90
  108.9 1.6 collective-permute-start.13
  110.7 1.6 collective-permute-start.16
  112.6 2.5 %shard_map.89 = (bf16[4,64,512]{2,1,0:T(8,128)(2,1)S(1)}, bf16[8,2,256,1024]{3,2,1,0:T(8,128)(2,1)}) custom-call(s32[12]{0:T(128)S(1)} %pad_add_fusion.table_ref, bf16[4,64,512]{2,1,0:T(8,128)(2,1)S(1)} %bitcast.81, bf16[4,64,1024]{2,1,0:T(8,128)(2,1)S(1)} %bitcast.78, f32[8,256,128]{2,1,0:T(8,128)S(1)} %broadcast_in_dim.20.live_ref, ...), custom_call_target="tpu_custom_call" | custom-call | flops 1342177280 | bytes 4194304 | tf_op jit(solution)/shard_map/pallas_call | solution.py:179
  115.8 2.3 collective-permute-done.13.q_ref
  118.1 2.5 %shard_map.90 = (bf16[4,64,512]{2,1,0:T(8,128)(2,1)}, bf16[8,2,256,1024]{3,2,1,0:T(8,128)(2,1)}) custom-call(s32[12]{0:T(128)S(1)} %pad_add_fusion.2.table_ref, bf16[4,64,512]{2,1,0:T(8,128)(2,1)S(1)} %collective-permute-done.13.q_ref, bf16[4,64,1024]{2,1,0:T(8,128)(2,1)S(1)} %collective-permute-done.5.g_ref, ...), custom_call_target="tpu_custom_call", output_to_operand_aliasing={{1}: (5, {})} | custom-call | flops 1342177280 | bytes 4194304 | tf_op jit(solution)/shard_map/pallas_call | solution.py:179
  120.6 3.2 %collective-permute-start.14 = (bf16[4,64,512]{2,1,0:T(8,128)(2,1)}, bf16[4,64,512]{2,1,0:T(8,128)(2,1)}, u32[]{:S(2)}, u32[]{:S(2)}) collective-permute-start(bf16[4,64,512]{2,1,0:T(8,128)(2,1)} %get-tuple-element.67), channel_id=1, source_target_pairs={{0,16},{16,0},{1,17},{17,1},{2,18},{18,2},{3,19},{19,3},{4,20},{20... | collective-permute-start | bytes 786440 | tf_op jit(solution)/shard_map/ppermute | solution.py:24
  123.8 1.6 copy-done.11
  126.5 2.5 %shard_map.91 = (bf16[4,64,512]{2,1,0:T(8,128)(2,1)S(1)}, bf16[8,2,256,1024]{3,2,1,0:T(8,128)(2,1)}) custom-call(s32[12]{0:T(128)S(1)} %pad_add_fusion.table_ref, bf16[4,64,512]{2,1,0:T(8,128)(2,1)S(1)} %bitcast.76, bf16[4,64,1024]{2,1,0:T(8,128)(2,1)S(1)} %bitcast.79, ...), custom_call_target="tpu_custom_call", output_to_operand_aliasing={{1}: (5, {})} | custom-call | flops 1342177280 | bytes 4194304 | tf_op jit(solution)/shard_map/pallas_call | solution.py:179
  129.0 4.0 %shard_map.92 = (bf16[4,64,512]{2,1,0:T(8,128)(2,1)S(1)}, bf16[8,2,256,1024]{3,2,1,0:T(8,128)(2,1)}) custom-call(s32[12]{0:T(128)S(1)} %pad_add_fusion.2.table_ref, bf16[4,64,512]{2,1,0:T(8,128)(2,1)} %collective-permute-done.16.q_ref, bf16[4,64,1024]{2,1,0:T(8,128)(2,1)S(1)} %copy-done.7, ...), custom_call_target="tpu_custom_call", output_to_operand_aliasing={{1}: (5, {})} | custom-call | flops 1342177280 | bytes 4194304 | tf_op jit(solution)/shard_map/pallas_call | solution.py:179
  133.0 3.0 %collective-permute-start.17 = (bf16[4,64,512]{2,1,0:T(8,128)(2,1)S(1)}, bf16[4,64,512]{2,1,0:T(8,128)(2,1)S(1)}, u32[]{:S(2)}, u32[]{:S(2)}) collective-permute-start(bf16[4,64,512]{2,1,0:T(8,128)(2,1)S(1)} %get-tuple-element.73), channel_id=1, source_target_pairs={{0,16},{16,0},{1,17},{17,1},{2,18},{18,2},{3,19},{19,3},{4,20},{20... | collective-permute-start | bytes 786440 | tf_op jit(solution)/shard_map/ppermute | solution.py:24
  139.4 2.4 %collective-permute-done.17 = bf16[4,64,512]{2,1,0:T(8,128)(2,1)S(1)} collective-permute-done((bf16[4,64,512]{2,1,0:T(8,128)(2,1)S(1)}, bf16[4,64,512]{2,1,0:T(8,128)(2,1)S(1)}, u32[]{:S(2)}, u32[]{:S(2)}) %collective-permute-start.17) | collective-permute-done | bytes 262176 | tf_op jit(solution)/shard_map/ppermute | solution.py:24
  143.5 3.1 %fusion.12 = bf16[512,1024]{1,0:T(8,128)(2,1)S(1)} fusion(bf16[4,1024,1024]{2,1,0:T(8,128)(2,1)} %copy-done, s32[]{:T(128)S(6)} %select_n.251, bf16[256,512]{1,0:T(8,128)(2,1)S(1)} %collective-permute-done.18, bf16[256,512]{1,0:T(8,128)(2,1)S(1)} %bitcast_add_fusion, bf16[256,512]{1,0:T(8,128)(2,1)} %copy-done.27, bf16[256,512]{1,0:T(8,128)(2,1)S(1)} %bitcast.84), kind=kOutput, calls=%fused_computation.22 | convolution fusion | flops 1078460416 | bytes 4194308 | tf_op jit(solution)/shard_map/dot_general | solution.py:18
  147.5 1.8 collective-permute-start.22
  150.4 2.7 %collective-permute-start.20 = (bf16[256,1024]{1,0:T(8,128)(2,1)S(1)}, bf16[256,1024]{1,0:T(8,128)(2,1)S(1)}, u32[]{:S(2)}, u32[]{:S(2)}) collective-permute-start(bf16[256,1024]{1,0:T(8,128)(2,1)S(1)} %get-tuple-element.98), channel_id=1, source_target_pairs={{0,12},{4,0},{8,4},{12,8},{1,13},{5,1},{9,5},{13,9},{2,14},{6,2},{... | collective-permute-start | bytes 1572872 | tf_op jit(solution)/shard_map/ppermute | solution.py:24
  156.9 1.3 fusion.21
  159.5 1.3 fusion.18
  160.8 1.3 fusion.15.own_ref
  162.2 5.3 %collective-permute-done.21 = bf16[1024,512]{1,0:T(8,128)(2,1)S(1)} collective-permute-done((bf16[1024,512]{1,0:T(8,128)(2,1)S(1)}, bf16[1024,512]{1,0:T(8,128)(2,1)S(1)}, u32[]{:S(2)}, u32[]{:S(2)}) %collective-permute-start.21) | collective-permute-done | bytes 1048608 | tf_op jit(solution)/shard_map/ppermute | solution.py:24
  167.5 5.3 %collective-permute-done.22 = bf16[1024,512]{1,0:T(8,128)(2,1)S(1)} collective-permute-done((bf16[1024,512]{1,0:T(8,128)(2,1)S(1)}, bf16[1024,512]{1,0:T(8,128)(2,1)S(1)}, u32[]{:S(2)}, u32[]{:S(2)}) %collective-permute-start.22) | collective-permute-done | bytes 1048608 | tf_op jit(solution)/shard_map/ppermute | solution.py:24
  172.8 2.3 collective-permute-done.20
  177.8 2.1 collective-permute-start.24
  180.2 23.3 %collective-permute-done.24.down_ref = bf16[512,1024]{1,0:T(8,128)(2,1)S(1)} collective-permute-done((bf16[512,1024]{1,0:T(8,128)(2,1)S(1)}, bf16[512,1024]{1,0:T(8,128)(2,1)S(1)}, u32[]{:S(2)}, u32[]{:S(2)}) %collective-permute-start.24) | collective-permute-done | bytes 1048608 | tf_op jit(solution)/shard_map/ppermute | solution.py:24
  203.5 21.3 %collective-permute-done.23.up_ref = bf16[512,1024]{1,0:T(8,128)(2,1)S(1)} collective-permute-done((bf16[512,1024]{1,0:T(8,128)(2,1)S(1)}, bf16[512,1024]{1,0:T(8,128)(2,1)S(1)}, u32[]{:S(2)}, u32[]{:S(2)}) %collective-permute-start.23) | collective-permute-done | bytes 1048608 | tf_op jit(solution)/shard_map/ppermute | solution.py:24
  225.2 1.9 collective-permute-done.25.arrived_ref
  227.1 1.6 shard_map.93
  228.7 3.7 %shard_map.94 = f32[1024,1024]{1,0:T(8,128)} custom-call(bf16[1024,1024]{1,0:T(8,128)(2,1)S(1)} %convolution_convert_fusion.2.refs_0_, bf16[1024,1024]{1,0:T(8,128)(2,1)S(1)} %collective-permute-done.26.refs_1_, bf16[1024,1024]{1,0:T(8,128)(2,1)S(1)} %collective-permute-done.27.refs_2_), custom_call_target="tpu_custom_call" | custom-call | flops 3145728 | bytes 10485760 | tf_op jit(solution)/shard_map/pallas_call | solution.py:237
  (138 shorter events, 31.7 us)
Async XLA Ops:
  0.6 29.3 %collective-permute-start = (bf16[256,2048]{1,0:T(8,128)(2,1)}, bf16[256,2048]{1,0:T(8,128)(2,1)S(1)}, u32[]{:S(2)}, u32[]{:S(2)}) collective-permute-start(bf16[256,2048]{1,0:T(8,128)(2,1)} %param.6), channel_id=1, source_target_pairs={{0,4},{4,8},{8,12},{12,0},{1,5},{5,9},{9,13},{13,1},{2,6},{6,10},{... | collective-permute-start | bytes 3145736 | tf_op jit(solution)/shard_map/ppermute | solution.py:24
  3.7 47.4 %collective-permute-start.1 = (bf16[256,2048]{1,0:T(8,128)(2,1)}, bf16[256,2048]{1,0:T(8,128)(2,1)}, u32[]{:S(2)}, u32[]{:S(2)}) collective-permute-start(bf16[256,2048]{1,0:T(8,128)(2,1)} %param.6), channel_id=1, source_target_pairs={{0,12},{4,0},{8,4},{12,8},{1,13},{5,1},{9,5},{13,9},{2,14},{6,2},{... | collective-permute-start | bytes 3145736 | tf_op jit(solution)/shard_map/ppermute | solution.py:24
  5.8 61.7 %collective-permute-start.2 = (bf16[1024,1024]{1,0:T(8,128)(2,1)}, bf16[1024,1024]{1,0:T(8,128)(2,1)S(1)}, u32[]{:S(2)}, u32[]{:S(2)}) collective-permute-start(bf16[1024,1024]{1,0:T(8,128)(2,1)} %param.7), channel_id=1, source_target_pairs={{0,16},{16,0},{1,17},{17,1},{2,18},{18,2},{3,19},{19,3},{4,20},{20... | collective-permute-start | bytes 6291464 | tf_op jit(solution)/shard_map/ppermute | solution.py:24
  7.4 60.3 %collective-permute-start.3 = (bf16[1024,1024]{1,0:T(8,128)(2,1)}, bf16[1024,1024]{1,0:T(8,128)(2,1)}, u32[]{:S(2)}, u32[]{:S(2)}) collective-permute-start(bf16[1024,1024]{1,0:T(8,128)(2,1)} %param.7), channel_id=1, source_target_pairs={{0,2},{1,3},{2,0},{3,1},{4,6},{5,7},{6,4},{7,5},{8,10},{9,11},{10,... | collective-permute-start | bytes 6291464 | tf_op jit(solution)/shard_map/ppermute | solution.py:24
  54.8 20.6 %collective-permute-start.4 = (bf16[768,1024]{1,0:T(8,128)(2,1)}, bf16[768,1024]{1,0:T(8,128)(2,1)}, u32[]{:S(2)}, u32[]{:S(2)}) collective-permute-start(bf16[768,1024]{1,0:T(8,128)(2,1)} %pad_maximum_fusion.1), channel_id=1, source_target_pairs={{0,1},{1,0},{2,3},{3,2},{4,5},{5,4},{6,7},{7,6},{8,9},{9,8},{10,11... | collective-permute-start | bytes 4718600 | tf_op jit(solution)/shard_map/ppermute | solution.py:28
  54.8 3.4 %copy-start.1 = (bf16[8,2,256,1024]{3,2,1,0:T(8,128)(2,1)S(1)}, bf16[8,2,256,1024]{3,2,1,0:T(8,128)(2,1)}, u32[]{:S(2)}) copy-start(bf16[8,2,256,1024]{3,2,1,0:T(8,128)(2,1)} %kv_ref.3) | copy-start | bytes 25165828
  68.9 32.5 %collective-permute-start.9 = (bf16[1024,640]{1,0:T(8,128)(2,1)S(1)}, bf16[1024,640]{1,0:T(8,128)(2,1)S(1)}, u32[]{:S(2)}, u32[]{:S(2)}) collective-permute-start(bf16[1024,640]{1,0:T(8,128)(2,1)S(1)} %slice.80), channel_id=1, source_target_pairs={{0,2},{1,3},{2,0},{3,1},{4,6},{5,7},{6,4},{7,5},{8,10},{9,11},{10,... | collective-permute-start | bytes 3932168 | tf_op jit(solution)/shard_map/ppermute | solution.py:24
  70.5 20.4 %collective-permute-start.10 = (bf16[1024,384]{1,0:T(8,128)(2,1)S(1)}, bf16[1024,384]{1,0:T(8,128)(2,1)S(1)}, u32[]{:S(2)}, u32[]{:S(2)}) collective-permute-start(bf16[1024,384]{1,0:T(8,128)(2,1)S(1)} %slice.81), channel_id=1, source_target_pairs={{0,16},{16,0},{1,17},{17,1},{2,18},{18,2},{3,19},{19,3},{4,20},{20... | collective-permute-start | bytes 2359304 | tf_op jit(solution)/shard_map/ppermute | solution.py:24
  72.0 16.6 %collective-permute-start.6 = (bf16[128,2048]{1,0:T(8,128)(2,1)S(1)}, bf16[128,2048]{1,0:T(8,128)(2,1)S(1)}, u32[]{:S(2)}, u32[]{:S(2)}) collective-permute-start(bf16[128,2048]{1,0:T(8,128)(2,1)S(1)} %slice.60), channel_id=1, source_target_pairs={{0,4},{4,8},{8,12},{12,0},{1,5},{5,9},{9,13},{13,1},{2,6},{6,10},{... | collective-permute-start | bytes 1572872 | tf_op jit(solution)/shard_map/ppermute | solution.py:24
  75.3 4.4 %copy-start.14 = (bf16[256,1024]{1,0:T(8,128)(2,1)S(1)}, bf16[256,1024]{1,0:T(8,128)(2,1)}, u32[]{:S(2)}) copy-start(bf16[256,1024]{1,0:T(8,128)(2,1)} %param.8) | copy-start | bytes 1572868
  75.3 5.0 %copy-start.24 = (bf16[256,1024]{1,0:T(8,128)(2,1)S(1)}, bf16[256,1024]{1,0:T(8,128)(2,1)}, u32[]{:S(2)}) copy-start(bf16[256,1024]{1,0:T(8,128)(2,1)} %get-tuple-element.100) | copy-start | bytes 1572868
  75.3 23.5 %collective-permute-start.7 = (bf16[128,2048]{1,0:T(8,128)(2,1)S(1)}, bf16[128,2048]{1,0:T(8,128)(2,1)S(1)}, u32[]{:S(2)}, u32[]{:S(2)}) collective-permute-start(bf16[128,2048]{1,0:T(8,128)(2,1)S(1)} %slice.61), channel_id=1, source_target_pairs={{0,12},{4,0},{8,4},{12,8},{1,13},{5,1},{9,5},{13,9},{2,14},{6,2},{... | collective-permute-start | bytes 1572872 | tf_op jit(solution)/shard_map/ppermute | solution.py:24
  79.7 9.0 %copy-start.23 = (bf16[256,1024]{1,0:T(8,128)(2,1)S(1)}, bf16[256,1024]{1,0:T(8,128)(2,1)}, u32[]{:S(2)}) copy-start(bf16[256,1024]{1,0:T(8,128)(2,1)} %get-tuple-element.111) | copy-start | bytes 1572868
  79.7 21.7 %collective-permute-start.5 = (bf16[4,64,1024]{2,1,0:T(8,128)(2,1)S(1)}, bf16[4,64,1024]{2,1,0:T(8,128)(2,1)S(1)}, u32[]{:S(2)}, u32[]{:S(2)}) collective-permute-start(bf16[4,64,1024]{2,1,0:T(8,128)(2,1)S(1)} %bitcast.77), channel_id=1, source_target_pairs={{0,16},{16,0},{1,17},{17,1},{2,18},{18,2},{3,19},{19,3},{4,20},{20... | collective-permute-start | bytes 1572872 | tf_op jit(solution)/shard_map/ppermute | solution.py:24
  80.4 8.4 %copy-start.25 = (bf16[256,1024]{1,0:T(8,128)(2,1)S(1)}, bf16[256,1024]{1,0:T(8,128)(2,1)}, u32[]{:S(2)}) copy-start(bf16[256,1024]{1,0:T(8,128)(2,1)} %get-tuple-element.106) | copy-start | bytes 1572868
  88.9 16.2 %copy-start.2 = (bf16[512,1024]{1,0:T(8,128)(2,1)}, bf16[512,1024]{1,0:T(8,128)(2,1)S(1)}, u32[]{:S(2)}) copy-start(bf16[512,1024]{1,0:T(8,128)(2,1)S(1)} %pad_maximum_fusion.2.refs_0_) | copy-start | bytes 3145732
  99.0 3.0 %collective-permute-start.8 = (bf16[256,1024]{1,0:T(8,128)(2,1)S(1)}, bf16[256,1024]{1,0:T(8,128)(2,1)S(1)}, u32[]{:S(2)}, u32[]{:S(2)}) collective-permute-start(bf16[256,1024]{1,0:T(8,128)(2,1)S(1)} %get-tuple-element.103), channel_id=1, source_target_pairs={{0,1},{1,0},{2,3},{3,2},{4,5},{5,4},{6,7},{7,6},{8,9},{9,8},{10,11... | collective-permute-start | bytes 1572872 | tf_op jit(solution)/shard_map/ppermute | solution.py:28
  101.4 16.6 %copy-start.6 = (bf16[4,64,1024]{2,1,0:T(8,128)(2,1)}, bf16[4,64,1024]{2,1,0:T(8,128)(2,1)S(1)}, u32[]{:S(2)}) copy-start(bf16[4,64,1024]{2,1,0:T(8,128)(2,1)S(1)} %collective-permute-done.5.g_ref) | copy-start | bytes 1572868
  101.9 3.3 %copy-start = (bf16[4,1024,1024]{2,1,0:T(8,128)(2,1)}, bf16[4,1024,1024]{2,1,0:T(8,128)(2,1)S(1)}, u32[]{:S(2)}) copy-start(bf16[4,1024,1024]{2,1,0:T(8,128)(2,1)S(1)} %bitcast_dynamic-update-slice_fusion.4.refs_4_) | copy-start | bytes 25165828
  102.0 3.6 %copy-start.4 = (bf16[512,1024]{1,0:T(8,128)(2,1)}, bf16[512,1024]{1,0:T(8,128)(2,1)S(1)}, u32[]{:S(2)}) copy-start(bf16[512,1024]{1,0:T(8,128)(2,1)S(1)} %pad_maximum_fusion.4.refs_2_) | copy-start | bytes 3145732
  105.0 3.8 %copy-start.26 = (s32[8,256]{1,0:T(8,128)S(1)}, s32[8,256]{1,0:T(8,128)}, u32[]{:S(2)}) copy-start(s32[8,256]{1,0:T(8,128)} %param.10) | copy-start | bytes 24580
  105.0 3.8 %collective-permute-start.11 = (f32[256,512]{1,0:T(8,128)S(1)}, f32[256,512]{1,0:T(8,128)S(1)}, u32[]{:S(2)}, u32[]{:S(2)}) collective-permute-start(f32[256,512]{1,0:T(8,128)S(1)} %slice.83), channel_id=1, source_target_pairs={{0,1},{1,0},{2,3},{3,2},{4,5},{5,4},{6,7},{7,6},{8,9},{9,8},{10,11... | collective-permute-start | bytes 1572872 | tf_op jit(solution)/shard_map/ppermute | solution.py:28
  108.6 4.0 %copy-start.19 = (bf16[4,2,256,512]{3,2,1,0:T(8,128)(2,1)S(1)}, bf16[4,2,256,512]{3,2,1,0:T(8,128)(2,1)}, u32[]{:S(2)}) copy-start(bf16[4,2,256,512]{3,2,1,0:T(8,128)(2,1)} %copy-done.18) | copy-start | bytes 6291460
  108.6 2.0 collective-permute-start.12
  108.9 9.2 %collective-permute-start.13 = (bf16[4,64,512]{2,1,0:T(8,128)(2,1)S(1)}, bf16[4,64,512]{2,1,0:T(8,128)(2,1)S(1)}, u32[]{:S(2)}, u32[]{:S(2)}) collective-permute-start(bf16[4,64,512]{2,1,0:T(8,128)(2,1)S(1)} %bitcast.80), channel_id=1, source_target_pairs={{0,16},{16,0},{1,17},{17,1},{2,18},{18,2},{3,19},{19,3},{4,20},{20... | collective-permute-start | bytes 786440 | tf_op jit(solution)/shard_map/ppermute | solution.py:24
  110.7 18.2 %collective-permute-start.16 = (bf16[4,64,512]{2,1,0:T(8,128)(2,1)S(1)}, bf16[4,64,512]{2,1,0:T(8,128)(2,1)}, u32[]{:S(2)}, u32[]{:S(2)}) collective-permute-start(bf16[4,64,512]{2,1,0:T(8,128)(2,1)S(1)} %bitcast.75), channel_id=1, source_target_pairs={{0,16},{16,0},{1,17},{17,1},{2,18},{18,2},{3,19},{19,3},{4,20},{20... | collective-permute-start | bytes 786440 | tf_op jit(solution)/shard_map/ppermute | solution.py:24
  112.6 5.5 %copy-start.13 = (bf16[4,2,256,512]{3,2,1,0:T(8,128)(2,1)S(1)}, bf16[4,2,256,512]{3,2,1,0:T(8,128)(2,1)}, u32[]{:S(2)}) copy-start(bf16[4,2,256,512]{3,2,1,0:T(8,128)(2,1)} %copy-done.12) | copy-start | bytes 6291460
  120.6 15.4 %collective-permute-start.14 = (bf16[4,64,512]{2,1,0:T(8,128)(2,1)}, bf16[4,64,512]{2,1,0:T(8,128)(2,1)}, u32[]{:S(2)}, u32[]{:S(2)}) collective-permute-start(bf16[4,64,512]{2,1,0:T(8,128)(2,1)} %get-tuple-element.67), channel_id=1, source_target_pairs={{0,16},{16,0},{1,17},{17,1},{2,18},{18,2},{3,19},{19,3},{4,20},{20... | collective-permute-start | bytes 786440 | tf_op jit(solution)/shard_map/ppermute | solution.py:24
  128.9 7.1 %copy-start.17 = (bf16[4,64,512]{2,1,0:T(8,128)(2,1)S(1)}, bf16[4,64,512]{2,1,0:T(8,128)(2,1)}, u32[]{:S(2)}) copy-start(bf16[4,64,512]{2,1,0:T(8,128)(2,1)} %copy-done.16) | copy-start | bytes 786436
  128.9 8.2 %copy-start.3 = (bf16[512,1024]{1,0:T(8,128)(2,1)S(1)}, bf16[512,1024]{1,0:T(8,128)(2,1)}, u32[]{:S(2)}) copy-start(bf16[512,1024]{1,0:T(8,128)(2,1)} %copy-done.2) | copy-start | bytes 3145732
  129.0 8.2 %copy-start.5 = (bf16[512,1024]{1,0:T(8,128)(2,1)S(1)}, bf16[512,1024]{1,0:T(8,128)(2,1)}, u32[]{:S(2)}) copy-start(bf16[512,1024]{1,0:T(8,128)(2,1)} %copy-done.4) | copy-start | bytes 3145732
  133.0 8.8 %collective-permute-start.17 = (bf16[4,64,512]{2,1,0:T(8,128)(2,1)S(1)}, bf16[4,64,512]{2,1,0:T(8,128)(2,1)S(1)}, u32[]{:S(2)}, u32[]{:S(2)}) collective-permute-start(bf16[4,64,512]{2,1,0:T(8,128)(2,1)S(1)} %get-tuple-element.73), channel_id=1, source_target_pairs={{0,16},{16,0},{1,17},{17,1},{2,18},{18,2},{3,19},{19,3},{4,20},{20... | collective-permute-start | bytes 786440 | tf_op jit(solution)/shard_map/ppermute | solution.py:24
  137.0 1.6 collective-permute-start.15
  137.7 4.1 %copy-start.20 = (bf16[4,512,1024]{2,1,0:T(8,128)(2,1)}, bf16[4,512,1024]{2,1,0:T(8,128)(2,1)S(1)}, u32[]{:S(2)}) copy-start(bf16[4,512,1024]{2,1,0:T(8,128)(2,1)S(1)} %pad_maximum_fusion) | copy-start | bytes 12582916
  138.6 3.2 %copy-start.27 = (bf16[256,512]{1,0:T(8,128)(2,1)}, bf16[256,512]{1,0:T(8,128)(2,1)S(1)}, u32[]{:S(2)}) copy-start(bf16[256,512]{1,0:T(8,128)(2,1)S(1)} %collective-permute-done.15) | copy-start | bytes 786436
  141.9 1.6 collective-permute-start.18
  142.1 25.5 %collective-permute-start.21 = (bf16[1024,512]{1,0:T(8,128)(2,1)S(1)}, bf16[1024,512]{1,0:T(8,128)(2,1)S(1)}, u32[]{:S(2)}, u32[]{:S(2)}) collective-permute-start(bf16[1024,512]{1,0:T(8,128)(2,1)S(1)} %convolution_convert_fusion.4), channel_id=1, source_target_pairs={{0,2},{1,3},{2,0},{3,1},{4,6},{5,7},{6,4},{7,5},{8,10},{9,11},{10,... | collective-permute-start | bytes 3145736 | tf_op jit(solution)/shard_map/ppermute | solution.py:24
  143.5 3.2 %copy-start.21 = (bf16[4,512,1024]{2,1,0:T(8,128)(2,1)S(1)}, bf16[4,512,1024]{2,1,0:T(8,128)(2,1)}, u32[]{:S(2)}) copy-start(bf16[4,512,1024]{2,1,0:T(8,128)(2,1)} %copy-done.20) | copy-start | bytes 12582916
  146.7 6.5 %copy-start.28 = (bf16[256,512]{1,0:T(8,128)(2,1)S(1)}, bf16[256,512]{1,0:T(8,128)(2,1)}, u32[]{:S(2)}) copy-start(bf16[256,512]{1,0:T(8,128)(2,1)} %copy-done.27) | copy-start | bytes 786436
  147.5 25.3 %collective-permute-start.22 = (bf16[1024,512]{1,0:T(8,128)(2,1)S(1)}, bf16[1024,512]{1,0:T(8,128)(2,1)S(1)}, u32[]{:S(2)}, u32[]{:S(2)}) collective-permute-start(bf16[1024,512]{1,0:T(8,128)(2,1)S(1)} %convolution_convert_fusion.3), channel_id=1, source_target_pairs={{0,16},{16,0},{1,17},{17,1},{2,18},{18,2},{3,19},{19,3},{4,20},{20... | collective-permute-start | bytes 3145736 | tf_op jit(solution)/shard_map/ppermute | solution.py:24
  149.3 23.5 %collective-permute-start.19 = (bf16[256,1024]{1,0:T(8,128)(2,1)S(1)}, bf16[256,1024]{1,0:T(8,128)(2,1)S(1)}, u32[]{:S(2)}, u32[]{:S(2)}) collective-permute-start(bf16[256,1024]{1,0:T(8,128)(2,1)S(1)} %get-tuple-element.99), channel_id=1, source_target_pairs={{0,4},{4,8},{8,12},{12,0},{1,5},{5,9},{9,13},{13,1},{2,6},{6,10},{... | collective-permute-start | bytes 1572872 | tf_op jit(solution)/shard_map/ppermute | solution.py:24
  150.4 24.6 %collective-permute-start.20 = (bf16[256,1024]{1,0:T(8,128)(2,1)S(1)}, bf16[256,1024]{1,0:T(8,128)(2,1)S(1)}, u32[]{:S(2)}, u32[]{:S(2)}) collective-permute-start(bf16[256,1024]{1,0:T(8,128)(2,1)S(1)} %get-tuple-element.98), channel_id=1, source_target_pairs={{0,12},{4,0},{8,4},{12,8},{1,13},{5,1},{9,5},{13,9},{2,14},{6,2},{... | collective-permute-start | bytes 1572872 | tf_op jit(solution)/shard_map/ppermute | solution.py:24
  153.1 2.6 %slice-start = ((s8[8388608]{0:T(1024)(128)(4,1)}), s8[4194304]{0:T(1024)(128)(4,1)S(1)}, s32[]{:S(2)}) async-start(s8[8388608]{0:T(1024)(128)(4,1)} %bitcast.69), calls=%async_computation | async-start | bytes 8388608
  175.7 52.9 %collective-permute-start.27 = (bf16[1024,1024]{1,0:T(8,128)(2,1)S(1)}, bf16[1024,1024]{1,0:T(8,128)(2,1)S(1)}, u32[]{:S(2)}, u32[]{:S(2)}) collective-permute-start(bf16[1024,1024]{1,0:T(8,128)(2,1)S(1)} %fusion.25), channel_id=1, source_target_pairs={{0,2},{1,3},{2,0},{3,1},{4,6},{5,7},{6,4},{7,5},{8,10},{9,11},{10,... | collective-permute-start | bytes 6291464 | tf_op jit(solution)/shard_map/ppermute | solution.py:24
  177.0 51.6 %collective-permute-start.26 = (bf16[1024,1024]{1,0:T(8,128)(2,1)S(1)}, bf16[1024,1024]{1,0:T(8,128)(2,1)S(1)}, u32[]{:S(2)}, u32[]{:S(2)}) collective-permute-start(bf16[1024,1024]{1,0:T(8,128)(2,1)S(1)} %fusion.24), channel_id=1, source_target_pairs={{0,16},{16,0},{1,17},{17,1},{2,18},{18,2},{3,19},{19,3},{4,20},{20... | collective-permute-start | bytes 6291464 | tf_op jit(solution)/shard_map/ppermute | solution.py:24
  177.8 25.7 %collective-permute-start.24 = (bf16[512,1024]{1,0:T(8,128)(2,1)S(1)}, bf16[512,1024]{1,0:T(8,128)(2,1)S(1)}, u32[]{:S(2)}, u32[]{:S(2)}) collective-permute-start(bf16[512,1024]{1,0:T(8,128)(2,1)S(1)} %fusion.37), channel_id=1, source_target_pairs={{0,12},{4,0},{8,4},{12,8},{1,13},{5,1},{9,5},{13,9},{2,14},{6,2},{... | collective-permute-start | bytes 3145736 | tf_op jit(solution)/shard_map/ppermute | solution.py:24
  180.1 44.7 %collective-permute-start.23 = (bf16[512,1024]{1,0:T(8,128)(2,1)S(1)}, bf16[512,1024]{1,0:T(8,128)(2,1)S(1)}, u32[]{:S(2)}, u32[]{:S(2)}) collective-permute-start(bf16[512,1024]{1,0:T(8,128)(2,1)S(1)} %fusion.36), channel_id=1, source_target_pairs={{0,4},{4,8},{8,12},{12,0},{1,5},{5,9},{9,13},{13,1},{2,6},{6,10},{... | collective-permute-start | bytes 3145736 | tf_op jit(solution)/shard_map/ppermute | solution.py:24
  225.1 2.0 collective-permute-start.25
  (11 other events, 17.6 us)

commit v8 on v7

--- a/solution.py
+++ b/solution.py
@@ -105,7 +105,7 @@
 def attend_block(q_ref, g_ref, kv_ref, live_ref, dq_ref, grad_ref):
     pairs = q_ref.shape[-1] // HD // 2
     scale = HD ** (-0.5)
-    live = live_ref[...] > 0.5
+    live = live_ref[...].astype(F32) > 0.5
     zero = jnp.zeros((SPAN, HD), BF16)
 
     def diagonal(ref, start):
@@ -144,52 +144,92 @@
         )
 
 
-def attend_kernel(table_ref, q_ref, g_ref, live_ref, kv_ref, *rest):
-    dq_ref, grad_ref = rest[-2:]
-    named = table_ref[pl.num_programs(0) + pl.program_id(0)]
-
-    @pl.when(named == 0)
-    def _():
-        dq_ref[...] = jnp.zeros_like(dq_ref)
-        grad_ref[...] = jnp.zeros_like(grad_ref)
-
-    @pl.when(named != 0)
-    def _():
-        refs = (q_ref, g_ref, kv_ref, live_ref, dq_ref, grad_ref)
-        attend_block(*(ref.at[0] for ref in refs))
-
-
-def attend(place, named, source, queries, grads, kv, live, part, before):
+def attend_kernel(part, table_ref, q_ref, g_ref, live_ref, kv_ref, *rest):
+    dq_ref, grad_ref, kv_buf, grad_buf, in_sem, out_sem = rest[-6:]
+    count, _, width = q_ref.shape
+    keys = kv_buf.shape[2]
+    columns = pl.ds(part * width, width)
+    pieces = [(i, h) for i in range(2) for h in range(2)]
+
+    def copies(r, back):
+        found = []
+        for n, (i, h) in enumerate(pieces):
+            some = pl.ds(h * (keys // 2), keys // 2)
+            if back:
+                far = grad_ref.at[table_ref[r], i, some, columns]
+                copy = pltpu.make_async_copy(grad_buf.at[r, i, some], far, out_sem.at[r, n])
+            else:
+                far = kv_ref.at[table_ref[r], i, some, columns]
+                copy = pltpu.make_async_copy(far, kv_buf.at[r, i, some], in_sem.at[r, n])
+            found.append(copy)
+        return found
+
+    @pl.loop(0, count)
+    def _(r):
+        @pl.when(table_ref[count + r] != 0)
+        def _():
+            for copy in copies(r, False):
+                copy.start()
+
+    @pl.loop(0, count)
+    def _(r):
+        @pl.when(table_ref[count + r] == 0)
+        def _():
+            dq_ref[r] = jnp.zeros(dq_ref.shape[1:], BF16)
+            grad_buf[r] = jnp.zeros(grad_buf.shape[1:], BF16)
+
+        @pl.when(table_ref[count + r] != 0)
+        def _():
+            for copy in copies(r, False):
+                copy.wait()
+            attend_block(
+                q_ref.at[r],
+                g_ref.at[r, :, columns],
+                kv_buf.at[r],
+                live_ref.at[table_ref[r]],
+                dq_ref.at[r],
+                grad_buf.at[r],
+            )
+
+        for copy in copies(r, True):
+            copy.start()
+
+    @pl.loop(0, count)
+    def _(r):
+        for copy in copies(r, True):
+            copy.wait()
+
+
+def attend(slots, named, queries, grads, kv, live, part, before):
     count, _, width = queries.shape
-    capacity, keys, _ = live.shape
+    keys = kv.shape[2]
     heads = width // HD
-    table = jnp.concatenate([place, named, source * count + place]).astype(jnp.int32)
-    span_block = pl.BlockSpec((1, SPAN, width), lambda r, t: (r, 0, 0))
-    part_block = pl.BlockSpec((1, SPAN, width), lambda r, t: (r, 0, part))
-    live_block = pl.BlockSpec((1, keys, HD), lambda r, t: (t[2 * count + r], 0, 0))
-    kv_block = pl.BlockSpec((1, 2, keys, width), lambda r, t: (t[r], 0, 0, 0))
-    grad_block = pl.BlockSpec((1, 2, keys, width), lambda r, t: (t[2 * count + r], 0, 0, part))
-    in_specs = [span_block, part_block, live_block, kv_block]
+    table = jnp.concatenate([slots, named]).astype(jnp.int32)
+    inside = pl.BlockSpec(memory_space=pltpu.VMEM)
+    outside = pl.BlockSpec(memory_space=pl.ANY)
+    in_specs = [pl.BlockSpec(memory_space=pltpu.SMEM), inside, inside, inside, outside]
     operands = [table, queries, grads, live, kv]
     aliases = {}
     if before is not None:
-        in_specs.append(pl.BlockSpec(memory_space=pl.ANY))
+        in_specs.append(outside)
         operands.append(before)
         aliases = {len(operands) - 1: 1}
     return pl.pallas_call(
-        attend_kernel,
-        grid_spec=pltpu.PrefetchScalarGridSpec(
-            num_scalar_prefetch=1,
-            grid=(count,),
-            in_specs=in_specs,
-            out_specs=[span_block, grad_block],
-        ),
+        functools.partial(attend_kernel, part),
+        in_specs=in_specs,
+        out_specs=[inside, outside],
         out_shape=[
             jax.ShapeDtypeStruct(queries.shape, BF16),
-            jax.ShapeDtypeStruct((capacity, 2, keys, 2 * width), BF16),
+            jax.ShapeDtypeStruct(kv.shape, BF16),
+        ],
+        scratch_shapes=[
+            pltpu.VMEM((count, 2, keys, width), BF16),
+            pltpu.VMEM((count, 2, keys, width), BF16),
+            pltpu.SemaphoreType.DMA((count, 4)),
+            pltpu.SemaphoreType.DMA((count, 4)),
         ],
         input_output_aliases=aliases,
-        compiler_params=pltpu.CompilerParams(vmem_limit_bytes=12 * 1024 * 1024),
+        compiler_params=pltpu.CompilerParams(vmem_limit_bytes=54 * 1024 * 1024),
         cost_estimate=pl.CostEstimate(
             flops=count * heads * 5 * 2 * SPAN * keys * HD * 4,
             bytes_accessed=count * 4 * keys * width * 2,
@@ -198,48 +238,30 @@
     )(*operands)
 
 
-def stage_kernel(source_ref, kv_ref, left_ref, right_ref):
-    width = left_ref.shape[-1]
-    left_ref[...] = kv_ref[:, :, :, :width]
-    right_ref[...] = kv_ref[:, :, :, width:]
-
-
-def stage(kv, source, count):
-    _, _, keys, width = kv.shape
-    half_block = pl.BlockSpec((1, 2, keys, width // 2), lambda r, t: (r, 0, 0, 0))
-    half_shape = jax.ShapeDtypeStruct((count, 2, keys, width // 2), kv.dtype)
-    return pl.pallas_call(
-        stage_kernel,
-        grid_spec=pltpu.PrefetchScalarGridSpec(
-            num_scalar_prefetch=1,
-            grid=(count,),
-            in_specs=[
-                pl.BlockSpec((1, 2, keys, width), lambda r, t: (t[0] * count + r, 0, 0, 0))
-            ],
-            out_specs=[half_block, half_block],
-        ),
-        out_shape=[half_shape, half_shape],
-        compiler_params=pltpu.CompilerParams(vmem_limit_bytes=12 * 1024 * 1024),
-        cost_estimate=pl.CostEstimate(
-            flops=0, bytes_accessed=8 * count * keys * width, transcendentals=0
-        ),
-    )(jnp.reshape(source, (1,)).astype(jnp.int32), kv)
-
-
-def total_kernel(*refs):
-    refs[-1][...] = total([ref[...] for ref in refs[:-1]])
+def total_kernel(tile, *refs):
+    out_ref, buf, sem = refs[-3:]
+    copies = []
+    for n in range(sem.shape[0]):
+        some = pl.ds(n * tile, tile)
+        buf[some] = total([ref[some] for ref in refs[:-3]])
+        copies.append(pltpu.make_async_copy(buf.at[some], out_ref.at[some], sem.at[n]))
+        copies[-1].start()
+    for copy in copies:
+        copy.wait()
 
 
 def summed(values):
     rows, columns = values[0].shape
-    tile = min(128, rows)
-    block = pl.BlockSpec((tile, columns), lambda r: (r, 0))
+    tile = min(64, rows)
     return pl.pallas_call(
-        total_kernel,
-        grid=(rows // tile,),
-        in_specs=[block] * len(values),
-        out_specs=block,
+        functools.partial(total_kernel, tile),
+        in_specs=[pl.BlockSpec(memory_space=pltpu.VMEM)] * len(values),
+        out_specs=pl.BlockSpec(memory_space=pl.ANY),
         out_shape=jax.ShapeDtypeStruct((rows, columns), F32),
+        scratch_shapes=[
+            pltpu.VMEM((rows, columns), F32),
+            pltpu.SemaphoreType.DMA((rows // tile,)),
+        ],
         compiler_params=pltpu.CompilerParams(vmem_limit_bytes=16 * 1024 * 1024),
         cost_estimate=pl.CostEstimate(
             flops=len(values) * rows * columns,
@@ -326,15 +348,15 @@
         return shift(value, "seq", step) if step else value
 
     cut = width * 5 // 8 // HD * HD
-    sources = [(seq_at - step) % seq_count for step in range(seq_count)]
-    staged = [stage(neighbour_kv, source, pairs) for source in sources]
+    up_from, down_from = raw[opposite - 1][:rows // 2], raw[opposite + 1][rows // 2:]
     left_from = [block[:, :cut] for block in along_seq[1:]]
     right_from = [block[:, cut:] for block in along_dp[1:]]
-    left_from, right_from, staged, grad_out = lax.optimization_barrier(
-        (left_from, right_from, staged, out_grad)
-    )
+    left_from, right_from, up_from = lax.optimization_barrier((left_from, right_from, up_from))
     corner_left = [gather_ring(block, "dp", couples) for block in left_from]
     corner_right = [gather_ring(block, "seq", seq_count) for block in right_from]
+    up = shift(up_from, "tensor", 1)
+    down_from = after(down_from, left_from, right_from)
+
     def columns_of(block, which):
         return jnp.concatenate(
             [
@@ -345,13 +367,13 @@
         )
 
     near = [k for k in range(tensor_count) if k != opposite]
-    others = swap(jnp.concatenate([columns_of(raw[k], 1 - core) for k in near], axis=0))
-    up_from, down_from = raw[opposite - 1][:rows // 2], raw[opposite + 1][rows // 2:]
-    up_from, down_from = lax.optimization_barrier((up_from, down_from, left_from, right_from))[:2]
-    up = shift(up_from, "tensor", 1)
-    down_from, grad_out, others = lax.optimization_barrier((down_from, grad_out, others))
+    others = [raw[k] for k in near]
+    others = after(others, down_from)
+    others = swap(jnp.concatenate([columns_of(block, 1 - core) for block in others], axis=0))
+    grad_out = after(out_grad, left_from, right_from)
+    grads = [to_owner(grad_out, step) for step in range(seq_count)]
+    down_from, grads, others = lax.optimization_barrier((down_from, grads, others))
     down = shift(down_from, "tensor", -1)
-    grads = [to_owner(grad_out, step) for step in range(seq_count)]
     raw[opposite] = jnp.concatenate([up, down], axis=0)
     others = {k: others[n * rows:(n + 1) * rows] for n, k in enumerate(near)}
     others[opposite] = swap(columns_of(raw[opposite], 1 - core))
@@ -359,7 +381,7 @@
         jnp.concatenate([columns_of(raw[k], core), others[k]], axis=0) for k in range(tensor_count)
     ]
     depth_blocks = [(tensor_at - k) % tensor_count for k in range(tensor_count)]
-    table = after(jnp.stack(depth_blocks).astype(jnp.int32), grads)
+    table = jnp.stack(depth_blocks).astype(jnp.int32)
 
     def block_at(i, j):
         block = ((seq_at - i) % seq_count) * dp_count + ((dp_at // 2 - j) % couples) * 2
@@ -388,14 +410,14 @@
         return value.reshape(rows, -1)
 
     def slots_of(step):
-        group = lax.dynamic_index_in_dim(groups, sources[step], 0, keepdims=False)
+        group = lax.dynamic_index_in_dim(groups, (seq_at - step) % seq_count, 0, keepdims=False)
         place, names = order(group, seq_at)
         if not whole_blocks:
             place = jnp.arange(pairs)
             names = (place < jnp.sum(names)).astype(jnp.int32)
-        return place, names, sources[step]
-
-    live = jnp.broadcast_to((neighbour_ids != 0).astype(F32)[:, :, None], (capacity, KEYS, HD))
+        return (seq_at - step) % seq_count * pairs + place, names
+
+    live = jnp.broadcast_to((neighbour_ids != 0).astype(BF16)[:, :, None], (capacity, KEYS, HD))
     slots = [slots_of(step) for step in range(seq_count)]
 
     queries = []
@@ -427,7 +449,7 @@
                 *slots[step],
                 asked[part][step],
                 grads[step],
-                staged[step][part],
+                neighbour_kv,
                 live,
                 part,
                 kv_grad,

time: 233 us -> 253 us (1.086)
  waiting for transfers between devices: 125 us -> 137 us
  starting transfers between devices: 35.6 us -> 41 us
    ppermute x21, waiting for transfers between devices: 122 us -> 134 us  [shift(): lax.ppermute(value, axis, [(i, (i + step * stride) % size) for i in range...]
    unnamed x63 -> x49, local copies, waits for them, and re-layouts: 14.4 us -> 4.31 us
    dynamic_update_slice x5, local copies, waits for them, and re-layouts: 2.88 us -> 8.49 us  [on_device(): lax.dynamic_update_slice(weights, piece[None], (at, inner * depth, start))]
    ppermute x21, starting transfers between devices: 35.2 us -> 40.1 us  [shift(): lax.ppermute(value, axis, [(i, (i + step * stride) % size) for i in range...]
    pallas_call x7 -> x5, Pallas kernels: 15.9 us -> 17 us  [the longest x4 14.8 us: attend(): pl.pallas_call(functools.partial(attend_kernel, part), in_specs=in_specs,...]
  transfers between devices with their start and end apart: 28 -> 28, of which waited for: 17 -> 17; matrix products, arithmetic and copies ran while one was open for 14% -> 15% of each run, Pallas kernels for 7% -> 8%
where the time goes in v8:
time: 253 us; the launch traced here: 252 us
  waiting for transfers between devices  137 us (54%)
  starting transfers between devices  41 us (16%)
  local copies, waits for them, and re-layouts  26.8 us (11%)
  Pallas kernels  24.4 us (10%)
  matrix products  14.2 us (6%)
  other arithmetic  6.98 us (3%)
    ppermute x21, waiting for transfers between devices, shift(): lax.ppermute(value, axis, [(i, (i + step * stride) % size) for i in range...  134 us
    ppermute x21, starting transfers between devices, shift(): lax.ppermute(value, axis, [(i, (i + step * stride) % size) for i in range...  40.1 us
    pallas_call x4, Pallas kernels, attend(): pl.pallas_call(functools.partial(attend_kernel, part), in_specs=in_specs,...  14.8 us
    dot_general x9, matrix products, dot(): lax.dot_general(a, b, (contract, ((), ())), preferred_element_type=F32)  14.2 us
    dynamic_update_slice x5, local copies, waits for them, and re-layouts, on_device(): lax.dynamic_update_slice(weights, piece[None], (at, inner * depth, start))  8.49 us
    pallas_call x2, Pallas kernels, product(): pl.pallas_call(functools.partial(product_kernel, count, start), out_shape...  5.81 us
  transfers between devices with their start and end apart: 28, of which 17 were waited for; matrix products, arithmetic and copies ran while one was open for 15% of the time, Pallas kernels for 8%

profile of v8, /device:TPU:0, one launch (start us, length us, event | category | flops | bytes accessed | tf_op | source)
XLA Modules:
  0.0 252.4 jit_solution(18005014875225388696)
XLA Ops:
  0.6 3.0 %collective-permute-start.2 = (bf16[1024,1024]{1,0:T(8,128)(2,1)}, bf16[1024,1024]{1,0:T(8,128)(2,1)S(1)}, u32[]{:S(2)}, u32[]{:S(2)}) collective-permute-start(bf16[1024,1024]{1,0:T(8,128)(2,1)} %param.7), channel_id=1, source_target_pairs={{0,16},{16,0},{1,17},{17,1},{2,18},{18,2},{3,19},{19,3},{4,20},{20... | collective-permute-start | bytes 6291464 | tf_op jit(solution)/shard_map/ppermute | solution.py:24
  3.6 1.5 collective-permute-start.3
  5.2 1.6 collective-permute-start
  6.7 2.2 collective-permute-start.1
  11.9 21.4 %collective-permute-done = bf16[256,2048]{1,0:T(8,128)(2,1)S(1)} collective-permute-done((bf16[256,2048]{1,0:T(8,128)(2,1)}, bf16[256,2048]{1,0:T(8,128)(2,1)S(1)}, u32[]{:S(2)}, u32[]{:S(2)}) %collective-permute-start) | collective-permute-done | bytes 1048608 | tf_op jit(solution)/shard_map/ppermute | solution.py:24
  33.3 20.3 %collective-permute-done.1 = bf16[256,2048]{1,0:T(8,128)(2,1)} collective-permute-done((bf16[256,2048]{1,0:T(8,128)(2,1)}, bf16[256,2048]{1,0:T(8,128)(2,1)}, u32[]{:S(2)}, u32[]{:S(2)}) %collective-permute-start.1) | collective-permute-done | bytes 1048608 | tf_op jit(solution)/shard_map/ppermute | solution.py:24
  54.4 1.9 slice.60
  57.5 2.1 slice.81
  66.1 1.5 collective-permute-start.4
  68.8 3.1 %bitcast_dynamic-update-slice_fusion.1 = bf16[4,1024,1024]{2,1,0:T(8,128)(2,1)} fusion(bf16[4,1024,1024]{2,1,0:T(8,128)(2,1)} %copy-done, s32[]{:T(128)S(6)} %select_n.245, bf16[1024,1024]{1,0:T(8,128)(2,1)} %collective-permute-done.3), kind=kLoop, calls=%fused_computation.10 | loop fusion | bytes 4194308 | tf_op jit(solution)/shard_map/dynamic_update_slice | solution.py:401
  71.9 1.5 bitcast_dynamic-update-slice_fusion
  73.4 9.5 %collective-permute-done.6 = bf16[128,2048]{1,0:T(8,128)(2,1)S(1)} collective-permute-done((bf16[128,2048]{1,0:T(8,128)(2,1)S(1)}, bf16[128,2048]{1,0:T(8,128)(2,1)S(1)}, u32[]{:S(2)}, u32[]{:S(2)}) %collective-permute-start.6) | collective-permute-done | bytes 524320 | tf_op jit(solution)/shard_map/ppermute | solution.py:24
  83.0 3.0 %collective-permute-done.10 = bf16[1024,384]{1,0:T(8,128)(2,1)S(1)} collective-permute-done((bf16[1024,384]{1,0:T(8,128)(2,1)S(1)}, bf16[1024,384]{1,0:T(8,128)(2,1)S(1)}, u32[]{:S(2)}, u32[]{:S(2)}) %collective-permute-start.10) | collective-permute-done | bytes 786464 | tf_op jit(solution)/shard_map/ppermute | solution.py:24
  86.0 9.1 %collective-permute-done.9 = bf16[1024,640]{1,0:T(8,128)(2,1)} collective-permute-done((bf16[1024,640]{1,0:T(8,128)(2,1)}, bf16[1024,640]{1,0:T(8,128)(2,1)}, u32[]{:S(2)}, u32[]{:S(2)}) %collective-permute-start.9) | collective-permute-done | bytes 1310752 | tf_op jit(solution)/shard_map/ppermute | solution.py:24
  95.1 1.4 collective-permute-done.4.g_ref
  96.5 2.5 collective-permute-start.7
  99.0 2.5 %bitcast_dynamic-update-slice_fusion.3 = bf16[4,1024,1024]{2,1,0:T(8,128)(2,1)} fusion(bf16[4,1024,1024]{2,1,0:T(8,128)(2,1)} %bitcast_dynamic-update-slice_fusion, s32[]{:T(128)S(6)} %select_n.250, bf16[1024,640]{1,0:T(8,128)(2,1)} %collective-permute-done.9), kind=kLoop, calls=%fused_computation.28 | loop fusion | bytes 2621444 | tf_op jit(solution)/shard_map/dynamic_update_slice | solution.py:401
  102.5 7.4 %collective-permute-done.7 = bf16[128,2048]{1,0:T(8,128)(2,1)S(1)} collective-permute-done((bf16[128,2048]{1,0:T(8,128)(2,1)S(1)}, bf16[128,2048]{1,0:T(8,128)(2,1)S(1)}, u32[]{:S(2)}, u32[]{:S(2)}) %collective-permute-start.7) | collective-permute-done | bytes 524320 | tf_op jit(solution)/shard_map/ppermute | solution.py:24
  110.2 1.5 fusion.59
  112.2 3.0 %copy-done.1 = bf16[4,1024,1024]{2,1,0:T(8,128)(2,1)S(1)} copy-done((bf16[4,1024,1024]{2,1,0:T(8,128)(2,1)S(1)}, bf16[4,1024,1024]{2,1,0:T(8,128)(2,1)}, u32[]{:S(2)}) %copy-start.1) | copy-done | bytes 8388632
  115.1 2.9 %shard_map.85 = f32[512,512]{1,0:T(8,128)S(1)} custom-call(s32[4]{0:T(128)S(1)} %pad_add_fusion.1.table_ref, bf16[512,1024]{1,0:T(8,128)(2,1)S(1)} %pad_maximum_fusion.2.refs_0_, bf16[512,1024]{1,0:T(8,128)(2,1)S(1)} %pad_maximum_fusion.3.refs_1_, bf16[512,1024]{1,0:T(8,128)(2,1)S(1)} %pad_maximum_fusion.4.refs_2_, ...), custom_call_target="tpu_custom_call" | custom-call | flops 2147483648 | bytes 9437184 | tf_op jit(solution)/shard_map/pallas_call | solution.py:90
  118.6 2.9 %shard_map.86 = f32[512,512]{1,0:T(8,128)S(1)} custom-call(s32[4]{0:T(128)S(1)} %pad_add_fusion.1.table_ref, bf16[512,1024]{1,0:T(8,128)(2,1)S(1)} %pad_maximum_fusion.2.refs_0_, bf16[512,1024]{1,0:T(8,128)(2,1)S(1)} %pad_maximum_fusion.3.refs_1_, bf16[512,1024]{1,0:T(8,128)(2,1)S(1)} %pad_maximum_fusion.4.refs_2_, ...), custom_call_target="tpu_custom_call" | custom-call | flops 2147483648 | bytes 9437184 | tf_op jit(solution)/shard_map/pallas_call | solution.py:90
  125.9 3.7 %shard_map.87 = (bf16[4,64,512]{2,1,0:T(8,128)(2,1)}, bf16[8,2,256,1024]{3,2,1,0:T(8,128)(2,1)}) custom-call(s32[8]{0:T(128)} %pad_add_fusion.table_ref, bf16[4,64,512]{2,1,0:T(8,128)(2,1)} %bitcast.77, bf16[4,64,1024]{2,1,0:T(8,128)(2,1)} %bitcast.73, bf16[8,256,128]{2,1,0:T(8,128)(2,1)} %broadcast_in_dim.20.live_ref, bf16[8,2,256,1024]{3,2,1,0:T(8,128)(2,1)} %kv_ref.7), custom_call_target="tpu_custom_call" | custom-call | flops 1342177280 | bytes 4194304 | tf_op jit(solution)/shard_map/pallas_call | solution.py:217
  129.6 2.1 collective-permute-done.13.q_ref
  132.3 3.7 %shard_map.88 = (bf16[4,64,512]{2,1,0:T(8,128)(2,1)}, bf16[8,2,256,1024]{3,2,1,0:T(8,128)(2,1)}) custom-call(s32[8]{0:T(128)} %pad_add_fusion.2.table_ref, bf16[4,64,512]{2,1,0:T(8,128)(2,1)} %copy-done.18, bf16[4,64,1024]{2,1,0:T(8,128)(2,1)} %copy-done.9, bf16[8,256,128]{2,1,0:T(8,128)(2,1)} %broadcast_in_dim.20.live_ref, ...), custom_call_target="tpu_custom_call", output_to_operand_aliasing={{1}: (5, {})} | custom-call | flops 1342177280 | bytes 4194304 | tf_op jit(solution)/shard_map/pallas_call | solution.py:217
  136.0 5.3 %collective-permute-start.14 = (bf16[4,64,512]{2,1,0:T(8,128)(2,1)}, bf16[4,64,512]{2,1,0:T(8,128)(2,1)}, u32[]{:S(2)}, u32[]{:S(2)}) collective-permute-start(bf16[4,64,512]{2,1,0:T(8,128)(2,1)} %get-tuple-element.59), channel_id=1, source_target_pairs={{0,16},{16,0},{1,17},{17,1},{2,18},{18,2},{3,19},{19,3},{4,20},{20... | collective-permute-start | bytes 786440 | tf_op jit(solution)/shard_map/ppermute | solution.py:24
  141.4 3.7 %shard_map.89 = (bf16[4,64,512]{2,1,0:T(8,128)(2,1)}, bf16[8,2,256,1024]{3,2,1,0:T(8,128)(2,1)}) custom-call(s32[8]{0:T(128)} %pad_add_fusion.table_ref, bf16[4,64,512]{2,1,0:T(8,128)(2,1)} %bitcast.79, bf16[4,64,1024]{2,1,0:T(8,128)(2,1)} %bitcast.74, bf16[8,256,128]{2,1,0:T(8,128)(2,1)} %broadcast_in_dim.20.live_ref, ...), custom_call_target="tpu_custom_call", output_to_operand_aliasing={{1}: (5, {})} | custom-call | flops 1342177280 | bytes 4194304 | tf_op jit(solution)/shard_map/pallas_call | solution.py:217
  145.1 3.8 %shard_map.90 = (bf16[4,64,512]{2,1,0:T(8,128)(2,1)}, bf16[8,2,256,1024]{3,2,1,0:T(8,128)(2,1)}) custom-call(s32[8]{0:T(128)} %pad_add_fusion.2.table_ref, bf16[4,64,512]{2,1,0:T(8,128)(2,1)} %collective-permute-done.16.q_ref, bf16[4,64,1024]{2,1,0:T(8,128)(2,1)} %copy-done.9, ...), custom_call_target="tpu_custom_call", output_to_operand_aliasing={{1}: (5, {})} | custom-call | flops 1342177280 | bytes 4194304 | tf_op jit(solution)/shard_map/pallas_call | solution.py:217
  148.9 6.4 %collective-permute-start.17 = (bf16[4,64,512]{2,1,0:T(8,128)(2,1)}, bf16[4,64,512]{2,1,0:T(8,128)(2,1)S(1)}, u32[]{:S(2)}, u32[]{:S(2)}) collective-permute-start(bf16[4,64,512]{2,1,0:T(8,128)(2,1)} %get-tuple-element.63), channel_id=1, source_target_pairs={{0,16},{16,0},{1,17},{17,1},{2,18},{18,2},{3,19},{19,3},{4,20},{20... | collective-permute-start | bytes 786440 | tf_op jit(solution)/shard_map/ppermute | solution.py:24
  158.7 3.9 %collective-permute-done.17 = bf16[4,64,512]{2,1,0:T(8,128)(2,1)S(1)} collective-permute-done((bf16[4,64,512]{2,1,0:T(8,128)(2,1)}, bf16[4,64,512]{2,1,0:T(8,128)(2,1)S(1)}, u32[]{:S(2)}, u32[]{:S(2)}) %collective-permute-start.17) | collective-permute-done | bytes 262176 | tf_op jit(solution)/shard_map/ppermute | solution.py:24
  162.8 1.6 collective-permute-start.21
  164.4 3.1 %fusion.12 = bf16[512,1024]{1,0:T(8,128)(2,1)S(1)} fusion(bf16[4,1024,1024]{2,1,0:T(8,128)(2,1)} %bitcast_dynamic-update-slice_fusion.4.refs_4_, s32[]{:T(128)S(6)} %select_n.255, bf16[256,512]{1,0:T(8,128)(2,1)S(1)} %collective-permute-done.18, bf16[256,512]{1,0:T(8,128)(2,1)S(1)} %bitcast_add_fusion, bf16[256,512]{1,0:T(8,128)(2,1)} %copy-done.20, ...), kind=kOutput, calls=%fused_computation.22 | convolution fusion | flops 1078460416 | bytes 4194308 | tf_op jit(solution)/shard_map/dot_general | solution.py:18
  168.8 3.2 %collective-permute-start.20 = (bf16[256,1024]{1,0:T(8,128)(2,1)S(1)}, bf16[256,1024]{1,0:T(8,128)(2,1)S(1)}, u32[]{:S(2)}, u32[]{:S(2)}) collective-permute-start(bf16[256,1024]{1,0:T(8,128)(2,1)S(1)} %get-tuple-element.88), channel_id=1, source_target_pairs={{0,12},{4,0},{8,4},{12,8},{1,13},{5,1},{9,5},{13,9},{2,14},{6,2},{... | collective-permute-start | bytes 1572872 | tf_op jit(solution)/shard_map/ppermute | solution.py:24
  173.2 3.0 %fusion.15.own_ref = bf16[512,1024]{1,0:T(8,128)(2,1)S(1)} fusion(bf16[4,1024,1024]{2,1,0:T(8,128)(2,1)} %bitcast_dynamic-update-slice_fusion.4.refs_4_, s32[]{:T(128)S(6)} %select_n.256, bf16[256,512]{1,0:T(8,128)(2,1)S(1)} %collective-permute-done.18, bf16[256,512]{1,0:T(8,128)(2,1)S(1)} %bitcast_add_fusion, bf16[256,512]{1,0:T(8,128)(2,1)S(1)} %copy-done.21, ...), kind=kOutput, calls=%fused_computation.23 | convolution fusion | flops 1078460416 | bytes 4194308 | tf_op jit(solution)/shard_map/dot_general | solution.py:18
  176.2 1.3 fusion.18
  177.6 1.3 fusion.21
  178.9 1.3 convolution_convert_fusion.2.refs_0_
  180.2 1.3 convolution_convert_fusion.1
  181.5 1.3 convolution_convert_fusion
  182.9 5.4 %collective-permute-done.21 = bf16[1024,512]{1,0:T(8,128)(2,1)S(1)} collective-permute-done((bf16[1024,512]{1,0:T(8,128)(2,1)S(1)}, bf16[1024,512]{1,0:T(8,128)(2,1)S(1)}, u32[]{:S(2)}, u32[]{:S(2)}) %collective-permute-start.21) | collective-permute-done | bytes 1048608 | tf_op jit(solution)/shard_map/ppermute | solution.py:24
  188.3 9.4 %collective-permute-done.22 = bf16[1024,512]{1,0:T(8,128)(2,1)S(1)} collective-permute-done((bf16[1024,512]{1,0:T(8,128)(2,1)S(1)}, bf16[1024,512]{1,0:T(8,128)(2,1)S(1)}, u32[]{:S(2)}, u32[]{:S(2)}) %collective-permute-start.22) | collective-permute-done | bytes 1048608 | tf_op jit(solution)/shard_map/ppermute | solution.py:24
  199.6 1.5 collective-permute-start.27
  201.4 3.9 %collective-permute-start.24 = (bf16[512,1024]{1,0:T(8,128)(2,1)S(1)}, bf16[512,1024]{1,0:T(8,128)(2,1)S(1)}, u32[]{:S(2)}, u32[]{:S(2)}) collective-permute-start(bf16[512,1024]{1,0:T(8,128)(2,1)S(1)} %fusion.37), channel_id=1, source_target_pairs={{0,12},{4,0},{8,4},{12,8},{1,13},{5,1},{9,5},{13,9},{2,14},{6,2},{... | collective-permute-start | bytes 3145736 | tf_op jit(solution)/shard_map/ppermute | solution.py:24
  205.2 20.7 %collective-permute-done.23.up_ref = bf16[512,1024]{1,0:T(8,128)(2,1)S(1)} collective-permute-done((bf16[512,1024]{1,0:T(8,128)(2,1)S(1)}, bf16[512,1024]{1,0:T(8,128)(2,1)S(1)}, u32[]{:S(2)}, u32[]{:S(2)}) %collective-permute-start.23) | collective-permute-done | bytes 1048608 | tf_op jit(solution)/shard_map/ppermute | solution.py:24
  225.9 20.3 %collective-permute-done.24.down_ref = bf16[512,1024]{1,0:T(8,128)(2,1)S(1)} collective-permute-done((bf16[512,1024]{1,0:T(8,128)(2,1)S(1)}, bf16[512,1024]{1,0:T(8,128)(2,1)S(1)}, u32[]{:S(2)}, u32[]{:S(2)}) %collective-permute-start.24) | collective-permute-done | bytes 1048608 | tf_op jit(solution)/shard_map/ppermute | solution.py:24
  246.5 1.9 collective-permute-done.25.arrived_ref
  248.4 1.6 shard_map.91
  250.1 2.2 shard_map.92
  (123 shorter events, 28.0 us)
Async XLA Ops:
  0.6 55.7 %collective-permute-start.2 = (bf16[1024,1024]{1,0:T(8,128)(2,1)}, bf16[1024,1024]{1,0:T(8,128)(2,1)S(1)}, u32[]{:S(2)}, u32[]{:S(2)}) collective-permute-start(bf16[1024,1024]{1,0:T(8,128)(2,1)} %param.7), channel_id=1, source_target_pairs={{0,16},{16,0},{1,17},{17,1},{2,18},{18,2},{3,19},{19,3},{4,20},{20... | collective-permute-start | bytes 6291464 | tf_op jit(solution)/shard_map/ppermute | solution.py:24
  3.6 53.9 %collective-permute-start.3 = (bf16[1024,1024]{1,0:T(8,128)(2,1)}, bf16[1024,1024]{1,0:T(8,128)(2,1)}, u32[]{:S(2)}, u32[]{:S(2)}) collective-permute-start(bf16[1024,1024]{1,0:T(8,128)(2,1)} %param.7), channel_id=1, source_target_pairs={{0,2},{1,3},{2,0},{3,1},{4,6},{5,7},{6,4},{7,5},{8,10},{9,11},{10,... | collective-permute-start | bytes 6291464 | tf_op jit(solution)/shard_map/ppermute | solution.py:24
  5.2 28.2 %collective-permute-start = (bf16[256,2048]{1,0:T(8,128)(2,1)}, bf16[256,2048]{1,0:T(8,128)(2,1)S(1)}, u32[]{:S(2)}, u32[]{:S(2)}) collective-permute-start(bf16[256,2048]{1,0:T(8,128)(2,1)} %param.6), channel_id=1, source_target_pairs={{0,4},{4,8},{8,12},{12,0},{1,5},{5,9},{9,13},{13,1},{2,6},{6,10},{... | collective-permute-start | bytes 3145736 | tf_op jit(solution)/shard_map/ppermute | solution.py:24
  6.7 46.8 %collective-permute-start.1 = (bf16[256,2048]{1,0:T(8,128)(2,1)}, bf16[256,2048]{1,0:T(8,128)(2,1)}, u32[]{:S(2)}, u32[]{:S(2)}) collective-permute-start(bf16[256,2048]{1,0:T(8,128)(2,1)} %param.6), channel_id=1, source_target_pairs={{0,12},{4,0},{8,4},{12,8},{1,13},{5,1},{9,5},{13,9},{2,14},{6,2},{... | collective-permute-start | bytes 3145736 | tf_op jit(solution)/shard_map/ppermute | solution.py:24
  11.9 50.2 %copy-start = (bf16[4,1024,1024]{2,1,0:T(8,128)(2,1)}, bf16[4,1024,1024]{2,1,0:T(8,128)(2,1)S(1)}, u32[]{:S(2)}) copy-start(bf16[4,1024,1024]{2,1,0:T(8,128)(2,1)S(1)} %bitcast_dynamic-update-slice_fusion.2) | copy-start | bytes 25165828
  56.3 3.3 %copy-start.11 = (bf16[256,2048]{1,0:T(8,128)(2,1)S(1)}, bf16[256,2048]{1,0:T(8,128)(2,1)}, u32[]{:S(2)}) copy-start(bf16[256,2048]{1,0:T(8,128)(2,1)} %param.6) | copy-start | bytes 3145732
  62.1 34.4 %collective-permute-start.5 = (bf16[768,1024]{1,0:T(8,128)(2,1)}, bf16[768,1024]{1,0:T(8,128)(2,1)}, u32[]{:S(2)}, u32[]{:S(2)}) collective-permute-start(bf16[768,1024]{1,0:T(8,128)(2,1)} %pad_maximum_fusion.1), channel_id=1, source_target_pairs={{0,1},{1,0},{2,3},{3,2},{4,5},{5,4},{6,7},{7,6},{8,9},{9,8},{10,11... | collective-permute-start | bytes 4718600 | tf_op jit(solution)/shard_map/ppermute | solution.py:28
  63.6 31.5 %collective-permute-start.9 = (bf16[1024,640]{1,0:T(8,128)(2,1)}, bf16[1024,640]{1,0:T(8,128)(2,1)}, u32[]{:S(2)}, u32[]{:S(2)}) collective-permute-start(bf16[1024,640]{1,0:T(8,128)(2,1)} %slice.80), channel_id=1, source_target_pairs={{0,2},{1,3},{2,0},{3,1},{4,6},{5,7},{6,4},{7,5},{8,10},{9,11},{10,... | collective-permute-start | bytes 3932168 | tf_op jit(solution)/shard_map/ppermute | solution.py:24
  64.2 1.9 copy-start.8
  64.2 3.4 %copy-start.15 = (bf16[128,2048]{1,0:T(8,128)(2,1)S(1)}, bf16[128,2048]{1,0:T(8,128)(2,1)}, u32[]{:S(2)}) copy-start(bf16[128,2048]{1,0:T(8,128)(2,1)} %slice.63) | copy-start | bytes 1572868
  65.5 20.4 %collective-permute-start.10 = (bf16[1024,384]{1,0:T(8,128)(2,1)S(1)}, bf16[1024,384]{1,0:T(8,128)(2,1)S(1)}, u32[]{:S(2)}, u32[]{:S(2)}) collective-permute-start(bf16[1024,384]{1,0:T(8,128)(2,1)S(1)} %copy-done.13), channel_id=1, source_target_pairs={{0,16},{16,0},{1,17},{17,1},{2,18},{18,2},{3,19},{19,3},{4,20},{20... | collective-permute-start | bytes 2359304 | tf_op jit(solution)/shard_map/ppermute | solution.py:24
  66.1 30.4 %collective-permute-start.4 = (bf16[4,64,1024]{2,1,0:T(8,128)(2,1)S(1)}, bf16[4,64,1024]{2,1,0:T(8,128)(2,1)S(1)}, u32[]{:S(2)}, u32[]{:S(2)}) collective-permute-start(bf16[4,64,1024]{2,1,0:T(8,128)(2,1)S(1)} %bitcast.75), channel_id=1, source_target_pairs={{0,16},{16,0},{1,17},{17,1},{2,18},{18,2},{3,19},{19,3},{4,20},{20... | collective-permute-start | bytes 1572872 | tf_op jit(solution)/shard_map/ppermute | solution.py:24
  67.6 15.3 %collective-permute-start.6 = (bf16[128,2048]{1,0:T(8,128)(2,1)S(1)}, bf16[128,2048]{1,0:T(8,128)(2,1)S(1)}, u32[]{:S(2)}, u32[]{:S(2)}) collective-permute-start(bf16[128,2048]{1,0:T(8,128)(2,1)S(1)} %copy-done.15), channel_id=1, source_target_pairs={{0,4},{4,8},{8,12},{12,0},{1,5},{5,9},{9,13},{13,1},{2,6},{6,10},{... | collective-permute-start | bytes 1572872 | tf_op jit(solution)/shard_map/ppermute | solution.py:24
  71.9 24.6 %copy-start.14 = (bf16[128,2048]{1,0:T(8,128)(2,1)S(1)}, bf16[128,2048]{1,0:T(8,128)(2,1)}, u32[]{:S(2)}) copy-start(bf16[128,2048]{1,0:T(8,128)(2,1)} %slice.60) | copy-start | bytes 1572868
  96.5 6.0 %copy-start.9 = (bf16[4,64,1024]{2,1,0:T(8,128)(2,1)}, bf16[4,64,1024]{2,1,0:T(8,128)(2,1)S(1)}, u32[]{:S(2)}) copy-start(bf16[4,64,1024]{2,1,0:T(8,128)(2,1)S(1)} %collective-permute-done.4.g_ref) | copy-start | bytes 1572868
  96.5 13.5 %collective-permute-start.7 = (bf16[128,2048]{1,0:T(8,128)(2,1)S(1)}, bf16[128,2048]{1,0:T(8,128)(2,1)S(1)}, u32[]{:S(2)}, u32[]{:S(2)}) collective-permute-start(bf16[128,2048]{1,0:T(8,128)(2,1)S(1)} %copy-done.14), channel_id=1, source_target_pairs={{0,12},{4,0},{8,4},{12,8},{1,13},{5,1},{9,5},{13,9},{2,14},{6,2},{... | collective-permute-start | bytes 1572872 | tf_op jit(solution)/shard_map/ppermute | solution.py:24
  110.1 2.0 collective-permute-start.8
  111.7 3.4 %copy-start.1 = (bf16[4,1024,1024]{2,1,0:T(8,128)(2,1)S(1)}, bf16[4,1024,1024]{2,1,0:T(8,128)(2,1)}, u32[]{:S(2)}) copy-start(bf16[4,1024,1024]{2,1,0:T(8,128)(2,1)} %bitcast_dynamic-update-slice_fusion.4.refs_4_) | copy-start | bytes 25165828
  115.1 3.5 %copy-start.2 = (bf16[512,1024]{1,0:T(8,128)(2,1)}, bf16[512,1024]{1,0:T(8,128)(2,1)S(1)}, u32[]{:S(2)}) copy-start(bf16[512,1024]{1,0:T(8,128)(2,1)S(1)} %pad_maximum_fusion.4.refs_2_) | copy-start | bytes 3145732
  118.1 4.3 %copy-start.19 = (s32[8,256]{1,0:T(8,128)S(1)}, s32[8,256]{1,0:T(8,128)}, u32[]{:S(2)}) copy-start(s32[8,256]{1,0:T(8,128)} %param.10) | copy-start | bytes 24580
  118.1 4.2 %collective-permute-start.11 = (f32[256,512]{1,0:T(8,128)S(1)}, f32[256,512]{1,0:T(8,128)S(1)}, u32[]{:S(2)}, u32[]{:S(2)}) collective-permute-start(f32[256,512]{1,0:T(8,128)S(1)} %slice.83), channel_id=1, source_target_pairs={{0,1},{1,0},{2,3},{3,2},{4,5},{5,4},{6,7},{7,6},{8,9},{9,8},{10,11... | collective-permute-start | bytes 1572872 | tf_op jit(solution)/shard_map/ppermute | solution.py:28
  121.6 2.0 collective-permute-start.12
  122.5 3.4 %copy-start.10 = (bf16[256,512]{1,0:T(8,128)(2,1)}, bf16[256,512]{1,0:T(8,128)(2,1)S(1)}, u32[]{:S(2)}) copy-start(bf16[256,512]{1,0:T(8,128)(2,1)S(1)} %fusion.39) | copy-start | bytes 786436
  122.5 9.2 %collective-permute-start.13 = (bf16[4,64,512]{2,1,0:T(8,128)(2,1)S(1)}, bf16[4,64,512]{2,1,0:T(8,128)(2,1)S(1)}, u32[]{:S(2)}, u32[]{:S(2)}) collective-permute-start(bf16[4,64,512]{2,1,0:T(8,128)(2,1)S(1)} %bitcast.76), channel_id=1, source_target_pairs={{0,16},{16,0},{1,17},{17,1},{2,18},{18,2},{3,19},{19,3},{4,20},{20... | collective-permute-start | bytes 786440 | tf_op jit(solution)/shard_map/ppermute | solution.py:24
  123.6 5.9 %copy-start.12 = (bf16[256,512]{1,0:T(8,128)(2,1)}, bf16[256,512]{1,0:T(8,128)(2,1)S(1)}, u32[]{:S(2)}) copy-start(bf16[256,512]{1,0:T(8,128)(2,1)S(1)} %fusion.38) | copy-start | bytes 786436
  123.7 21.4 %collective-permute-start.16 = (bf16[4,64,512]{2,1,0:T(8,128)(2,1)S(1)}, bf16[4,64,512]{2,1,0:T(8,128)(2,1)}, u32[]{:S(2)}, u32[]{:S(2)}) collective-permute-start(bf16[4,64,512]{2,1,0:T(8,128)(2,1)S(1)} %bitcast.78), channel_id=1, source_target_pairs={{0,16},{16,0},{1,17},{17,1},{2,18},{18,2},{3,19},{19,3},{4,20},{20... | collective-permute-start | bytes 786440 | tf_op jit(solution)/shard_map/ppermute | solution.py:24
  136.0 19.2 %collective-permute-start.14 = (bf16[4,64,512]{2,1,0:T(8,128)(2,1)}, bf16[4,64,512]{2,1,0:T(8,128)(2,1)}, u32[]{:S(2)}, u32[]{:S(2)}) collective-permute-start(bf16[4,64,512]{2,1,0:T(8,128)(2,1)} %get-tuple-element.59), channel_id=1, source_target_pairs={{0,16},{16,0},{1,17},{17,1},{2,18},{18,2},{3,19},{19,3},{4,20},{20... | collective-permute-start | bytes 786440 | tf_op jit(solution)/shard_map/ppermute | solution.py:24
  145.1 10.2 %copy-start.16 = (bf16[4,64,512]{2,1,0:T(8,128)(2,1)S(1)}, bf16[4,64,512]{2,1,0:T(8,128)(2,1)}, u32[]{:S(2)}) copy-start(bf16[4,64,512]{2,1,0:T(8,128)(2,1)} %get-tuple-element.56) | copy-start | bytes 786436
  145.1 11.3 %copy-start.3 = (bf16[512,1024]{1,0:T(8,128)(2,1)S(1)}, bf16[512,1024]{1,0:T(8,128)(2,1)}, u32[]{:S(2)}) copy-start(bf16[512,1024]{1,0:T(8,128)(2,1)} %copy-done.2) | copy-start | bytes 3145732
  148.9 13.7 %collective-permute-start.17 = (bf16[4,64,512]{2,1,0:T(8,128)(2,1)}, bf16[4,64,512]{2,1,0:T(8,128)(2,1)S(1)}, u32[]{:S(2)}, u32[]{:S(2)}) collective-permute-start(bf16[4,64,512]{2,1,0:T(8,128)(2,1)} %get-tuple-element.63), channel_id=1, source_target_pairs={{0,16},{16,0},{1,17},{17,1},{2,18},{18,2},{3,19},{19,3},{4,20},{20... | collective-permute-start | bytes 786440 | tf_op jit(solution)/shard_map/ppermute | solution.py:24
  156.3 1.6 collective-permute-start.15
  157.0 5.7 %copy-start.4 = (bf16[4,512,1024]{2,1,0:T(8,128)(2,1)}, bf16[4,512,1024]{2,1,0:T(8,128)(2,1)S(1)}, u32[]{:S(2)}) copy-start(bf16[4,512,1024]{2,1,0:T(8,128)(2,1)S(1)} %pad_maximum_fusion) | copy-start | bytes 12582916
  157.0 5.6 %copy-start.17 = (bf16[4,64,512]{2,1,0:T(8,128)(2,1)S(1)}, bf16[4,64,512]{2,1,0:T(8,128)(2,1)}, u32[]{:S(2)}) copy-start(bf16[4,64,512]{2,1,0:T(8,128)(2,1)} %get-tuple-element.61) | copy-start | bytes 786436
  157.9 4.7 %copy-start.20 = (bf16[256,512]{1,0:T(8,128)(2,1)}, bf16[256,512]{1,0:T(8,128)(2,1)S(1)}, u32[]{:S(2)}) copy-start(bf16[256,512]{1,0:T(8,128)(2,1)S(1)} %collective-permute-done.15) | copy-start | bytes 786436
  162.7 1.8 collective-permute-start.18
  162.8 25.5 %collective-permute-start.21 = (bf16[1024,512]{1,0:T(8,128)(2,1)S(1)}, bf16[1024,512]{1,0:T(8,128)(2,1)S(1)}, u32[]{:S(2)}, u32[]{:S(2)}) collective-permute-start(bf16[1024,512]{1,0:T(8,128)(2,1)S(1)} %convolution_convert_fusion.4), channel_id=1, source_target_pairs={{0,2},{1,3},{2,0},{3,1},{4,6},{5,7},{6,4},{7,5},{8,10},{9,11},{10,... | collective-permute-start | bytes 3145736 | tf_op jit(solution)/shard_map/ppermute | solution.py:24
  164.4 7.6 %copy-start.5 = (bf16[4,512,1024]{2,1,0:T(8,128)(2,1)S(1)}, bf16[4,512,1024]{2,1,0:T(8,128)(2,1)}, u32[]{:S(2)}) copy-start(bf16[4,512,1024]{2,1,0:T(8,128)(2,1)} %copy-done.4) | copy-start | bytes 12582916
  164.4 11.8 %slice-start = ((s8[8388608]{0:T(1024)(128)(4,1)}), s8[4194304]{0:T(1024)(128)(4,1)S(1)}, s32[]{:S(2)}) async-start(s8[8388608]{0:T(1024)(128)(4,1)} %bitcast.67), calls=%async_computation | async-start | bytes 8388608
  167.6 30.1 %collective-permute-start.19 = (bf16[256,1024]{1,0:T(8,128)(2,1)S(1)}, bf16[256,1024]{1,0:T(8,128)(2,1)S(1)}, u32[]{:S(2)}, u32[]{:S(2)}) collective-permute-start(bf16[256,1024]{1,0:T(8,128)(2,1)S(1)} %get-tuple-element.89), channel_id=1, source_target_pairs={{0,4},{4,8},{8,12},{12,0},{1,5},{5,9},{9,13},{13,1},{2,6},{6,10},{... | collective-permute-start | bytes 1572872 | tf_op jit(solution)/shard_map/ppermute | solution.py:24
  168.8 4.4 %copy-start.21 = (bf16[256,512]{1,0:T(8,128)(2,1)S(1)}, bf16[256,512]{1,0:T(8,128)(2,1)}, u32[]{:S(2)}) copy-start(bf16[256,512]{1,0:T(8,128)(2,1)} %copy-done.20) | copy-start | bytes 786436
  168.8 28.9 %collective-permute-start.20 = (bf16[256,1024]{1,0:T(8,128)(2,1)S(1)}, bf16[256,1024]{1,0:T(8,128)(2,1)S(1)}, u32[]{:S(2)}, u32[]{:S(2)}) collective-permute-start(bf16[256,1024]{1,0:T(8,128)(2,1)S(1)} %get-tuple-element.88), channel_id=1, source_target_pairs={{0,12},{4,0},{8,4},{12,8},{1,13},{5,1},{9,5},{13,9},{2,14},{6,2},{... | collective-permute-start | bytes 1572872 | tf_op jit(solution)/shard_map/ppermute | solution.py:24
  172.0 4.2 %slice-start.1 = ((s8[8388608]{0:T(1024)(128)(4,1)}), s8[4194304]{0:T(1024)(128)(4,1)S(1)}, s32[]{:S(2)}) async-start(s8[8388608]{0:T(1024)(128)(4,1)} %bitcast.67), calls=%async_computation.1 | async-start | bytes 8388608
  172.8 24.9 %collective-permute-start.22 = (bf16[1024,512]{1,0:T(8,128)(2,1)S(1)}, bf16[1024,512]{1,0:T(8,128)(2,1)S(1)}, u32[]{:S(2)}, u32[]{:S(2)}) collective-permute-start(bf16[1024,512]{1,0:T(8,128)(2,1)S(1)} %convolution_convert_fusion.3), channel_id=1, source_target_pairs={{0,16},{16,0},{1,17},{17,1},{2,18},{18,2},{3,19},{19,3},{4,20},{20... | collective-permute-start | bytes 3145736 | tf_op jit(solution)/shard_map/ppermute | solution.py:24
  197.9 28.0 %collective-permute-start.23 = (bf16[512,1024]{1,0:T(8,128)(2,1)S(1)}, bf16[512,1024]{1,0:T(8,128)(2,1)S(1)}, u32[]{:S(2)}, u32[]{:S(2)}) collective-permute-start(bf16[512,1024]{1,0:T(8,128)(2,1)S(1)} %fusion.36), channel_id=1, source_target_pairs={{0,4},{4,8},{8,12},{12,0},{1,5},{5,9},{9,13},{13,1},{2,6},{6,10},{... | collective-permute-start | bytes 3145736 | tf_op jit(solution)/shard_map/ppermute | solution.py:24
  198.6 51.4 %collective-permute-start.26 = (bf16[1024,1024]{1,0:T(8,128)(2,1)S(1)}, bf16[1024,1024]{1,0:T(8,128)(2,1)S(1)}, u32[]{:S(2)}, u32[]{:S(2)}) collective-permute-start(bf16[1024,1024]{1,0:T(8,128)(2,1)S(1)} %fusion.24), channel_id=1, source_target_pairs={{0,16},{16,0},{1,17},{17,1},{2,18},{18,2},{3,19},{19,3},{4,20},{20... | collective-permute-start | bytes 6291464 | tf_op jit(solution)/shard_map/ppermute | solution.py:24
  199.6 50.4 %collective-permute-start.27 = (bf16[1024,1024]{1,0:T(8,128)(2,1)S(1)}, bf16[1024,1024]{1,0:T(8,128)(2,1)S(1)}, u32[]{:S(2)}, u32[]{:S(2)}) collective-permute-start(bf16[1024,1024]{1,0:T(8,128)(2,1)S(1)} %fusion.25), channel_id=1, source_target_pairs={{0,2},{1,3},{2,0},{3,1},{4,6},{5,7},{6,4},{7,5},{8,10},{9,11},{10,... | collective-permute-start | bytes 6291464 | tf_op jit(solution)/shard_map/ppermute | solution.py:24
  201.4 44.8 %collective-permute-start.24 = (bf16[512,1024]{1,0:T(8,128)(2,1)S(1)}, bf16[512,1024]{1,0:T(8,128)(2,1)S(1)}, u32[]{:S(2)}, u32[]{:S(2)}) collective-permute-start(bf16[512,1024]{1,0:T(8,128)(2,1)S(1)} %fusion.37), channel_id=1, source_target_pairs={{0,12},{4,0},{8,4},{12,8},{1,13},{5,1},{9,5},{13,9},{2,14},{6,2},{... | collective-permute-start | bytes 3145736 | tf_op jit(solution)/shard_map/ppermute | solution.py:24
  246.5 2.0 collective-permute-start.25
  (4 other events, 5.2 us)

commit v9 on v7

--- a/solution.py
+++ b/solution.py
@@ -226,20 +226,30 @@
     )(jnp.reshape(source, (1,)).astype(jnp.int32), kv)
 
 
-def total_kernel(*refs):
-    refs[-1][...] = total([ref[...] for ref in refs[:-1]])
+def total_kernel(tile, *refs):
+    out_ref, buf, sem = refs[-3:]
+    copies = []
+    for n in range(sem.shape[0]):
+        some = pl.ds(n * tile, tile)
+        buf[some] = total([ref[some] for ref in refs[:-3]])
+        copies.append(pltpu.make_async_copy(buf.at[some], out_ref.at[some], sem.at[n]))
+        copies[-1].start()
+    for copy in copies:
+        copy.wait()
 
 
 def summed(values):
     rows, columns = values[0].shape
-    tile = min(128, rows)
-    block = pl.BlockSpec((tile, columns), lambda r: (r, 0))
+    tile = min(64, rows)
     return pl.pallas_call(
-        total_kernel,
-        grid=(rows // tile,),
-        in_specs=[block] * len(values),
-        out_specs=block,
+        functools.partial(total_kernel, tile),
+        in_specs=[pl.BlockSpec(memory_space=pltpu.VMEM)] * len(values),
+        out_specs=pl.BlockSpec(memory_space=pl.ANY),
         out_shape=jax.ShapeDtypeStruct((rows, columns), F32),
+        scratch_shapes=[
+            pltpu.VMEM((rows, columns), F32),
+            pltpu.SemaphoreType.DMA((rows // tile,)),
+        ],
         compiler_params=pltpu.CompilerParams(vmem_limit_bytes=16 * 1024 * 1024),
         cost_estimate=pl.CostEstimate(
             flops=len(values) * rows * columns,
@@ -325,16 +335,27 @@
             )
         return shift(value, "seq", step) if step else value
 
-    cut = width * 5 // 8 // HD * HD
     sources = [(seq_at - step) % seq_count for step in range(seq_count)]
     staged = [stage(neighbour_kv, source, pairs) for source in sources]
+    near = [k for k in range(tensor_count) if k != opposite]
+    raw, along_seq, along_dp, staged, grad_out = lax.optimization_barrier(
+        ([raw[k] for k in near], along_seq, along_dp, staged, out_grad)
+    )
+    raw = dict(zip(near, raw))
+
+    cut = width * 5 // 8 // HD * HD
     left_from = [block[:, :cut] for block in along_seq[1:]]
     right_from = [block[:, cut:] for block in along_dp[1:]]
-    left_from, right_from, staged, grad_out = lax.optimization_barrier(
-        (left_from, right_from, staged, out_grad)
-    )
+    left_from, right_from = lax.optimization_barrier((left_from, right_from))
     corner_left = [gather_ring(block, "dp", couples) for block in left_from]
     corner_right = [gather_ring(block, "seq", seq_count) for block in right_from]
+    grads = [to_owner(grad_out, step) for step in range(seq_count)]
+    up_from, down_from = raw[opposite - 1][:rows // 2], raw[opposite + 1][rows // 2:]
+    up_from, down_from = lax.optimization_barrier((up_from, down_from, left_from, right_from))[:2]
+    raw[opposite] = jnp.concatenate(
+        [shift(up_from, "tensor", 1), shift(down_from, "tensor", -1)], axis=0
+    )
+
     def columns_of(block, which):
         return jnp.concatenate(
             [
@@ -344,22 +365,15 @@
             axis=1,
         )
 
-    near = [k for k in range(tensor_count) if k != opposite]
-    others = swap(jnp.concatenate([columns_of(raw[k], 1 - core) for k in near], axis=0))
-    up_from, down_from = raw[opposite - 1][:rows // 2], raw[opposite + 1][rows // 2:]
-    up_from, down_from = lax.optimization_barrier((up_from, down_from, left_from, right_from))[:2]
-    up = shift(up_from, "tensor", 1)
-    down_from, grad_out, others = lax.optimization_barrier((down_from, grad_out, others))
-    down = shift(down_from, "tensor", -1)
-    grads = [to_owner(grad_out, step) for step in range(seq_count)]
-    raw[opposite] = jnp.concatenate([up, down], axis=0)
+    others = lax.optimization_barrier(([raw[k] for k in near], down_from, grads))[0]
+    others = swap(jnp.concatenate([columns_of(block, 1 - core) for block in others], axis=0))
     others = {k: others[n * rows:(n + 1) * rows] for n, k in enumerate(near)}
     others[opposite] = swap(columns_of(raw[opposite], 1 - core))
     acts = [
         jnp.concatenate([columns_of(raw[k], core), others[k]], axis=0) for k in range(tensor_count)
     ]
     depth_blocks = [(tensor_at - k) % tensor_count for k in range(tensor_count)]
-    table = after(jnp.stack(depth_blocks).astype(jnp.int32), grads)
+    table = jnp.stack(depth_blocks).astype(jnp.int32)
 
     def block_at(i, j):
         block = ((seq_at - i) % seq_count) * dp_count + ((dp_at // 2 - j) % couples) * 2
@@ -418,34 +432,39 @@
         return lax.optimization_barrier(found.astype(BF16))
 
     kv_grad = None
+    answers = [[None] * seq_count for _ in range(2)]
+    calls = [(0, 0), (1, 0)] + [(part, step) for part in range(2) for step in range(1, seq_count)]
+    for part, step in calls:
+        answer, kv_grad = attend(
+            *slots[step],
+            asked[part][step],
+            grads[step],
+            staged[step][part],
+            live,
+            part,
+            kv_grad,
+        )
+        answers[part][step] = from_owner(answer, step)
+
+    far_weights = lax.dynamic_index_in_dim(weights, depth_blocks[opposite], 0, keepdims=False)
+    far_weights = after(far_weights, queries[1])
     both_grads, corners = [], []
     corner_places = [(i, j) for i in range(1, seq_count) for j in range(1, couples)]
     for part in range(2):
-        answers = []
-        for step in range(seq_count):
-            answer, kv_grad = attend(
-                *slots[step],
-                asked[part][step],
-                grads[step],
-                staged[step][part],
-                live,
-                part,
-                kv_grad,
-            )
-            answers.append(from_owner(answer, step))
         if part:
-            answers[-1] = after(answers[-1], corners[0][corner_places[-1]])
-        grad = sum(answers[1:], answers[0])
+            answers[1][-1] = after(answers[1][-1], corners[0][corner_places[-1]])
+        grad = sum(answers[part][1:], answers[part][0])
         both_grads.append(jnp.concatenate([grad, swap(grad)], axis=0))
         if part == 0:
             corners.append({at: weight_product(*at, both_grads[0]) for at in corner_places[::-1]})
     both_grad = jnp.concatenate(both_grads, axis=1)
 
-    def act_product(k):
-        block = lax.dynamic_index_in_dim(weights, depth_blocks[k], 0, keepdims=False)
+    def act_product(k, block=None):
+        if block is None:
+            block = lax.dynamic_index_in_dim(weights, depth_blocks[k], 0, keepdims=False)
         return lax.optimization_barrier(dot(both_grad, block, ((1,), (1,))).astype(BF16))
 
-    far = act_product(opposite)
+    far = act_product(opposite, far_weights)
     up, down = shift(far[:rows], "tensor", 1), shift(far[rows:], "tensor", -1)
 
     late_grad = after(both_grads[1], far)

time: 233 us -> 227 us (0.974)
  waiting for transfers between devices: 125 us -> 121 us
  local copies, waits for them, and re-layouts: 28 us -> 30.8 us
    ppermute x21, waiting for transfers between devices: 122 us -> 118 us  [shift(): lax.ppermute(value, axis, [(i, (i + step * stride) % size) for i in range...]
    ppermute x21, starting transfers between devices: 35.2 us -> 32.8 us  [shift(): lax.ppermute(value, axis, [(i, (i + step * stride) % size) for i in range...]
  transfers between devices with their start and end apart: 28 -> 28, of which waited for: 17 -> 13; matrix products, arithmetic and copies ran while one was open for 14% -> 12% of each run, Pallas kernels for 7% -> 7%
where the time goes in v9:
time: 227 us; the launch traced here: 226 us
  waiting for transfers between devices  121 us (53%)
  starting transfers between devices  34.5 us (15%)
  local copies, waits for them, and re-layouts  30.8 us (14%)
  Pallas kernels  21.9 us (10%)
  matrix products  10.7 us (5%)
  other arithmetic  4.91 us (2%)
    ppermute x21, waiting for transfers between devices, shift(): lax.ppermute(value, axis, [(i, (i + step * stride) % size) for i in range...  118 us
    ppermute x21, starting transfers between devices, shift(): lax.ppermute(value, axis, [(i, (i + step * stride) % size) for i in range...  32.8 us
    unnamed x63, local copies, waits for them, and re-layouts  14.6 us
    pallas_call x4, Pallas kernels, attend(): pl.pallas_call(attend_kernel, grid_spec=pltpu.PrefetchScalarGridSpec(num_...  11.7 us
    dot_general x9, matrix products, dot(): lax.dot_general(a, b, (contract, ((), ())), preferred_element_type=F32)  10.7 us
    pallas_call x2, Pallas kernels, product(): pl.pallas_call(functools.partial(product_kernel, count, start), out_shape...  5.81 us
  transfers between devices with their start and end apart: 28, of which 13 were waited for; matrix products, arithmetic and copies ran while one was open for 12% of the time, Pallas kernels for 7%

profile of v9, /device:TPU:0, one launch (start us, length us, event | category | flops | bytes accessed | tf_op | source)
XLA Modules:
  0.0 226.0 jit_solution(6982405369310362327)
XLA Ops:
  0.6 3.0 %collective-permute-start.2 = (bf16[1024,1024]{1,0:T(8,128)(2,1)}, bf16[1024,1024]{1,0:T(8,128)(2,1)S(1)}, u32[]{:S(2)}, u32[]{:S(2)}) collective-permute-start(bf16[1024,1024]{1,0:T(8,128)(2,1)} %param.7), channel_id=1, source_target_pairs={{0,16},{16,0},{1,17},{17,1},{2,18},{18,2},{3,19},{19,3},{4,20},{20... | collective-permute-start | bytes 6291464 | tf_op jit(solution)/shard_map/ppermute | solution.py:24
  3.6 1.5 collective-permute-start.3
  5.2 1.6 collective-permute-start
  6.7 2.2 collective-permute-start.1
  9.0 3.4 %copy-done.1 = bf16[8,2,256,1024]{3,2,1,0:T(8,128)(2,1)S(1)} copy-done((bf16[8,2,256,1024]{3,2,1,0:T(8,128)(2,1)S(1)}, bf16[8,2,256,1024]{3,2,1,0:T(8,128)(2,1)}, u32[]{:S(2)}) %copy-start.1) | copy-done | bytes 8388632
  12.7 1.3 copy-done.8
  14.0 1.3 copy-done.10
  15.7 1.4 copy-done.12
  17.1 1.3 copy-done.19
  19.2 14.2 %collective-permute-done = bf16[256,2048]{1,0:T(8,128)(2,1)S(1)} collective-permute-done((bf16[256,2048]{1,0:T(8,128)(2,1)}, bf16[256,2048]{1,0:T(8,128)(2,1)S(1)}, u32[]{:S(2)}, u32[]{:S(2)}) %collective-permute-start) | collective-permute-done | bytes 1048608 | tf_op jit(solution)/shard_map/ppermute | solution.py:24
  33.3 20.3 %collective-permute-done.1 = bf16[256,2048]{1,0:T(8,128)(2,1)} collective-permute-done((bf16[256,2048]{1,0:T(8,128)(2,1)}, bf16[256,2048]{1,0:T(8,128)(2,1)}, u32[]{:S(2)}, u32[]{:S(2)}) %collective-permute-start.1) | collective-permute-done | bytes 1048608 | tf_op jit(solution)/shard_map/ppermute | solution.py:24
  53.7 2.1 slice.63
  56.7 1.9 slice.61
  59.6 1.5 collective-permute-start.4
  62.2 2.7 %collective-permute-start.7 = (bf16[128,2048]{1,0:T(8,128)(2,1)}, bf16[128,2048]{1,0:T(8,128)(2,1)}, u32[]{:S(2)}, u32[]{:S(2)}) collective-permute-start(bf16[128,2048]{1,0:T(8,128)(2,1)} %slice.61), channel_id=1, source_target_pairs={{0,12},{4,0},{8,4},{12,8},{1,13},{5,1},{9,5},{13,9},{2,14},{6,2},{... | collective-permute-start | bytes 1572872 | tf_op jit(solution)/shard_map/ppermute | solution.py:24
  66.3 1.9 bitcast_dynamic-update-slice_fusion.1
  68.3 20.8 %collective-permute-done.4.g_ref = bf16[4,64,1024]{2,1,0:T(8,128)(2,1)S(1)} collective-permute-done((bf16[4,64,1024]{2,1,0:T(8,128)(2,1)S(1)}, bf16[4,64,1024]{2,1,0:T(8,128)(2,1)S(1)}, u32[]{:S(2)}, u32[]{:S(2)}) %collective-permute-start.4) | collective-permute-done | bytes 524320 | tf_op jit(solution)/shard_map/ppermute | solution.py:24
  95.3 1.4 bitcast_dynamic-update-slice_fusion.4.refs_4_
  97.1 2.9 %shard_map.87 = f32[512,512]{1,0:T(8,128)S(1)} custom-call(s32[4]{0:T(128)S(1)} %pad_add_fusion.1.table_ref, bf16[512,1024]{1,0:T(8,128)(2,1)S(1)} %pad_maximum_fusion.2.refs_0_, bf16[512,1024]{1,0:T(8,128)(2,1)S(1)} %pad_maximum_fusion.3.refs_1_, bf16[512,1024]{1,0:T(8,128)(2,1)S(1)} %pad_maximum_fusion.4.refs_2_, ...), custom_call_target="tpu_custom_call" | custom-call | flops 2147483648 | bytes 9437184 | tf_op jit(solution)/shard_map/pallas_call | solution.py:90
  100.7 2.9 %shard_map.88 = f32[512,512]{1,0:T(8,128)S(1)} custom-call(s32[4]{0:T(128)S(1)} %pad_add_fusion.1.table_ref, bf16[512,1024]{1,0:T(8,128)(2,1)S(1)} %pad_maximum_fusion.2.refs_0_, bf16[512,1024]{1,0:T(8,128)(2,1)S(1)} %pad_maximum_fusion.3.refs_1_, bf16[512,1024]{1,0:T(8,128)(2,1)S(1)} %pad_maximum_fusion.4.refs_2_, ...), custom_call_target="tpu_custom_call" | custom-call | flops 2147483648 | bytes 9437184 | tf_op jit(solution)/shard_map/pallas_call | solution.py:90
  106.9 2.6 %shard_map.89 = (bf16[4,64,512]{2,1,0:T(8,128)(2,1)S(1)}, bf16[8,2,256,1024]{3,2,1,0:T(8,128)(2,1)}) custom-call(s32[12]{0:T(128)S(1)} %pad_add_fusion.table_ref, bf16[4,64,512]{2,1,0:T(8,128)(2,1)S(1)} %bitcast.79, bf16[4,64,1024]{2,1,0:T(8,128)(2,1)S(1)} %bitcast.76, f32[8,256,128]{2,1,0:T(8,128)S(1)} %broadcast_in_dim.20.live_ref, ...), custom_call_target="tpu_custom_call" | custom-call | flops 1342177280 | bytes 4194304 | tf_op jit(solution)/shard_map/pallas_call | solution.py:179
  109.6 2.5 %shard_map.90 = (bf16[4,64,512]{2,1,0:T(8,128)(2,1)S(1)}, bf16[8,2,256,1024]{3,2,1,0:T(8,128)(2,1)}) custom-call(s32[12]{0:T(128)S(1)} %pad_add_fusion.table_ref, bf16[4,64,512]{2,1,0:T(8,128)(2,1)S(1)} %bitcast.74, bf16[4,64,1024]{2,1,0:T(8,128)(2,1)S(1)} %bitcast.77, ...), custom_call_target="tpu_custom_call", output_to_operand_aliasing={{1}: (5, {})} | custom-call | flops 1342177280 | bytes 4194304 | tf_op jit(solution)/shard_map/pallas_call | solution.py:179
  112.0 1.5 collective-permute-done.13.q_ref
  113.5 2.5 %shard_map.91 = (bf16[4,64,512]{2,1,0:T(8,128)(2,1)}, bf16[8,2,256,1024]{3,2,1,0:T(8,128)(2,1)}) custom-call(s32[12]{0:T(128)S(1)} %pad_add_fusion.2.table_ref, bf16[4,64,512]{2,1,0:T(8,128)(2,1)S(1)} %collective-permute-done.13.q_ref, bf16[4,64,1024]{2,1,0:T(8,128)(2,1)S(1)} %collective-permute-done.4.g_ref, ...), custom_call_target="tpu_custom_call", output_to_operand_aliasing={{1}: (5, {})} | custom-call | flops 1342177280 | bytes 4194304 | tf_op jit(solution)/shard_map/pallas_call | solution.py:179
  116.1 5.0 %collective-permute-start.14 = (bf16[4,64,512]{2,1,0:T(8,128)(2,1)}, bf16[4,64,512]{2,1,0:T(8,128)(2,1)}, u32[]{:S(2)}, u32[]{:S(2)}) collective-permute-start(bf16[4,64,512]{2,1,0:T(8,128)(2,1)} %get-tuple-element.80), channel_id=1, source_target_pairs={{0,16},{16,0},{1,17},{17,1},{2,18},{18,2},{3,19},{19,3},{4,20},{20... | collective-permute-start | bytes 786440 | tf_op jit(solution)/shard_map/ppermute | solution.py:24
  122.1 1.6 copy-done.9
  123.7 4.1 %shard_map.92 = (bf16[4,64,512]{2,1,0:T(8,128)(2,1)S(1)}, bf16[8,2,256,1024]{3,2,1,0:T(8,128)(2,1)}) custom-call(s32[12]{0:T(128)S(1)} %pad_add_fusion.2.table_ref, bf16[4,64,512]{2,1,0:T(8,128)(2,1)} %collective-permute-done.16.q_ref, bf16[4,64,1024]{2,1,0:T(8,128)(2,1)S(1)} %copy-done.7, ...), custom_call_target="tpu_custom_call", output_to_operand_aliasing={{1}: (5, {})} | custom-call | flops 1342177280 | bytes 4194304 | tf_op jit(solution)/shard_map/pallas_call | solution.py:179
  132.4 3.4 %collective-permute-done.17 = bf16[4,64,512]{2,1,0:T(8,128)(2,1)S(1)} collective-permute-done((bf16[4,64,512]{2,1,0:T(8,128)(2,1)S(1)}, bf16[4,64,512]{2,1,0:T(8,128)(2,1)S(1)}, u32[]{:S(2)}, u32[]{:S(2)}) %collective-permute-start.17) | collective-permute-done | bytes 262176 | tf_op jit(solution)/shard_map/ppermute | solution.py:24
  136.1 1.8 dynamic-slice_bitcast_fusion
  137.9 1.5 collective-permute-start.21
  139.5 1.3 convolution_convert_fusion.3
  142.4 1.6 collective-permute-start.22
  144.1 1.8 collective-permute-start.19
  145.9 2.0 collective-permute-start.20
  147.9 1.3 convolution_convert_fusion
  149.2 1.3 convolution_convert_fusion.1
  151.6 1.3 fusion.15
  152.9 1.3 convolution_convert_fusion.2.refs_0_
  154.3 1.3 fusion.12
  155.6 1.3 fusion.9.own_ref
  156.9 6.5 %collective-permute-done.21 = bf16[1024,512]{1,0:T(8,128)(2,1)S(1)} collective-permute-done((bf16[1024,512]{1,0:T(8,128)(2,1)S(1)}, bf16[1024,512]{1,0:T(8,128)(2,1)S(1)}, u32[]{:S(2)}, u32[]{:S(2)}) %collective-permute-start.21) | collective-permute-done | bytes 1048608 | tf_op jit(solution)/shard_map/ppermute | solution.py:24
  163.5 4.2 %collective-permute-done.22 = bf16[1024,512]{1,0:T(8,128)(2,1)S(1)} collective-permute-done((bf16[1024,512]{1,0:T(8,128)(2,1)S(1)}, bf16[1024,512]{1,0:T(8,128)(2,1)S(1)}, u32[]{:S(2)}, u32[]{:S(2)}) %collective-permute-start.22) | collective-permute-done | bytes 1048608 | tf_op jit(solution)/shard_map/ppermute | solution.py:24
  167.7 2.8 %collective-permute-done.20 = bf16[256,1024]{1,0:T(8,128)(2,1)S(1)} collective-permute-done((bf16[256,1024]{1,0:T(8,128)(2,1)S(1)}, bf16[256,1024]{1,0:T(8,128)(2,1)S(1)}, u32[]{:S(2)}, u32[]{:S(2)}) %collective-permute-start.20) | collective-permute-done | bytes 524320 | tf_op jit(solution)/shard_map/ppermute | solution.py:24
  173.1 2.1 collective-permute-start.24
  175.6 44.2 %collective-permute-done.24.down_ref = bf16[512,1024]{1,0:T(8,128)(2,1)S(1)} collective-permute-done((bf16[512,1024]{1,0:T(8,128)(2,1)S(1)}, bf16[512,1024]{1,0:T(8,128)(2,1)S(1)}, u32[]{:S(2)}, u32[]{:S(2)}) %collective-permute-start.24) | collective-permute-done | bytes 1048608 | tf_op jit(solution)/shard_map/ppermute | solution.py:24
  220.2 1.9 collective-permute-done.25.arrived_ref
  222.1 1.6 shard_map.93
  223.7 2.2 shard_map.94
  (141 shorter events, 28.0 us)
Async XLA Ops:
  0.6 52.9 %collective-permute-start.2 = (bf16[1024,1024]{1,0:T(8,128)(2,1)}, bf16[1024,1024]{1,0:T(8,128)(2,1)S(1)}, u32[]{:S(2)}, u32[]{:S(2)}) collective-permute-start(bf16[1024,1024]{1,0:T(8,128)(2,1)} %param.7), channel_id=1, source_target_pairs={{0,16},{16,0},{1,17},{17,1},{2,18},{18,2},{3,19},{19,3},{4,20},{20... | collective-permute-start | bytes 6291464 | tf_op jit(solution)/shard_map/ppermute | solution.py:24
  3.6 49.9 %collective-permute-start.3 = (bf16[1024,1024]{1,0:T(8,128)(2,1)}, bf16[1024,1024]{1,0:T(8,128)(2,1)}, u32[]{:S(2)}, u32[]{:S(2)}) collective-permute-start(bf16[1024,1024]{1,0:T(8,128)(2,1)} %param.7), channel_id=1, source_target_pairs={{0,2},{1,3},{2,0},{3,1},{4,6},{5,7},{6,4},{7,5},{8,10},{9,11},{10,... | collective-permute-start | bytes 6291464 | tf_op jit(solution)/shard_map/ppermute | solution.py:24
  5.2 28.2 %collective-permute-start = (bf16[256,2048]{1,0:T(8,128)(2,1)}, bf16[256,2048]{1,0:T(8,128)(2,1)S(1)}, u32[]{:S(2)}, u32[]{:S(2)}) collective-permute-start(bf16[256,2048]{1,0:T(8,128)(2,1)} %param.6), channel_id=1, source_target_pairs={{0,4},{4,8},{8,12},{12,0},{1,5},{5,9},{9,13},{13,1},{2,6},{6,10},{... | collective-permute-start | bytes 3145736 | tf_op jit(solution)/shard_map/ppermute | solution.py:24
  6.7 46.8 %collective-permute-start.1 = (bf16[256,2048]{1,0:T(8,128)(2,1)}, bf16[256,2048]{1,0:T(8,128)(2,1)}, u32[]{:S(2)}, u32[]{:S(2)}) collective-permute-start(bf16[256,2048]{1,0:T(8,128)(2,1)} %param.6), channel_id=1, source_target_pairs={{0,12},{4,0},{8,4},{12,8},{1,13},{5,1},{9,5},{13,9},{2,14},{6,2},{... | collective-permute-start | bytes 3145736 | tf_op jit(solution)/shard_map/ppermute | solution.py:24
  9.0 3.4 %copy-start.1 = (bf16[8,2,256,1024]{3,2,1,0:T(8,128)(2,1)S(1)}, bf16[8,2,256,1024]{3,2,1,0:T(8,128)(2,1)}, u32[]{:S(2)}) copy-start(bf16[8,2,256,1024]{3,2,1,0:T(8,128)(2,1)} %kv_ref.3) | copy-start | bytes 25165828
  15.3 3.1 %copy-start.26 = (s32[32]{0:T(128)S(1)}, s32[32]{0:T(128)}, u32[]{:S(2)}) copy-start(s32[32]{0:T(128)} %param.11) | copy-start | bytes 388
  53.7 5.9 %copy-start.14 = (bf16[256,1024]{1,0:T(8,128)(2,1)S(1)}, bf16[256,1024]{1,0:T(8,128)(2,1)}, u32[]{:S(2)}) copy-start(bf16[256,1024]{1,0:T(8,128)(2,1)} %param.8) | copy-start | bytes 1572868
  58.6 36.4 %collective-permute-start.9 = (bf16[1024,640]{1,0:T(8,128)(2,1)S(1)}, bf16[1024,640]{1,0:T(8,128)(2,1)S(1)}, u32[]{:S(2)}, u32[]{:S(2)}) collective-permute-start(bf16[1024,640]{1,0:T(8,128)(2,1)S(1)} %slice.62), channel_id=1, source_target_pairs={{0,2},{1,3},{2,0},{3,1},{4,6},{5,7},{6,4},{7,5},{8,10},{9,11},{10,... | collective-permute-start | bytes 3932168 | tf_op jit(solution)/shard_map/ppermute | solution.py:24
  59.1 35.8 %collective-permute-start.10 = (bf16[1024,384]{1,0:T(8,128)(2,1)}, bf16[1024,384]{1,0:T(8,128)(2,1)}, u32[]{:S(2)}, u32[]{:S(2)}) collective-permute-start(bf16[1024,384]{1,0:T(8,128)(2,1)} %slice.63), channel_id=1, source_target_pairs={{0,16},{16,0},{1,17},{17,1},{2,18},{18,2},{3,19},{19,3},{4,20},{20... | collective-permute-start | bytes 2359304 | tf_op jit(solution)/shard_map/ppermute | solution.py:24
  59.6 6.4 %copy-start.23 = (bf16[1024,1024]{1,0:T(8,128)(2,1)S(1)}, bf16[1024,1024]{1,0:T(8,128)(2,1)}, u32[]{:S(2)}) copy-start(bf16[1024,1024]{1,0:T(8,128)(2,1)} %param.7) | copy-start | bytes 6291460
  59.6 29.4 %collective-permute-start.4 = (bf16[4,64,1024]{2,1,0:T(8,128)(2,1)S(1)}, bf16[4,64,1024]{2,1,0:T(8,128)(2,1)S(1)}, u32[]{:S(2)}, u32[]{:S(2)}) collective-permute-start(bf16[4,64,1024]{2,1,0:T(8,128)(2,1)S(1)} %bitcast.75), channel_id=1, source_target_pairs={{0,16},{16,0},{1,17},{17,1},{2,18},{18,2},{3,19},{19,3},{4,20},{20... | collective-permute-start | bytes 1572872 | tf_op jit(solution)/shard_map/ppermute | solution.py:24
  61.1 29.5 %collective-permute-start.6 = (bf16[128,2048]{1,0:T(8,128)(2,1)}, bf16[128,2048]{1,0:T(8,128)(2,1)}, u32[]{:S(2)}, u32[]{:S(2)}) collective-permute-start(bf16[128,2048]{1,0:T(8,128)(2,1)} %slice.60), channel_id=1, source_target_pairs={{0,4},{4,8},{8,12},{12,0},{1,5},{5,9},{9,13},{13,1},{2,6},{6,10},{... | collective-permute-start | bytes 1572872 | tf_op jit(solution)/shard_map/ppermute | solution.py:24
  62.2 29.4 %collective-permute-start.7 = (bf16[128,2048]{1,0:T(8,128)(2,1)}, bf16[128,2048]{1,0:T(8,128)(2,1)}, u32[]{:S(2)}, u32[]{:S(2)}) collective-permute-start(bf16[128,2048]{1,0:T(8,128)(2,1)} %slice.61), channel_id=1, source_target_pairs={{0,12},{4,0},{8,4},{12,8},{1,13},{5,1},{9,5},{13,9},{2,14},{6,2},{... | collective-permute-start | bytes 1572872 | tf_op jit(solution)/shard_map/ppermute | solution.py:24
  66.3 22.7 %copy-start.24 = (bf16[256,2048]{1,0:T(8,128)(2,1)S(1)}, bf16[256,2048]{1,0:T(8,128)(2,1)}, u32[]{:S(2)}) copy-start(bf16[256,2048]{1,0:T(8,128)(2,1)} %param.6) | copy-start | bytes 3145732
  89.0 24.5 %copy-start.6 = (bf16[4,64,1024]{2,1,0:T(8,128)(2,1)}, bf16[4,64,1024]{2,1,0:T(8,128)(2,1)S(1)}, u32[]{:S(2)}) copy-start(bf16[4,64,1024]{2,1,0:T(8,128)(2,1)S(1)} %collective-permute-done.4.g_ref) | copy-start | bytes 1572868
  90.5 6.2 %collective-permute-start.5 = (bf16[768,1024]{1,0:T(8,128)(2,1)S(1)}, bf16[768,1024]{1,0:T(8,128)(2,1)S(1)}, u32[]{:S(2)}, u32[]{:S(2)}) collective-permute-start(bf16[768,1024]{1,0:T(8,128)(2,1)S(1)} %pad_maximum_fusion.1), channel_id=1, source_target_pairs={{0,1},{1,0},{2,3},{3,2},{4,5},{5,4},{6,7},{7,6},{8,9},{9,8},{10,11... | collective-permute-start | bytes 4718600 | tf_op jit(solution)/shard_map/ppermute | solution.py:28
  92.8 2.1 collective-permute-start.8
  96.7 3.8 %copy-start = (bf16[4,1024,1024]{2,1,0:T(8,128)(2,1)}, bf16[4,1024,1024]{2,1,0:T(8,128)(2,1)S(1)}, u32[]{:S(2)}) copy-start(bf16[4,1024,1024]{2,1,0:T(8,128)(2,1)S(1)} %bitcast_dynamic-update-slice_fusion.4.refs_4_) | copy-start | bytes 25165828
  97.0 3.5 %copy-start.2 = (bf16[512,1024]{1,0:T(8,128)(2,1)}, bf16[512,1024]{1,0:T(8,128)(2,1)S(1)}, u32[]{:S(2)}) copy-start(bf16[512,1024]{1,0:T(8,128)(2,1)S(1)} %pad_maximum_fusion.3.refs_1_) | copy-start | bytes 3145732
  97.1 3.7 %copy-start.4 = (bf16[512,1024]{1,0:T(8,128)(2,1)}, bf16[512,1024]{1,0:T(8,128)(2,1)S(1)}, u32[]{:S(2)}) copy-start(bf16[512,1024]{1,0:T(8,128)(2,1)S(1)} %pad_maximum_fusion.2.refs_0_) | copy-start | bytes 3145732
  100.0 4.2 %copy-start.25 = (s32[8,256]{1,0:T(8,128)S(1)}, s32[8,256]{1,0:T(8,128)}, u32[]{:S(2)}) copy-start(s32[8,256]{1,0:T(8,128)} %param.10) | copy-start | bytes 24580
  100.0 4.2 %collective-permute-start.11 = (f32[256,512]{1,0:T(8,128)S(1)}, f32[256,512]{1,0:T(8,128)S(1)}, u32[]{:S(2)}, u32[]{:S(2)}) collective-permute-start(f32[256,512]{1,0:T(8,128)S(1)} %slice.84), channel_id=1, source_target_pairs={{0,1},{1,0},{2,3},{3,2},{4,5},{5,4},{6,7},{7,6},{8,9},{9,8},{10,11... | collective-permute-start | bytes 1572872 | tf_op jit(solution)/shard_map/ppermute | solution.py:28
  103.7 3.2 %copy-start.20 = (bf16[4,2,256,512]{3,2,1,0:T(8,128)(2,1)S(1)}, bf16[4,2,256,512]{3,2,1,0:T(8,128)(2,1)}, u32[]{:S(2)}) copy-start(bf16[4,2,256,512]{3,2,1,0:T(8,128)(2,1)} %copy-done.19) | copy-start | bytes 6291460
  103.7 2.0 collective-permute-start.12
  104.3 9.2 %collective-permute-start.13 = (bf16[4,64,512]{2,1,0:T(8,128)(2,1)S(1)}, bf16[4,64,512]{2,1,0:T(8,128)(2,1)S(1)}, u32[]{:S(2)}, u32[]{:S(2)}) collective-permute-start(bf16[4,64,512]{2,1,0:T(8,128)(2,1)S(1)} %bitcast.78), channel_id=1, source_target_pairs={{0,16},{16,0},{1,17},{17,1},{2,18},{18,2},{3,19},{19,3},{4,20},{20... | collective-permute-start | bytes 786440 | tf_op jit(solution)/shard_map/ppermute | solution.py:24
  105.8 15.3 %collective-permute-start.16 = (bf16[4,64,512]{2,1,0:T(8,128)(2,1)S(1)}, bf16[4,64,512]{2,1,0:T(8,128)(2,1)}, u32[]{:S(2)}, u32[]{:S(2)}) collective-permute-start(bf16[4,64,512]{2,1,0:T(8,128)(2,1)S(1)} %bitcast.73), channel_id=1, source_target_pairs={{0,16},{16,0},{1,17},{17,1},{2,18},{18,2},{3,19},{19,3},{4,20},{20... | collective-permute-start | bytes 786440 | tf_op jit(solution)/shard_map/ppermute | solution.py:24
  109.6 4.0 %copy-start.11 = (bf16[4,2,256,512]{3,2,1,0:T(8,128)(2,1)S(1)}, bf16[4,2,256,512]{3,2,1,0:T(8,128)(2,1)}, u32[]{:S(2)}) copy-start(bf16[4,2,256,512]{3,2,1,0:T(8,128)(2,1)} %copy-done.10) | copy-start | bytes 6291460
  112.0 4.0 %copy-start.15 = (bf16[4,64,512]{2,1,0:T(8,128)(2,1)}, bf16[4,64,512]{2,1,0:T(8,128)(2,1)S(1)}, u32[]{:S(2)}) copy-start(bf16[4,64,512]{2,1,0:T(8,128)(2,1)S(1)} %get-tuple-element.81) | copy-start | bytes 786436
  116.1 13.0 %collective-permute-start.14 = (bf16[4,64,512]{2,1,0:T(8,128)(2,1)}, bf16[4,64,512]{2,1,0:T(8,128)(2,1)}, u32[]{:S(2)}, u32[]{:S(2)}) collective-permute-start(bf16[4,64,512]{2,1,0:T(8,128)(2,1)} %get-tuple-element.80), channel_id=1, source_target_pairs={{0,16},{16,0},{1,17},{17,1},{2,18},{18,2},{3,19},{19,3},{4,20},{20... | collective-permute-start | bytes 786440 | tf_op jit(solution)/shard_map/ppermute | solution.py:24
  123.7 5.4 %copy-start.18 = (bf16[4,64,512]{2,1,0:T(8,128)(2,1)S(1)}, bf16[4,64,512]{2,1,0:T(8,128)(2,1)}, u32[]{:S(2)}) copy-start(bf16[4,64,512]{2,1,0:T(8,128)(2,1)} %copy-done.17) | copy-start | bytes 786436
  123.7 6.5 %copy-start.3 = (bf16[512,1024]{1,0:T(8,128)(2,1)S(1)}, bf16[512,1024]{1,0:T(8,128)(2,1)}, u32[]{:S(2)}) copy-start(bf16[512,1024]{1,0:T(8,128)(2,1)} %copy-done.2) | copy-start | bytes 3145732
  123.7 6.5 %copy-start.5 = (bf16[512,1024]{1,0:T(8,128)(2,1)S(1)}, bf16[512,1024]{1,0:T(8,128)(2,1)}, u32[]{:S(2)}) copy-start(bf16[512,1024]{1,0:T(8,128)(2,1)} %copy-done.4) | copy-start | bytes 3145732
  127.8 8.1 %collective-permute-start.17 = (bf16[4,64,512]{2,1,0:T(8,128)(2,1)S(1)}, bf16[4,64,512]{2,1,0:T(8,128)(2,1)S(1)}, u32[]{:S(2)}, u32[]{:S(2)}) collective-permute-start(bf16[4,64,512]{2,1,0:T(8,128)(2,1)S(1)} %get-tuple-element.84), channel_id=1, source_target_pairs={{0,16},{16,0},{1,17},{17,1},{2,18},{18,2},{3,19},{19,3},{4,20},{20... | collective-permute-start | bytes 786440 | tf_op jit(solution)/shard_map/ppermute | solution.py:24
  130.1 1.6 collective-permute-start.15
  130.8 5.1 %copy-start.21 = (bf16[4,512,1024]{2,1,0:T(8,128)(2,1)}, bf16[4,512,1024]{2,1,0:T(8,128)(2,1)S(1)}, u32[]{:S(2)}) copy-start(bf16[4,512,1024]{2,1,0:T(8,128)(2,1)S(1)} %pad_maximum_fusion) | copy-start | bytes 12582916
  130.8 5.1 %copy-start.16 = (bf16[4,64,512]{2,1,0:T(8,128)(2,1)S(1)}, bf16[4,64,512]{2,1,0:T(8,128)(2,1)}, u32[]{:S(2)}) copy-start(bf16[4,64,512]{2,1,0:T(8,128)(2,1)} %copy-done.15) | copy-start | bytes 786436
  131.7 4.2 %copy-start.27 = (bf16[256,512]{1,0:T(8,128)(2,1)}, bf16[256,512]{1,0:T(8,128)(2,1)S(1)}, u32[]{:S(2)}) copy-start(bf16[256,512]{1,0:T(8,128)(2,1)S(1)} %collective-permute-done.15) | copy-start | bytes 786436
  135.9 3.5 %collective-permute-start.18 = (bf16[256,512]{1,0:T(8,128)(2,1)S(1)}, bf16[256,512]{1,0:T(8,128)(2,1)S(1)}, u32[]{:S(2)}, u32[]{:S(2)}) collective-permute-start(bf16[256,512]{1,0:T(8,128)(2,1)S(1)} %bitcast_add_fusion), channel_id=1, source_target_pairs={{0,1},{1,0},{2,3},{3,2},{4,5},{5,4},{6,7},{7,6},{8,9},{9,8},{10,11... | collective-permute-start | bytes 786440 | tf_op jit(solution)/shard_map/ppermute | solution.py:28
  136.1 3.4 %copy-start.28 = (bf16[256,512]{1,0:T(8,128)(2,1)S(1)}, bf16[256,512]{1,0:T(8,128)(2,1)}, u32[]{:S(2)}) copy-start(bf16[256,512]{1,0:T(8,128)(2,1)} %copy-done.27) | copy-start | bytes 786436
  137.9 25.5 %collective-permute-start.21 = (bf16[1024,512]{1,0:T(8,128)(2,1)S(1)}, bf16[1024,512]{1,0:T(8,128)(2,1)S(1)}, u32[]{:S(2)}, u32[]{:S(2)}) collective-permute-start(bf16[1024,512]{1,0:T(8,128)(2,1)S(1)} %convolution_convert_fusion.5), channel_id=1, source_target_pairs={{0,2},{1,3},{2,0},{3,1},{4,6},{5,7},{6,4},{7,5},{8,10},{9,11},{10,... | collective-permute-start | bytes 3145736 | tf_op jit(solution)/shard_map/ppermute | solution.py:24
  142.4 25.2 %collective-permute-start.22 = (bf16[1024,512]{1,0:T(8,128)(2,1)S(1)}, bf16[1024,512]{1,0:T(8,128)(2,1)S(1)}, u32[]{:S(2)}, u32[]{:S(2)}) collective-permute-start(bf16[1024,512]{1,0:T(8,128)(2,1)S(1)} %convolution_convert_fusion.4), channel_id=1, source_target_pairs={{0,16},{16,0},{1,17},{17,1},{2,18},{18,2},{3,19},{19,3},{4,20},{20... | collective-permute-start | bytes 3145736 | tf_op jit(solution)/shard_map/ppermute | solution.py:24
  144.1 23.6 %collective-permute-start.19 = (bf16[256,1024]{1,0:T(8,128)(2,1)S(1)}, bf16[256,1024]{1,0:T(8,128)(2,1)S(1)}, u32[]{:S(2)}, u32[]{:S(2)}) collective-permute-start(bf16[256,1024]{1,0:T(8,128)(2,1)S(1)} %get-tuple-element.111), channel_id=1, source_target_pairs={{0,4},{4,8},{8,12},{12,0},{1,5},{5,9},{9,13},{13,1},{2,6},{6,10},{... | collective-permute-start | bytes 1572872 | tf_op jit(solution)/shard_map/ppermute | solution.py:24
  145.9 24.6 %collective-permute-start.20 = (bf16[256,1024]{1,0:T(8,128)(2,1)S(1)}, bf16[256,1024]{1,0:T(8,128)(2,1)S(1)}, u32[]{:S(2)}, u32[]{:S(2)}) collective-permute-start(bf16[256,1024]{1,0:T(8,128)(2,1)S(1)} %get-tuple-element.110), channel_id=1, source_target_pairs={{0,12},{4,0},{8,4},{12,8},{1,13},{5,1},{9,5},{13,9},{2,14},{6,2},{... | collective-permute-start | bytes 1572872 | tf_op jit(solution)/shard_map/ppermute | solution.py:24
  171.1 52.6 %collective-permute-start.27 = (bf16[1024,1024]{1,0:T(8,128)(2,1)S(1)}, bf16[1024,1024]{1,0:T(8,128)(2,1)S(1)}, u32[]{:S(2)}, u32[]{:S(2)}) collective-permute-start(bf16[1024,1024]{1,0:T(8,128)(2,1)S(1)} %fusion.19), channel_id=1, source_target_pairs={{0,2},{1,3},{2,0},{3,1},{4,6},{5,7},{6,4},{7,5},{8,10},{9,11},{10,... | collective-permute-start | bytes 6291464 | tf_op jit(solution)/shard_map/ppermute | solution.py:24
  172.1 51.5 %collective-permute-start.26 = (bf16[1024,1024]{1,0:T(8,128)(2,1)S(1)}, bf16[1024,1024]{1,0:T(8,128)(2,1)S(1)}, u32[]{:S(2)}, u32[]{:S(2)}) collective-permute-start(bf16[1024,1024]{1,0:T(8,128)(2,1)S(1)} %fusion.18), channel_id=1, source_target_pairs={{0,16},{16,0},{1,17},{17,1},{2,18},{18,2},{3,19},{19,3},{4,20},{20... | collective-permute-start | bytes 6291464 | tf_op jit(solution)/shard_map/ppermute | solution.py:24
  173.1 46.7 %collective-permute-start.24 = (bf16[512,1024]{1,0:T(8,128)(2,1)S(1)}, bf16[512,1024]{1,0:T(8,128)(2,1)S(1)}, u32[]{:S(2)}, u32[]{:S(2)}) collective-permute-start(bf16[512,1024]{1,0:T(8,128)(2,1)S(1)} %fusion.31), channel_id=1, source_target_pairs={{0,12},{4,0},{8,4},{12,8},{1,13},{5,1},{9,5},{13,9},{2,14},{6,2},{... | collective-permute-start | bytes 3145736 | tf_op jit(solution)/shard_map/ppermute | solution.py:24
  175.5 44.3 %collective-permute-start.23 = (bf16[512,1024]{1,0:T(8,128)(2,1)S(1)}, bf16[512,1024]{1,0:T(8,128)(2,1)S(1)}, u32[]{:S(2)}, u32[]{:S(2)}) collective-permute-start(bf16[512,1024]{1,0:T(8,128)(2,1)S(1)} %fusion.30), channel_id=1, source_target_pairs={{0,4},{4,8},{8,12},{12,0},{1,5},{5,9},{9,13},{13,1},{2,6},{6,10},{... | collective-permute-start | bytes 3145736 | tf_op jit(solution)/shard_map/ppermute | solution.py:24
  220.1 2.0 collective-permute-start.25
  (11 other events, 20.4 us)

commit v10 on v9

--- a/solution.py
+++ b/solution.py
@@ -226,6 +226,31 @@
     )(jnp.reshape(source, (1,)).astype(jnp.int32), kv)
 
 
+def pick_kernel(depth, which_ref, *refs):
+    out_ref = refs[-1]
+    rows = refs[0].shape[0]
+    for n, ref in enumerate(refs[:-1]):
+        for p in range(out_ref.shape[1] // depth):
+            start = pl.multiple_of((2 * p + which_ref[0]) * depth, depth)
+            out_ref[n * rows:(n + 1) * rows, p * depth:(p + 1) * depth] = ref[:, pl.ds(start, depth)]
+
+
+def picked(blocks, which, depth):
+    rows, columns = blocks[0].shape
+    shape = (len(blocks) * rows, columns // 2)
+    return pl.pallas_call(
+        functools.partial(pick_kernel, depth),
+        in_specs=[pl.BlockSpec(memory_space=pltpu.SMEM)]
+        + [pl.BlockSpec(memory_space=pltpu.VMEM)] * len(blocks),
+        out_specs=pl.BlockSpec(memory_space=pltpu.VMEM),
+        out_shape=jax.ShapeDtypeStruct(shape, BF16),
+        compiler_params=pltpu.CompilerParams(vmem_limit_bytes=16 * 1024 * 1024),
+        cost_estimate=pl.CostEstimate(
+            flops=0, bytes_accessed=4 * shape[0] * shape[1], transcendentals=0
+        ),
+    )(jnp.reshape(which, (1,)).astype(jnp.int32), *blocks)
+
+
 def total_kernel(tile, *refs):
     out_ref, buf, sem = refs[-3:]
     copies = []
@@ -338,23 +363,20 @@
     sources = [(seq_at - step) % seq_count for step in range(seq_count)]
     staged = [stage(neighbour_kv, source, pairs) for source in sources]
     near = [k for k in range(tensor_count) if k != opposite]
-    raw, along_seq, along_dp, staged, grad_out = lax.optimization_barrier(
-        ([raw[k] for k in near], along_seq, along_dp, staged, out_grad)
-    )
-    raw = dict(zip(near, raw))
-
     cut = width * 5 // 8 // HD * HD
     left_from = [block[:, :cut] for block in along_seq[1:]]
     right_from = [block[:, cut:] for block in along_dp[1:]]
-    left_from, right_from = lax.optimization_barrier((left_from, right_from))
+    left_from, right_from, raw, staged = lax.optimization_barrier(
+        (left_from, right_from, [raw[k] for k in near], staged)
+    )
+    raw = dict(zip(near, raw))
+
     corner_left = [gather_ring(block, "dp", couples) for block in left_from]
     corner_right = [gather_ring(block, "seq", seq_count) for block in right_from]
+    up = shift(raw[opposite - 1][:rows // 2], "tensor", 1)
+    down = shift(raw[opposite + 1][rows // 2:], "tensor", -1)
+    grad_out = after(out_grad, corner_right)
     grads = [to_owner(grad_out, step) for step in range(seq_count)]
-    up_from, down_from = raw[opposite - 1][:rows // 2], raw[opposite + 1][rows // 2:]
-    up_from, down_from = lax.optimization_barrier((up_from, down_from, left_from, right_from))[:2]
-    raw[opposite] = jnp.concatenate(
-        [shift(up_from, "tensor", 1), shift(down_from, "tensor", -1)], axis=0
-    )
 
     def columns_of(block, which):
         return jnp.concatenate(
@@ -365,8 +387,9 @@
             axis=1,
         )
 
-    others = lax.optimization_barrier(([raw[k] for k in near], down_from, grads))[0]
-    others = swap(jnp.concatenate([columns_of(block, 1 - core) for block in others], axis=0))
+    others = swap(picked([raw[k] for k in near], 1 - core, depth))
+    up, down, others = lax.optimization_barrier((up, down, others))
+    raw[opposite] = jnp.concatenate([up, down], axis=0)
     others = {k: others[n * rows:(n + 1) * rows] for n, k in enumerate(near)}
     others[opposite] = swap(columns_of(raw[opposite], 1 - core))
     acts = [
@@ -416,6 +439,8 @@
     for part in range(2):
         partial = product(acts, weights, table, part * half, half)
         arrived = swap(partial[rows:])
+        if part:
+            partial = after(partial, grads)
         queries.append((partial[:rows] + arrived).astype(BF16))
     asked = [[to_owner(value, step) for step in range(seq_count)] for value in queries]
     asked[0][0] = after(asked[0][0], queries[1])
@@ -451,8 +476,8 @@
     both_grads, corners = [], []
     corner_places = [(i, j) for i in range(1, seq_count) for j in range(1, couples)]
     for part in range(2):
-        if part:
-            answers[1][-1] = after(answers[1][-1], corners[0][corner_places[-1]])
+        ahead = corners[0][corner_places[-1]] if part else far_weights
+        answers[part][-1] = after(answers[part][-1], ahead)
         grad = sum(answers[part][1:], answers[part][0])
         both_grads.append(jnp.concatenate([grad, swap(grad)], axis=0))
         if part == 0:
@@ -510,9 +535,10 @@
     ]
     from_dp = reduce_rings([([None] + beside_dp, True)], "dp")[0][1:]
 
-    arrived = swap(total([part[rows:] for part in (act_parts[0], up, down)]).astype(BF16))
+    weight_grad = summed([own] + from_seq + from_dp)
+    others = after([part[rows:] for part in (act_parts[0], up, down)], weight_grad)
+    arrived = swap(total(others).astype(BF16))
     act_grad = assemble(core, act_parts[0], up, down, arrived, depth)
-    weight_grad = summed([own] + from_seq + from_dp)
     return (act_grad, weight_grad, kv_grad)
 
 

time: 227 us -> 237 us (1.044)
  waiting for transfers between devices: 121 us -> 108 us
  Pallas kernels: 21.9 us -> 32.2 us
  local copies, waits for them, and re-layouts: 30.8 us -> 38.1 us
  matrix products: 10.7 us -> 17.4 us
  starting transfers between devices: 34.5 us -> 31.9 us
    ppermute x21, waiting for transfers between devices: 118 us -> 103 us  [shift(): lax.ppermute(value, axis, [(i, (i + step * stride) % size) for i in range...]
    dynamic_update_slice x5, local copies, waits for them, and re-layouts: 4.11 us -> 11.4 us  [on_device(): lax.dynamic_update_slice(weights, piece[None], (at, inner * depth, start))]
    dot_general x9, matrix products: 10.7 us -> 17.4 us  [dot(): lax.dot_general(a, b, (contract, ((), ())), preferred_element_type=F32)]
    pallas_call x2, Pallas kernels: 5.81 us -> 11.8 us  [product(): pl.pallas_call(functools.partial(product_kernel, count, start), out_shape...]
    pallas_call x4, Pallas kernels: 11.7 us -> 15.8 us  [attend(): pl.pallas_call(attend_kernel, grid_spec=pltpu.PrefetchScalarGridSpec(num_...]
    broadcast_in_dim x1, local copies, waits for them, and re-layouts: 1.06 us -> 4.38 us  [on_device(): weights = jnp.zeros((tensor_count, per * depth, width), BF16)]
    unnamed x63 -> x53, local copies, waits for them, and re-layouts: 14.6 us -> 12 us
    slice x2 -> x6, local copies, waits for them, and re-layouts: 2.67 us -> 0.16 us  [the longest x4 0.08 us: on_device(): part[rows:]]
  transfers between devices with their start and end apart: 28 -> 28, of which waited for: 13 -> 13; matrix products, arithmetic and copies ran while one was open for 12% -> 20% of each run, Pallas kernels for 7% -> 12%
where the time goes in v10:
time: 237 us; the launch traced here: 236 us
  waiting for transfers between devices  108 us (46%)
  local copies, waits for them, and re-layouts  38.1 us (16%)
  Pallas kernels  32.2 us (14%)
  starting transfers between devices  31.9 us (13%)
  matrix products  17.4 us (7%)
  other arithmetic  6.3 us (3%)
    ppermute x21, waiting for transfers between devices, shift(): lax.ppermute(value, axis, [(i, (i + step * stride) % size) for i in range...  103 us
    ppermute x21, starting transfers between devices, shift(): lax.ppermute(value, axis, [(i, (i + step * stride) % size) for i in range...  31 us
    dot_general x9, matrix products, dot(): lax.dot_general(a, b, (contract, ((), ())), preferred_element_type=F32)  17.4 us
    pallas_call x4, Pallas kernels, attend(): pl.pallas_call(attend_kernel, grid_spec=pltpu.PrefetchScalarGridSpec(num_...  15.8 us
    unnamed x53, local copies, waits for them, and re-layouts  12 us
    pallas_call x2, Pallas kernels, product(): pl.pallas_call(functools.partial(product_kernel, count, start), out_shape...  11.8 us
    dynamic_update_slice x5, local copies, waits for them, and re-layouts, on_device(): lax.dynamic_update_slice(weights, piece[None], (at, inner * depth, start))  11.4 us
    ppermute x7, waiting for transfers between devices, swap(): lax.ppermute(value, 'dp', [(i, i ^ 1) for i in range(lax.axis_size('dp'))])  5.25 us
  transfers between devices with their start and end apart: 28, of which 13 were waited for; matrix products, arithmetic and copies ran while one was open for 20% of the time, Pallas kernels for 12%

profile of v10, /device:TPU:0, one launch (start us, length us, event | category | flops | bytes accessed | tf_op | source)
XLA Modules:
  0.0 235.5 jit_solution(10156365568640637967)
XLA Ops:
  0.6 3.0 %collective-permute-start = (bf16[1024,1024]{1,0:T(8,128)(2,1)}, bf16[1024,1024]{1,0:T(8,128)(2,1)}, u32[]{:S(2)}, u32[]{:S(2)}) collective-permute-start(bf16[1024,1024]{1,0:T(8,128)(2,1)} %param.7), channel_id=1, source_target_pairs={{0,16},{16,0},{1,17},{17,1},{2,18},{18,2},{3,19},{19,3},{4,20},{20... | collective-permute-start | bytes 6291464 | tf_op jit(solution)/shard_map/ppermute | solution.py:24
  3.6 1.5 collective-permute-start.1
  5.2 1.6 collective-permute-start.2
  6.7 2.2 collective-permute-start.3
  9.0 3.4 %copy-done = bf16[8,2,256,1024]{3,2,1,0:T(8,128)(2,1)S(1)} copy-done((bf16[8,2,256,1024]{3,2,1,0:T(8,128)(2,1)S(1)}, bf16[8,2,256,1024]{3,2,1,0:T(8,128)(2,1)}, u32[]{:S(2)}) %copy-start) | copy-done | bytes 8388632
  15.3 1.9 copy-done.1
  17.6 1.4 copy-done.13
  20.9 4.4 %broadcast_in_dim.14 = bf16[4,1024,1024]{2,1,0:T(8,128)(2,1)} broadcast(bf16[]{:T(256)} %constant.311.clone.1), dimensions={} | broadcast | bytes 8388610 | tf_op jit(solution)/shard_map/broadcast_in_dim | solution.py:406
  25.2 1.5 bitcast_dynamic-update-slice_fusion.2
  26.8 6.5 %collective-permute-done.2.refs_1_ = bf16[256,2048]{1,0:T(8,128)(2,1)S(1)} collective-permute-done((bf16[256,2048]{1,0:T(8,128)(2,1)}, bf16[256,2048]{1,0:T(8,128)(2,1)S(1)}, u32[]{:S(2)}, u32[]{:S(2)}) %collective-permute-start.2) | collective-permute-done | bytes 1048608 | tf_op jit(solution)/shard_map/ppermute | solution.py:24
  33.3 20.2 %collective-permute-done.3.refs_2_ = bf16[256,2048]{1,0:T(8,128)(2,1)S(1)} collective-permute-done((bf16[256,2048]{1,0:T(8,128)(2,1)}, bf16[256,2048]{1,0:T(8,128)(2,1)S(1)}, u32[]{:S(2)}, u32[]{:S(2)}) %collective-permute-start.3) | collective-permute-done | bytes 1048608 | tf_op jit(solution)/shard_map/ppermute | solution.py:24
  53.5 2.5 %slice.80 = bf16[1024,640]{1,0:T(8,128)(2,1)} slice(bf16[1024,1024]{1,0:T(8,128)(2,1)} %collective-permute-done), slice={[0:1024], [0:640]} | slice | bytes 2621440 | tf_op jit(solution)/shard_map/slice | solution.py:367
  56.0 2.1 slice.81
  60.4 2.7 %collective-permute-start.5 = (bf16[128,2048]{1,0:T(8,128)(2,1)S(1)}, bf16[128,2048]{1,0:T(8,128)(2,1)S(1)}, u32[]{:S(2)}, u32[]{:S(2)}) collective-permute-start(bf16[128,2048]{1,0:T(8,128)(2,1)S(1)} %slice.63), channel_id=1, source_target_pairs={{0,12},{4,0},{8,4},{12,8},{1,13},{5,1},{9,5},{13,9},{2,14},{6,2},{... | collective-permute-start | bytes 1572872 | tf_op jit(solution)/shard_map/ppermute | solution.py:24
  63.7 3.1 %bitcast_dynamic-update-slice_fusion.1 = bf16[4,1024,1024]{2,1,0:T(8,128)(2,1)} fusion(bf16[4,1024,1024]{2,1,0:T(8,128)(2,1)} %bitcast_dynamic-update-slice_fusion.2, s32[]{:T(128)S(6)} %select_n.239, bf16[1024,1024]{1,0:T(8,128)(2,1)} %collective-permute-done.1), kind=kLoop, calls=%fused_computation.8 | loop fusion | bytes 4194308 | tf_op jit(solution)/shard_map/dynamic_update_slice | solution.py:416
  66.9 3.1 %bitcast_dynamic-update-slice_fusion = bf16[4,1024,1024]{2,1,0:T(8,128)(2,1)} fusion(bf16[4,1024,1024]{2,1,0:T(8,128)(2,1)} %bitcast_dynamic-update-slice_fusion.1, s32[]{:T(128)S(6)} %select_n.241, bf16[1024,1024]{1,0:T(8,128)(2,1)} %collective-permute-done), kind=kLoop, calls=%fused_computation.7 | loop fusion | bytes 4194308 | tf_op jit(solution)/shard_map/dynamic_update_slice | solution.py:416
  70.0 12.5 %collective-permute-done.9 = bf16[1024,384]{1,0:T(8,128)(2,1)S(1)} collective-permute-done((bf16[1024,384]{1,0:T(8,128)(2,1)S(1)}, bf16[1024,384]{1,0:T(8,128)(2,1)S(1)}, u32[]{:S(2)}, u32[]{:S(2)}) %collective-permute-start.9) | collective-permute-done | bytes 786464 | tf_op jit(solution)/shard_map/ppermute | solution.py:24
  83.0 5.4 %collective-permute-done.8 = bf16[1024,640]{1,0:T(8,128)(2,1)} collective-permute-done((bf16[1024,640]{1,0:T(8,128)(2,1)}, bf16[1024,640]{1,0:T(8,128)(2,1)}, u32[]{:S(2)}, u32[]{:S(2)}) %collective-permute-start.8) | collective-permute-done | bytes 1310752 | tf_op jit(solution)/shard_map/ppermute | solution.py:24
  88.4 2.5 %bitcast_dynamic-update-slice_fusion.3 = bf16[4,1024,1024]{2,1,0:T(8,128)(2,1)} fusion(bf16[4,1024,1024]{2,1,0:T(8,128)(2,1)} %bitcast_dynamic-update-slice_fusion, s32[]{:T(128)S(6)} %select_n.243, bf16[1024,640]{1,0:T(8,128)(2,1)} %collective-permute-done.8), kind=kLoop, calls=%fused_computation.25 | loop fusion | bytes 2621444 | tf_op jit(solution)/shard_map/dynamic_update_slice | solution.py:416
  92.6 1.5 collective-permute-done.7
  94.3 6.1 %shard_map.88 = f32[512,512]{1,0:T(8,128)S(1)} custom-call(s32[4]{0:T(128)S(1)} %pad_add_fusion.1.table_ref, bf16[512,1024]{1,0:T(8,128)(2,1)S(1)} %pad_maximum_fusion.1.refs_0_, bf16[512,1024]{1,0:T(8,128)(2,1)S(1)} %pad_maximum_fusion.2.refs_1_, bf16[512,1024]{1,0:T(8,128)(2,1)S(1)} %pad_maximum_fusion.3.refs_2_, ...), custom_call_target="tpu_custom_call" | custom-call | flops 2147483648 | bytes 9437184 | tf_op jit(solution)/shard_map/pallas_call | solution.py:90
  101.7 5.7 %shard_map.89 = f32[512,512]{1,0:T(8,128)S(1)} custom-call(s32[4]{0:T(128)S(1)} %pad_add_fusion.1.table_ref, bf16[512,1024]{1,0:T(8,128)(2,1)S(1)} %pad_maximum_fusion.1.refs_0_, bf16[512,1024]{1,0:T(8,128)(2,1)S(1)} %pad_maximum_fusion.2.refs_1_, bf16[512,1024]{1,0:T(8,128)(2,1)S(1)} %pad_maximum_fusion.3.refs_2_, ...), custom_call_target="tpu_custom_call" | custom-call | flops 2147483648 | bytes 9437184 | tf_op jit(solution)/shard_map/pallas_call | solution.py:90
  109.7 1.4 fusion.32
  113.0 1.6 collective-permute-start.16
  114.9 4.0 %shard_map.90 = (bf16[4,64,512]{2,1,0:T(8,128)(2,1)S(1)}, bf16[8,2,256,1024]{3,2,1,0:T(8,128)(2,1)}) custom-call(s32[12]{0:T(128)S(1)} %pad_add_fusion.table_ref, bf16[4,64,512]{2,1,0:T(8,128)(2,1)S(1)} %bitcast.77, bf16[4,64,1024]{2,1,0:T(8,128)(2,1)} %bitcast.15.g_ref, f32[8,256,128]{2,1,0:T(8,128)S(1)} %broadcast_in_dim.20.live_ref, ...), custom_call_target="tpu_custom_call" | custom-call | flops 1342177280 | bytes 4194304 | tf_op jit(solution)/shard_map/pallas_call | solution.py:179
  118.9 4.0 %shard_map.91 = (bf16[4,64,512]{2,1,0:T(8,128)(2,1)S(1)}, bf16[8,2,256,1024]{3,2,1,0:T(8,128)(2,1)}) custom-call(s32[12]{0:T(128)S(1)} %pad_add_fusion.table_ref, bf16[4,64,512]{2,1,0:T(8,128)(2,1)S(1)} %bitcast.75, bf16[4,64,1024]{2,1,0:T(8,128)(2,1)} %bitcast.15.g_ref, ...), custom_call_target="tpu_custom_call", output_to_operand_aliasing={{1}: (5, {})} | custom-call | flops 1342177280 | bytes 4194304 | tf_op jit(solution)/shard_map/pallas_call | solution.py:179
  122.9 3.9 %shard_map.92 = (bf16[4,64,512]{2,1,0:T(8,128)(2,1)S(1)}, bf16[8,2,256,1024]{3,2,1,0:T(8,128)(2,1)}) custom-call(s32[12]{0:T(128)S(1)} %pad_add_fusion.2.table_ref, bf16[4,64,512]{2,1,0:T(8,128)(2,1)S(1)} %collective-permute-done.13.q_ref, bf16[4,64,1024]{2,1,0:T(8,128)(2,1)} %collective-permute-done.11.g_ref, ...), custom_call_target="tpu_custom_call", output_to_operand_aliasing={{1}: (5, {})} | custom-call | flops 1342177280 | bytes 4194304 | tf_op jit(solution)/shard_map/pallas_call | solution.py:179
  126.8 4.3 %collective-permute-start.14 = (bf16[4,64,512]{2,1,0:T(8,128)(2,1)S(1)}, bf16[4,64,512]{2,1,0:T(8,128)(2,1)S(1)}, u32[]{:S(2)}, u32[]{:S(2)}) collective-permute-start(bf16[4,64,512]{2,1,0:T(8,128)(2,1)S(1)} %get-tuple-element.76), channel_id=1, source_target_pairs={{0,16},{16,0},{1,17},{17,1},{2,18},{18,2},{3,19},{19,3},{4,20},{20... | collective-permute-start | bytes 786440 | tf_op jit(solution)/shard_map/ppermute | solution.py:24
  131.2 3.1 %dynamic-slice_bitcast_fusion = bf16[1024,1024]{1,0:T(8,128)(2,1)} fusion(bf16[4,1024,1024]{2,1,0:T(8,128)(2,1)} %bitcast_dynamic-update-slice_fusion.4.refs_4_, s32[]{:T(128)S(6)} %select_n.246), kind=kLoop, calls=%fused_computation.15 | loop fusion | bytes 4194308 | tf_op jit(solution)/shard_map/jit(dynamic_index_in_dim)/squeeze | solution.py:474
  134.2 3.9 %shard_map.93 = (bf16[4,64,512]{2,1,0:T(8,128)(2,1)S(1)}, bf16[8,2,256,1024]{3,2,1,0:T(8,128)(2,1)}) custom-call(s32[12]{0:T(128)S(1)} %pad_add_fusion.2.table_ref, bf16[4,64,512]{2,1,0:T(8,128)(2,1)S(1)} %collective-permute-done.16.q_ref, bf16[4,64,1024]{2,1,0:T(8,128)(2,1)} %collective-permute-done.11.g_ref, ...), custom_call_target="tpu_custom_call", output_to_operand_aliasing={{1}: (5, {})} | custom-call | flops 1342177280 | bytes 4194304 | tf_op jit(solution)/shard_map/pallas_call | solution.py:179
  138.2 1.4 collective-permute-start.17
  141.2 1.7 convolution_convert_fusion.5
  143.0 3.9 %collective-permute-done.17 = bf16[4,64,512]{2,1,0:T(8,128)(2,1)S(1)} collective-permute-done((bf16[4,64,512]{2,1,0:T(8,128)(2,1)S(1)}, bf16[4,64,512]{2,1,0:T(8,128)(2,1)S(1)}, u32[]{:S(2)}, u32[]{:S(2)}) %collective-permute-start.17) | collective-permute-done | bytes 262176 | tf_op jit(solution)/shard_map/ppermute | solution.py:24
  148.6 2.4 %convolution_convert_fusion.3 = bf16[512,1024]{1,0:T(8,128)(2,1)S(1)} fusion(bf16[1024,1024]{1,0:T(8,128)(2,1)S(1)} %copy-done.20, bf16[256,512]{1,0:T(8,128)(2,1)S(1)} %collective-permute-done.18, bf16[256,512]{1,0:T(8,128)(2,1)S(1)} %bitcast_add_fusion, bf16[256,512]{1,0:T(8,128)(2,1)} %copy-done.24, bf16[256,512]{1,0:T(8,128)(2,1)S(1)} %bitcast_add_fusion.1), kind=kOutput, calls=%fused_computation.22 | convolution fusion | flops 1078460416 | bytes 4194304 | tf_op jit(solution)/shard_map/dot_general | solution.py:18
  152.3 1.8 collective-permute-start.19
  154.1 2.0 collective-permute-start.20
  158.7 2.9 %fusion.15 = bf16[512,1024]{1,0:T(8,128)(2,1)S(1)} fusion(bf16[4,1024,1024]{2,1,0:T(8,128)(2,1)} %bitcast_dynamic-update-slice_fusion.4.refs_4_, s32[]{:T(128)S(6)} %select_n.251, bf16[256,512]{1,0:T(8,128)(2,1)S(1)} %collective-permute-done.18, bf16[256,512]{1,0:T(8,128)(2,1)S(1)} %bitcast_add_fusion, bf16[256,512]{1,0:T(8,128)(2,1)S(1)} %copy-done.25, ...), kind=kOutput, calls=%fused_computation.21 | convolution fusion | flops 1078460416 | bytes 4194308 | tf_op jit(solution)/shard_map/dot_general | solution.py:18
  162.9 2.9 %fusion.12 = bf16[512,1024]{1,0:T(8,128)(2,1)S(1)} fusion(bf16[4,1024,1024]{2,1,0:T(8,128)(2,1)} %bitcast_dynamic-update-slice_fusion.4.refs_4_, s32[]{:T(128)S(6)} %select_n.250, bf16[256,512]{1,0:T(8,128)(2,1)S(1)} %collective-permute-done.18, bf16[256,512]{1,0:T(8,128)(2,1)S(1)} %bitcast_add_fusion, bf16[256,512]{1,0:T(8,128)(2,1)S(1)} %copy-done.25, ...), kind=kOutput, calls=%fused_computation.20 | convolution fusion | flops 1078460416 | bytes 4194308 | tf_op jit(solution)/shard_map/dot_general | solution.py:18
  165.8 2.9 %fusion.9.own_ref = bf16[512,1024]{1,0:T(8,128)(2,1)S(1)} fusion(bf16[4,1024,1024]{2,1,0:T(8,128)(2,1)} %bitcast_dynamic-update-slice_fusion.4.refs_4_, s32[]{:T(128)S(6)} %select_n.249, bf16[256,512]{1,0:T(8,128)(2,1)S(1)} %collective-permute-done.18, bf16[256,512]{1,0:T(8,128)(2,1)S(1)} %bitcast_add_fusion, bf16[256,512]{1,0:T(8,128)(2,1)S(1)} %copy-done.25, ...), kind=kOutput, calls=%fused_computation.19 | convolution fusion | flops 1078460416 | bytes 4194308 | tf_op jit(solution)/shard_map/dot_general | solution.py:18
  168.7 4.1 %collective-permute-done.21 = bf16[1024,512]{1,0:T(8,128)(2,1)S(1)} collective-permute-done((bf16[1024,512]{1,0:T(8,128)(2,1)}, bf16[1024,512]{1,0:T(8,128)(2,1)S(1)}, u32[]{:S(2)}, u32[]{:S(2)}) %collective-permute-start.21) | collective-permute-done | bytes 1048608 | tf_op jit(solution)/shard_map/ppermute | solution.py:24
  172.8 4.3 %collective-permute-done.22 = bf16[1024,512]{1,0:T(8,128)(2,1)S(1)} collective-permute-done((bf16[1024,512]{1,0:T(8,128)(2,1)S(1)}, bf16[1024,512]{1,0:T(8,128)(2,1)S(1)}, u32[]{:S(2)}, u32[]{:S(2)}) %collective-permute-start.22) | collective-permute-done | bytes 1048608 | tf_op jit(solution)/shard_map/ppermute | solution.py:24
  177.2 1.6 collective-permute-done.20
  180.7 1.7 collective-permute-start.25
  182.7 2.1 collective-permute-start.24
  185.1 44.2 %collective-permute-done.24.down_ref = bf16[512,1024]{1,0:T(8,128)(2,1)S(1)} collective-permute-done((bf16[512,1024]{1,0:T(8,128)(2,1)S(1)}, bf16[512,1024]{1,0:T(8,128)(2,1)S(1)}, u32[]{:S(2)}, u32[]{:S(2)}) %collective-permute-start.24) | collective-permute-done | bytes 1048608 | tf_op jit(solution)/shard_map/ppermute | solution.py:24
  229.4 2.2 shard_map.94
  232.0 1.9 collective-permute-done.27.arrived_ref
  233.9 1.6 shard_map.95
  (132 shorter events, 27.1 us)
Async XLA Ops:
  0.6 52.8 %collective-permute-start = (bf16[1024,1024]{1,0:T(8,128)(2,1)}, bf16[1024,1024]{1,0:T(8,128)(2,1)}, u32[]{:S(2)}, u32[]{:S(2)}) collective-permute-start(bf16[1024,1024]{1,0:T(8,128)(2,1)} %param.7), channel_id=1, source_target_pairs={{0,16},{16,0},{1,17},{17,1},{2,18},{18,2},{3,19},{19,3},{4,20},{20... | collective-permute-start | bytes 6291464 | tf_op jit(solution)/shard_map/ppermute | solution.py:24
  3.6 52.3 %collective-permute-start.1 = (bf16[1024,1024]{1,0:T(8,128)(2,1)}, bf16[1024,1024]{1,0:T(8,128)(2,1)}, u32[]{:S(2)}, u32[]{:S(2)}) collective-permute-start(bf16[1024,1024]{1,0:T(8,128)(2,1)} %param.7), channel_id=1, source_target_pairs={{0,2},{1,3},{2,0},{3,1},{4,6},{5,7},{6,4},{7,5},{8,10},{9,11},{10,... | collective-permute-start | bytes 6291464 | tf_op jit(solution)/shard_map/ppermute | solution.py:24
  5.2 28.2 %collective-permute-start.2 = (bf16[256,2048]{1,0:T(8,128)(2,1)}, bf16[256,2048]{1,0:T(8,128)(2,1)S(1)}, u32[]{:S(2)}, u32[]{:S(2)}) collective-permute-start(bf16[256,2048]{1,0:T(8,128)(2,1)} %refs_0_), channel_id=1, source_target_pairs={{0,4},{4,8},{8,12},{12,0},{1,5},{5,9},{9,13},{13,1},{2,6},{6,10},{... | collective-permute-start | bytes 3145736 | tf_op jit(solution)/shard_map/ppermute | solution.py:24
  6.7 46.7 %collective-permute-start.3 = (bf16[256,2048]{1,0:T(8,128)(2,1)}, bf16[256,2048]{1,0:T(8,128)(2,1)S(1)}, u32[]{:S(2)}, u32[]{:S(2)}) collective-permute-start(bf16[256,2048]{1,0:T(8,128)(2,1)} %refs_0_), channel_id=1, source_target_pairs={{0,12},{4,0},{8,4},{12,8},{1,13},{5,1},{9,5},{13,9},{2,14},{6,2},{... | collective-permute-start | bytes 3145736 | tf_op jit(solution)/shard_map/ppermute | solution.py:24
  9.0 3.4 %copy-start = (bf16[8,2,256,1024]{3,2,1,0:T(8,128)(2,1)S(1)}, bf16[8,2,256,1024]{3,2,1,0:T(8,128)(2,1)}, u32[]{:S(2)}) copy-start(bf16[8,2,256,1024]{3,2,1,0:T(8,128)(2,1)} %kv_ref.3) | copy-start | bytes 25165828
  12.4 4.9 %copy-start.1 = (bf16[8,2,256,1024]{3,2,1,0:T(8,128)(2,1)S(1)}, bf16[8,2,256,1024]{3,2,1,0:T(8,128)(2,1)}, u32[]{:S(2)}) copy-start(bf16[8,2,256,1024]{3,2,1,0:T(8,128)(2,1)} %kv_ref.3) | copy-start | bytes 25165828
  17.3 3.1 %copy-start.23 = (s32[32]{0:T(128)S(1)}, s32[32]{0:T(128)}, u32[]{:S(2)}) copy-start(s32[32]{0:T(128)} %param.11) | copy-start | bytes 388
  20.8 4.4 %copy-start.19 = (bf16[1024,1024]{1,0:T(8,128)(2,1)S(1)}, bf16[1024,1024]{1,0:T(8,128)(2,1)}, u32[]{:S(2)}) copy-start(bf16[1024,1024]{1,0:T(8,128)(2,1)} %param.7) | copy-start | bytes 6291460
  26.8 32.0 %copy-start.8 = (bf16[256,2048]{1,0:T(8,128)(2,1)S(1)}, bf16[256,2048]{1,0:T(8,128)(2,1)}, u32[]{:S(2)}) copy-start(bf16[256,2048]{1,0:T(8,128)(2,1)} %refs_0_) | copy-start | bytes 3145732
  58.1 30.3 %collective-permute-start.8 = (bf16[1024,640]{1,0:T(8,128)(2,1)}, bf16[1024,640]{1,0:T(8,128)(2,1)}, u32[]{:S(2)}, u32[]{:S(2)}) collective-permute-start(bf16[1024,640]{1,0:T(8,128)(2,1)} %slice.80), channel_id=1, source_target_pairs={{0,2},{1,3},{2,0},{3,1},{4,6},{5,7},{6,4},{7,5},{8,10},{9,11},{10,... | collective-permute-start | bytes 3932168 | tf_op jit(solution)/shard_map/ppermute | solution.py:24
  58.9 4.2 %copy-start.21 = (bf16[1024,384]{1,0:T(8,128)(2,1)S(1)}, bf16[1024,384]{1,0:T(8,128)(2,1)}, u32[]{:S(2)}) copy-start(bf16[1024,384]{1,0:T(8,128)(2,1)} %slice.81) | copy-start | bytes 2359300
  58.9 33.1 %collective-permute-start.6 = (bf16[768,1024]{1,0:T(8,128)(2,1)S(1)}, bf16[768,1024]{1,0:T(8,128)(2,1)S(1)}, u32[]{:S(2)}, u32[]{:S(2)}) collective-permute-start(bf16[768,1024]{1,0:T(8,128)(2,1)S(1)} %shard_map.87), channel_id=1, source_target_pairs={{0,1},{1,0},{2,3},{3,2},{4,5},{5,4},{6,7},{7,6},{8,9},{9,8},{10,11... | collective-permute-start | bytes 4718600 | tf_op jit(solution)/shard_map/ppermute | solution.py:28
  59.2 32.8 %collective-permute-start.4 = (bf16[128,2048]{1,0:T(8,128)(2,1)S(1)}, bf16[128,2048]{1,0:T(8,128)(2,1)S(1)}, u32[]{:S(2)}, u32[]{:S(2)}) collective-permute-start(bf16[128,2048]{1,0:T(8,128)(2,1)S(1)} %slice.62), channel_id=1, source_target_pairs={{0,4},{4,8},{8,12},{12,0},{1,5},{5,9},{9,13},{13,1},{2,6},{6,10},{... | collective-permute-start | bytes 1572872 | tf_op jit(solution)/shard_map/ppermute | solution.py:24
  60.4 31.6 %collective-permute-start.5 = (bf16[128,2048]{1,0:T(8,128)(2,1)S(1)}, bf16[128,2048]{1,0:T(8,128)(2,1)S(1)}, u32[]{:S(2)}, u32[]{:S(2)}) collective-permute-start(bf16[128,2048]{1,0:T(8,128)(2,1)S(1)} %slice.63), channel_id=1, source_target_pairs={{0,12},{4,0},{8,4},{12,8},{1,13},{5,1},{9,5},{13,9},{2,14},{6,2},{... | collective-permute-start | bytes 1572872 | tf_op jit(solution)/shard_map/ppermute | solution.py:24
  63.1 19.4 %collective-permute-start.9 = (bf16[1024,384]{1,0:T(8,128)(2,1)S(1)}, bf16[1024,384]{1,0:T(8,128)(2,1)S(1)}, u32[]{:S(2)}, u32[]{:S(2)}) collective-permute-start(bf16[1024,384]{1,0:T(8,128)(2,1)S(1)} %copy-done.21), channel_id=1, source_target_pairs={{0,16},{16,0},{1,17},{17,1},{2,18},{18,2},{3,19},{19,3},{4,20},{20... | collective-permute-start | bytes 2359304 | tf_op jit(solution)/shard_map/ppermute | solution.py:24
  82.5 27.2 %collective-permute-start.11 = (bf16[4,64,1024]{2,1,0:T(8,128)(2,1)}, bf16[4,64,1024]{2,1,0:T(8,128)(2,1)}, u32[]{:S(2)}, u32[]{:S(2)}) collective-permute-start(bf16[4,64,1024]{2,1,0:T(8,128)(2,1)} %bitcast.15.g_ref), channel_id=1, source_target_pairs={{0,16},{16,0},{1,17},{17,1},{2,18},{18,2},{3,19},{19,3},{4,20},{20... | collective-permute-start | bytes 1572872 | tf_op jit(solution)/shard_map/ppermute | solution.py:24
  92.2 2.0 collective-permute-start.7
  94.2 7.4 %copy-start.2 = (bf16[512,1024]{1,0:T(8,128)(2,1)}, bf16[512,1024]{1,0:T(8,128)(2,1)S(1)}, u32[]{:S(2)}) copy-start(bf16[512,1024]{1,0:T(8,128)(2,1)S(1)} %pad_maximum_fusion.3.refs_2_) | copy-start | bytes 3145732
  101.5 8.1 %copy-start.22 = (s32[8,256]{1,0:T(8,128)S(1)}, s32[8,256]{1,0:T(8,128)}, u32[]{:S(2)}) copy-start(s32[8,256]{1,0:T(8,128)} %param.10) | copy-start | bytes 24580
  101.5 8.2 %collective-permute-start.10 = (f32[256,512]{1,0:T(8,128)}, f32[256,512]{1,0:T(8,128)}, u32[]{:S(2)}, u32[]{:S(2)}) collective-permute-start(f32[256,512]{1,0:T(8,128)} %slice.83), channel_id=1, source_target_pairs={{0,1},{1,0},{2,3},{3,2},{4,5},{5,4},{6,7},{7,6},{8,9},{9,8},{10,11... | collective-permute-start | bytes 1572872 | tf_op jit(solution)/shard_map/ppermute | solution.py:28
  109.2 2.5 %collective-permute-start.12 = (f32[256,512]{1,0:T(8,128)}, f32[256,512]{1,0:T(8,128)}, u32[]{:S(2)}, u32[]{:S(2)}) collective-permute-start(f32[256,512]{1,0:T(8,128)} %slice.84), channel_id=1, source_target_pairs={{0,1},{1,0},{2,3},{3,2},{4,5},{5,4},{6,7},{7,6},{8,9},{9,8},{10,11... | collective-permute-start | bytes 1572872 | tf_op jit(solution)/shard_map/ppermute | solution.py:28
  109.7 5.2 %copy-start.16 = (bf16[4,2,256,512]{3,2,1,0:T(8,128)(2,1)S(1)}, bf16[4,2,256,512]{3,2,1,0:T(8,128)(2,1)}, u32[]{:S(2)}) copy-start(bf16[4,2,256,512]{3,2,1,0:T(8,128)(2,1)} %copy-done.15) | copy-start | bytes 6291460
  111.1 11.8 %collective-permute-start.13 = (bf16[4,64,512]{2,1,0:T(8,128)(2,1)S(1)}, bf16[4,64,512]{2,1,0:T(8,128)(2,1)S(1)}, u32[]{:S(2)}, u32[]{:S(2)}) collective-permute-start(bf16[4,64,512]{2,1,0:T(8,128)(2,1)S(1)} %bitcast.76), channel_id=1, source_target_pairs={{0,16},{16,0},{1,17},{17,1},{2,18},{18,2},{3,19},{19,3},{4,20},{20... | collective-permute-start | bytes 786440 | tf_op jit(solution)/shard_map/ppermute | solution.py:24
  113.0 21.3 %collective-permute-start.16 = (bf16[4,64,512]{2,1,0:T(8,128)(2,1)S(1)}, bf16[4,64,512]{2,1,0:T(8,128)(2,1)S(1)}, u32[]{:S(2)}, u32[]{:S(2)}) collective-permute-start(bf16[4,64,512]{2,1,0:T(8,128)(2,1)S(1)} %bitcast.74), channel_id=1, source_target_pairs={{0,16},{16,0},{1,17},{17,1},{2,18},{18,2},{3,19},{19,3},{4,20},{20... | collective-permute-start | bytes 786440 | tf_op jit(solution)/shard_map/ppermute | solution.py:24
  114.9 4.0 %copy-start.14 = (bf16[4,2,256,512]{3,2,1,0:T(8,128)(2,1)S(1)}, bf16[4,2,256,512]{3,2,1,0:T(8,128)(2,1)}, u32[]{:S(2)}) copy-start(bf16[4,2,256,512]{3,2,1,0:T(8,128)(2,1)} %copy-done.13) | copy-start | bytes 6291460
  118.9 4.0 %copy-start.12 = (bf16[4,2,256,512]{3,2,1,0:T(8,128)(2,1)S(1)}, bf16[4,2,256,512]{3,2,1,0:T(8,128)(2,1)}, u32[]{:S(2)}) copy-start(bf16[4,2,256,512]{3,2,1,0:T(8,128)(2,1)} %copy-done.11) | copy-start | bytes 6291460
  126.8 7.4 %copy-start.10 = (bf16[4,2,256,512]{3,2,1,0:T(8,128)(2,1)S(1)}, bf16[4,2,256,512]{3,2,1,0:T(8,128)(2,1)}, u32[]{:S(2)}) copy-start(bf16[4,2,256,512]{3,2,1,0:T(8,128)(2,1)} %copy-done.9) | copy-start | bytes 6291460
  126.8 12.8 %collective-permute-start.14 = (bf16[4,64,512]{2,1,0:T(8,128)(2,1)S(1)}, bf16[4,64,512]{2,1,0:T(8,128)(2,1)S(1)}, u32[]{:S(2)}, u32[]{:S(2)}) collective-permute-start(bf16[4,64,512]{2,1,0:T(8,128)(2,1)S(1)} %get-tuple-element.76), channel_id=1, source_target_pairs={{0,16},{16,0},{1,17},{17,1},{2,18},{18,2},{3,19},{19,3},{4,20},{20... | collective-permute-start | bytes 786440 | tf_op jit(solution)/shard_map/ppermute | solution.py:24
  134.2 5.5 %copy-start.3 = (bf16[512,1024]{1,0:T(8,128)(2,1)S(1)}, bf16[512,1024]{1,0:T(8,128)(2,1)}, u32[]{:S(2)}) copy-start(bf16[512,1024]{1,0:T(8,128)(2,1)} %copy-done.2) | copy-start | bytes 3145732
  138.2 8.8 %collective-permute-start.17 = (bf16[4,64,512]{2,1,0:T(8,128)(2,1)S(1)}, bf16[4,64,512]{2,1,0:T(8,128)(2,1)S(1)}, u32[]{:S(2)}, u32[]{:S(2)}) collective-permute-start(bf16[4,64,512]{2,1,0:T(8,128)(2,1)S(1)} %get-tuple-element.82), channel_id=1, source_target_pairs={{0,16},{16,0},{1,17},{17,1},{2,18},{18,2},{3,19},{19,3},{4,20},{20... | collective-permute-start | bytes 786440 | tf_op jit(solution)/shard_map/ppermute | solution.py:24
  139.6 1.6 collective-permute-start.15
  140.3 6.7 %copy-start.17 = (bf16[4,512,1024]{2,1,0:T(8,128)(2,1)}, bf16[4,512,1024]{2,1,0:T(8,128)(2,1)S(1)}, u32[]{:S(2)}) copy-start(bf16[4,512,1024]{2,1,0:T(8,128)(2,1)S(1)} %pad_maximum_fusion) | copy-start | bytes 12582916
  140.3 8.3 %copy-start.20 = (bf16[1024,1024]{1,0:T(8,128)(2,1)S(1)}, bf16[1024,1024]{1,0:T(8,128)(2,1)}, u32[]{:S(2)}) copy-start(bf16[1024,1024]{1,0:T(8,128)(2,1)} %dynamic-slice_bitcast_fusion) | copy-start | bytes 6291460
  141.2 5.7 %copy-start.24 = (bf16[256,512]{1,0:T(8,128)(2,1)}, bf16[256,512]{1,0:T(8,128)(2,1)S(1)}, u32[]{:S(2)}) copy-start(bf16[256,512]{1,0:T(8,128)(2,1)S(1)} %collective-permute-done.15) | copy-start | bytes 786436
  147.0 1.6 collective-permute-start.18
  147.2 25.7 %collective-permute-start.21 = (bf16[1024,512]{1,0:T(8,128)(2,1)}, bf16[1024,512]{1,0:T(8,128)(2,1)S(1)}, u32[]{:S(2)}, u32[]{:S(2)}) collective-permute-start(bf16[1024,512]{1,0:T(8,128)(2,1)} %convolution_convert_fusion.5), channel_id=1, source_target_pairs={{0,2},{1,3},{2,0},{3,1},{4,6},{5,7},{6,4},{7,5},{8,10},{9,11},{10,... | collective-permute-start | bytes 3145736 | tf_op jit(solution)/shard_map/ppermute | solution.py:24
  148.6 2.5 %copy-start.18 = (bf16[4,512,1024]{2,1,0:T(8,128)(2,1)S(1)}, bf16[4,512,1024]{2,1,0:T(8,128)(2,1)}, u32[]{:S(2)}) copy-start(bf16[4,512,1024]{2,1,0:T(8,128)(2,1)} %copy-done.17) | copy-start | bytes 12582916
  151.1 5.0 %copy-start.25 = (bf16[256,512]{1,0:T(8,128)(2,1)S(1)}, bf16[256,512]{1,0:T(8,128)(2,1)}, u32[]{:S(2)}) copy-start(bf16[256,512]{1,0:T(8,128)(2,1)} %copy-done.24) | copy-start | bytes 786436
  151.9 25.3 %collective-permute-start.22 = (bf16[1024,512]{1,0:T(8,128)(2,1)S(1)}, bf16[1024,512]{1,0:T(8,128)(2,1)S(1)}, u32[]{:S(2)}, u32[]{:S(2)}) collective-permute-start(bf16[1024,512]{1,0:T(8,128)(2,1)S(1)} %convolution_convert_fusion.4), channel_id=1, source_target_pairs={{0,16},{16,0},{1,17},{17,1},{2,18},{18,2},{3,19},{19,3},{4,20},{20... | collective-permute-start | bytes 3145736 | tf_op jit(solution)/shard_map/ppermute | solution.py:24
  152.3 24.9 %collective-permute-start.19 = (bf16[256,1024]{1,0:T(8,128)(2,1)S(1)}, bf16[256,1024]{1,0:T(8,128)(2,1)S(1)}, u32[]{:S(2)}, u32[]{:S(2)}) collective-permute-start(bf16[256,1024]{1,0:T(8,128)(2,1)S(1)} %get-tuple-element.111), channel_id=1, source_target_pairs={{0,4},{4,8},{8,12},{12,0},{1,5},{5,9},{9,13},{13,1},{2,6},{6,10},{... | collective-permute-start | bytes 1572872 | tf_op jit(solution)/shard_map/ppermute | solution.py:24
  154.1 24.7 %collective-permute-start.20 = (bf16[256,1024]{1,0:T(8,128)(2,1)S(1)}, bf16[256,1024]{1,0:T(8,128)(2,1)S(1)}, u32[]{:S(2)}, u32[]{:S(2)}) collective-permute-start(bf16[256,1024]{1,0:T(8,128)(2,1)S(1)} %get-tuple-element.110), channel_id=1, source_target_pairs={{0,12},{4,0},{8,4},{12,8},{1,13},{5,1},{9,5},{13,9},{2,14},{6,2},{... | collective-permute-start | bytes 1572872 | tf_op jit(solution)/shard_map/ppermute | solution.py:24
  168.7 16.4 %copy-start.6 = (bf16[512,1024]{1,0:T(8,128)(2,1)}, bf16[512,1024]{1,0:T(8,128)(2,1)S(1)}, u32[]{:S(2)}) copy-start(bf16[512,1024]{1,0:T(8,128)(2,1)S(1)} %fusion.9.own_ref) | copy-start | bytes 3145732
  179.4 50.0 %collective-permute-start.26 = (bf16[1024,1024]{1,0:T(8,128)(2,1)S(1)}, bf16[1024,1024]{1,0:T(8,128)(2,1)S(1)}, u32[]{:S(2)}, u32[]{:S(2)}) collective-permute-start(bf16[1024,1024]{1,0:T(8,128)(2,1)S(1)} %fusion.19), channel_id=1, source_target_pairs={{0,2},{1,3},{2,0},{3,1},{4,6},{5,7},{6,4},{7,5},{8,10},{9,11},{10,... | collective-permute-start | bytes 6291464 | tf_op jit(solution)/shard_map/ppermute | solution.py:24
  180.7 48.7 %collective-permute-start.25 = (bf16[1024,1024]{1,0:T(8,128)(2,1)S(1)}, bf16[1024,1024]{1,0:T(8,128)(2,1)S(1)}, u32[]{:S(2)}, u32[]{:S(2)}) collective-permute-start(bf16[1024,1024]{1,0:T(8,128)(2,1)S(1)} %fusion.18), channel_id=1, source_target_pairs={{0,16},{16,0},{1,17},{17,1},{2,18},{18,2},{3,19},{19,3},{4,20},{20... | collective-permute-start | bytes 6291464 | tf_op jit(solution)/shard_map/ppermute | solution.py:24
  182.7 46.6 %collective-permute-start.24 = (bf16[512,1024]{1,0:T(8,128)(2,1)S(1)}, bf16[512,1024]{1,0:T(8,128)(2,1)S(1)}, u32[]{:S(2)}, u32[]{:S(2)}) collective-permute-start(bf16[512,1024]{1,0:T(8,128)(2,1)S(1)} %fusion.31), channel_id=1, source_target_pairs={{0,12},{4,0},{8,4},{12,8},{1,13},{5,1},{9,5},{13,9},{2,14},{6,2},{... | collective-permute-start | bytes 3145736 | tf_op jit(solution)/shard_map/ppermute | solution.py:24
  185.0 44.3 %collective-permute-start.23 = (bf16[512,1024]{1,0:T(8,128)(2,1)S(1)}, bf16[512,1024]{1,0:T(8,128)(2,1)S(1)}, u32[]{:S(2)}, u32[]{:S(2)}) collective-permute-start(bf16[512,1024]{1,0:T(8,128)(2,1)S(1)} %fusion.30), channel_id=1, source_target_pairs={{0,4},{4,8},{8,12},{12,0},{1,5},{5,9},{9,13},{13,1},{2,6},{6,10},{... | collective-permute-start | bytes 3145736 | tf_op jit(solution)/shard_map/ppermute | solution.py:24
  231.7 2.3 copy-start.7
  231.9 2.0 collective-permute-start.27
  (7 other events, 9.7 us)

commit v11 on v10

--- a/solution.py
+++ b/solution.py
@@ -93,7 +93,7 @@
         in_specs=[pl.BlockSpec(memory_space=pltpu.SMEM)]
         + [pl.BlockSpec(memory_space=pltpu.VMEM)] * (count + 1),
         out_specs=pl.BlockSpec(memory_space=pltpu.VMEM),
-        compiler_params=pltpu.CompilerParams(vmem_limit_bytes=16 * 1024 * 1024),
+        compiler_params=pltpu.CompilerParams(vmem_limit_bytes=4 * 1024 * 1024),
         cost_estimate=pl.CostEstimate(
             flops=2 * rows * count * depth * width,
             bytes_accessed=2 * count * depth * (rows + width) + 4 * rows * width,
@@ -189,7 +189,7 @@
             jax.ShapeDtypeStruct((capacity, 2, keys, 2 * width), BF16),
         ],
         input_output_aliases=aliases,
-        compiler_params=pltpu.CompilerParams(vmem_limit_bytes=12 * 1024 * 1024),
+        compiler_params=pltpu.CompilerParams(vmem_limit_bytes=6 * 1024 * 1024),
         cost_estimate=pl.CostEstimate(
             flops=count * heads * 5 * 2 * SPAN * keys * HD * 4,
             bytes_accessed=count * 4 * keys * width * 2,
@@ -219,36 +219,11 @@
             out_specs=[half_block, half_block],
         ),
         out_shape=[half_shape, half_shape],
-        compiler_params=pltpu.CompilerParams(vmem_limit_bytes=12 * 1024 * 1024),
+        compiler_params=pltpu.CompilerParams(vmem_limit_bytes=8 * 1024 * 1024),
         cost_estimate=pl.CostEstimate(
             flops=0, bytes_accessed=8 * count * keys * width, transcendentals=0
         ),
     )(jnp.reshape(source, (1,)).astype(jnp.int32), kv)
-
-
-def pick_kernel(depth, which_ref, *refs):
-    out_ref = refs[-1]
-    rows = refs[0].shape[0]
-    for n, ref in enumerate(refs[:-1]):
-        for p in range(out_ref.shape[1] // depth):
-            start = pl.multiple_of((2 * p + which_ref[0]) * depth, depth)
-            out_ref[n * rows:(n + 1) * rows, p * depth:(p + 1) * depth] = ref[:, pl.ds(start, depth)]
-
-
-def picked(blocks, which, depth):
-    rows, columns = blocks[0].shape
-    shape = (len(blocks) * rows, columns // 2)
-    return pl.pallas_call(
-        functools.partial(pick_kernel, depth),
-        in_specs=[pl.BlockSpec(memory_space=pltpu.SMEM)]
-        + [pl.BlockSpec(memory_space=pltpu.VMEM)] * len(blocks),
-        out_specs=pl.BlockSpec(memory_space=pltpu.VMEM),
-        out_shape=jax.ShapeDtypeStruct(shape, BF16),
-        compiler_params=pltpu.CompilerParams(vmem_limit_bytes=16 * 1024 * 1024),
-        cost_estimate=pl.CostEstimate(
-            flops=0, bytes_accessed=4 * shape[0] * shape[1], transcendentals=0
-        ),
-    )(jnp.reshape(which, (1,)).astype(jnp.int32), *blocks)
 
 
 def total_kernel(tile, *refs):
@@ -275,7 +250,7 @@
             pltpu.VMEM((rows, columns), F32),
             pltpu.SemaphoreType.DMA((rows // tile,)),
         ],
-        compiler_params=pltpu.CompilerParams(vmem_limit_bytes=16 * 1024 * 1024),
+        compiler_params=pltpu.CompilerParams(vmem_limit_bytes=6 * 1024 * 1024),
         cost_estimate=pl.CostEstimate(
             flops=len(values) * rows * columns,
             bytes_accessed=(2 * len(values) + 4) * rows * columns,
@@ -304,7 +279,7 @@
         in_specs=[pl.BlockSpec(memory_space=pltpu.SMEM)] + [block] * 4,
         out_specs=pl.BlockSpec((tile, 2 * columns), lambda r: (r, 0)),
         out_shape=jax.ShapeDtypeStruct((rows, 2 * columns), BF16),
-        compiler_params=pltpu.CompilerParams(vmem_limit_bytes=16 * 1024 * 1024),
+        compiler_params=pltpu.CompilerParams(vmem_limit_bytes=4 * 1024 * 1024),
         cost_estimate=pl.CostEstimate(
             flops=2 * rows * columns, bytes_accessed=12 * rows * columns, transcendentals=0
         ),
@@ -387,7 +362,7 @@
             axis=1,
         )
 
-    others = swap(picked([raw[k] for k in near], 1 - core, depth))
+    others = swap(jnp.concatenate([columns_of(raw[k], 1 - core) for k in near], axis=0))
     up, down, others = lax.optimization_barrier((up, down, others))
     raw[opposite] = jnp.concatenate([up, down], axis=0)
     others = {k: others[n * rows:(n + 1) * rows] for n, k in enumerate(near)}
@@ -476,8 +451,8 @@
     both_grads, corners = [], []
     corner_places = [(i, j) for i in range(1, seq_count) for j in range(1, couples)]
     for part in range(2):
-        ahead = corners[0][corner_places[-1]] if part else far_weights
-        answers[part][-1] = after(answers[part][-1], ahead)
+        if part:
+            answers[1][-1] = after(answers[1][-1], corners[0][corner_places[-1]])
         grad = sum(answers[part][1:], answers[part][0])
         both_grads.append(jnp.concatenate([grad, swap(grad)], axis=0))
         if part == 0:

time: 237 us -> 226 us (0.954)
  matrix products: 17.4 us -> 10.7 us
  starting transfers between devices: 31.9 us -> 27.3 us
  Pallas kernels: 32.2 us -> 28.2 us
  waiting for transfers between devices: 108 us -> 112 us
    dot_general x9, matrix products: 17.4 us -> 10.7 us  [dot(): lax.dot_general(a, b, (contract, ((), ())), preferred_element_type=F32)]
    pallas_call x2, Pallas kernels: 11.8 us -> 5.77 us  [product(): pl.pallas_call(functools.partial(product_kernel, count, start), out_shape...]
    ppermute x21, waiting for transfers between devices: 103 us -> 109 us  [shift(): lax.ppermute(value, axis, [(i, (i + step * stride) % size) for i in range...]
    ppermute x21, starting transfers between devices: 31 us -> 26.4 us  [shift(): lax.ppermute(value, axis, [(i, (i + step * stride) % size) for i in range...]
    unnamed x53 -> x77, local copies, waits for them, and re-layouts: 12 us -> 16.6 us
    broadcast_in_dim x1, local copies, waits for them, and re-layouts: 4.38 us -> 1.06 us  [on_device(): weights = jnp.zeros((tensor_count, per * depth, width), BF16)]
    dynamic_slice x3, local copies, waits for them, and re-layouts: 0.19 us -> 3.33 us  [columns_of(): lax.dynamic_slice(block, (0, (2 * p + which) * depth), (block.shape[0], d...]
    convert_element_type x2, other arithmetic: 2.69 us -> 0.2 us  [on_device(): queries.append((partial[:rows] + arrived).astype(BF16))]
  transfers between devices with their start and end apart: 28 -> 28, of which waited for: 13 -> 12; matrix products, arithmetic and copies ran while one was open for 20% -> 16% of each run, Pallas kernels for 12% -> 11%
where the time goes in v11:
time: 226 us; the launch traced here: 225 us
  waiting for transfers between devices  112 us (50%)
  local copies, waits for them, and re-layouts  39.2 us (17%)
  Pallas kernels  28.2 us (12%)
  starting transfers between devices  27.3 us (12%)
  matrix products  10.7 us (5%)
  other arithmetic  6.01 us (3%)
    ppermute x21, waiting for transfers between devices, shift(): lax.ppermute(value, axis, [(i, (i + step * stride) % size) for i in range...  109 us
    ppermute x21, starting transfers between devices, shift(): lax.ppermute(value, axis, [(i, (i + step * stride) % size) for i in range...  26.4 us
    pallas_call x4, Pallas kernels, attend(): pl.pallas_call(attend_kernel, grid_spec=pltpu.PrefetchScalarGridSpec(num_...  18 us
    unnamed x77, local copies, waits for them, and re-layouts  16.6 us
    dot_general x9, matrix products, dot(): lax.dot_general(a, b, (contract, ((), ())), preferred_element_type=F32)  10.7 us
    dynamic_update_slice x5, local copies, waits for them, and re-layouts, on_device(): lax.dynamic_update_slice(weights, piece[None], (at, inner * depth, start))  9.7 us
    pallas_call x2, Pallas kernels, product(): pl.pallas_call(functools.partial(product_kernel, count, start), out_shape...  5.77 us
  transfers between devices with their start and end apart: 28, of which 12 were waited for; matrix products, arithmetic and copies ran while one was open for 16% of the time, Pallas kernels for 11%

profile of v11, /device:TPU:0, one launch (start us, length us, event | category | flops | bytes accessed | tf_op | source)
XLA Modules:
  0.0 225.2 jit_solution(5309331407367929351)
XLA Ops:
  0.6 3.0 %collective-permute-start = (bf16[1024,1024]{1,0:T(8,128)(2,1)}, bf16[1024,1024]{1,0:T(8,128)(2,1)S(1)}, u32[]{:S(2)}, u32[]{:S(2)}) collective-permute-start(bf16[1024,1024]{1,0:T(8,128)(2,1)} %param.7), channel_id=1, source_target_pairs={{0,16},{16,0},{1,17},{17,1},{2,18},{18,2},{3,19},{19,3},{4,20},{20... | collective-permute-start | bytes 6291464 | tf_op jit(solution)/shard_map/ppermute | solution.py:24
  3.6 1.5 collective-permute-start.1
  5.2 1.6 collective-permute-start.2
  6.7 2.2 collective-permute-start.3
  9.0 3.4 %copy-done.1 = bf16[8,2,256,1024]{3,2,1,0:T(8,128)(2,1)S(1)} copy-done((bf16[8,2,256,1024]{3,2,1,0:T(8,128)(2,1)S(1)}, bf16[8,2,256,1024]{3,2,1,0:T(8,128)(2,1)}, u32[]{:S(2)}) %copy-start.1) | copy-done | bytes 8388632
  14.0 1.3 copy-done.12
  15.7 1.4 copy-done.14
  17.1 1.3 copy-done.21
  20.9 12.4 %collective-permute-done.2 = bf16[256,2048]{1,0:T(8,128)(2,1)S(1)} collective-permute-done((bf16[256,2048]{1,0:T(8,128)(2,1)}, bf16[256,2048]{1,0:T(8,128)(2,1)S(1)}, u32[]{:S(2)}, u32[]{:S(2)}) %collective-permute-start.2) | collective-permute-done | bytes 1048608 | tf_op jit(solution)/shard_map/ppermute | solution.py:24
  33.3 20.3 %collective-permute-done.3 = bf16[256,2048]{1,0:T(8,128)(2,1)} collective-permute-done((bf16[256,2048]{1,0:T(8,128)(2,1)}, bf16[256,2048]{1,0:T(8,128)(2,1)}, u32[]{:S(2)}, u32[]{:S(2)}) %collective-permute-start.3) | collective-permute-done | bytes 1048608 | tf_op jit(solution)/shard_map/ppermute | solution.py:24
  54.8 2.1 slice.81
  57.4 2.4 %constant_dynamic-slice_fusion.1 = (bf16[256,1024]{1,0:T(8,128)(2,1)}, bf16[256,1024]{1,0:T(8,128)(2,1)S(1)}, bf16[256,1024]{1,0:T(8,128)(2,1)S(1)}, bf16[256,1024]{1,0:T(8,128)(2,1)}) fusion(bf16[256,2048]{1,0:T(8,128)(2,1)} %collective-permute-done.3, s32[]{:T(128)S(6)} %select_n.234, s32[]{:T(128)S(6)} %select_n.235, ...), kind=kLoop, calls=%fused_computation.68 | loop fusion | bytes 4194312 | tf_op jit(solution)/shard_map/dynamic_slice | solution.py:359
  65.1 2.7 %collective-permute-start.5 = (bf16[128,2048]{1,0:T(8,128)(2,1)S(1)}, bf16[128,2048]{1,0:T(8,128)(2,1)S(1)}, u32[]{:S(2)}, u32[]{:S(2)}) collective-permute-start(bf16[128,2048]{1,0:T(8,128)(2,1)S(1)} %slice.63), channel_id=1, source_target_pairs={{0,12},{4,0},{8,4},{12,8},{1,13},{5,1},{9,5},{13,9},{2,14},{6,2},{... | collective-permute-start | bytes 1572872 | tf_op jit(solution)/shard_map/ppermute | solution.py:24
  67.8 3.1 %bitcast_dynamic-update-slice_fusion.1 = bf16[4,1024,1024]{2,1,0:T(8,128)(2,1)} fusion(bf16[4,1024,1024]{2,1,0:T(8,128)(2,1)} %copy-done, s32[]{:T(128)S(6)} %select_n.242, bf16[1024,1024]{1,0:T(8,128)(2,1)} %collective-permute-done.1), kind=kLoop, calls=%fused_computation.8 | loop fusion | bytes 4194308 | tf_op jit(solution)/shard_map/dynamic_update_slice | solution.py:391
  70.9 1.5 bitcast_dynamic-update-slice_fusion
  72.4 9.7 %collective-permute-done.9 = bf16[1024,384]{1,0:T(8,128)(2,1)} collective-permute-done((bf16[1024,384]{1,0:T(8,128)(2,1)}, bf16[1024,384]{1,0:T(8,128)(2,1)}, u32[]{:S(2)}, u32[]{:S(2)}) %collective-permute-start.9) | collective-permute-done | bytes 786464 | tf_op jit(solution)/shard_map/ppermute | solution.py:24
  82.7 4.5 %collective-permute-done.8 = bf16[1024,640]{1,0:T(8,128)(2,1)} collective-permute-done((bf16[1024,640]{1,0:T(8,128)(2,1)}, bf16[1024,640]{1,0:T(8,128)(2,1)}, u32[]{:S(2)}, u32[]{:S(2)}) %collective-permute-start.8) | collective-permute-done | bytes 1310752 | tf_op jit(solution)/shard_map/ppermute | solution.py:24
  87.2 2.6 %bitcast_dynamic-update-slice_fusion.3 = bf16[4,1024,1024]{2,1,0:T(8,128)(2,1)} fusion(bf16[4,1024,1024]{2,1,0:T(8,128)(2,1)} %bitcast_dynamic-update-slice_fusion, s32[]{:T(128)S(6)} %select_n.246, bf16[1024,640]{1,0:T(8,128)(2,1)} %collective-permute-done.8), kind=kLoop, calls=%fused_computation.26 | loop fusion | bytes 2621444 | tf_op jit(solution)/shard_map/dynamic_update_slice | solution.py:391
  89.8 2.2 bitcast_dynamic-update-slice_fusion.4.refs_4_
  92.3 1.6 fusion.51
  95.3 1.7 slice-done.1
  97.0 2.9 %shard_map.87 = f32[512,512]{1,0:T(8,128)S(1)} custom-call(s32[4]{0:T(128)S(1)} %pad_add_fusion.1.table_ref, bf16[512,1024]{1,0:T(8,128)(2,1)S(1)} %pad_maximum_fusion.2.refs_0_, bf16[512,1024]{1,0:T(8,128)(2,1)S(1)} %pad_maximum_fusion.3.refs_1_, bf16[512,1024]{1,0:T(8,128)(2,1)S(1)} %pad_maximum_fusion.4.refs_2_, ...), custom_call_target="tpu_custom_call" | custom-call | flops 2147483648 | bytes 9437184 | tf_op jit(solution)/shard_map/pallas_call | solution.py:90
  100.1 2.9 %shard_map.88 = f32[512,512]{1,0:T(8,128)S(1)} custom-call(s32[4]{0:T(128)S(1)} %pad_add_fusion.1.table_ref, bf16[512,1024]{1,0:T(8,128)(2,1)S(1)} %pad_maximum_fusion.2.refs_0_, bf16[512,1024]{1,0:T(8,128)(2,1)S(1)} %pad_maximum_fusion.3.refs_1_, bf16[512,1024]{1,0:T(8,128)(2,1)S(1)} %pad_maximum_fusion.4.refs_2_, ...), custom_call_target="tpu_custom_call" | custom-call | flops 2147483648 | bytes 9437184 | tf_op jit(solution)/shard_map/pallas_call | solution.py:90
  106.4 4.2 %shard_map.89 = (bf16[4,64,512]{2,1,0:T(8,128)(2,1)S(1)}, bf16[8,2,256,1024]{3,2,1,0:T(8,128)(2,1)}) custom-call(s32[12]{0:T(128)S(1)} %pad_add_fusion.table_ref, bf16[4,64,512]{2,1,0:T(8,128)(2,1)S(1)} %bitcast.81, bf16[4,64,1024]{2,1,0:T(8,128)(2,1)S(1)} %bitcast.78, f32[8,256,128]{2,1,0:T(8,128)S(1)} %broadcast_in_dim.20.live_ref, ...), custom_call_target="tpu_custom_call" | custom-call | flops 1342177280 | bytes 4194304 | tf_op jit(solution)/shard_map/pallas_call | solution.py:179
  110.6 4.2 %shard_map.90 = (bf16[4,64,512]{2,1,0:T(8,128)(2,1)S(1)}, bf16[8,2,256,1024]{3,2,1,0:T(8,128)(2,1)}) custom-call(s32[12]{0:T(128)S(1)} %pad_add_fusion.table_ref, bf16[4,64,512]{2,1,0:T(8,128)(2,1)S(1)} %bitcast.76, bf16[4,64,1024]{2,1,0:T(8,128)(2,1)S(1)} %bitcast.79, ...), custom_call_target="tpu_custom_call", output_to_operand_aliasing={{1}: (5, {})} | custom-call | flops 1342177280 | bytes 4194304 | tf_op jit(solution)/shard_map/pallas_call | solution.py:179
  114.8 4.3 %shard_map.91 = (bf16[4,64,512]{2,1,0:T(8,128)(2,1)}, bf16[8,2,256,1024]{3,2,1,0:T(8,128)(2,1)}) custom-call(s32[12]{0:T(128)S(1)} %pad_add_fusion.2.table_ref, bf16[4,64,512]{2,1,0:T(8,128)(2,1)S(1)} %collective-permute-done.13.q_ref, bf16[4,64,1024]{2,1,0:T(8,128)(2,1)S(1)} %collective-permute-done.11.g_ref, ...), custom_call_target="tpu_custom_call", output_to_operand_aliasing={{1}: (5, {})} | custom-call | flops 1342177280 | bytes 4194304 | tf_op jit(solution)/shard_map/pallas_call | solution.py:179
  120.1 1.6 copy-done.11
  121.7 5.3 %shard_map.92 = (bf16[4,64,512]{2,1,0:T(8,128)(2,1)S(1)}, bf16[8,2,256,1024]{3,2,1,0:T(8,128)(2,1)}) custom-call(s32[12]{0:T(128)S(1)} %pad_add_fusion.2.table_ref, bf16[4,64,512]{2,1,0:T(8,128)(2,1)} %collective-permute-done.16.q_ref, bf16[4,64,1024]{2,1,0:T(8,128)(2,1)S(1)} %copy-done.9, ...), custom_call_target="tpu_custom_call", output_to_operand_aliasing={{1}: (5, {})} | custom-call | flops 1342177280 | bytes 4194304 | tf_op jit(solution)/shard_map/pallas_call | solution.py:179
  131.2 3.9 %collective-permute-done.17 = bf16[4,64,512]{2,1,0:T(8,128)(2,1)S(1)} collective-permute-done((bf16[4,64,512]{2,1,0:T(8,128)(2,1)S(1)}, bf16[4,64,512]{2,1,0:T(8,128)(2,1)S(1)}, u32[]{:S(2)}, u32[]{:S(2)}) %collective-permute-start.17) | collective-permute-done | bytes 262176 | tf_op jit(solution)/shard_map/ppermute | solution.py:24
  135.4 1.8 dynamic-slice_bitcast_fusion
  137.8 1.3 convolution_convert_fusion.3
  140.7 1.6 collective-permute-start.22
  142.3 1.8 collective-permute-start.19
  144.1 2.0 collective-permute-start.20
  147.5 1.3 convolution_convert_fusion.1
  149.9 1.3 fusion.15
  151.2 1.3 convolution_convert_fusion.2.refs_0_
  152.5 1.3 fusion.12
  153.9 1.3 fusion.9.own_ref
  155.2 7.5 %collective-permute-done.21 = bf16[1024,512]{1,0:T(8,128)(2,1)S(1)} collective-permute-done((bf16[1024,512]{1,0:T(8,128)(2,1)S(1)}, bf16[1024,512]{1,0:T(8,128)(2,1)S(1)}, u32[]{:S(2)}, u32[]{:S(2)}) %collective-permute-start.21) | collective-permute-done | bytes 1048608 | tf_op jit(solution)/shard_map/ppermute | solution.py:24
  162.7 3.2 %collective-permute-done.22 = bf16[1024,512]{1,0:T(8,128)(2,1)S(1)} collective-permute-done((bf16[1024,512]{1,0:T(8,128)(2,1)S(1)}, bf16[1024,512]{1,0:T(8,128)(2,1)S(1)}, u32[]{:S(2)}, u32[]{:S(2)}) %collective-permute-start.22) | collective-permute-done | bytes 1048608 | tf_op jit(solution)/shard_map/ppermute | solution.py:24
  165.9 2.8 %collective-permute-done.20 = bf16[256,1024]{1,0:T(8,128)(2,1)S(1)} collective-permute-done((bf16[256,1024]{1,0:T(8,128)(2,1)S(1)}, bf16[256,1024]{1,0:T(8,128)(2,1)S(1)}, u32[]{:S(2)}, u32[]{:S(2)}) %collective-permute-start.20) | collective-permute-done | bytes 524320 | tf_op jit(solution)/shard_map/ppermute | solution.py:24
  170.5 1.6 collective-permute-start.25
  172.4 2.1 collective-permute-start.24
  174.8 44.2 %collective-permute-done.24.down_ref = bf16[512,1024]{1,0:T(8,128)(2,1)S(1)} collective-permute-done((bf16[512,1024]{1,0:T(8,128)(2,1)S(1)}, bf16[512,1024]{1,0:T(8,128)(2,1)S(1)}, u32[]{:S(2)}, u32[]{:S(2)}) %collective-permute-start.24) | collective-permute-done | bytes 1048608 | tf_op jit(solution)/shard_map/ppermute | solution.py:24
  219.2 2.2 shard_map.93
  221.7 1.9 collective-permute-done.27.arrived_ref
  223.6 1.6 shard_map.94
  (158 shorter events, 29.3 us)
Async XLA Ops:
  0.6 52.9 %collective-permute-start = (bf16[1024,1024]{1,0:T(8,128)(2,1)}, bf16[1024,1024]{1,0:T(8,128)(2,1)S(1)}, u32[]{:S(2)}, u32[]{:S(2)}) collective-permute-start(bf16[1024,1024]{1,0:T(8,128)(2,1)} %param.7), channel_id=1, source_target_pairs={{0,16},{16,0},{1,17},{17,1},{2,18},{18,2},{3,19},{19,3},{4,20},{20... | collective-permute-start | bytes 6291464 | tf_op jit(solution)/shard_map/ppermute | solution.py:24
  3.6 51.2 %collective-permute-start.1 = (bf16[1024,1024]{1,0:T(8,128)(2,1)}, bf16[1024,1024]{1,0:T(8,128)(2,1)}, u32[]{:S(2)}, u32[]{:S(2)}) collective-permute-start(bf16[1024,1024]{1,0:T(8,128)(2,1)} %param.7), channel_id=1, source_target_pairs={{0,2},{1,3},{2,0},{3,1},{4,6},{5,7},{6,4},{7,5},{8,10},{9,11},{10,... | collective-permute-start | bytes 6291464 | tf_op jit(solution)/shard_map/ppermute | solution.py:24
  5.2 28.2 %collective-permute-start.2 = (bf16[256,2048]{1,0:T(8,128)(2,1)}, bf16[256,2048]{1,0:T(8,128)(2,1)S(1)}, u32[]{:S(2)}, u32[]{:S(2)}) collective-permute-start(bf16[256,2048]{1,0:T(8,128)(2,1)} %param.6), channel_id=1, source_target_pairs={{0,4},{4,8},{8,12},{12,0},{1,5},{5,9},{9,13},{13,1},{2,6},{6,10},{... | collective-permute-start | bytes 3145736 | tf_op jit(solution)/shard_map/ppermute | solution.py:24
  6.7 46.8 %collective-permute-start.3 = (bf16[256,2048]{1,0:T(8,128)(2,1)}, bf16[256,2048]{1,0:T(8,128)(2,1)}, u32[]{:S(2)}, u32[]{:S(2)}) collective-permute-start(bf16[256,2048]{1,0:T(8,128)(2,1)} %param.6), channel_id=1, source_target_pairs={{0,12},{4,0},{8,4},{12,8},{1,13},{5,1},{9,5},{13,9},{2,14},{6,2},{... | collective-permute-start | bytes 3145736 | tf_op jit(solution)/shard_map/ppermute | solution.py:24
  9.0 3.4 %copy-start.1 = (bf16[8,2,256,1024]{3,2,1,0:T(8,128)(2,1)S(1)}, bf16[8,2,256,1024]{3,2,1,0:T(8,128)(2,1)}, u32[]{:S(2)}) copy-start(bf16[8,2,256,1024]{3,2,1,0:T(8,128)(2,1)} %kv_ref.3) | copy-start | bytes 25165828
  15.3 3.1 %copy-start.31 = (s32[32]{0:T(128)S(1)}, s32[32]{0:T(128)}, u32[]{:S(2)}) copy-start(s32[32]{0:T(128)} %param.11) | copy-start | bytes 388
  20.9 41.0 %copy-start = (bf16[4,1024,1024]{2,1,0:T(8,128)(2,1)}, bf16[4,1024,1024]{2,1,0:T(8,128)(2,1)S(1)}, u32[]{:S(2)}) copy-start(bf16[4,1024,1024]{2,1,0:T(8,128)(2,1)S(1)} %bitcast_dynamic-update-slice_fusion.2) | copy-start | bytes 25165828
  56.9 30.3 %collective-permute-start.8 = (bf16[1024,640]{1,0:T(8,128)(2,1)}, bf16[1024,640]{1,0:T(8,128)(2,1)}, u32[]{:S(2)}, u32[]{:S(2)}) collective-permute-start(bf16[1024,640]{1,0:T(8,128)(2,1)} %slice.80), channel_id=1, source_target_pairs={{0,2},{1,3},{2,0},{3,1},{4,6},{5,7},{6,4},{7,5},{8,10},{9,11},{10,... | collective-permute-start | bytes 3932168 | tf_op jit(solution)/shard_map/ppermute | solution.py:24
  61.9 30.1 %collective-permute-start.6 = (bf16[768,1024]{1,0:T(8,128)(2,1)}, bf16[768,1024]{1,0:T(8,128)(2,1)}, u32[]{:S(2)}, u32[]{:S(2)}) collective-permute-start(bf16[768,1024]{1,0:T(8,128)(2,1)} %pad_maximum_fusion.1), channel_id=1, source_target_pairs={{0,1},{1,0},{2,3},{3,2},{4,5},{5,4},{6,7},{7,6},{8,9},{9,8},{10,11... | collective-permute-start | bytes 4718600 | tf_op jit(solution)/shard_map/ppermute | solution.py:28
  61.9 20.3 %collective-permute-start.9 = (bf16[1024,384]{1,0:T(8,128)(2,1)}, bf16[1024,384]{1,0:T(8,128)(2,1)}, u32[]{:S(2)}, u32[]{:S(2)}) collective-permute-start(bf16[1024,384]{1,0:T(8,128)(2,1)} %slice.81), channel_id=1, source_target_pairs={{0,16},{16,0},{1,17},{17,1},{2,18},{18,2},{3,19},{19,3},{4,20},{20... | collective-permute-start | bytes 2359304 | tf_op jit(solution)/shard_map/ppermute | solution.py:24
  63.9 28.1 %collective-permute-start.4 = (bf16[128,2048]{1,0:T(8,128)(2,1)S(1)}, bf16[128,2048]{1,0:T(8,128)(2,1)S(1)}, u32[]{:S(2)}, u32[]{:S(2)}) collective-permute-start(bf16[128,2048]{1,0:T(8,128)(2,1)S(1)} %slice.62), channel_id=1, source_target_pairs={{0,4},{4,8},{8,12},{12,0},{1,5},{5,9},{9,13},{13,1},{2,6},{6,10},{... | collective-permute-start | bytes 1572872 | tf_op jit(solution)/shard_map/ppermute | solution.py:24
  65.1 26.9 %collective-permute-start.5 = (bf16[128,2048]{1,0:T(8,128)(2,1)S(1)}, bf16[128,2048]{1,0:T(8,128)(2,1)S(1)}, u32[]{:S(2)}, u32[]{:S(2)}) collective-permute-start(bf16[128,2048]{1,0:T(8,128)(2,1)S(1)} %slice.63), channel_id=1, source_target_pairs={{0,12},{4,0},{8,4},{12,8},{1,13},{5,1},{9,5},{13,9},{2,14},{6,2},{... | collective-permute-start | bytes 1572872 | tf_op jit(solution)/shard_map/ppermute | solution.py:24
  70.9 11.3 %copy-start.16 = (bf16[256,1024]{1,0:T(8,128)(2,1)S(1)}, bf16[256,1024]{1,0:T(8,128)(2,1)}, u32[]{:S(2)}) copy-start(bf16[256,1024]{1,0:T(8,128)(2,1)} %param.8) | copy-start | bytes 1572868
  82.2 21.5 %collective-permute-start.11 = (bf16[4,64,1024]{2,1,0:T(8,128)(2,1)S(1)}, bf16[4,64,1024]{2,1,0:T(8,128)(2,1)S(1)}, u32[]{:S(2)}, u32[]{:S(2)}) collective-permute-start(bf16[4,64,1024]{2,1,0:T(8,128)(2,1)S(1)} %bitcast.77), channel_id=1, source_target_pairs={{0,16},{16,0},{1,17},{17,1},{2,18},{18,2},{3,19},{19,3},{4,20},{20... | collective-permute-start | bytes 1572872 | tf_op jit(solution)/shard_map/ppermute | solution.py:24
  92.0 3.3 %slice-start = ((s8[8388608]{0:T(1024)(128)(4,1)}), s8[4194304]{0:T(1024)(128)(4,1)S(1)}, s32[]{:S(2)}) async-start(s8[8388608]{0:T(1024)(128)(4,1)} %bitcast.67), calls=%async_computation | async-start | bytes 8388608
  92.2 3.0 %collective-permute-start.7 = (bf16[256,1024]{1,0:T(8,128)(2,1)S(1)}, bf16[256,1024]{1,0:T(8,128)(2,1)S(1)}, u32[]{:S(2)}, u32[]{:S(2)}) collective-permute-start(bf16[256,1024]{1,0:T(8,128)(2,1)S(1)} %get-tuple-element.113), channel_id=1, source_target_pairs={{0,1},{1,0},{2,3},{3,2},{4,5},{5,4},{6,7},{7,6},{8,9},{9,8},{10,11... | collective-permute-start | bytes 1572872 | tf_op jit(solution)/shard_map/ppermute | solution.py:28
  95.2 4.9 %copy-start.2 = (bf16[512,1024]{1,0:T(8,128)(2,1)}, bf16[512,1024]{1,0:T(8,128)(2,1)S(1)}, u32[]{:S(2)}) copy-start(bf16[512,1024]{1,0:T(8,128)(2,1)S(1)} %pad_maximum_fusion.2.refs_0_) | copy-start | bytes 3145732
  100.0 3.7 %copy-start.30 = (s32[8,256]{1,0:T(8,128)S(1)}, s32[8,256]{1,0:T(8,128)}, u32[]{:S(2)}) copy-start(s32[8,256]{1,0:T(8,128)} %param.10) | copy-start | bytes 24580
  100.0 3.7 %collective-permute-start.10 = (f32[256,512]{1,0:T(8,128)S(1)}, f32[256,512]{1,0:T(8,128)S(1)}, u32[]{:S(2)}, u32[]{:S(2)}) collective-permute-start(f32[256,512]{1,0:T(8,128)S(1)} %slice.83), channel_id=1, source_target_pairs={{0,1},{1,0},{2,3},{3,2},{4,5},{5,4},{6,7},{7,6},{8,9},{9,8},{10,11... | collective-permute-start | bytes 1572872 | tf_op jit(solution)/shard_map/ppermute | solution.py:28
  103.0 3.4 %copy-start.22 = (bf16[4,2,256,512]{3,2,1,0:T(8,128)(2,1)S(1)}, bf16[4,2,256,512]{3,2,1,0:T(8,128)(2,1)}, u32[]{:S(2)}) copy-start(bf16[4,2,256,512]{3,2,1,0:T(8,128)(2,1)} %copy-done.21) | copy-start | bytes 6291460
  103.0 2.1 collective-permute-start.12
  103.6 11.1 %copy-start.8 = (bf16[4,64,1024]{2,1,0:T(8,128)(2,1)}, bf16[4,64,1024]{2,1,0:T(8,128)(2,1)S(1)}, u32[]{:S(2)}) copy-start(bf16[4,64,1024]{2,1,0:T(8,128)(2,1)S(1)} %collective-permute-done.11.g_ref) | copy-start | bytes 1572868
  103.8 11.0 %collective-permute-start.13 = (bf16[4,64,512]{2,1,0:T(8,128)(2,1)S(1)}, bf16[4,64,512]{2,1,0:T(8,128)(2,1)S(1)}, u32[]{:S(2)}, u32[]{:S(2)}) collective-permute-start(bf16[4,64,512]{2,1,0:T(8,128)(2,1)S(1)} %bitcast.80), channel_id=1, source_target_pairs={{0,16},{16,0},{1,17},{17,1},{2,18},{18,2},{3,19},{19,3},{4,20},{20... | collective-permute-start | bytes 786440 | tf_op jit(solution)/shard_map/ppermute | solution.py:24
  105.2 13.9 %collective-permute-start.16 = (bf16[4,64,512]{2,1,0:T(8,128)(2,1)S(1)}, bf16[4,64,512]{2,1,0:T(8,128)(2,1)}, u32[]{:S(2)}, u32[]{:S(2)}) collective-permute-start(bf16[4,64,512]{2,1,0:T(8,128)(2,1)S(1)} %bitcast.75), channel_id=1, source_target_pairs={{0,16},{16,0},{1,17},{17,1},{2,18},{18,2},{3,19},{19,3},{4,20},{20... | collective-permute-start | bytes 786440 | tf_op jit(solution)/shard_map/ppermute | solution.py:24
  106.4 4.2 %copy-start.15 = (bf16[4,2,256,512]{3,2,1,0:T(8,128)(2,1)S(1)}, bf16[4,2,256,512]{3,2,1,0:T(8,128)(2,1)}, u32[]{:S(2)}) copy-start(bf16[4,2,256,512]{3,2,1,0:T(8,128)(2,1)} %copy-done.14) | copy-start | bytes 6291460
  110.6 4.2 %copy-start.19 = (bf16[4,64,512]{2,1,0:T(8,128)(2,1)}, bf16[4,64,512]{2,1,0:T(8,128)(2,1)S(1)}, u32[]{:S(2)}) copy-start(bf16[4,64,512]{2,1,0:T(8,128)(2,1)S(1)} %get-tuple-element.70) | copy-start | bytes 786436
  110.6 4.2 %copy-start.13 = (bf16[4,2,256,512]{3,2,1,0:T(8,128)(2,1)S(1)}, bf16[4,2,256,512]{3,2,1,0:T(8,128)(2,1)}, u32[]{:S(2)}) copy-start(bf16[4,2,256,512]{3,2,1,0:T(8,128)(2,1)} %copy-done.12) | copy-start | bytes 6291460
  114.8 4.3 %copy-start.17 = (bf16[4,64,512]{2,1,0:T(8,128)(2,1)}, bf16[4,64,512]{2,1,0:T(8,128)(2,1)S(1)}, u32[]{:S(2)}) copy-start(bf16[4,64,512]{2,1,0:T(8,128)(2,1)S(1)} %get-tuple-element.76) | copy-start | bytes 786436
  119.1 8.7 %collective-permute-start.14 = (bf16[4,64,512]{2,1,0:T(8,128)(2,1)}, bf16[4,64,512]{2,1,0:T(8,128)(2,1)}, u32[]{:S(2)}, u32[]{:S(2)}) collective-permute-start(bf16[4,64,512]{2,1,0:T(8,128)(2,1)} %get-tuple-element.75), channel_id=1, source_target_pairs={{0,16},{16,0},{1,17},{17,1},{2,18},{18,2},{3,19},{19,3},{4,20},{20... | collective-permute-start | bytes 786440 | tf_op jit(solution)/shard_map/ppermute | solution.py:24
  121.7 6.1 %copy-start.20 = (bf16[4,64,512]{2,1,0:T(8,128)(2,1)S(1)}, bf16[4,64,512]{2,1,0:T(8,128)(2,1)}, u32[]{:S(2)}) copy-start(bf16[4,64,512]{2,1,0:T(8,128)(2,1)} %copy-done.19) | copy-start | bytes 786436
  121.7 7.2 %copy-start.3 = (bf16[512,1024]{1,0:T(8,128)(2,1)S(1)}, bf16[512,1024]{1,0:T(8,128)(2,1)}, u32[]{:S(2)}) copy-start(bf16[512,1024]{1,0:T(8,128)(2,1)} %copy-done.2) | copy-start | bytes 3145732
  121.7 7.2 %copy-start.5 = (bf16[512,1024]{1,0:T(8,128)(2,1)S(1)}, bf16[512,1024]{1,0:T(8,128)(2,1)}, u32[]{:S(2)}) copy-start(bf16[512,1024]{1,0:T(8,128)(2,1)} %copy-done.4) | copy-start | bytes 3145732
  127.1 8.0 %collective-permute-start.17 = (bf16[4,64,512]{2,1,0:T(8,128)(2,1)S(1)}, bf16[4,64,512]{2,1,0:T(8,128)(2,1)S(1)}, u32[]{:S(2)}, u32[]{:S(2)}) collective-permute-start(bf16[4,64,512]{2,1,0:T(8,128)(2,1)S(1)} %get-tuple-element.79), channel_id=1, source_target_pairs={{0,16},{16,0},{1,17},{17,1},{2,18},{18,2},{3,19},{19,3},{4,20},{20... | collective-permute-start | bytes 786440 | tf_op jit(solution)/shard_map/ppermute | solution.py:24
  128.8 1.6 collective-permute-start.15
  129.5 5.6 %copy-start.23 = (bf16[4,512,1024]{2,1,0:T(8,128)(2,1)}, bf16[4,512,1024]{2,1,0:T(8,128)(2,1)S(1)}, u32[]{:S(2)}) copy-start(bf16[4,512,1024]{2,1,0:T(8,128)(2,1)S(1)} %pad_maximum_fusion) | copy-start | bytes 12582916
  129.5 5.6 %copy-start.18 = (bf16[4,64,512]{2,1,0:T(8,128)(2,1)S(1)}, bf16[4,64,512]{2,1,0:T(8,128)(2,1)}, u32[]{:S(2)}) copy-start(bf16[4,64,512]{2,1,0:T(8,128)(2,1)} %copy-done.17) | copy-start | bytes 786436
  130.4 4.7 %copy-start.32 = (bf16[256,512]{1,0:T(8,128)(2,1)}, bf16[256,512]{1,0:T(8,128)(2,1)S(1)}, u32[]{:S(2)}) copy-start(bf16[256,512]{1,0:T(8,128)(2,1)S(1)} %collective-permute-done.15) | copy-start | bytes 786436
  135.2 2.6 %collective-permute-start.18 = (bf16[256,512]{1,0:T(8,128)(2,1)S(1)}, bf16[256,512]{1,0:T(8,128)(2,1)S(1)}, u32[]{:S(2)}, u32[]{:S(2)}) collective-permute-start(bf16[256,512]{1,0:T(8,128)(2,1)S(1)} %bitcast_add_fusion), channel_id=1, source_target_pairs={{0,1},{1,0},{2,3},{3,2},{4,5},{5,4},{6,7},{7,6},{8,9},{9,8},{10,11... | collective-permute-start | bytes 786440 | tf_op jit(solution)/shard_map/ppermute | solution.py:28
  137.2 25.5 %collective-permute-start.21 = (bf16[1024,512]{1,0:T(8,128)(2,1)S(1)}, bf16[1024,512]{1,0:T(8,128)(2,1)S(1)}, u32[]{:S(2)}, u32[]{:S(2)}) collective-permute-start(bf16[1024,512]{1,0:T(8,128)(2,1)S(1)} %convolution_convert_fusion.5), channel_id=1, source_target_pairs={{0,2},{1,3},{2,0},{3,1},{4,6},{5,7},{6,4},{7,5},{8,10},{9,11},{10,... | collective-permute-start | bytes 3145736 | tf_op jit(solution)/shard_map/ppermute | solution.py:24
  140.7 25.2 %collective-permute-start.22 = (bf16[1024,512]{1,0:T(8,128)(2,1)S(1)}, bf16[1024,512]{1,0:T(8,128)(2,1)S(1)}, u32[]{:S(2)}, u32[]{:S(2)}) collective-permute-start(bf16[1024,512]{1,0:T(8,128)(2,1)S(1)} %convolution_convert_fusion.4), channel_id=1, source_target_pairs={{0,16},{16,0},{1,17},{17,1},{2,18},{18,2},{3,19},{19,3},{4,20},{20... | collective-permute-start | bytes 3145736 | tf_op jit(solution)/shard_map/ppermute | solution.py:24
  142.3 23.6 %collective-permute-start.19 = (bf16[256,1024]{1,0:T(8,128)(2,1)S(1)}, bf16[256,1024]{1,0:T(8,128)(2,1)S(1)}, u32[]{:S(2)}, u32[]{:S(2)}) collective-permute-start(bf16[256,1024]{1,0:T(8,128)(2,1)S(1)} %get-tuple-element.109), channel_id=1, source_target_pairs={{0,4},{4,8},{8,12},{12,0},{1,5},{5,9},{9,13},{13,1},{2,6},{6,10},{... | collective-permute-start | bytes 1572872 | tf_op jit(solution)/shard_map/ppermute | solution.py:24
  144.1 24.6 %collective-permute-start.20 = (bf16[256,1024]{1,0:T(8,128)(2,1)S(1)}, bf16[256,1024]{1,0:T(8,128)(2,1)S(1)}, u32[]{:S(2)}, u32[]{:S(2)}) collective-permute-start(bf16[256,1024]{1,0:T(8,128)(2,1)S(1)} %get-tuple-element.108), channel_id=1, source_target_pairs={{0,12},{4,0},{8,4},{12,8},{1,13},{5,1},{9,5},{13,9},{2,14},{6,2},{... | collective-permute-start | bytes 1572872 | tf_op jit(solution)/shard_map/ppermute | solution.py:24
  155.2 19.6 %copy-start.6 = (bf16[512,1024]{1,0:T(8,128)(2,1)}, bf16[512,1024]{1,0:T(8,128)(2,1)S(1)}, u32[]{:S(2)}) copy-start(bf16[512,1024]{1,0:T(8,128)(2,1)S(1)} %fusion.9.own_ref) | copy-start | bytes 3145732
  169.4 49.8 %collective-permute-start.26 = (bf16[1024,1024]{1,0:T(8,128)(2,1)S(1)}, bf16[1024,1024]{1,0:T(8,128)(2,1)S(1)}, u32[]{:S(2)}, u32[]{:S(2)}) collective-permute-start(bf16[1024,1024]{1,0:T(8,128)(2,1)S(1)} %fusion.19), channel_id=1, source_target_pairs={{0,2},{1,3},{2,0},{3,1},{4,6},{5,7},{6,4},{7,5},{8,10},{9,11},{10,... | collective-permute-start | bytes 6291464 | tf_op jit(solution)/shard_map/ppermute | solution.py:24
  170.5 48.6 %collective-permute-start.25 = (bf16[1024,1024]{1,0:T(8,128)(2,1)S(1)}, bf16[1024,1024]{1,0:T(8,128)(2,1)S(1)}, u32[]{:S(2)}, u32[]{:S(2)}) collective-permute-start(bf16[1024,1024]{1,0:T(8,128)(2,1)S(1)} %fusion.18), channel_id=1, source_target_pairs={{0,16},{16,0},{1,17},{17,1},{2,18},{18,2},{3,19},{19,3},{4,20},{20... | collective-permute-start | bytes 6291464 | tf_op jit(solution)/shard_map/ppermute | solution.py:24
  172.4 46.7 %collective-permute-start.24 = (bf16[512,1024]{1,0:T(8,128)(2,1)S(1)}, bf16[512,1024]{1,0:T(8,128)(2,1)S(1)}, u32[]{:S(2)}, u32[]{:S(2)}) collective-permute-start(bf16[512,1024]{1,0:T(8,128)(2,1)S(1)} %fusion.31), channel_id=1, source_target_pairs={{0,12},{4,0},{8,4},{12,8},{1,13},{5,1},{9,5},{13,9},{2,14},{6,2},{... | collective-permute-start | bytes 3145736 | tf_op jit(solution)/shard_map/ppermute | solution.py:24
  174.7 44.3 %collective-permute-start.23 = (bf16[512,1024]{1,0:T(8,128)(2,1)S(1)}, bf16[512,1024]{1,0:T(8,128)(2,1)S(1)}, u32[]{:S(2)}, u32[]{:S(2)}) collective-permute-start(bf16[512,1024]{1,0:T(8,128)(2,1)S(1)} %fusion.30), channel_id=1, source_target_pairs={{0,4},{4,8},{8,12},{12,0},{1,5},{5,9},{9,13},{13,1},{2,6},{6,10},{... | collective-permute-start | bytes 3145736 | tf_op jit(solution)/shard_map/ppermute | solution.py:24
  221.6 2.0 collective-permute-start.27
  (19 other events, 37.5 us)

commit v12 on v11

--- a/solution.py
+++ b/solution.py
@@ -73,22 +73,25 @@
     return functools.reduce(lambda a, b: a + b, [value.astype(F32) for value in values])
 
 
-def product_kernel(count, start, table_ref, *refs):
-    blocks, weight_ref, out_ref = refs[:count], refs[count], refs[count + 1]
+def product_kernel(count, depth, part, table_ref, act_ref, *refs):
+    out_ref = refs[-1]
     tile = min(256, out_ref.shape[1])
     for at in range(0, out_ref.shape[1], tile):
-        total = None
-        for k in range(count):
-            weight = weight_ref[table_ref[k], :, start + at:start + at + tile]
-            part = dot(blocks[k][...], weight, ((1,), (0,)))
-            total = part if total is None else total + part
-        out_ref[:, at:at + tile] = total
-
-
-def product(blocks, weights, table, start, width):
-    count, (rows, depth) = len(blocks), blocks[0].shape
+        found = None
+        for n, weight_ref in enumerate(refs[:-1]):
+            inner = pl.ds(pl.multiple_of(table_ref[count + n] * depth, depth), depth)
+            act = act_ref[table_ref[n], :, inner]
+            start = at + (part * out_ref.shape[1] if weight_ref.shape[1] > out_ref.shape[1] else 0)
+            more = dot(act, weight_ref[:, start:start + tile], ((1,), (0,)))
+            found = more if found is None else found + more
+        out_ref[:, at:at + tile] = found
+
+
+def product(acts, weights, table, part):
+    count, rows = len(weights), acts.shape[1]
+    depth, width = weights[0].shape[0], min(block.shape[1] for block in weights)
     return pl.pallas_call(
-        functools.partial(product_kernel, count, start),
+        functools.partial(product_kernel, count, depth, part),
         out_shape=jax.ShapeDtypeStruct((rows, width), F32),
         in_specs=[pl.BlockSpec(memory_space=pltpu.SMEM)]
         + [pl.BlockSpec(memory_space=pltpu.VMEM)] * (count + 1),
@@ -99,7 +102,7 @@
             bytes_accessed=2 * count * depth * (rows + width) + 4 * rows * width,
             transcendentals=0,
         ),
-    )(table, *blocks, weights)
+    )(table, acts, *weights)
 
 
 def attend_block(q_ref, g_ref, kv_ref, live_ref, dq_ref, grad_ref):
@@ -338,9 +341,8 @@
     sources = [(seq_at - step) % seq_count for step in range(seq_count)]
     staged = [stage(neighbour_kv, source, pairs) for source in sources]
     near = [k for k in range(tensor_count) if k != opposite]
-    cut = width * 5 // 8 // HD * HD
-    left_from = [block[:, :cut] for block in along_seq[1:]]
-    right_from = [block[:, cut:] for block in along_dp[1:]]
+    left_from = [block[:, :half] for block in along_seq[1:]]
+    right_from = [block[:, half:] for block in along_dp[1:]]
     left_from, right_from, raw, staged = lax.optimization_barrier(
         (left_from, right_from, [raw[k] for k in near], staged)
     )
@@ -350,9 +352,6 @@
     corner_right = [gather_ring(block, "seq", seq_count) for block in right_from]
     up = shift(raw[opposite - 1][:rows // 2], "tensor", 1)
     down = shift(raw[opposite + 1][rows // 2:], "tensor", -1)
-    grad_out = after(out_grad, corner_right)
-    grads = [to_owner(grad_out, step) for step in range(seq_count)]
-
     def columns_of(block, which):
         return jnp.concatenate(
             [
@@ -363,32 +362,46 @@
         )
 
     others = swap(jnp.concatenate([columns_of(raw[k], 1 - core) for k in near], axis=0))
-    up, down, others = lax.optimization_barrier((up, down, others))
-    raw[opposite] = jnp.concatenate([up, down], axis=0)
+    grad_out, others = lax.optimization_barrier((out_grad, others, corner_right))[:2]
+    grads = [to_owner(grad_out, step) for step in range(seq_count)]
     others = {k: others[n * rows:(n + 1) * rows] for n, k in enumerate(near)}
-    others[opposite] = swap(columns_of(raw[opposite], 1 - core))
-    acts = [
-        jnp.concatenate([columns_of(raw[k], core), others[k]], axis=0) for k in range(tensor_count)
-    ]
     depth_blocks = [(tensor_at - k) % tensor_count for k in range(tensor_count)]
-    table = jnp.stack(depth_blocks).astype(jnp.int32)
 
     def block_at(i, j):
         block = ((seq_at - i) % seq_count) * dp_count + ((dp_at // 2 - j) % couples) * 2
-        return block // (2 * per), (block % (2 * per)) // 2
+        return (tensor_at - block // (2 * per)) % tensor_count, (block % (2 * per)) // 2
 
     places = [(i, j) for i in range(seq_count) for j in range(couples)]
-    weights = jnp.zeros((tensor_count, per * depth, width), BF16)
+    table = [block_at(i, j) for i, j in places]
+    table = jnp.stack([k for k, _ in table] + [inner for _, inner in table]).astype(jnp.int32)
+
+    acts = jnp.zeros((tensor_count, 2 * rows, per * depth), BF16)
+    for k in near:
+        block = jnp.concatenate([columns_of(raw[k], core), others[k]], axis=0)
+        acts = lax.dynamic_update_slice(acts, block[None], (k, 0, 0))
+
+    def placed(weights, piece, i, j, column):
+        k, inner = block_at(i, j)
+        at = ((tensor_at - k) % tensor_count, inner * depth, column)
+        return lax.dynamic_update_slice(weights, piece[None], at)
+
+    by_depth = jnp.zeros((tensor_count, per * depth, width), BF16)
     for i, j in places:
-        at, inner = block_at(i, j)
+        if i == 0 or j == 0:
+            by_depth = placed(by_depth, along_seq[i] if j == 0 else along_dp[j], i, j, 0)
+
+    acts, by_depth, up, down = lax.optimization_barrier((acts, by_depth, up, down))
+    for n, which in enumerate((core, 1 - core)):
+        block = jnp.concatenate([columns_of(block, which) for block in (up, down)], axis=0)
+        block = swap(block) if n else block
+        acts = lax.dynamic_update_slice(acts, block[None], (opposite, n * rows, 0))
+
+    def weight_pieces(i, j):
         if j == 0:
-            pieces = [(along_seq[i], 0)]
-        elif i == 0:
-            pieces = [(along_dp[j], 0)]
-        else:
-            pieces = [(corner_left[i - 1][j], 0), (corner_right[j - 1][i], cut)]
-        for piece, start in pieces:
-            weights = lax.dynamic_update_slice(weights, piece[None], (at, inner * depth, start))
+            return [along_seq[i]]
+        if i == 0:
+            return [along_dp[j]]
+        return [corner_left[i - 1][j], corner_right[j - 1][i]]
 
     def from_owner(value, step):
         value = shift(value, "seq", -step) if step else value
@@ -412,7 +425,8 @@
 
     queries = []
     for part in range(2):
-        partial = product(acts, weights, table, part * half, half)
+        weights = [weight_pieces(i, j)[part if i and j else 0] for i, j in places]
+        partial = product(acts, weights, table, part)
         arrived = swap(partial[rows:])
         if part:
             partial = after(partial, grads)
@@ -420,12 +434,15 @@
     asked = [[to_owner(value, step) for step in range(seq_count)] for value in queries]
     asked[0][0] = after(asked[0][0], queries[1])
 
-    stacked = jnp.stack(after(acts, queries[1]))
+    weights = by_depth
+    for i, j in places:
+        if i and j:
+            for n, piece in enumerate(after(weight_pieces(i, j), queries[1])):
+                weights = placed(weights, piece, i, j, n * half)
 
     def act_block(i, j):
-        at, inner = block_at(i, j)
-        k = (tensor_at - at) % tensor_count
-        return lax.dynamic_slice(stacked, (k, 0, inner * depth), (1, 2 * rows, depth))[0]
+        k, inner = block_at(i, j)
+        return lax.dynamic_slice(acts, (k, 0, inner * depth), (1, 2 * rows, depth))[0]
 
     def weight_product(i, j, grad):
         found = dot(act_block(i, j), grad, ((0,), (0,)))
@@ -511,9 +528,8 @@
     from_dp = reduce_rings([([None] + beside_dp, True)], "dp")[0][1:]
 
     weight_grad = summed([own] + from_seq + from_dp)
-    others = after([part[rows:] for part in (act_parts[0], up, down)], weight_grad)
-    arrived = swap(total(others).astype(BF16))
-    act_grad = assemble(core, act_parts[0], up, down, arrived, depth)
+    arrived = swap(total([part[rows:] for part in (act_parts[0], up, down)]).astype(BF16))
+    act_grad = assemble(after(core, weight_grad), act_parts[0], up, down, arrived, depth)
     return (act_grad, weight_grad, kv_grad)
 
 

time: 226 us -> 227 us (level)
  starting transfers between devices: 27.3 us -> 33.9 us
  Pallas kernels: 28.2 us -> 23.9 us
  waiting for transfers between devices: 112 us -> 115 us
  local copies, waits for them, and re-layouts: 39.2 us -> 36.9 us
    pallas_call x4, Pallas kernels: 18 us -> 9.91 us  [attend(): pl.pallas_call(attend_kernel, grid_spec=pltpu.PrefetchScalarGridSpec(num_...]
    ppermute x21, starting transfers between devices: 26.4 us -> 33 us  [shift(): lax.ppermute(value, axis, [(i, (i + step * stride) % size) for i in range...]
    ppermute x21, waiting for transfers between devices: 109 us -> 115 us  [shift(): lax.ppermute(value, axis, [(i, (i + step * stride) % size) for i in range...]
    dynamic_update_slice x5 -> x7, local copies, waits for them, and re-layouts: 9.7 us -> 5.22 us  [the longest x5 4.67 us: placed(): return lax.dynamic_update_slice(weights, piece[None], at)]
    pallas_call x2, Pallas kernels: 5.77 us -> 9.49 us  [product(): pl.pallas_call(functools.partial(product_kernel, count, depth, part), out...]
    ppermute x7, waiting for transfers between devices: 3.56 us -> 0.41 us  [swap(): lax.ppermute(value, 'dp', [(i, i ^ 1) for i in range(lax.axis_size('dp'))])]
    unnamed x77 -> x64, local copies, waits for them, and re-layouts: 16.6 us -> 17.5 us
  transfers between devices with their start and end apart: 28 -> 28, of which waited for: 12 -> 16; matrix products, arithmetic and copies ran while one was open for 16% -> 12% of each run, Pallas kernels for 11% -> 10%
where the time goes in v12:
time: 227 us; the launch traced here: 226 us
  waiting for transfers between devices  115 us (51%)
  local copies, waits for them, and re-layouts  36.9 us (16%)
  starting transfers between devices  33.9 us (15%)
  Pallas kernels  23.9 us (11%)
  matrix products  10.6 us (5%)
  other arithmetic  4.41 us (2%)
    ppermute x21, waiting for transfers between devices, shift(): lax.ppermute(value, axis, [(i, (i + step * stride) % size) for i in range...  115 us
    ppermute x21, starting transfers between devices, shift(): lax.ppermute(value, axis, [(i, (i + step * stride) % size) for i in range...  33 us
    unnamed x64, local copies, waits for them, and re-layouts  17.5 us
    dot_general x9, matrix products, dot(): lax.dot_general(a, b, (contract, ((), ())), preferred_element_type=F32)  10.6 us
    pallas_call x4, Pallas kernels, attend(): pl.pallas_call(attend_kernel, grid_spec=pltpu.PrefetchScalarGridSpec(num_...  9.91 us
    pallas_call x2, Pallas kernels, product(): pl.pallas_call(functools.partial(product_kernel, count, depth, part), out...  9.49 us
    dynamic_update_slice x5, local copies, waits for them, and re-layouts, placed(): return lax.dynamic_update_slice(weights, piece[None], at)  4.67 us
  transfers between devices with their start and end apart: 28, of which 16 were waited for; matrix products, arithmetic and copies ran while one was open for 12% of the time, Pallas kernels for 10%

profile of v12, /device:TPU:0, one launch (start us, length us, event | category | flops | bytes accessed | tf_op | source)
XLA Modules:
  0.0 226.4 jit_solution(11582752451532110700)
XLA Ops:
  0.6 3.0 %collective-permute-start = (bf16[1024,1024]{1,0:T(8,128)(2,1)}, bf16[1024,1024]{1,0:T(8,128)(2,1)S(1)}, u32[]{:S(2)}, u32[]{:S(2)}) collective-permute-start(bf16[1024,1024]{1,0:T(8,128)(2,1)} %refs_0_.3), channel_id=1, source_target_pairs={{0,16},{16,0},{1,17},{17,1},{2,18},{18,2},{3,19},{19,3},{4,20},{20... | collective-permute-start | bytes 6291464 | tf_op jit(solution)/shard_map/ppermute | solution.py:24
  3.6 1.5 collective-permute-start.1
  5.2 1.6 collective-permute-start.2
  6.7 2.2 collective-permute-start.3
  9.0 3.4 %copy-done.2 = bf16[8,2,256,1024]{3,2,1,0:T(8,128)(2,1)S(1)} copy-done((bf16[8,2,256,1024]{3,2,1,0:T(8,128)(2,1)S(1)}, bf16[8,2,256,1024]{3,2,1,0:T(8,128)(2,1)}, u32[]{:S(2)}) %copy-start.2) | copy-done | bytes 8388632
  12.7 1.3 copy-done.9
  14.0 1.3 copy-done.11
  15.3 1.9 copy-done.3
  18.9 1.3 copy-done.20
  20.2 13.2 %collective-permute-done.2 = bf16[256,2048]{1,0:T(8,128)(2,1)} collective-permute-done((bf16[256,2048]{1,0:T(8,128)(2,1)}, bf16[256,2048]{1,0:T(8,128)(2,1)}, u32[]{:S(2)}, u32[]{:S(2)}) %collective-permute-start.2) | collective-permute-done | bytes 1048608 | tf_op jit(solution)/shard_map/ppermute | solution.py:24
  33.4 20.2 %collective-permute-done.3 = bf16[256,2048]{1,0:T(8,128)(2,1)} collective-permute-done((bf16[256,2048]{1,0:T(8,128)(2,1)}, bf16[256,2048]{1,0:T(8,128)(2,1)}, u32[]{:S(2)}, u32[]{:S(2)}) %collective-permute-start.3) | collective-permute-done | bytes 1048608 | tf_op jit(solution)/shard_map/ppermute | solution.py:24
  54.7 2.3 %slice.81 = bf16[1024,512]{1,0:T(8,128)(2,1)} slice(bf16[1024,1024]{1,0:T(8,128)(2,1)} %collective-permute-done.1.refs_1_), slice={[0:1024], [512:1024]} | slice | bytes 2097152 | tf_op jit(solution)/shard_map/slice | solution.py:345
  57.9 2.7 %constant_dynamic-slice_fusion.5 = (bf16[256,1024]{1,0:T(8,128)(2,1)}, bf16[256,1024]{1,0:T(8,128)(2,1)S(1)}, bf16[256,1024]{1,0:T(8,128)(2,1)S(1)}, bf16[256,1024]{1,0:T(8,128)(2,1)}) fusion(bf16[256,2048]{1,0:T(8,128)(2,1)} %collective-permute-done.3, s32[]{:T(128)S(6)} %select_n.348, s32[]{:T(128)S(6)} %select_n.349, ...), kind=kLoop, calls=%fused_computation.75 | loop fusion | bytes 4194312 | tf_op jit(solution)/shard_map/dynamic_slice | solution.py:358
  68.1 2.7 %collective-permute-start.7 = (bf16[128,2048]{1,0:T(8,128)(2,1)S(1)}, bf16[128,2048]{1,0:T(8,128)(2,1)S(1)}, u32[]{:S(2)}, u32[]{:S(2)}) collective-permute-start(bf16[128,2048]{1,0:T(8,128)(2,1)S(1)} %slice.66), channel_id=1, source_target_pairs={{0,12},{4,0},{8,4},{12,8},{1,13},{5,1},{9,5},{13,9},{2,14},{6,2},{... | collective-permute-start | bytes 1572872 | tf_op jit(solution)/shard_map/ppermute | solution.py:24
  71.3 1.9 bitcast_dynamic-update-slice_fusion.1
  73.5 14.5 %collective-permute-done.5.refs_3_ = bf16[1024,512]{1,0:T(8,128)(2,1)S(1)} collective-permute-done((bf16[1024,512]{1,0:T(8,128)(2,1)}, bf16[1024,512]{1,0:T(8,128)(2,1)S(1)}, u32[]{:S(2)}, u32[]{:S(2)}) %collective-permute-start.5) | collective-permute-done | bytes 1048608 | tf_op jit(solution)/shard_map/ppermute | solution.py:24
  87.9 1.5 fusion.54
  91.2 2.1 collective-permute-done.7
  93.8 1.9 collective-permute-done.9.refs_3_
  97.1 5.5 %shard_map.87 = f32[512,512]{1,0:T(8,128)S(1)} custom-call(s32[8]{0:T(128)S(1)} %stack.35.table_ref, bf16[4,512,1024]{2,1,0:T(8,128)(2,1)S(1)} %bitcast_dynamic-update-slice_fusion.5.act_ref, bf16[1024,1024]{1,0:T(8,128)(2,1)S(1)} %copy-done.4, bf16[1024,1024]{1,0:T(8,128)(2,1)} %collective-permute-done.1.refs_1_, ...), custom_call_target="tpu_custom_call" | custom-call | flops 2147483648 | bytes 9437184 | tf_op jit(solution)/shard_map/pallas_call | solution.py:93
  102.8 4.0 %shard_map.88 = f32[512,512]{1,0:T(8,128)S(1)} custom-call(s32[8]{0:T(128)S(1)} %stack.35.table_ref, bf16[4,512,1024]{2,1,0:T(8,128)(2,1)S(1)} %bitcast_dynamic-update-slice_fusion.5.act_ref, bf16[1024,1024]{1,0:T(8,128)(2,1)S(1)} %copy-done.4, bf16[1024,1024]{1,0:T(8,128)(2,1)} %collective-permute-done.1.refs_1_, ...), custom_call_target="tpu_custom_call" | custom-call | flops 2147483648 | bytes 9437184 | tf_op jit(solution)/shard_map/pallas_call | solution.py:93
  111.3 2.5 %shard_map.89 = (bf16[4,64,512]{2,1,0:T(8,128)(2,1)S(1)}, bf16[8,2,256,1024]{3,2,1,0:T(8,128)(2,1)}) custom-call(s32[12]{0:T(128)S(1)} %pad_add_fusion.table_ref, bf16[4,64,512]{2,1,0:T(8,128)(2,1)S(1)} %bitcast.89, bf16[4,64,1024]{2,1,0:T(8,128)(2,1)S(1)} %bitcast.86, f32[8,256,128]{2,1,0:T(8,128)S(1)} %broadcast_in_dim.61.live_ref, ...), custom_call_target="tpu_custom_call" | custom-call | flops 1342177280 | bytes 4194304 | tf_op jit(solution)/shard_map/pallas_call | solution.py:182
  113.8 2.5 %shard_map.90 = (bf16[4,64,512]{2,1,0:T(8,128)(2,1)S(1)}, bf16[8,2,256,1024]{3,2,1,0:T(8,128)(2,1)}) custom-call(s32[12]{0:T(128)S(1)} %pad_add_fusion.table_ref, bf16[4,64,512]{2,1,0:T(8,128)(2,1)S(1)} %bitcast.84, bf16[4,64,1024]{2,1,0:T(8,128)(2,1)S(1)} %bitcast.87, ...), custom_call_target="tpu_custom_call", output_to_operand_aliasing={{1}: (5, {})} | custom-call | flops 1342177280 | bytes 4194304 | tf_op jit(solution)/shard_map/pallas_call | solution.py:182
  116.2 1.8 collective-permute-done.13.q_ref
  118.0 2.5 %shard_map.91 = (bf16[4,64,512]{2,1,0:T(8,128)(2,1)}, bf16[8,2,256,1024]{3,2,1,0:T(8,128)(2,1)}) custom-call(s32[12]{0:T(128)S(1)} %pad_add_fusion.1.table_ref, bf16[4,64,512]{2,1,0:T(8,128)(2,1)S(1)} %collective-permute-done.13.q_ref, bf16[4,64,1024]{2,1,0:T(8,128)(2,1)S(1)} %collective-permute-done.11.g_ref, ...), custom_call_target="tpu_custom_call", output_to_operand_aliasing={{1}: (5, {})} | custom-call | flops 1342177280 | bytes 4194304 | tf_op jit(solution)/shard_map/pallas_call | solution.py:182
  120.5 4.5 %collective-permute-start.14 = (bf16[4,64,512]{2,1,0:T(8,128)(2,1)}, bf16[4,64,512]{2,1,0:T(8,128)(2,1)S(1)}, u32[]{:S(2)}, u32[]{:S(2)}) collective-permute-start(bf16[4,64,512]{2,1,0:T(8,128)(2,1)} %get-tuple-element.74), channel_id=1, source_target_pairs={{0,16},{16,0},{1,17},{17,1},{2,18},{18,2},{3,19},{19,3},{4,20},{20... | collective-permute-start | bytes 786440 | tf_op jit(solution)/shard_map/ppermute | solution.py:24
  126.8 1.6 copy-done.10
  129.3 2.5 %shard_map.92 = (bf16[4,64,512]{2,1,0:T(8,128)(2,1)S(1)}, bf16[8,2,256,1024]{3,2,1,0:T(8,128)(2,1)}) custom-call(s32[12]{0:T(128)S(1)} %pad_add_fusion.1.table_ref, bf16[4,64,512]{2,1,0:T(8,128)(2,1)S(1)} %copy-done.19, bf16[4,64,1024]{2,1,0:T(8,128)(2,1)S(1)} %copy-done.8, ...), custom_call_target="tpu_custom_call", output_to_operand_aliasing={{1}: (5, {})} | custom-call | flops 1342177280 | bytes 4194304 | tf_op jit(solution)/shard_map/pallas_call | solution.py:182
  131.8 1.7 collective-permute-start.17
  135.9 3.7 %collective-permute-done.17 = bf16[4,64,512]{2,1,0:T(8,128)(2,1)S(1)} collective-permute-done((bf16[4,64,512]{2,1,0:T(8,128)(2,1)S(1)}, bf16[4,64,512]{2,1,0:T(8,128)(2,1)S(1)}, u32[]{:S(2)}, u32[]{:S(2)}) %collective-permute-start.17) | collective-permute-done | bytes 262176 | tf_op jit(solution)/shard_map/ppermute | solution.py:24
  141.0 1.8 dynamic-slice_bitcast_fusion
  143.3 1.3 convolution_convert_fusion.3
  145.9 3.8 %collective-permute-start.20 = (bf16[256,1024]{1,0:T(8,128)(2,1)S(1)}, bf16[256,1024]{1,0:T(8,128)(2,1)S(1)}, u32[]{:S(2)}, u32[]{:S(2)}) collective-permute-start(bf16[256,1024]{1,0:T(8,128)(2,1)S(1)} %get-tuple-element.104), channel_id=1, source_target_pairs={{0,12},{4,0},{8,4},{12,8},{1,13},{5,1},{9,5},{13,9},{2,14},{6,2},{... | collective-permute-start | bytes 1572872 | tf_op jit(solution)/shard_map/ppermute | solution.py:24
  149.7 1.3 convolution_convert_fusion
  151.0 1.3 convolution_convert_fusion.1
  154.7 1.3 convolution_convert_fusion.2.refs_0_
  156.0 1.3 fusion.12
  157.3 1.3 fusion.9.own_ref
  158.6 9.8 %collective-permute-done.21 = bf16[1024,512]{1,0:T(8,128)(2,1)S(1)} collective-permute-done((bf16[1024,512]{1,0:T(8,128)(2,1)S(1)}, bf16[1024,512]{1,0:T(8,128)(2,1)S(1)}, u32[]{:S(2)}, u32[]{:S(2)}) %collective-permute-start.21) | collective-permute-done | bytes 1048608 | tf_op jit(solution)/shard_map/ppermute | solution.py:24
  168.3 2.5 %collective-permute-done.22 = bf16[1024,512]{1,0:T(8,128)(2,1)S(1)} collective-permute-done((bf16[1024,512]{1,0:T(8,128)(2,1)S(1)}, bf16[1024,512]{1,0:T(8,128)(2,1)S(1)}, u32[]{:S(2)}, u32[]{:S(2)}) %collective-permute-start.22) | collective-permute-done | bytes 1048608 | tf_op jit(solution)/shard_map/ppermute | solution.py:24
  171.5 2.0 collective-permute-start.26
  174.1 1.6 collective-permute-start.24
  176.3 1.7 collective-permute-start.23
  178.3 18.8 %collective-permute-done.26.down_ref = bf16[512,1024]{1,0:T(8,128)(2,1)S(1)} collective-permute-done((bf16[512,1024]{1,0:T(8,128)(2,1)S(1)}, bf16[512,1024]{1,0:T(8,128)(2,1)S(1)}, u32[]{:S(2)}, u32[]{:S(2)}) %collective-permute-start.26) | collective-permute-done | bytes 1048608 | tf_op jit(solution)/shard_map/ppermute | solution.py:24
  197.1 22.7 %collective-permute-done.25.up_ref = bf16[512,1024]{1,0:T(8,128)(2,1)S(1)} collective-permute-done((bf16[512,1024]{1,0:T(8,128)(2,1)S(1)}, bf16[512,1024]{1,0:T(8,128)(2,1)S(1)}, u32[]{:S(2)}, u32[]{:S(2)}) %collective-permute-start.25) | collective-permute-done | bytes 1048608 | tf_op jit(solution)/shard_map/ppermute | solution.py:24
  220.8 1.8 collective-permute-done.23.refs_1_
  222.6 2.2 shard_map.93
  224.8 1.6 shard_map.94
  (142 shorter events, 34.1 us)
Async XLA Ops:
  0.6 52.9 %collective-permute-start = (bf16[1024,1024]{1,0:T(8,128)(2,1)}, bf16[1024,1024]{1,0:T(8,128)(2,1)S(1)}, u32[]{:S(2)}, u32[]{:S(2)}) collective-permute-start(bf16[1024,1024]{1,0:T(8,128)(2,1)} %refs_0_.3), channel_id=1, source_target_pairs={{0,16},{16,0},{1,17},{17,1},{2,18},{18,2},{3,19},{19,3},{4,20},{20... | collective-permute-start | bytes 6291464 | tf_op jit(solution)/shard_map/ppermute | solution.py:24
  3.6 51.0 %collective-permute-start.1 = (bf16[1024,1024]{1,0:T(8,128)(2,1)}, bf16[1024,1024]{1,0:T(8,128)(2,1)}, u32[]{:S(2)}, u32[]{:S(2)}) collective-permute-start(bf16[1024,1024]{1,0:T(8,128)(2,1)} %refs_0_.3), channel_id=1, source_target_pairs={{0,2},{1,3},{2,0},{3,1},{4,6},{5,7},{6,4},{7,5},{8,10},{9,11},{10,... | collective-permute-start | bytes 6291464 | tf_op jit(solution)/shard_map/ppermute | solution.py:24
  5.2 28.3 %collective-permute-start.2 = (bf16[256,2048]{1,0:T(8,128)(2,1)}, bf16[256,2048]{1,0:T(8,128)(2,1)}, u32[]{:S(2)}, u32[]{:S(2)}) collective-permute-start(bf16[256,2048]{1,0:T(8,128)(2,1)} %param.6), channel_id=1, source_target_pairs={{0,4},{4,8},{8,12},{12,0},{1,5},{5,9},{9,13},{13,1},{2,6},{6,10},{... | collective-permute-start | bytes 3145736 | tf_op jit(solution)/shard_map/ppermute | solution.py:24
  6.7 46.8 %collective-permute-start.3 = (bf16[256,2048]{1,0:T(8,128)(2,1)}, bf16[256,2048]{1,0:T(8,128)(2,1)}, u32[]{:S(2)}, u32[]{:S(2)}) collective-permute-start(bf16[256,2048]{1,0:T(8,128)(2,1)} %param.6), channel_id=1, source_target_pairs={{0,12},{4,0},{8,4},{12,8},{1,13},{5,1},{9,5},{13,9},{2,14},{6,2},{... | collective-permute-start | bytes 3145736 | tf_op jit(solution)/shard_map/ppermute | solution.py:24
  9.0 3.4 %copy-start.2 = (bf16[8,2,256,1024]{3,2,1,0:T(8,128)(2,1)S(1)}, bf16[8,2,256,1024]{3,2,1,0:T(8,128)(2,1)}, u32[]{:S(2)}) copy-start(bf16[8,2,256,1024]{3,2,1,0:T(8,128)(2,1)} %kv_ref.3) | copy-start | bytes 25165828
  12.4 4.9 %copy-start.3 = (bf16[8,2,256,1024]{3,2,1,0:T(8,128)(2,1)S(1)}, bf16[8,2,256,1024]{3,2,1,0:T(8,128)(2,1)}, u32[]{:S(2)}) copy-start(bf16[8,2,256,1024]{3,2,1,0:T(8,128)(2,1)} %kv_ref.3) | copy-start | bytes 25165828
  20.2 36.7 %copy-start.27 = (bf16[256,2048]{1,0:T(8,128)(2,1)S(1)}, bf16[256,2048]{1,0:T(8,128)(2,1)}, u32[]{:S(2)}) copy-start(bf16[256,2048]{1,0:T(8,128)(2,1)} %param.6) | copy-start | bytes 3145732
  61.8 26.2 %collective-permute-start.4 = (bf16[768,1024]{1,0:T(8,128)(2,1)}, bf16[768,1024]{1,0:T(8,128)(2,1)}, u32[]{:S(2)}, u32[]{:S(2)}) collective-permute-start(bf16[768,1024]{1,0:T(8,128)(2,1)} %pad_maximum_fusion), channel_id=1, source_target_pairs={{0,1},{1,0},{2,3},{3,2},{4,5},{5,4},{6,7},{7,6},{8,9},{9,8},{10,11... | collective-permute-start | bytes 4718600 | tf_op jit(solution)/shard_map/ppermute | solution.py:28
  62.1 25.8 %collective-permute-start.5 = (bf16[1024,512]{1,0:T(8,128)(2,1)}, bf16[1024,512]{1,0:T(8,128)(2,1)S(1)}, u32[]{:S(2)}, u32[]{:S(2)}) collective-permute-start(bf16[1024,512]{1,0:T(8,128)(2,1)} %slice.81), channel_id=1, source_target_pairs={{0,16},{16,0},{1,17},{17,1},{2,18},{18,2},{3,19},{19,3},{4,20},{20... | collective-permute-start | bytes 3145736 | tf_op jit(solution)/shard_map/ppermute | solution.py:24
  64.7 6.1 %copy-start.26 = (bf16[1024,512]{1,0:T(8,128)(2,1)S(1)}, bf16[1024,512]{1,0:T(8,128)(2,1)}, u32[]{:S(2)}) copy-start(bf16[1024,512]{1,0:T(8,128)(2,1)} %slice.80) | copy-start | bytes 3145732
  66.9 24.3 %collective-permute-start.6 = (bf16[128,2048]{1,0:T(8,128)(2,1)S(1)}, bf16[128,2048]{1,0:T(8,128)(2,1)S(1)}, u32[]{:S(2)}, u32[]{:S(2)}) collective-permute-start(bf16[128,2048]{1,0:T(8,128)(2,1)S(1)} %slice.65), channel_id=1, source_target_pairs={{0,4},{4,8},{8,12},{12,0},{1,5},{5,9},{9,13},{13,1},{2,6},{6,10},{... | collective-permute-start | bytes 1572872 | tf_op jit(solution)/shard_map/ppermute | solution.py:24
  68.1 25.2 %collective-permute-start.7 = (bf16[128,2048]{1,0:T(8,128)(2,1)S(1)}, bf16[128,2048]{1,0:T(8,128)(2,1)S(1)}, u32[]{:S(2)}, u32[]{:S(2)}) collective-permute-start(bf16[128,2048]{1,0:T(8,128)(2,1)S(1)} %slice.66), channel_id=1, source_target_pairs={{0,12},{4,0},{8,4},{12,8},{1,13},{5,1},{9,5},{13,9},{2,14},{6,2},{... | collective-permute-start | bytes 1572872 | tf_op jit(solution)/shard_map/ppermute | solution.py:24
  70.8 24.9 %collective-permute-start.9 = (bf16[1024,512]{1,0:T(8,128)(2,1)S(1)}, bf16[1024,512]{1,0:T(8,128)(2,1)S(1)}, u32[]{:S(2)}, u32[]{:S(2)}) collective-permute-start(bf16[1024,512]{1,0:T(8,128)(2,1)S(1)} %copy-done.26), channel_id=1, source_target_pairs={{0,2},{1,3},{2,0},{3,1},{4,6},{5,7},{6,4},{7,5},{8,10},{9,11},{10,... | collective-permute-start | bytes 3145736 | tf_op jit(solution)/shard_map/ppermute | solution.py:24
  73.5 17.2 %copy-start.22 = (bf16[4,1024,1024]{2,1,0:T(8,128)(2,1)}, bf16[4,1024,1024]{2,1,0:T(8,128)(2,1)S(1)}, u32[]{:S(2)}) copy-start(bf16[4,1024,1024]{2,1,0:T(8,128)(2,1)S(1)} %bitcast_dynamic-update-slice_fusion) | copy-start | bytes 25165828
  73.5 15.9 %copy-start.25 = (bf16[256,1024]{1,0:T(8,128)(2,1)S(1)}, bf16[256,1024]{1,0:T(8,128)(2,1)}, u32[]{:S(2)}) copy-start(bf16[256,1024]{1,0:T(8,128)(2,1)} %get-tuple-element.110) | copy-start | bytes 1572868
  91.2 4.6 %copy-start.15 = (bf16[256,1024]{1,0:T(8,128)(2,1)S(1)}, bf16[256,1024]{1,0:T(8,128)(2,1)}, u32[]{:S(2)}) copy-start(bf16[256,1024]{1,0:T(8,128)(2,1)} %param.8) | copy-start | bytes 1572868
  93.5 3.6 %collective-permute-start.8 = (bf16[256,1024]{1,0:T(8,128)(2,1)S(1)}, bf16[256,1024]{1,0:T(8,128)(2,1)S(1)}, u32[]{:S(2)}, u32[]{:S(2)}) collective-permute-start(bf16[256,1024]{1,0:T(8,128)(2,1)S(1)} %pad_maximum_fusion.1), channel_id=1, source_target_pairs={{0,1},{1,0},{2,3},{3,2},{4,5},{5,4},{6,7},{7,6},{8,9},{9,8},{10,11... | collective-permute-start | bytes 1572872 | tf_op jit(solution)/shard_map/ppermute | solution.py:28
  95.7 6.9 %copy-start.5 = (bf16[1024,512]{1,0:T(8,128)(2,1)}, bf16[1024,512]{1,0:T(8,128)(2,1)S(1)}, u32[]{:S(2)}) copy-start(bf16[1024,512]{1,0:T(8,128)(2,1)S(1)} %collective-permute-done.9.refs_3_) | copy-start | bytes 3145732
  95.7 12.8 %collective-permute-start.11 = (bf16[4,64,1024]{2,1,0:T(8,128)(2,1)S(1)}, bf16[4,64,1024]{2,1,0:T(8,128)(2,1)S(1)}, u32[]{:S(2)}, u32[]{:S(2)}) collective-permute-start(bf16[4,64,1024]{2,1,0:T(8,128)(2,1)S(1)} %bitcast.85), channel_id=1, source_target_pairs={{0,16},{16,0},{1,17},{17,1},{2,18},{18,2},{3,19},{19,3},{4,20},{20... | collective-permute-start | bytes 1572872 | tf_op jit(solution)/shard_map/ppermute | solution.py:24
  97.1 5.7 %copy-start = (bf16[4,512,1024]{2,1,0:T(8,128)(2,1)}, bf16[4,512,1024]{2,1,0:T(8,128)(2,1)S(1)}, u32[]{:S(2)}) copy-start(bf16[4,512,1024]{2,1,0:T(8,128)(2,1)S(1)} %bitcast_dynamic-update-slice_fusion.5.act_ref) | copy-start | bytes 12582916
  102.7 4.8 %copy-start.28 = (s32[8,256]{1,0:T(8,128)S(1)}, s32[8,256]{1,0:T(8,128)}, u32[]{:S(2)}) copy-start(s32[8,256]{1,0:T(8,128)} %param.10) | copy-start | bytes 24580
  102.7 5.9 %collective-permute-start.10 = (f32[256,512]{1,0:T(8,128)S(1)}, f32[256,512]{1,0:T(8,128)S(1)}, u32[]{:S(2)}, u32[]{:S(2)}) collective-permute-start(f32[256,512]{1,0:T(8,128)S(1)} %slice.83), channel_id=1, source_target_pairs={{0,1},{1,0},{2,3},{3,2},{4,5},{5,4},{6,7},{7,6},{8,9},{9,8},{10,11... | collective-permute-start | bytes 1572872 | tf_op jit(solution)/shard_map/ppermute | solution.py:28
  106.8 4.4 %copy-start.21 = (bf16[4,2,256,512]{3,2,1,0:T(8,128)(2,1)S(1)}, bf16[4,2,256,512]{3,2,1,0:T(8,128)(2,1)}, u32[]{:S(2)}) copy-start(bf16[4,2,256,512]{3,2,1,0:T(8,128)(2,1)} %copy-done.20) | copy-start | bytes 6291460
  106.8 3.0 %collective-permute-start.12 = (f32[256,512]{1,0:T(8,128)S(1)}, f32[256,512]{1,0:T(8,128)S(1)}, u32[]{:S(2)}, u32[]{:S(2)}) collective-permute-start(f32[256,512]{1,0:T(8,128)S(1)} %slice.84), channel_id=1, source_target_pairs={{0,1},{1,0},{2,3},{3,2},{4,5},{5,4},{6,7},{7,6},{8,9},{9,8},{10,11... | collective-permute-start | bytes 1572872 | tf_op jit(solution)/shard_map/ppermute | solution.py:28
  108.6 9.4 %copy-start.7 = (bf16[4,64,1024]{2,1,0:T(8,128)(2,1)}, bf16[4,64,1024]{2,1,0:T(8,128)(2,1)S(1)}, u32[]{:S(2)}) copy-start(bf16[4,64,1024]{2,1,0:T(8,128)(2,1)S(1)} %collective-permute-done.11.g_ref) | copy-start | bytes 1572868
  108.7 9.3 %collective-permute-start.13 = (bf16[4,64,512]{2,1,0:T(8,128)(2,1)S(1)}, bf16[4,64,512]{2,1,0:T(8,128)(2,1)S(1)}, u32[]{:S(2)}, u32[]{:S(2)}) collective-permute-start(bf16[4,64,512]{2,1,0:T(8,128)(2,1)S(1)} %bitcast.88), channel_id=1, source_target_pairs={{0,16},{16,0},{1,17},{17,1},{2,18},{18,2},{3,19},{19,3},{4,20},{20... | collective-permute-start | bytes 786440 | tf_op jit(solution)/shard_map/ppermute | solution.py:24
  109.9 15.1 %collective-permute-start.16 = (bf16[4,64,512]{2,1,0:T(8,128)(2,1)S(1)}, bf16[4,64,512]{2,1,0:T(8,128)(2,1)S(1)}, u32[]{:S(2)}, u32[]{:S(2)}) collective-permute-start(bf16[4,64,512]{2,1,0:T(8,128)(2,1)S(1)} %bitcast.83), channel_id=1, source_target_pairs={{0,16},{16,0},{1,17},{17,1},{2,18},{18,2},{3,19},{19,3},{4,20},{20... | collective-permute-start | bytes 786440 | tf_op jit(solution)/shard_map/ppermute | solution.py:24
  111.3 2.5 %copy-start.14 = (bf16[4,2,256,512]{3,2,1,0:T(8,128)(2,1)S(1)}, bf16[4,2,256,512]{3,2,1,0:T(8,128)(2,1)}, u32[]{:S(2)}) copy-start(bf16[4,2,256,512]{3,2,1,0:T(8,128)(2,1)} %copy-done.13) | copy-start | bytes 6291460
  113.7 2.5 %copy-start.16 = (bf16[4,64,512]{2,1,0:T(8,128)(2,1)}, bf16[4,64,512]{2,1,0:T(8,128)(2,1)S(1)}, u32[]{:S(2)}) copy-start(bf16[4,64,512]{2,1,0:T(8,128)(2,1)S(1)} %get-tuple-element.69) | copy-start | bytes 786436
  113.7 4.2 %copy-start.12 = (bf16[4,2,256,512]{3,2,1,0:T(8,128)(2,1)S(1)}, bf16[4,2,256,512]{3,2,1,0:T(8,128)(2,1)}, u32[]{:S(2)}) copy-start(bf16[4,2,256,512]{3,2,1,0:T(8,128)(2,1)} %copy-done.11) | copy-start | bytes 6291460
  120.5 13.0 %collective-permute-start.14 = (bf16[4,64,512]{2,1,0:T(8,128)(2,1)}, bf16[4,64,512]{2,1,0:T(8,128)(2,1)S(1)}, u32[]{:S(2)}, u32[]{:S(2)}) collective-permute-start(bf16[4,64,512]{2,1,0:T(8,128)(2,1)} %get-tuple-element.74), channel_id=1, source_target_pairs={{0,16},{16,0},{1,17},{17,1},{2,18},{18,2},{3,19},{19,3},{4,20},{20... | collective-permute-start | bytes 786440 | tf_op jit(solution)/shard_map/ppermute | solution.py:24
  129.3 4.2 %copy-start.17 = (bf16[4,64,512]{2,1,0:T(8,128)(2,1)S(1)}, bf16[4,64,512]{2,1,0:T(8,128)(2,1)}, u32[]{:S(2)}) copy-start(bf16[4,64,512]{2,1,0:T(8,128)(2,1)} %copy-done.16) | copy-start | bytes 786436
  129.3 4.3 %copy-start.6 = (bf16[1024,512]{1,0:T(8,128)(2,1)S(1)}, bf16[1024,512]{1,0:T(8,128)(2,1)}, u32[]{:S(2)}) copy-start(bf16[1024,512]{1,0:T(8,128)(2,1)} %copy-done.5) | copy-start | bytes 3145732
  129.3 5.9 %copy-start.1 = (bf16[4,512,1024]{2,1,0:T(8,128)(2,1)S(1)}, bf16[4,512,1024]{2,1,0:T(8,128)(2,1)}, u32[]{:S(2)}) copy-start(bf16[4,512,1024]{2,1,0:T(8,128)(2,1)} %copy-done) | copy-start | bytes 12582916
  131.8 7.9 %collective-permute-start.17 = (bf16[4,64,512]{2,1,0:T(8,128)(2,1)S(1)}, bf16[4,64,512]{2,1,0:T(8,128)(2,1)S(1)}, u32[]{:S(2)}, u32[]{:S(2)}) collective-permute-start(bf16[4,64,512]{2,1,0:T(8,128)(2,1)S(1)} %get-tuple-element.78), channel_id=1, source_target_pairs={{0,16},{16,0},{1,17},{17,1},{2,18},{18,2},{3,19},{19,3},{4,20},{20... | collective-permute-start | bytes 786440 | tf_op jit(solution)/shard_map/ppermute | solution.py:24
  133.6 1.6 collective-permute-start.15
  139.7 3.6 %collective-permute-start.18 = (bf16[256,512]{1,0:T(8,128)(2,1)S(1)}, bf16[256,512]{1,0:T(8,128)(2,1)S(1)}, u32[]{:S(2)}, u32[]{:S(2)}) collective-permute-start(bf16[256,512]{1,0:T(8,128)(2,1)S(1)} %bitcast_add_fusion), channel_id=1, source_target_pairs={{0,1},{1,0},{2,3},{3,2},{4,5},{5,4},{6,7},{7,6},{8,9},{9,8},{10,11... | collective-permute-start | bytes 786440 | tf_op jit(solution)/shard_map/ppermute | solution.py:28
  142.7 25.6 %collective-permute-start.21 = (bf16[1024,512]{1,0:T(8,128)(2,1)S(1)}, bf16[1024,512]{1,0:T(8,128)(2,1)S(1)}, u32[]{:S(2)}, u32[]{:S(2)}) collective-permute-start(bf16[1024,512]{1,0:T(8,128)(2,1)S(1)} %convolution_convert_fusion.5), channel_id=1, source_target_pairs={{0,2},{1,3},{2,0},{3,1},{4,6},{5,7},{6,4},{7,5},{8,10},{9,11},{10,... | collective-permute-start | bytes 3145736 | tf_op jit(solution)/shard_map/ppermute | solution.py:24
  145.6 25.3 %collective-permute-start.22 = (bf16[1024,512]{1,0:T(8,128)(2,1)S(1)}, bf16[1024,512]{1,0:T(8,128)(2,1)S(1)}, u32[]{:S(2)}, u32[]{:S(2)}) collective-permute-start(bf16[1024,512]{1,0:T(8,128)(2,1)S(1)} %convolution_convert_fusion.4), channel_id=1, source_target_pairs={{0,16},{16,0},{1,17},{17,1},{2,18},{18,2},{3,19},{19,3},{4,20},{20... | collective-permute-start | bytes 3145736 | tf_op jit(solution)/shard_map/ppermute | solution.py:24
  145.9 25.0 %collective-permute-start.19 = (bf16[256,1024]{1,0:T(8,128)(2,1)S(1)}, bf16[256,1024]{1,0:T(8,128)(2,1)S(1)}, u32[]{:S(2)}, u32[]{:S(2)}) collective-permute-start(bf16[256,1024]{1,0:T(8,128)(2,1)S(1)} %get-tuple-element.105), channel_id=1, source_target_pairs={{0,4},{4,8},{8,12},{12,0},{1,5},{5,9},{9,13},{13,1},{2,6},{6,10},{... | collective-permute-start | bytes 1572872 | tf_op jit(solution)/shard_map/ppermute | solution.py:24
  145.9 25.4 %collective-permute-start.20 = (bf16[256,1024]{1,0:T(8,128)(2,1)S(1)}, bf16[256,1024]{1,0:T(8,128)(2,1)S(1)}, u32[]{:S(2)}, u32[]{:S(2)}) collective-permute-start(bf16[256,1024]{1,0:T(8,128)(2,1)S(1)} %get-tuple-element.104), channel_id=1, source_target_pairs={{0,12},{4,0},{8,4},{12,8},{1,13},{5,1},{9,5},{13,9},{2,14},{6,2},{... | collective-permute-start | bytes 1572872 | tf_op jit(solution)/shard_map/ppermute | solution.py:24
  149.7 2.6 %slice-start = ((s8[8388608]{0:T(1024)(128)(4,1)}), s8[4194304]{0:T(1024)(128)(4,1)S(1)}, s32[]{:S(2)}) async-start(s8[8388608]{0:T(1024)(128)(4,1)} %bitcast.90), calls=%async_computation | async-start | bytes 8388608
  151.0 2.4 %slice-start.1 = ((s8[8388608]{0:T(1024)(128)(4,1)}), s8[4194304]{0:T(1024)(128)(4,1)S(1)}, s32[]{:S(2)}) async-start(s8[8388608]{0:T(1024)(128)(4,1)} %bitcast.90), calls=%async_computation.1 | async-start | bytes 8388608
  171.5 25.6 %collective-permute-start.26 = (bf16[512,1024]{1,0:T(8,128)(2,1)S(1)}, bf16[512,1024]{1,0:T(8,128)(2,1)S(1)}, u32[]{:S(2)}, u32[]{:S(2)}) collective-permute-start(bf16[512,1024]{1,0:T(8,128)(2,1)S(1)} %fusion.33), channel_id=1, source_target_pairs={{0,12},{4,0},{8,4},{12,8},{1,13},{5,1},{9,5},{13,9},{2,14},{6,2},{... | collective-permute-start | bytes 3145736 | tf_op jit(solution)/shard_map/ppermute | solution.py:24
  174.1 46.8 %collective-permute-start.24 = (bf16[1024,1024]{1,0:T(8,128)(2,1)S(1)}, bf16[1024,1024]{1,0:T(8,128)(2,1)S(1)}, u32[]{:S(2)}, u32[]{:S(2)}) collective-permute-start(bf16[1024,1024]{1,0:T(8,128)(2,1)S(1)} %fusion.19), channel_id=1, source_target_pairs={{0,2},{1,3},{2,0},{3,1},{4,6},{5,7},{6,4},{7,5},{8,10},{9,11},{10,... | collective-permute-start | bytes 6291464 | tf_op jit(solution)/shard_map/ppermute | solution.py:24
  176.3 46.3 %collective-permute-start.23 = (bf16[1024,1024]{1,0:T(8,128)(2,1)S(1)}, bf16[1024,1024]{1,0:T(8,128)(2,1)S(1)}, u32[]{:S(2)}, u32[]{:S(2)}) collective-permute-start(bf16[1024,1024]{1,0:T(8,128)(2,1)S(1)} %fusion.18), channel_id=1, source_target_pairs={{0,16},{16,0},{1,17},{17,1},{2,18},{18,2},{3,19},{19,3},{4,20},{20... | collective-permute-start | bytes 6291464 | tf_op jit(solution)/shard_map/ppermute | solution.py:24
  178.2 41.6 %collective-permute-start.25 = (bf16[512,1024]{1,0:T(8,128)(2,1)S(1)}, bf16[512,1024]{1,0:T(8,128)(2,1)S(1)}, u32[]{:S(2)}, u32[]{:S(2)}) collective-permute-start(bf16[512,1024]{1,0:T(8,128)(2,1)S(1)} %fusion.32), channel_id=1, source_target_pairs={{0,4},{4,8},{8,12},{12,0},{1,5},{5,9},{9,13},{13,1},{2,6},{6,10},{... | collective-permute-start | bytes 3145736 | tf_op jit(solution)/shard_map/ppermute | solution.py:24
  220.1 4.7 %collective-permute-start.27 = (bf16[256,1024]{1,0:T(8,128)(2,1)S(1)}, bf16[256,1024]{1,0:T(8,128)(2,1)S(1)}, u32[]{:S(2)}, u32[]{:S(2)}) collective-permute-start(bf16[256,1024]{1,0:T(8,128)(2,1)S(1)} %add_convert_fusion.2), channel_id=1, source_target_pairs={{0,1},{1,0},{2,3},{3,2},{4,5},{5,4},{6,7},{7,6},{8,9},{9,8},{10,11... | collective-permute-start | bytes 1572872 | tf_op jit(solution)/shard_map/ppermute | solution.py:28
  (12 other events, 14.5 us)

commit v13 on v11

--- a/solution.py
+++ b/solution.py
@@ -305,7 +305,19 @@
     half = width // 2
     opposite = tensor_count // 2
 
-    raw = gather_ring(span_act, "tensor", tensor_count, opposite - 1)
+    def columns_of(which):
+        return jnp.concatenate(
+            [
+                lax.dynamic_slice(span_act, (0, (2 * p + which) * depth), (rows, depth))
+                for p in range(per)
+            ],
+            axis=1,
+        )
+
+    act_both = jnp.concatenate([columns_of(core), swap(columns_of(1 - core))], axis=0)
+
+    act_both, q_weight = lax.optimization_barrier((act_both, q_weight))
+    acts = gather_ring(act_both, "tensor", tensor_count, opposite - 1)
     along_seq = gather_ring(q_weight, "seq", seq_count)
     along_dp = gather_ring(q_weight, "dp", couples)
 
@@ -341,35 +353,18 @@
     cut = width * 5 // 8 // HD * HD
     left_from = [block[:, :cut] for block in along_seq[1:]]
     right_from = [block[:, cut:] for block in along_dp[1:]]
-    left_from, right_from, raw, staged = lax.optimization_barrier(
-        (left_from, right_from, [raw[k] for k in near], staged)
+    left_from, right_from, found, staged = lax.optimization_barrier(
+        (left_from, right_from, [acts[k] for k in near], staged)
     )
-    raw = dict(zip(near, raw))
+    acts = found[:opposite] + [None] + found[opposite:]
 
     corner_left = [gather_ring(block, "dp", couples) for block in left_from]
     corner_right = [gather_ring(block, "seq", seq_count) for block in right_from]
-    up = shift(raw[opposite - 1][:rows // 2], "tensor", 1)
-    down = shift(raw[opposite + 1][rows // 2:], "tensor", -1)
+    up = shift(acts[opposite - 1][:rows], "tensor", 1)
+    down = shift(acts[opposite + 1][rows:], "tensor", -1)
+    acts[opposite] = jnp.concatenate([up, down], axis=0)
     grad_out = after(out_grad, corner_right)
     grads = [to_owner(grad_out, step) for step in range(seq_count)]
-
-    def columns_of(block, which):
-        return jnp.concatenate(
-            [
-                lax.dynamic_slice(block, (0, (2 * p + which) * depth), (block.shape[0], depth))
-                for p in range(per)
-            ],
-            axis=1,
-        )
-
-    others = swap(jnp.concatenate([columns_of(raw[k], 1 - core) for k in near], axis=0))
-    up, down, others = lax.optimization_barrier((up, down, others))
-    raw[opposite] = jnp.concatenate([up, down], axis=0)
-    others = {k: others[n * rows:(n + 1) * rows] for n, k in enumerate(near)}
-    others[opposite] = swap(columns_of(raw[opposite], 1 - core))
-    acts = [
-        jnp.concatenate([columns_of(raw[k], core), others[k]], axis=0) for k in range(tensor_count)
-    ]
     depth_blocks = [(tensor_at - k) % tensor_count for k in range(tensor_count)]
     table = jnp.stack(depth_blocks).astype(jnp.int32)
 
@@ -511,9 +506,8 @@
     from_dp = reduce_rings([([None] + beside_dp, True)], "dp")[0][1:]
 
     weight_grad = summed([own] + from_seq + from_dp)
-    others = after([part[rows:] for part in (act_parts[0], up, down)], weight_grad)
-    arrived = swap(total(others).astype(BF16))
-    act_grad = assemble(core, act_parts[0], up, down, arrived, depth)
+    arrived = swap(total([part[rows:] for part in (act_parts[0], up, down)]).astype(BF16))
+    act_grad = assemble(after(core, weight_grad), act_parts[0], up, down, arrived, depth)
     return (act_grad, weight_grad, kv_grad)
 
 

time: 226 us -> 221 us (0.978)
  local copies, waits for them, and re-layouts: 39.2 us -> 27.4 us
  waiting for transfers between devices: 112 us -> 121 us
  Pallas kernels: 28.2 us -> 21.8 us
  starting transfers between devices: 27.3 us -> 32.8 us
    ppermute x21, waiting for transfers between devices: 109 us -> 119 us  [shift(): lax.ppermute(value, axis, [(i, (i + step * stride) % size) for i in range...]
    pallas_call x4, Pallas kernels: 18 us -> 11.5 us  [attend(): pl.pallas_call(attend_kernel, grid_spec=pltpu.PrefetchScalarGridSpec(num_...]
    ppermute x21, starting transfers between devices: 26.4 us -> 31.7 us  [shift(): lax.ppermute(value, axis, [(i, (i + step * stride) % size) for i in range...]
    dynamic_update_slice x5, local copies, waits for them, and re-layouts: 9.7 us -> 6.07 us  [on_device(): lax.dynamic_update_slice(weights, piece[None], (at, inner * depth, start))]
    unnamed x77 -> x59, local copies, waits for them, and re-layouts: 16.6 us -> 13.5 us
    slice x7 -> x2, local copies, waits for them, and re-layouts: 2.82 us -> 0.07 us  [the longest x1 0.04 us: on_device(): up = shift(acts[opposite - 1][:rows], 'tensor', 1)]
  transfers between devices with their start and end apart: 28 -> 27, of which waited for: 12 -> 16; matrix products, arithmetic and copies ran while one was open for 16% -> 12% of each run, Pallas kernels for 11% -> 9%
where the time goes in v13:
time: 221 us; the launch traced here: 220 us
  waiting for transfers between devices  121 us (55%)
  starting transfers between devices  32.8 us (15%)
  local copies, waits for them, and re-layouts  27.4 us (12%)
  Pallas kernels  21.8 us (10%)
  matrix products  10.7 us (5%)
  other arithmetic  4.55 us (2%)
    ppermute x21, waiting for transfers between devices, shift(): lax.ppermute(value, axis, [(i, (i + step * stride) % size) for i in range...  119 us
    ppermute x21, starting transfers between devices, shift(): lax.ppermute(value, axis, [(i, (i + step * stride) % size) for i in range...  31.7 us
    unnamed x59, local copies, waits for them, and re-layouts  13.5 us
    pallas_call x4, Pallas kernels, attend(): pl.pallas_call(attend_kernel, grid_spec=pltpu.PrefetchScalarGridSpec(num_...  11.5 us
    dot_general x9, matrix products, dot(): lax.dot_general(a, b, (contract, ((), ())), preferred_element_type=F32)  10.7 us
    dynamic_update_slice x5, local copies, waits for them, and re-layouts, on_device(): lax.dynamic_update_slice(weights, piece[None], (at, inner * depth, start))  6.07 us
    pallas_call x2, Pallas kernels, product(): pl.pallas_call(functools.partial(product_kernel, count, start), out_shape...  5.79 us
  transfers between devices with their start and end apart: 27, of which 16 were waited for; matrix products, arithmetic and copies ran while one was open for 12% of the time, Pallas kernels for 9%

profile of v13, /device:TPU:0, one launch (start us, length us, event | category | flops | bytes accessed | tf_op | source)
XLA Modules:
  0.0 220.0 jit_solution(2717424131019049069)
XLA Ops:
  2.4 1.5 collective-permute-done
  4.1 2.9 %collective-permute-start.1 = (bf16[1024,1024]{1,0:T(8,128)(2,1)}, bf16[1024,1024]{1,0:T(8,128)(2,1)}, u32[]{:S(2)}, u32[]{:S(2)}) collective-permute-start(bf16[1024,1024]{1,0:T(8,128)(2,1)} %param.7), channel_id=1, source_target_pairs={{0,16},{16,0},{1,17},{17,1},{2,18},{18,2},{3,19},{19,3},{4,20},{20... | collective-permute-start | bytes 6291464 | tf_op jit(solution)/shard_map/ppermute | solution.py:24
  7.0 1.5 collective-permute-start.2
  8.5 1.6 collective-permute-start.3
  10.1 2.2 %collective-permute-start.4 = (bf16[512,1024]{1,0:T(8,128)(2,1)S(1)}, bf16[512,1024]{1,0:T(8,128)(2,1)S(1)}, u32[]{:S(2)}, u32[]{:S(2)}) collective-permute-start(bf16[512,1024]{1,0:T(8,128)(2,1)S(1)} %pad_maximum_fusion.1.refs_0_), channel_id=1, source_target_pairs={{0,12},{4,0},{8,4},{12,8},{1,13},{5,1},{9,5},{13,9},{2,14},{6,2},{... | collective-permute-start | bytes 3145736 | tf_op jit(solution)/shard_map/ppermute | solution.py:24
  12.3 3.4 %copy-done.1 = bf16[8,2,256,1024]{3,2,1,0:T(8,128)(2,1)S(1)} copy-done((bf16[8,2,256,1024]{3,2,1,0:T(8,128)(2,1)S(1)}, bf16[8,2,256,1024]{3,2,1,0:T(8,128)(2,1)}, u32[]{:S(2)}) %copy-start.1) | copy-done | bytes 8388632
  16.1 1.3 copy-done.8
  19.0 1.4 copy-done.12
  20.4 1.3 copy-done.19
  22.4 14.0 %collective-permute-done.3.refs_1_ = bf16[512,1024]{1,0:T(8,128)(2,1)S(1)} collective-permute-done((bf16[512,1024]{1,0:T(8,128)(2,1)S(1)}, bf16[512,1024]{1,0:T(8,128)(2,1)S(1)}, u32[]{:S(2)}, u32[]{:S(2)}) %collective-permute-start.3) | collective-permute-done | bytes 1048608 | tf_op jit(solution)/shard_map/ppermute | solution.py:24
  36.4 20.5 %collective-permute-done.4.refs_3_ = bf16[512,1024]{1,0:T(8,128)(2,1)S(1)} collective-permute-done((bf16[512,1024]{1,0:T(8,128)(2,1)S(1)}, bf16[512,1024]{1,0:T(8,128)(2,1)S(1)}, u32[]{:S(2)}, u32[]{:S(2)}) %collective-permute-start.4) | collective-permute-done | bytes 1048608 | tf_op jit(solution)/shard_map/ppermute | solution.py:24
  56.9 1.8 slice.68
  61.7 1.9 bitcast_dynamic-update-slice_fusion.2
  64.8 2.9 %collective-permute-start.6 = (bf16[256,1024]{1,0:T(8,128)(2,1)S(1)}, bf16[256,1024]{1,0:T(8,128)(2,1)S(1)}, u32[]{:S(2)}, u32[]{:S(2)}) collective-permute-start(bf16[256,1024]{1,0:T(8,128)(2,1)S(1)} %slice.54), channel_id=1, source_target_pairs={{0,12},{4,0},{8,4},{12,8},{1,13},{5,1},{9,5},{13,9},{2,14},{6,2},{... | collective-permute-start | bytes 1572872 | tf_op jit(solution)/shard_map/ppermute | solution.py:24
  68.3 1.9 bitcast_dynamic-update-slice_fusion.1
  70.1 1.9 bitcast_dynamic-update-slice_fusion
  72.0 8.3 %collective-permute-done.5 = bf16[256,1024]{1,0:T(8,128)(2,1)S(1)} collective-permute-done((bf16[256,1024]{1,0:T(8,128)(2,1)S(1)}, bf16[256,1024]{1,0:T(8,128)(2,1)S(1)}, u32[]{:S(2)}, u32[]{:S(2)}) %collective-permute-start.5) | collective-permute-done | bytes 524320 | tf_op jit(solution)/shard_map/ppermute | solution.py:24
  80.3 9.2 %collective-permute-done.6 = bf16[256,1024]{1,0:T(8,128)(2,1)S(1)} collective-permute-done((bf16[256,1024]{1,0:T(8,128)(2,1)S(1)}, bf16[256,1024]{1,0:T(8,128)(2,1)S(1)}, u32[]{:S(2)}, u32[]{:S(2)}) %collective-permute-start.6) | collective-permute-done | bytes 524320 | tf_op jit(solution)/shard_map/ppermute | solution.py:24
  90.7 2.9 %shard_map.87 = f32[512,512]{1,0:T(8,128)S(1)} custom-call(s32[4]{0:T(128)S(1)} %pad_add_fusion.1.table_ref, bf16[512,1024]{1,0:T(8,128)(2,1)S(1)} %pad_maximum_fusion.1.refs_0_, bf16[512,1024]{1,0:T(8,128)(2,1)S(1)} %collective-permute-done.3.refs_1_, bf16[512,1024]{1,0:T(8,128)(2,1)S(1)} %constant_dynamic-update-slice_fusion.refs_2_, ...), custom_call_target="tpu_custom_call" | custom-call | flops 2147483648 | bytes 9437184 | tf_op jit(solution)/shard_map/pallas_call | solution.py:90
  94.0 2.9 %shard_map.88 = f32[512,512]{1,0:T(8,128)S(1)} custom-call(s32[4]{0:T(128)S(1)} %pad_add_fusion.1.table_ref, bf16[512,1024]{1,0:T(8,128)(2,1)S(1)} %pad_maximum_fusion.1.refs_0_, bf16[512,1024]{1,0:T(8,128)(2,1)S(1)} %collective-permute-done.3.refs_1_, bf16[512,1024]{1,0:T(8,128)(2,1)S(1)} %constant_dynamic-update-slice_fusion.refs_2_, ...), custom_call_target="tpu_custom_call" | custom-call | flops 2147483648 | bytes 9437184 | tf_op jit(solution)/shard_map/pallas_call | solution.py:90
  97.4 6.1 %collective-permute-done.10.g_ref = bf16[4,64,1024]{2,1,0:T(8,128)(2,1)S(1)} collective-permute-done((bf16[4,64,1024]{2,1,0:T(8,128)(2,1)S(1)}, bf16[4,64,1024]{2,1,0:T(8,128)(2,1)S(1)}, u32[]{:S(2)}, u32[]{:S(2)}) %collective-permute-start.10) | collective-permute-done | bytes 524320 | tf_op jit(solution)/shard_map/ppermute | solution.py:24
  104.3 1.6 collective-permute-start.15
  106.2 2.5 %shard_map.89 = (bf16[4,64,512]{2,1,0:T(8,128)(2,1)S(1)}, bf16[8,2,256,1024]{3,2,1,0:T(8,128)(2,1)}) custom-call(s32[12]{0:T(128)S(1)} %pad_add_fusion.table_ref, bf16[4,64,512]{2,1,0:T(8,128)(2,1)S(1)} %bitcast.79, bf16[4,64,1024]{2,1,0:T(8,128)(2,1)S(1)} %bitcast.76, f32[8,256,128]{2,1,0:T(8,128)S(1)} %broadcast_in_dim.20.live_ref, ...), custom_call_target="tpu_custom_call" | custom-call | flops 1342177280 | bytes 4194304 | tf_op jit(solution)/shard_map/pallas_call | solution.py:179
  108.6 2.5 %shard_map.90 = (bf16[4,64,512]{2,1,0:T(8,128)(2,1)S(1)}, bf16[8,2,256,1024]{3,2,1,0:T(8,128)(2,1)}) custom-call(s32[12]{0:T(128)S(1)} %pad_add_fusion.table_ref, bf16[4,64,512]{2,1,0:T(8,128)(2,1)S(1)} %bitcast.74, bf16[4,64,1024]{2,1,0:T(8,128)(2,1)S(1)} %bitcast.77, ...), custom_call_target="tpu_custom_call", output_to_operand_aliasing={{1}: (5, {})} | custom-call | flops 1342177280 | bytes 4194304 | tf_op jit(solution)/shard_map/pallas_call | solution.py:179
  111.1 1.8 collective-permute-done.12.q_ref
  112.9 2.5 %shard_map.91 = (bf16[4,64,512]{2,1,0:T(8,128)(2,1)}, bf16[8,2,256,1024]{3,2,1,0:T(8,128)(2,1)}) custom-call(s32[12]{0:T(128)S(1)} %pad_add_fusion.2.table_ref, bf16[4,64,512]{2,1,0:T(8,128)(2,1)S(1)} %collective-permute-done.12.q_ref, bf16[4,64,1024]{2,1,0:T(8,128)(2,1)S(1)} %collective-permute-done.10.g_ref, ...), custom_call_target="tpu_custom_call", output_to_operand_aliasing={{1}: (5, {})} | custom-call | flops 1342177280 | bytes 4194304 | tf_op jit(solution)/shard_map/pallas_call | solution.py:179
  115.4 4.0 %collective-permute-start.13 = (bf16[4,64,512]{2,1,0:T(8,128)(2,1)}, bf16[4,64,512]{2,1,0:T(8,128)(2,1)}, u32[]{:S(2)}, u32[]{:S(2)}) collective-permute-start(bf16[4,64,512]{2,1,0:T(8,128)(2,1)} %get-tuple-element.71), channel_id=1, source_target_pairs={{0,16},{16,0},{1,17},{17,1},{2,18},{18,2},{3,19},{19,3},{4,20},{20... | collective-permute-start | bytes 786440 | tf_op jit(solution)/shard_map/ppermute | solution.py:24
  120.4 1.6 copy-done.9
  122.0 4.1 %shard_map.92 = (bf16[4,64,512]{2,1,0:T(8,128)(2,1)S(1)}, bf16[8,2,256,1024]{3,2,1,0:T(8,128)(2,1)}) custom-call(s32[12]{0:T(128)S(1)} %pad_add_fusion.2.table_ref, bf16[4,64,512]{2,1,0:T(8,128)(2,1)} %collective-permute-done.15.q_ref, bf16[4,64,1024]{2,1,0:T(8,128)(2,1)S(1)} %copy-done.7, ...), custom_call_target="tpu_custom_call", output_to_operand_aliasing={{1}: (5, {})} | custom-call | flops 1342177280 | bytes 4194304 | tf_op jit(solution)/shard_map/pallas_call | solution.py:179
  130.8 2.8 %collective-permute-done.16 = bf16[4,64,512]{2,1,0:T(8,128)(2,1)S(1)} collective-permute-done((bf16[4,64,512]{2,1,0:T(8,128)(2,1)S(1)}, bf16[4,64,512]{2,1,0:T(8,128)(2,1)S(1)}, u32[]{:S(2)}, u32[]{:S(2)}) %collective-permute-start.16) | collective-permute-done | bytes 262176 | tf_op jit(solution)/shard_map/ppermute | solution.py:24
  133.8 1.8 dynamic-slice_bitcast_fusion
  135.6 1.6 collective-permute-start.20
  137.3 1.3 convolution_convert_fusion.3
  140.7 3.8 %collective-permute-start.19 = (bf16[256,1024]{1,0:T(8,128)(2,1)S(1)}, bf16[256,1024]{1,0:T(8,128)(2,1)S(1)}, u32[]{:S(2)}, u32[]{:S(2)}) collective-permute-start(bf16[256,1024]{1,0:T(8,128)(2,1)S(1)} %get-tuple-element.99), channel_id=1, source_target_pairs={{0,12},{4,0},{8,4},{12,8},{1,13},{5,1},{9,5},{13,9},{2,14},{6,2},{... | collective-permute-start | bytes 1572872 | tf_op jit(solution)/shard_map/ppermute | solution.py:24
  144.6 1.3 convolution_convert_fusion
  145.9 1.3 convolution_convert_fusion.1
  148.3 1.3 fusion.15
  149.6 1.3 convolution_convert_fusion.2.refs_0_
  150.9 1.3 fusion.12
  152.3 1.3 fusion.9.own_ref
  153.6 7.6 %collective-permute-done.20 = bf16[1024,512]{1,0:T(8,128)(2,1)S(1)} collective-permute-done((bf16[1024,512]{1,0:T(8,128)(2,1)S(1)}, bf16[1024,512]{1,0:T(8,128)(2,1)S(1)}, u32[]{:S(2)}, u32[]{:S(2)}) %collective-permute-start.20) | collective-permute-done | bytes 1048608 | tf_op jit(solution)/shard_map/ppermute | solution.py:24
  161.2 4.3 %collective-permute-done.21 = bf16[1024,512]{1,0:T(8,128)(2,1)S(1)} collective-permute-done((bf16[1024,512]{1,0:T(8,128)(2,1)S(1)}, bf16[1024,512]{1,0:T(8,128)(2,1)S(1)}, u32[]{:S(2)}, u32[]{:S(2)}) %collective-permute-start.21) | collective-permute-done | bytes 1048608 | tf_op jit(solution)/shard_map/ppermute | solution.py:24
  166.0 2.0 collective-permute-start.25
  169.8 1.6 collective-permute-start.22
  171.8 19.9 %collective-permute-done.25.down_ref = bf16[512,1024]{1,0:T(8,128)(2,1)S(1)} collective-permute-done((bf16[512,1024]{1,0:T(8,128)(2,1)S(1)}, bf16[512,1024]{1,0:T(8,128)(2,1)S(1)}, u32[]{:S(2)}, u32[]{:S(2)}) %collective-permute-start.25) | collective-permute-done | bytes 1048608 | tf_op jit(solution)/shard_map/ppermute | solution.py:24
  191.6 22.6 %collective-permute-done.24.up_ref = bf16[512,1024]{1,0:T(8,128)(2,1)S(1)} collective-permute-done((bf16[512,1024]{1,0:T(8,128)(2,1)S(1)}, bf16[512,1024]{1,0:T(8,128)(2,1)S(1)}, u32[]{:S(2)}, u32[]{:S(2)}) %collective-permute-start.24) | collective-permute-done | bytes 1048608 | tf_op jit(solution)/shard_map/ppermute | solution.py:24
  216.1 2.2 shard_map.93
  218.3 1.6 shard_map.94
  (126 shorter events, 25.8 us)
Async XLA Ops:
  1.9 2.1 collective-permute-start
  4.1 52.9 %collective-permute-start.1 = (bf16[1024,1024]{1,0:T(8,128)(2,1)}, bf16[1024,1024]{1,0:T(8,128)(2,1)}, u32[]{:S(2)}, u32[]{:S(2)}) collective-permute-start(bf16[1024,1024]{1,0:T(8,128)(2,1)} %param.7), channel_id=1, source_target_pairs={{0,16},{16,0},{1,17},{17,1},{2,18},{18,2},{3,19},{19,3},{4,20},{20... | collective-permute-start | bytes 6291464 | tf_op jit(solution)/shard_map/ppermute | solution.py:24
  7.0 51.7 %collective-permute-start.2 = (bf16[1024,1024]{1,0:T(8,128)(2,1)}, bf16[1024,1024]{1,0:T(8,128)(2,1)}, u32[]{:S(2)}, u32[]{:S(2)}) collective-permute-start(bf16[1024,1024]{1,0:T(8,128)(2,1)} %param.7), channel_id=1, source_target_pairs={{0,2},{1,3},{2,0},{3,1},{4,6},{5,7},{6,4},{7,5},{8,10},{9,11},{10,... | collective-permute-start | bytes 6291464 | tf_op jit(solution)/shard_map/ppermute | solution.py:24
  8.5 27.9 %collective-permute-start.3 = (bf16[512,1024]{1,0:T(8,128)(2,1)S(1)}, bf16[512,1024]{1,0:T(8,128)(2,1)S(1)}, u32[]{:S(2)}, u32[]{:S(2)}) collective-permute-start(bf16[512,1024]{1,0:T(8,128)(2,1)S(1)} %pad_maximum_fusion.1.refs_0_), channel_id=1, source_target_pairs={{0,4},{4,8},{8,12},{12,0},{1,5},{5,9},{9,13},{13,1},{2,6},{6,10},{... | collective-permute-start | bytes 3145736 | tf_op jit(solution)/shard_map/ppermute | solution.py:24
  10.1 46.8 %collective-permute-start.4 = (bf16[512,1024]{1,0:T(8,128)(2,1)S(1)}, bf16[512,1024]{1,0:T(8,128)(2,1)S(1)}, u32[]{:S(2)}, u32[]{:S(2)}) collective-permute-start(bf16[512,1024]{1,0:T(8,128)(2,1)S(1)} %pad_maximum_fusion.1.refs_0_), channel_id=1, source_target_pairs={{0,12},{4,0},{8,4},{12,8},{1,13},{5,1},{9,5},{13,9},{2,14},{6,2},{... | collective-permute-start | bytes 3145736 | tf_op jit(solution)/shard_map/ppermute | solution.py:24
  12.3 3.4 %copy-start.1 = (bf16[8,2,256,1024]{3,2,1,0:T(8,128)(2,1)S(1)}, bf16[8,2,256,1024]{3,2,1,0:T(8,128)(2,1)}, u32[]{:S(2)}) copy-start(bf16[8,2,256,1024]{3,2,1,0:T(8,128)(2,1)} %kv_ref.3) | copy-start | bytes 25165828
  18.7 3.1 %copy-start.24 = (s32[32]{0:T(128)S(1)}, s32[32]{0:T(128)}, u32[]{:S(2)}) copy-start(s32[32]{0:T(128)} %param.11) | copy-start | bytes 388
  56.9 36.9 %copy-start.2 = (bf16[512,1024]{1,0:T(8,128)(2,1)}, bf16[512,1024]{1,0:T(8,128)(2,1)S(1)}, u32[]{:S(2)}) copy-start(bf16[512,1024]{1,0:T(8,128)(2,1)S(1)} %collective-permute-done.4.refs_3_) | copy-start | bytes 3145732
  60.0 30.3 %collective-permute-start.7 = (bf16[1024,640]{1,0:T(8,128)(2,1)S(1)}, bf16[1024,640]{1,0:T(8,128)(2,1)S(1)}, u32[]{:S(2)}, u32[]{:S(2)}) collective-permute-start(bf16[1024,640]{1,0:T(8,128)(2,1)S(1)} %slice.68), channel_id=1, source_target_pairs={{0,2},{1,3},{2,0},{3,1},{4,6},{5,7},{6,4},{7,5},{8,10},{9,11},{10,... | collective-permute-start | bytes 3932168 | tf_op jit(solution)/shard_map/ppermute | solution.py:24
  63.6 16.7 %collective-permute-start.5 = (bf16[256,1024]{1,0:T(8,128)(2,1)S(1)}, bf16[256,1024]{1,0:T(8,128)(2,1)S(1)}, u32[]{:S(2)}, u32[]{:S(2)}) collective-permute-start(bf16[256,1024]{1,0:T(8,128)(2,1)S(1)} %slice.53), channel_id=1, source_target_pairs={{0,4},{4,8},{8,12},{12,0},{1,5},{5,9},{9,13},{13,1},{2,6},{6,10},{... | collective-permute-start | bytes 1572872 | tf_op jit(solution)/shard_map/ppermute | solution.py:24
  64.8 24.8 %collective-permute-start.6 = (bf16[256,1024]{1,0:T(8,128)(2,1)S(1)}, bf16[256,1024]{1,0:T(8,128)(2,1)S(1)}, u32[]{:S(2)}, u32[]{:S(2)}) collective-permute-start(bf16[256,1024]{1,0:T(8,128)(2,1)S(1)} %slice.54), channel_id=1, source_target_pairs={{0,12},{4,0},{8,4},{12,8},{1,13},{5,1},{9,5},{13,9},{2,14},{6,2},{... | collective-permute-start | bytes 1572872 | tf_op jit(solution)/shard_map/ppermute | solution.py:24
  67.7 21.9 %collective-permute-start.8 = (bf16[1024,384]{1,0:T(8,128)(2,1)S(1)}, bf16[1024,384]{1,0:T(8,128)(2,1)S(1)}, u32[]{:S(2)}, u32[]{:S(2)}) collective-permute-start(bf16[1024,384]{1,0:T(8,128)(2,1)S(1)} %slice.69), channel_id=1, source_target_pairs={{0,16},{16,0},{1,17},{17,1},{2,18},{18,2},{3,19},{19,3},{4,20},{20... | collective-permute-start | bytes 2359304 | tf_op jit(solution)/shard_map/ppermute | solution.py:24
  72.0 17.6 %copy-start.14 = (bf16[256,1024]{1,0:T(8,128)(2,1)S(1)}, bf16[256,1024]{1,0:T(8,128)(2,1)}, u32[]{:S(2)}) copy-start(bf16[256,1024]{1,0:T(8,128)(2,1)} %param.8) | copy-start | bytes 1572868
  89.6 4.2 %copy-start.4 = (bf16[512,1024]{1,0:T(8,128)(2,1)}, bf16[512,1024]{1,0:T(8,128)(2,1)S(1)}, u32[]{:S(2)}) copy-start(bf16[512,1024]{1,0:T(8,128)(2,1)S(1)} %constant_dynamic-update-slice_fusion.refs_2_) | copy-start | bytes 3145732
  89.6 13.8 %collective-permute-start.10 = (bf16[4,64,1024]{2,1,0:T(8,128)(2,1)S(1)}, bf16[4,64,1024]{2,1,0:T(8,128)(2,1)S(1)}, u32[]{:S(2)}, u32[]{:S(2)}) collective-permute-start(bf16[4,64,1024]{2,1,0:T(8,128)(2,1)S(1)} %bitcast.75), channel_id=1, source_target_pairs={{0,16},{16,0},{1,17},{17,1},{2,18},{18,2},{3,19},{19,3},{4,20},{20... | collective-permute-start | bytes 1572872 | tf_op jit(solution)/shard_map/ppermute | solution.py:24
  90.7 3.3 %copy-start = (bf16[4,1024,1024]{2,1,0:T(8,128)(2,1)}, bf16[4,1024,1024]{2,1,0:T(8,128)(2,1)S(1)}, u32[]{:S(2)}) copy-start(bf16[4,1024,1024]{2,1,0:T(8,128)(2,1)S(1)} %bitcast_dynamic-update-slice_fusion.4.refs_4_) | copy-start | bytes 25165828
  93.7 3.7 %copy-start.23 = (s32[8,256]{1,0:T(8,128)S(1)}, s32[8,256]{1,0:T(8,128)}, u32[]{:S(2)}) copy-start(s32[8,256]{1,0:T(8,128)} %param.10) | copy-start | bytes 24580
  93.7 9.8 %collective-permute-start.9 = (f32[256,512]{1,0:T(8,128)S(1)}, f32[256,512]{1,0:T(8,128)S(1)}, u32[]{:S(2)}, u32[]{:S(2)}) collective-permute-start(f32[256,512]{1,0:T(8,128)S(1)} %slice.71), channel_id=1, source_target_pairs={{0,1},{1,0},{2,3},{3,2},{4,5},{5,4},{6,7},{7,6},{8,9},{9,8},{10,11... | collective-permute-start | bytes 1572872 | tf_op jit(solution)/shard_map/ppermute | solution.py:28
  97.0 9.2 %copy-start.20 = (bf16[4,2,256,512]{3,2,1,0:T(8,128)(2,1)S(1)}, bf16[4,2,256,512]{3,2,1,0:T(8,128)(2,1)}, u32[]{:S(2)}) copy-start(bf16[4,2,256,512]{3,2,1,0:T(8,128)(2,1)} %copy-done.19) | copy-start | bytes 6291460
  97.0 7.2 %collective-permute-start.11 = (f32[256,512]{1,0:T(8,128)S(1)}, f32[256,512]{1,0:T(8,128)S(1)}, u32[]{:S(2)}, u32[]{:S(2)}) collective-permute-start(f32[256,512]{1,0:T(8,128)S(1)} %slice.72), channel_id=1, source_target_pairs={{0,1},{1,0},{2,3},{3,2},{4,5},{5,4},{6,7},{7,6},{8,9},{9,8},{10,11... | collective-permute-start | bytes 1572872 | tf_op jit(solution)/shard_map/ppermute | solution.py:28
  103.5 9.4 %copy-start.6 = (bf16[4,64,1024]{2,1,0:T(8,128)(2,1)}, bf16[4,64,1024]{2,1,0:T(8,128)(2,1)S(1)}, u32[]{:S(2)}) copy-start(bf16[4,64,1024]{2,1,0:T(8,128)(2,1)S(1)} %collective-permute-done.10.g_ref) | copy-start | bytes 1572868
  103.6 9.3 %collective-permute-start.12 = (bf16[4,64,512]{2,1,0:T(8,128)(2,1)S(1)}, bf16[4,64,512]{2,1,0:T(8,128)(2,1)S(1)}, u32[]{:S(2)}, u32[]{:S(2)}) collective-permute-start(bf16[4,64,512]{2,1,0:T(8,128)(2,1)S(1)} %bitcast.78), channel_id=1, source_target_pairs={{0,16},{16,0},{1,17},{17,1},{2,18},{18,2},{3,19},{19,3},{4,20},{20... | collective-permute-start | bytes 786440 | tf_op jit(solution)/shard_map/ppermute | solution.py:24
  104.3 15.1 %collective-permute-start.15 = (bf16[4,64,512]{2,1,0:T(8,128)(2,1)S(1)}, bf16[4,64,512]{2,1,0:T(8,128)(2,1)}, u32[]{:S(2)}, u32[]{:S(2)}) collective-permute-start(bf16[4,64,512]{2,1,0:T(8,128)(2,1)S(1)} %bitcast.73), channel_id=1, source_target_pairs={{0,16},{16,0},{1,17},{17,1},{2,18},{18,2},{3,19},{19,3},{4,20},{20... | collective-permute-start | bytes 786440 | tf_op jit(solution)/shard_map/ppermute | solution.py:24
  106.2 2.5 %copy-start.13 = (bf16[4,2,256,512]{3,2,1,0:T(8,128)(2,1)S(1)}, bf16[4,2,256,512]{3,2,1,0:T(8,128)(2,1)}, u32[]{:S(2)}) copy-start(bf16[4,2,256,512]{3,2,1,0:T(8,128)(2,1)} %copy-done.12) | copy-start | bytes 6291460
  108.6 2.5 %copy-start.17 = (bf16[4,64,512]{2,1,0:T(8,128)(2,1)}, bf16[4,64,512]{2,1,0:T(8,128)(2,1)S(1)}, u32[]{:S(2)}) copy-start(bf16[4,64,512]{2,1,0:T(8,128)(2,1)S(1)} %get-tuple-element.66) | copy-start | bytes 786436
  108.6 4.2 %copy-start.11 = (bf16[4,2,256,512]{3,2,1,0:T(8,128)(2,1)S(1)}, bf16[4,2,256,512]{3,2,1,0:T(8,128)(2,1)}, u32[]{:S(2)}) copy-start(bf16[4,2,256,512]{3,2,1,0:T(8,128)(2,1)} %copy-done.10) | copy-start | bytes 6291460
  111.1 4.3 %copy-start.15 = (bf16[4,64,512]{2,1,0:T(8,128)(2,1)}, bf16[4,64,512]{2,1,0:T(8,128)(2,1)S(1)}, u32[]{:S(2)}) copy-start(bf16[4,64,512]{2,1,0:T(8,128)(2,1)S(1)} %get-tuple-element.72) | copy-start | bytes 786436
  115.4 12.0 %collective-permute-start.13 = (bf16[4,64,512]{2,1,0:T(8,128)(2,1)}, bf16[4,64,512]{2,1,0:T(8,128)(2,1)}, u32[]{:S(2)}, u32[]{:S(2)}) collective-permute-start(bf16[4,64,512]{2,1,0:T(8,128)(2,1)} %get-tuple-element.71), channel_id=1, source_target_pairs={{0,16},{16,0},{1,17},{17,1},{2,18},{18,2},{3,19},{19,3},{4,20},{20... | collective-permute-start | bytes 786440 | tf_op jit(solution)/shard_map/ppermute | solution.py:24
  122.0 5.4 %copy-start.18 = (bf16[4,64,512]{2,1,0:T(8,128)(2,1)S(1)}, bf16[4,64,512]{2,1,0:T(8,128)(2,1)}, u32[]{:S(2)}) copy-start(bf16[4,64,512]{2,1,0:T(8,128)(2,1)} %copy-done.17) | copy-start | bytes 786436
  122.0 6.5 %copy-start.3 = (bf16[512,1024]{1,0:T(8,128)(2,1)S(1)}, bf16[512,1024]{1,0:T(8,128)(2,1)}, u32[]{:S(2)}) copy-start(bf16[512,1024]{1,0:T(8,128)(2,1)} %copy-done.2) | copy-start | bytes 3145732
  122.0 6.5 %copy-start.5 = (bf16[512,1024]{1,0:T(8,128)(2,1)S(1)}, bf16[512,1024]{1,0:T(8,128)(2,1)}, u32[]{:S(2)}) copy-start(bf16[512,1024]{1,0:T(8,128)(2,1)} %copy-done.4) | copy-start | bytes 3145732
  126.1 7.5 %collective-permute-start.16 = (bf16[4,64,512]{2,1,0:T(8,128)(2,1)S(1)}, bf16[4,64,512]{2,1,0:T(8,128)(2,1)S(1)}, u32[]{:S(2)}, u32[]{:S(2)}) collective-permute-start(bf16[4,64,512]{2,1,0:T(8,128)(2,1)S(1)} %get-tuple-element.75), channel_id=1, source_target_pairs={{0,16},{16,0},{1,17},{17,1},{2,18},{18,2},{3,19},{19,3},{4,20},{20... | collective-permute-start | bytes 786440 | tf_op jit(solution)/shard_map/ppermute | solution.py:24
  128.4 1.6 collective-permute-start.14
  129.1 4.5 %copy-start.21 = (bf16[4,512,1024]{2,1,0:T(8,128)(2,1)}, bf16[4,512,1024]{2,1,0:T(8,128)(2,1)S(1)}, u32[]{:S(2)}) copy-start(bf16[4,512,1024]{2,1,0:T(8,128)(2,1)S(1)} %pad_maximum_fusion) | copy-start | bytes 12582916
  129.1 4.5 %copy-start.16 = (bf16[4,64,512]{2,1,0:T(8,128)(2,1)S(1)}, bf16[4,64,512]{2,1,0:T(8,128)(2,1)}, u32[]{:S(2)}) copy-start(bf16[4,64,512]{2,1,0:T(8,128)(2,1)} %copy-done.15) | copy-start | bytes 786436
  130.0 3.6 %copy-start.25 = (bf16[256,512]{1,0:T(8,128)(2,1)}, bf16[256,512]{1,0:T(8,128)(2,1)S(1)}, u32[]{:S(2)}) copy-start(bf16[256,512]{1,0:T(8,128)(2,1)S(1)} %collective-permute-done.14) | copy-start | bytes 786436
  133.6 3.6 %collective-permute-start.17 = (bf16[256,512]{1,0:T(8,128)(2,1)S(1)}, bf16[256,512]{1,0:T(8,128)(2,1)S(1)}, u32[]{:S(2)}, u32[]{:S(2)}) collective-permute-start(bf16[256,512]{1,0:T(8,128)(2,1)S(1)} %bitcast_add_fusion), channel_id=1, source_target_pairs={{0,1},{1,0},{2,3},{3,2},{4,5},{5,4},{6,7},{7,6},{8,9},{9,8},{10,11... | collective-permute-start | bytes 786440 | tf_op jit(solution)/shard_map/ppermute | solution.py:28
  133.8 3.4 %copy-start.26 = (bf16[256,512]{1,0:T(8,128)(2,1)S(1)}, bf16[256,512]{1,0:T(8,128)(2,1)}, u32[]{:S(2)}) copy-start(bf16[256,512]{1,0:T(8,128)(2,1)} %copy-done.25) | copy-start | bytes 786436
  135.6 25.5 %collective-permute-start.20 = (bf16[1024,512]{1,0:T(8,128)(2,1)S(1)}, bf16[1024,512]{1,0:T(8,128)(2,1)S(1)}, u32[]{:S(2)}, u32[]{:S(2)}) collective-permute-start(bf16[1024,512]{1,0:T(8,128)(2,1)S(1)} %convolution_convert_fusion.5), channel_id=1, source_target_pairs={{0,2},{1,3},{2,0},{3,1},{4,6},{5,7},{6,4},{7,5},{8,10},{9,11},{10,... | collective-permute-start | bytes 3145736 | tf_op jit(solution)/shard_map/ppermute | solution.py:24
  140.2 25.2 %collective-permute-start.21 = (bf16[1024,512]{1,0:T(8,128)(2,1)S(1)}, bf16[1024,512]{1,0:T(8,128)(2,1)S(1)}, u32[]{:S(2)}, u32[]{:S(2)}) collective-permute-start(bf16[1024,512]{1,0:T(8,128)(2,1)S(1)} %convolution_convert_fusion.4), channel_id=1, source_target_pairs={{0,16},{16,0},{1,17},{17,1},{2,18},{18,2},{3,19},{19,3},{4,20},{20... | collective-permute-start | bytes 3145736 | tf_op jit(solution)/shard_map/ppermute | solution.py:24
  140.7 24.7 %collective-permute-start.18 = (bf16[256,1024]{1,0:T(8,128)(2,1)S(1)}, bf16[256,1024]{1,0:T(8,128)(2,1)S(1)}, u32[]{:S(2)}, u32[]{:S(2)}) collective-permute-start(bf16[256,1024]{1,0:T(8,128)(2,1)S(1)} %get-tuple-element.100), channel_id=1, source_target_pairs={{0,4},{4,8},{8,12},{12,0},{1,5},{5,9},{9,13},{13,1},{2,6},{6,10},{... | collective-permute-start | bytes 1572872 | tf_op jit(solution)/shard_map/ppermute | solution.py:24
  140.7 25.0 %collective-permute-start.19 = (bf16[256,1024]{1,0:T(8,128)(2,1)S(1)}, bf16[256,1024]{1,0:T(8,128)(2,1)S(1)}, u32[]{:S(2)}, u32[]{:S(2)}) collective-permute-start(bf16[256,1024]{1,0:T(8,128)(2,1)S(1)} %get-tuple-element.99), channel_id=1, source_target_pairs={{0,12},{4,0},{8,4},{12,8},{1,13},{5,1},{9,5},{13,9},{2,14},{6,2},{... | collective-permute-start | bytes 1572872 | tf_op jit(solution)/shard_map/ppermute | solution.py:24
  144.6 2.6 %slice-start = ((s8[8388608]{0:T(1024)(128)(4,1)}), s8[4194304]{0:T(1024)(128)(4,1)S(1)}, s32[]{:S(2)}) async-start(s8[8388608]{0:T(1024)(128)(4,1)} %bitcast.67), calls=%async_computation | async-start | bytes 8388608
  166.0 25.6 %collective-permute-start.25 = (bf16[512,1024]{1,0:T(8,128)(2,1)S(1)}, bf16[512,1024]{1,0:T(8,128)(2,1)S(1)}, u32[]{:S(2)}, u32[]{:S(2)}) collective-permute-start(bf16[512,1024]{1,0:T(8,128)(2,1)S(1)} %fusion.31), channel_id=1, source_target_pairs={{0,12},{4,0},{8,4},{12,8},{1,13},{5,1},{9,5},{13,9},{2,14},{6,2},{... | collective-permute-start | bytes 3145736 | tf_op jit(solution)/shard_map/ppermute | solution.py:24
  168.6 46.6 %collective-permute-start.23 = (bf16[1024,1024]{1,0:T(8,128)(2,1)S(1)}, bf16[1024,1024]{1,0:T(8,128)(2,1)S(1)}, u32[]{:S(2)}, u32[]{:S(2)}) collective-permute-start(bf16[1024,1024]{1,0:T(8,128)(2,1)S(1)} %fusion.19), channel_id=1, source_target_pairs={{0,2},{1,3},{2,0},{3,1},{4,6},{5,7},{6,4},{7,5},{8,10},{9,11},{10,... | collective-permute-start | bytes 6291464 | tf_op jit(solution)/shard_map/ppermute | solution.py:24
  169.8 46.3 %collective-permute-start.22 = (bf16[1024,1024]{1,0:T(8,128)(2,1)S(1)}, bf16[1024,1024]{1,0:T(8,128)(2,1)S(1)}, u32[]{:S(2)}, u32[]{:S(2)}) collective-permute-start(bf16[1024,1024]{1,0:T(8,128)(2,1)S(1)} %fusion.18), channel_id=1, source_target_pairs={{0,16},{16,0},{1,17},{17,1},{2,18},{18,2},{3,19},{19,3},{4,20},{20... | collective-permute-start | bytes 6291464 | tf_op jit(solution)/shard_map/ppermute | solution.py:24
  171.7 42.5 %collective-permute-start.24 = (bf16[512,1024]{1,0:T(8,128)(2,1)S(1)}, bf16[512,1024]{1,0:T(8,128)(2,1)S(1)}, u32[]{:S(2)}, u32[]{:S(2)}) collective-permute-start(bf16[512,1024]{1,0:T(8,128)(2,1)S(1)} %fusion.30), channel_id=1, source_target_pairs={{0,4},{4,8},{8,12},{12,0},{1,5},{5,9},{9,13},{13,1},{2,6},{6,10},{... | collective-permute-start | bytes 3145736 | tf_op jit(solution)/shard_map/ppermute | solution.py:24
  214.5 3.8 %collective-permute-start.26 = (bf16[256,1024]{1,0:T(8,128)(2,1)S(1)}, bf16[256,1024]{1,0:T(8,128)(2,1)S(1)}, u32[]{:S(2)}, u32[]{:S(2)}) collective-permute-start(bf16[256,1024]{1,0:T(8,128)(2,1)S(1)} %add_convert_fusion.2), channel_id=1, source_target_pairs={{0,1},{1,0},{2,3},{3,2},{4,5},{5,4},{6,7},{7,6},{8,9},{9,8},{10,11... | collective-permute-start | bytes 1572872 | tf_op jit(solution)/shard_map/ppermute | solution.py:28
  (8 other events, 12.6 us)

commit v14 on v13

--- a/solution.py
+++ b/solution.py
@@ -165,11 +165,10 @@
     heads = width // HD
     table = jnp.concatenate([place, named, source * count + place]).astype(jnp.int32)
     span_block = pl.BlockSpec((1, SPAN, width), lambda r, t: (r, 0, 0))
-    part_block = pl.BlockSpec((1, SPAN, width), lambda r, t: (r, 0, part))
     live_block = pl.BlockSpec((1, keys, HD), lambda r, t: (t[2 * count + r], 0, 0))
     kv_block = pl.BlockSpec((1, 2, keys, width), lambda r, t: (t[r], 0, 0, 0))
     grad_block = pl.BlockSpec((1, 2, keys, width), lambda r, t: (t[2 * count + r], 0, 0, part))
-    in_specs = [span_block, part_block, live_block, kv_block]
+    in_specs = [span_block, span_block, live_block, kv_block]
     operands = [table, queries, grads, live, kv]
     aliases = {}
     if before is not None:
@@ -353,8 +352,9 @@
     cut = width * 5 // 8 // HD * HD
     left_from = [block[:, :cut] for block in along_seq[1:]]
     right_from = [block[:, cut:] for block in along_dp[1:]]
-    left_from, right_from, found, staged = lax.optimization_barrier(
-        (left_from, right_from, [acts[k] for k in near], staged)
+    grads = [[to_owner(out_grad[:, :half], step) for step in range(seq_count)]]
+    left_from, right_from, found, staged, grads = lax.optimization_barrier(
+        (left_from, right_from, [acts[k] for k in near], staged, grads)
     )
     acts = found[:opposite] + [None] + found[opposite:]
 
@@ -363,8 +363,8 @@
     up = shift(acts[opposite - 1][:rows], "tensor", 1)
     down = shift(acts[opposite + 1][rows:], "tensor", -1)
     acts[opposite] = jnp.concatenate([up, down], axis=0)
-    grad_out = after(out_grad, corner_right)
-    grads = [to_owner(grad_out, step) for step in range(seq_count)]
+    grad_out = after(out_grad[:, half:], corner_right)
+    grads.append([to_owner(grad_out, step) for step in range(seq_count)])
     depth_blocks = [(tensor_at - k) % tensor_count for k in range(tensor_count)]
     table = jnp.stack(depth_blocks).astype(jnp.int32)
 
@@ -410,7 +410,7 @@
         partial = product(acts, weights, table, part * half, half)
         arrived = swap(partial[rows:])
         if part:
-            partial = after(partial, grads)
+            partial = after(partial, grads[1])
         queries.append((partial[:rows] + arrived).astype(BF16))
     asked = [[to_owner(value, step) for step in range(seq_count)] for value in queries]
     asked[0][0] = after(asked[0][0], queries[1])
@@ -433,7 +433,7 @@
         answer, kv_grad = attend(
             *slots[step],
             asked[part][step],
-            grads[step],
+            grads[part][step],
             staged[step][part],
             live,
             part,

time: 221 us -> 220 us (level)
  Pallas kernels: 21.8 us -> 30.4 us
  waiting for transfers between devices: 121 us -> 113 us
  starting transfers between devices: 32.8 us -> 30.5 us
    ppermute x21 -> x22, waiting for transfers between devices: 119 us -> 110 us  [shift(): lax.ppermute(value, axis, [(i, (i + step * stride) % size) for i in range...]
    pallas_call x4, Pallas kernels: 11.5 us -> 20.1 us  [attend(): pl.pallas_call(attend_kernel, grid_spec=pltpu.PrefetchScalarGridSpec(num_...]
    ppermute x21 -> x22, starting transfers between devices: 31.7 us -> 29.3 us  [shift(): lax.ppermute(value, axis, [(i, (i + step * stride) % size) for i in range...]
    unnamed x59 -> x63, local copies, waits for them, and re-layouts: 13.5 us -> 13.4 us
  transfers between devices with their start and end apart: 27 -> 28, of which waited for: 16 -> 15; matrix products, arithmetic and copies ran while one was open for 12% -> 13% of each run, Pallas kernels for 9% -> 13%
where the time goes in v14:
time: 220 us; the launch traced here: 219 us
  waiting for transfers between devices  113 us (51%)
  starting transfers between devices  30.5 us (14%)
  Pallas kernels  30.4 us (14%)
  local copies, waits for them, and re-layouts  28.1 us (13%)
  matrix products  10.7 us (5%)
  other arithmetic  4.56 us (2%)
    ppermute x22, waiting for transfers between devices, shift(): lax.ppermute(value, axis, [(i, (i + step * stride) % size) for i in range...  110 us
    ppermute x22, starting transfers between devices, shift(): lax.ppermute(value, axis, [(i, (i + step * stride) % size) for i in range...  29.3 us
    pallas_call x4, Pallas kernels, attend(): pl.pallas_call(attend_kernel, grid_spec=pltpu.PrefetchScalarGridSpec(num_...  20.1 us
    unnamed x63, local copies, waits for them, and re-layouts  13.4 us
    dot_general x9, matrix products, dot(): lax.dot_general(a, b, (contract, ((), ())), preferred_element_type=F32)  10.7 us
    dynamic_update_slice x5, local copies, waits for them, and re-layouts, on_device(): lax.dynamic_update_slice(weights, piece[None], (at, inner * depth, start))  6.07 us
    pallas_call x2, Pallas kernels, product(): pl.pallas_call(functools.partial(product_kernel, count, start), out_shape...  5.79 us
  transfers between devices with their start and end apart: 28, of which 15 were waited for; matrix products, arithmetic and copies ran while one was open for 13% of the time, Pallas kernels for 13%

profile of v14, /device:TPU:0, one launch (start us, length us, event | category | flops | bytes accessed | tf_op | source)
XLA Modules:
  0.0 218.6 jit_solution(1229693994306011328)
XLA Ops:
  0.7 1.3 constant_dynamic-slice_fusion.2
  2.5 1.5 collective-permute-done
  4.1 2.9 %collective-permute-start.1 = (bf16[1024,1024]{1,0:T(8,128)(2,1)}, bf16[1024,1024]{1,0:T(8,128)(2,1)}, u32[]{:S(2)}, u32[]{:S(2)}) collective-permute-start(bf16[1024,1024]{1,0:T(8,128)(2,1)} %param.7), channel_id=1, source_target_pairs={{0,16},{16,0},{1,17},{17,1},{2,18},{18,2},{3,19},{19,3},{4,20},{20... | collective-permute-start | bytes 6291464 | tf_op jit(solution)/shard_map/ppermute | solution.py:24
  7.1 1.5 collective-permute-start.2
  8.6 1.6 collective-permute-start.3
  10.2 2.2 %collective-permute-start.4 = (bf16[512,1024]{1,0:T(8,128)(2,1)S(1)}, bf16[512,1024]{1,0:T(8,128)(2,1)S(1)}, u32[]{:S(2)}, u32[]{:S(2)}) collective-permute-start(bf16[512,1024]{1,0:T(8,128)(2,1)S(1)} %pad_maximum_fusion.1.refs_0_), channel_id=1, source_target_pairs={{0,12},{4,0},{8,4},{12,8},{1,13},{5,1},{9,5},{13,9},{2,14},{6,2},{... | collective-permute-start | bytes 3145736 | tf_op jit(solution)/shard_map/ppermute | solution.py:24
  14.4 3.4 %copy-done.1 = bf16[8,2,256,1024]{3,2,1,0:T(8,128)(2,1)S(1)} copy-done((bf16[8,2,256,1024]{3,2,1,0:T(8,128)(2,1)S(1)}, bf16[8,2,256,1024]{3,2,1,0:T(8,128)(2,1)}, u32[]{:S(2)}) %copy-start.1) | copy-done | bytes 8388632
  18.2 1.3 copy-done.6
  19.5 1.3 copy-done.8
  21.2 1.4 copy-done.10
  22.6 1.3 copy-done.20
  23.9 12.6 %collective-permute-done.3.refs_1_ = bf16[512,1024]{1,0:T(8,128)(2,1)S(1)} collective-permute-done((bf16[512,1024]{1,0:T(8,128)(2,1)S(1)}, bf16[512,1024]{1,0:T(8,128)(2,1)S(1)}, u32[]{:S(2)}, u32[]{:S(2)}) %collective-permute-start.3) | collective-permute-done | bytes 1048608 | tf_op jit(solution)/shard_map/ppermute | solution.py:24
  36.5 20.5 %collective-permute-done.4.refs_3_ = bf16[512,1024]{1,0:T(8,128)(2,1)S(1)} collective-permute-done((bf16[512,1024]{1,0:T(8,128)(2,1)S(1)}, bf16[512,1024]{1,0:T(8,128)(2,1)S(1)}, u32[]{:S(2)}, u32[]{:S(2)}) %collective-permute-start.4) | collective-permute-done | bytes 1048608 | tf_op jit(solution)/shard_map/ppermute | solution.py:24
  57.0 1.8 slice.77
  61.8 1.9 bitcast_dynamic-update-slice_fusion.2
  63.8 1.6 collective-permute-start.6
  65.4 2.5 %collective-permute-start.7 = (bf16[256,1024]{1,0:T(8,128)(2,1)S(1)}, bf16[256,1024]{1,0:T(8,128)(2,1)S(1)}, u32[]{:S(2)}, u32[]{:S(2)}) collective-permute-start(bf16[256,1024]{1,0:T(8,128)(2,1)S(1)} %slice.62), channel_id=1, source_target_pairs={{0,12},{4,0},{8,4},{12,8},{1,13},{5,1},{9,5},{13,9},{2,14},{6,2},{... | collective-permute-start | bytes 1572872 | tf_op jit(solution)/shard_map/ppermute | solution.py:24
  67.9 1.5 collective-permute-start.9
  69.4 1.9 bitcast_dynamic-update-slice_fusion.1
  71.3 1.9 bitcast_dynamic-update-slice_fusion
  73.1 7.4 %collective-permute-done.6 = bf16[256,1024]{1,0:T(8,128)(2,1)S(1)} collective-permute-done((bf16[256,1024]{1,0:T(8,128)(2,1)S(1)}, bf16[256,1024]{1,0:T(8,128)(2,1)S(1)}, u32[]{:S(2)}, u32[]{:S(2)}) %collective-permute-start.6) | collective-permute-done | bytes 524320 | tf_op jit(solution)/shard_map/ppermute | solution.py:24
  80.6 9.2 %collective-permute-done.7 = bf16[256,1024]{1,0:T(8,128)(2,1)S(1)} collective-permute-done((bf16[256,1024]{1,0:T(8,128)(2,1)S(1)}, bf16[256,1024]{1,0:T(8,128)(2,1)S(1)}, u32[]{:S(2)}, u32[]{:S(2)}) %collective-permute-start.7) | collective-permute-done | bytes 524320 | tf_op jit(solution)/shard_map/ppermute | solution.py:24
  91.6 2.9 %shard_map.87 = f32[512,512]{1,0:T(8,128)S(1)} custom-call(s32[4]{0:T(128)S(1)} %pad_add_fusion.1.table_ref, bf16[512,1024]{1,0:T(8,128)(2,1)S(1)} %pad_maximum_fusion.1.refs_0_, bf16[512,1024]{1,0:T(8,128)(2,1)S(1)} %collective-permute-done.3.refs_1_, bf16[512,1024]{1,0:T(8,128)(2,1)S(1)} %constant_dynamic-update-slice_fusion.refs_2_, ...), custom_call_target="tpu_custom_call" | custom-call | flops 2147483648 | bytes 9437184 | tf_op jit(solution)/shard_map/pallas_call | solution.py:90
  94.9 2.9 %shard_map.88 = f32[512,512]{1,0:T(8,128)S(1)} custom-call(s32[4]{0:T(128)S(1)} %pad_add_fusion.1.table_ref, bf16[512,1024]{1,0:T(8,128)(2,1)S(1)} %pad_maximum_fusion.1.refs_0_, bf16[512,1024]{1,0:T(8,128)(2,1)S(1)} %collective-permute-done.3.refs_1_, bf16[512,1024]{1,0:T(8,128)(2,1)S(1)} %constant_dynamic-update-slice_fusion.refs_2_, ...), custom_call_target="tpu_custom_call" | custom-call | flops 2147483648 | bytes 9437184 | tf_op jit(solution)/shard_map/pallas_call | solution.py:90
  101.2 5.3 %shard_map.89 = (bf16[4,64,512]{2,1,0:T(8,128)(2,1)S(1)}, bf16[8,2,256,1024]{3,2,1,0:T(8,128)(2,1)}) custom-call(s32[12]{0:T(128)S(1)} %pad_add_fusion.table_ref, bf16[4,64,512]{2,1,0:T(8,128)(2,1)S(1)} %bitcast.79, bf16[4,64,512]{2,1,0:T(8,128)(2,1)} %bitcast.7.g_ref, f32[8,256,128]{2,1,0:T(8,128)S(1)} %broadcast_in_dim.20.live_ref, ...), custom_call_target="tpu_custom_call" | custom-call | flops 1342177280 | bytes 4194304 | tf_op jit(solution)/shard_map/pallas_call | solution.py:178
  106.5 4.1 %shard_map.90 = (bf16[4,64,512]{2,1,0:T(8,128)(2,1)S(1)}, bf16[8,2,256,1024]{3,2,1,0:T(8,128)(2,1)}) custom-call(s32[12]{0:T(128)S(1)} %pad_add_fusion.table_ref, bf16[4,64,512]{2,1,0:T(8,128)(2,1)S(1)} %bitcast.75, bf16[4,64,512]{2,1,0:T(8,128)(2,1)S(1)} %bitcast.77, f32[8,256,128]{2,1,0:T(8,128)S(1)} %broadcast_in_dim.20.live_ref, ...), custom_call_target="tpu_custom_call", output_to_operand_aliasing={{1}: (5, {})} | custom-call | flops 1342177280 | bytes 4194304 | tf_op jit(solution)/shard_map/pallas_call | solution.py:178
  110.7 5.3 %shard_map.91 = (bf16[4,64,512]{2,1,0:T(8,128)(2,1)}, bf16[8,2,256,1024]{3,2,1,0:T(8,128)(2,1)}) custom-call(s32[12]{0:T(128)S(1)} %pad_add_fusion.2.table_ref, bf16[4,64,512]{2,1,0:T(8,128)(2,1)S(1)} %collective-permute-done.13.q_ref, bf16[4,64,512]{2,1,0:T(8,128)(2,1)} %collective-permute-done.5.g_ref, ...), custom_call_target="tpu_custom_call", output_to_operand_aliasing={{1}: (5, {})} | custom-call | flops 1342177280 | bytes 4194304 | tf_op jit(solution)/shard_map/pallas_call | solution.py:178
  116.0 1.6 copy-done.7
  118.6 5.3 %shard_map.92 = (bf16[4,64,512]{2,1,0:T(8,128)(2,1)S(1)}, bf16[8,2,256,1024]{3,2,1,0:T(8,128)(2,1)}) custom-call(s32[12]{0:T(128)S(1)} %pad_add_fusion.2.table_ref, bf16[4,64,512]{2,1,0:T(8,128)(2,1)} %collective-permute-done.16.q_ref, bf16[4,64,512]{2,1,0:T(8,128)(2,1)S(1)} %copy-done.15, ...), custom_call_target="tpu_custom_call", output_to_operand_aliasing={{1}: (5, {})} | custom-call | flops 1342177280 | bytes 4194304 | tf_op jit(solution)/shard_map/pallas_call | solution.py:178
  128.0 4.1 %collective-permute-done.17 = bf16[4,64,512]{2,1,0:T(8,128)(2,1)S(1)} collective-permute-done((bf16[4,64,512]{2,1,0:T(8,128)(2,1)S(1)}, bf16[4,64,512]{2,1,0:T(8,128)(2,1)S(1)}, u32[]{:S(2)}, u32[]{:S(2)}) %collective-permute-start.17) | collective-permute-done | bytes 262176 | tf_op jit(solution)/shard_map/ppermute | solution.py:24
  132.4 1.8 dynamic-slice_bitcast_fusion
  134.2 1.6 collective-permute-start.21
  135.8 1.3 convolution_convert_fusion.3
  139.5 3.5 %collective-permute-start.20 = (bf16[256,1024]{1,0:T(8,128)(2,1)S(1)}, bf16[256,1024]{1,0:T(8,128)(2,1)S(1)}, u32[]{:S(2)}, u32[]{:S(2)}) collective-permute-start(bf16[256,1024]{1,0:T(8,128)(2,1)S(1)} %get-tuple-element.103), channel_id=1, source_target_pairs={{0,12},{4,0},{8,4},{12,8},{1,13},{5,1},{9,5},{13,9},{2,14},{6,2},{... | collective-permute-start | bytes 1572872 | tf_op jit(solution)/shard_map/ppermute | solution.py:24
  143.1 1.3 convolution_convert_fusion
  144.4 1.3 convolution_convert_fusion.1
  146.8 1.3 fusion.15
  148.1 1.3 convolution_convert_fusion.2.refs_0_
  149.4 1.3 fusion.12
  150.8 1.3 fusion.9.own_ref
  152.1 7.6 %collective-permute-done.21 = bf16[1024,512]{1,0:T(8,128)(2,1)S(1)} collective-permute-done((bf16[1024,512]{1,0:T(8,128)(2,1)S(1)}, bf16[1024,512]{1,0:T(8,128)(2,1)S(1)}, u32[]{:S(2)}, u32[]{:S(2)}) %collective-permute-start.21) | collective-permute-done | bytes 1048608 | tf_op jit(solution)/shard_map/ppermute | solution.py:24
  159.7 4.3 %collective-permute-done.22 = bf16[1024,512]{1,0:T(8,128)(2,1)S(1)} collective-permute-done((bf16[1024,512]{1,0:T(8,128)(2,1)S(1)}, bf16[1024,512]{1,0:T(8,128)(2,1)S(1)}, u32[]{:S(2)}, u32[]{:S(2)}) %collective-permute-start.22) | collective-permute-done | bytes 1048608 | tf_op jit(solution)/shard_map/ppermute | solution.py:24
  164.5 2.2 %collective-permute-start.26 = (bf16[512,1024]{1,0:T(8,128)(2,1)S(1)}, bf16[512,1024]{1,0:T(8,128)(2,1)S(1)}, u32[]{:S(2)}, u32[]{:S(2)}) collective-permute-start(bf16[512,1024]{1,0:T(8,128)(2,1)S(1)} %fusion.31), channel_id=1, source_target_pairs={{0,12},{4,0},{8,4},{12,8},{1,13},{5,1},{9,5},{13,9},{2,14},{6,2},{... | collective-permute-start | bytes 3145736 | tf_op jit(solution)/shard_map/ppermute | solution.py:24
  168.7 1.7 collective-permute-start.23
  170.6 19.7 %collective-permute-done.26.down_ref = bf16[512,1024]{1,0:T(8,128)(2,1)S(1)} collective-permute-done((bf16[512,1024]{1,0:T(8,128)(2,1)S(1)}, bf16[512,1024]{1,0:T(8,128)(2,1)S(1)}, u32[]{:S(2)}, u32[]{:S(2)}) %collective-permute-start.26) | collective-permute-done | bytes 1048608 | tf_op jit(solution)/shard_map/ppermute | solution.py:24
  190.4 22.3 %collective-permute-done.25.up_ref = bf16[512,1024]{1,0:T(8,128)(2,1)S(1)} collective-permute-done((bf16[512,1024]{1,0:T(8,128)(2,1)S(1)}, bf16[512,1024]{1,0:T(8,128)(2,1)S(1)}, u32[]{:S(2)}, u32[]{:S(2)}) %collective-permute-start.25) | collective-permute-done | bytes 1048608 | tf_op jit(solution)/shard_map/ppermute | solution.py:24
  214.7 2.2 shard_map.93
  216.9 1.6 shard_map.94
  (133 shorter events, 25.1 us)
Async XLA Ops:
  0.7 11.8 %copy-start.24 = (bf16[256,1024]{1,0:T(8,128)(2,1)S(1)}, bf16[256,1024]{1,0:T(8,128)(2,1)}, u32[]{:S(2)}) copy-start(bf16[256,1024]{1,0:T(8,128)(2,1)} %param.8) | copy-start | bytes 1572868
  2.0 11.7 %copy-start.26 = (s32[32]{0:T(128)S(1)}, s32[32]{0:T(128)}, u32[]{:S(2)}) copy-start(s32[32]{0:T(128)} %param.11) | copy-start | bytes 388
  2.0 2.1 collective-permute-start
  4.1 52.9 %collective-permute-start.1 = (bf16[1024,1024]{1,0:T(8,128)(2,1)}, bf16[1024,1024]{1,0:T(8,128)(2,1)}, u32[]{:S(2)}, u32[]{:S(2)}) collective-permute-start(bf16[1024,1024]{1,0:T(8,128)(2,1)} %param.7), channel_id=1, source_target_pairs={{0,16},{16,0},{1,17},{17,1},{2,18},{18,2},{3,19},{19,3},{4,20},{20... | collective-permute-start | bytes 6291464 | tf_op jit(solution)/shard_map/ppermute | solution.py:24
  7.1 51.7 %collective-permute-start.2 = (bf16[1024,1024]{1,0:T(8,128)(2,1)}, bf16[1024,1024]{1,0:T(8,128)(2,1)}, u32[]{:S(2)}, u32[]{:S(2)}) collective-permute-start(bf16[1024,1024]{1,0:T(8,128)(2,1)} %param.7), channel_id=1, source_target_pairs={{0,2},{1,3},{2,0},{3,1},{4,6},{5,7},{6,4},{7,5},{8,10},{9,11},{10,... | collective-permute-start | bytes 6291464 | tf_op jit(solution)/shard_map/ppermute | solution.py:24
  8.6 27.9 %collective-permute-start.3 = (bf16[512,1024]{1,0:T(8,128)(2,1)S(1)}, bf16[512,1024]{1,0:T(8,128)(2,1)S(1)}, u32[]{:S(2)}, u32[]{:S(2)}) collective-permute-start(bf16[512,1024]{1,0:T(8,128)(2,1)S(1)} %pad_maximum_fusion.1.refs_0_), channel_id=1, source_target_pairs={{0,4},{4,8},{8,12},{12,0},{1,5},{5,9},{9,13},{13,1},{2,6},{6,10},{... | collective-permute-start | bytes 3145736 | tf_op jit(solution)/shard_map/ppermute | solution.py:24
  10.2 46.8 %collective-permute-start.4 = (bf16[512,1024]{1,0:T(8,128)(2,1)S(1)}, bf16[512,1024]{1,0:T(8,128)(2,1)S(1)}, u32[]{:S(2)}, u32[]{:S(2)}) collective-permute-start(bf16[512,1024]{1,0:T(8,128)(2,1)S(1)} %pad_maximum_fusion.1.refs_0_), channel_id=1, source_target_pairs={{0,12},{4,0},{8,4},{12,8},{1,13},{5,1},{9,5},{13,9},{2,14},{6,2},{... | collective-permute-start | bytes 3145736 | tf_op jit(solution)/shard_map/ppermute | solution.py:24
  13.2 76.6 %copy-start.12 = (bf16[256,512]{1,0:T(8,128)(2,1)}, bf16[256,512]{1,0:T(8,128)(2,1)S(1)}, u32[]{:S(2)}) copy-start(bf16[256,512]{1,0:T(8,128)(2,1)S(1)} %get-tuple-element.64) | copy-start | bytes 786436
  13.2 46.9 %collective-permute-start.5 = (bf16[4,64,512]{2,1,0:T(8,128)(2,1)}, bf16[4,64,512]{2,1,0:T(8,128)(2,1)}, u32[]{:S(2)}, u32[]{:S(2)}) collective-permute-start(bf16[4,64,512]{2,1,0:T(8,128)(2,1)} %bitcast.7.g_ref), channel_id=1, source_target_pairs={{0,16},{16,0},{1,17},{17,1},{2,18},{18,2},{3,19},{19,3},{4,20},{20... | collective-permute-start | bytes 786440 | tf_op jit(solution)/shard_map/ppermute | solution.py:24
  14.4 3.4 %copy-start.1 = (bf16[8,2,256,1024]{3,2,1,0:T(8,128)(2,1)S(1)}, bf16[8,2,256,1024]{3,2,1,0:T(8,128)(2,1)}, u32[]{:S(2)}) copy-start(bf16[8,2,256,1024]{3,2,1,0:T(8,128)(2,1)} %kv_ref.3) | copy-start | bytes 25165828
  57.0 37.7 %copy-start.2 = (bf16[512,1024]{1,0:T(8,128)(2,1)}, bf16[512,1024]{1,0:T(8,128)(2,1)S(1)}, u32[]{:S(2)}) copy-start(bf16[512,1024]{1,0:T(8,128)(2,1)S(1)} %collective-permute-done.4.refs_3_) | copy-start | bytes 3145732
  60.0 31.1 %collective-permute-start.8 = (bf16[1024,640]{1,0:T(8,128)(2,1)S(1)}, bf16[1024,640]{1,0:T(8,128)(2,1)S(1)}, u32[]{:S(2)}, u32[]{:S(2)}) collective-permute-start(bf16[1024,640]{1,0:T(8,128)(2,1)S(1)} %slice.77), channel_id=1, source_target_pairs={{0,2},{1,3},{2,0},{3,1},{4,6},{5,7},{6,4},{7,5},{8,10},{9,11},{10,... | collective-permute-start | bytes 3932168 | tf_op jit(solution)/shard_map/ppermute | solution.py:24
  63.8 16.8 %collective-permute-start.6 = (bf16[256,1024]{1,0:T(8,128)(2,1)S(1)}, bf16[256,1024]{1,0:T(8,128)(2,1)S(1)}, u32[]{:S(2)}, u32[]{:S(2)}) collective-permute-start(bf16[256,1024]{1,0:T(8,128)(2,1)S(1)} %slice.61), channel_id=1, source_target_pairs={{0,4},{4,8},{8,12},{12,0},{1,5},{5,9},{9,13},{13,1},{2,6},{6,10},{... | collective-permute-start | bytes 1572872 | tf_op jit(solution)/shard_map/ppermute | solution.py:24
  65.4 24.3 %collective-permute-start.7 = (bf16[256,1024]{1,0:T(8,128)(2,1)S(1)}, bf16[256,1024]{1,0:T(8,128)(2,1)S(1)}, u32[]{:S(2)}, u32[]{:S(2)}) collective-permute-start(bf16[256,1024]{1,0:T(8,128)(2,1)S(1)} %slice.62), channel_id=1, source_target_pairs={{0,12},{4,0},{8,4},{12,8},{1,13},{5,1},{9,5},{13,9},{2,14},{6,2},{... | collective-permute-start | bytes 1572872 | tf_op jit(solution)/shard_map/ppermute | solution.py:24
  67.9 21.9 %collective-permute-start.9 = (bf16[1024,384]{1,0:T(8,128)(2,1)S(1)}, bf16[1024,384]{1,0:T(8,128)(2,1)S(1)}, u32[]{:S(2)}, u32[]{:S(2)}) collective-permute-start(bf16[1024,384]{1,0:T(8,128)(2,1)S(1)} %slice.78), channel_id=1, source_target_pairs={{0,16},{16,0},{1,17},{17,1},{2,18},{18,2},{3,19},{19,3},{4,20},{20... | collective-permute-start | bytes 2359304 | tf_op jit(solution)/shard_map/ppermute | solution.py:24
  89.8 4.9 %copy-start.4 = (bf16[512,1024]{1,0:T(8,128)(2,1)}, bf16[512,1024]{1,0:T(8,128)(2,1)S(1)}, u32[]{:S(2)}) copy-start(bf16[512,1024]{1,0:T(8,128)(2,1)S(1)} %constant_dynamic-update-slice_fusion.refs_2_) | copy-start | bytes 3145732
  89.8 8.4 %collective-permute-start.11 = (bf16[4,64,512]{2,1,0:T(8,128)(2,1)S(1)}, bf16[4,64,512]{2,1,0:T(8,128)(2,1)S(1)}, u32[]{:S(2)}, u32[]{:S(2)}) collective-permute-start(bf16[4,64,512]{2,1,0:T(8,128)(2,1)S(1)} %bitcast.76), channel_id=1, source_target_pairs={{0,16},{16,0},{1,17},{17,1},{2,18},{18,2},{3,19},{19,3},{4,20},{20... | collective-permute-start | bytes 786440 | tf_op jit(solution)/shard_map/ppermute | solution.py:24
  94.6 3.7 %copy-start.25 = (s32[8,256]{1,0:T(8,128)S(1)}, s32[8,256]{1,0:T(8,128)}, u32[]{:S(2)}) copy-start(s32[8,256]{1,0:T(8,128)} %param.10) | copy-start | bytes 24580
  94.6 3.7 %collective-permute-start.10 = (f32[256,512]{1,0:T(8,128)S(1)}, f32[256,512]{1,0:T(8,128)S(1)}, u32[]{:S(2)}, u32[]{:S(2)}) collective-permute-start(f32[256,512]{1,0:T(8,128)S(1)} %slice.80), channel_id=1, source_target_pairs={{0,1},{1,0},{2,3},{3,2},{4,5},{5,4},{6,7},{7,6},{8,9},{9,8},{10,11... | collective-permute-start | bytes 1572872 | tf_op jit(solution)/shard_map/ppermute | solution.py:28
  97.9 2.0 collective-permute-start.12
  98.3 8.3 %copy-start.14 = (bf16[4,64,512]{2,1,0:T(8,128)(2,1)}, bf16[4,64,512]{2,1,0:T(8,128)(2,1)S(1)}, u32[]{:S(2)}) copy-start(bf16[4,64,512]{2,1,0:T(8,128)(2,1)S(1)} %collective-permute-done.11.g_ref) | copy-start | bytes 786436
  98.4 12.3 %collective-permute-start.13 = (bf16[4,64,512]{2,1,0:T(8,128)(2,1)S(1)}, bf16[4,64,512]{2,1,0:T(8,128)(2,1)S(1)}, u32[]{:S(2)}, u32[]{:S(2)}) collective-permute-start(bf16[4,64,512]{2,1,0:T(8,128)(2,1)S(1)} %bitcast.78), channel_id=1, source_target_pairs={{0,16},{16,0},{1,17},{17,1},{2,18},{18,2},{3,19},{19,3},{4,20},{20... | collective-permute-start | bytes 786440 | tf_op jit(solution)/shard_map/ppermute | solution.py:24
  99.9 16.1 %collective-permute-start.16 = (bf16[4,64,512]{2,1,0:T(8,128)(2,1)S(1)}, bf16[4,64,512]{2,1,0:T(8,128)(2,1)}, u32[]{:S(2)}, u32[]{:S(2)}) collective-permute-start(bf16[4,64,512]{2,1,0:T(8,128)(2,1)S(1)} %bitcast.74), channel_id=1, source_target_pairs={{0,16},{16,0},{1,17},{17,1},{2,18},{18,2},{3,19},{19,3},{4,20},{20... | collective-permute-start | bytes 786440 | tf_op jit(solution)/shard_map/ppermute | solution.py:24
  101.2 5.4 %copy-start.11 = (bf16[4,2,256,512]{3,2,1,0:T(8,128)(2,1)S(1)}, bf16[4,2,256,512]{3,2,1,0:T(8,128)(2,1)}, u32[]{:S(2)}) copy-start(bf16[4,2,256,512]{3,2,1,0:T(8,128)(2,1)} %copy-done.10) | copy-start | bytes 6291460
  101.2 5.4 %copy-start.13 = (bf16[256,512]{1,0:T(8,128)(2,1)S(1)}, bf16[256,512]{1,0:T(8,128)(2,1)}, u32[]{:S(2)}) copy-start(bf16[256,512]{1,0:T(8,128)(2,1)} %copy-done.12) | copy-start | bytes 786436
  106.5 4.2 %copy-start.18 = (bf16[4,64,512]{2,1,0:T(8,128)(2,1)}, bf16[4,64,512]{2,1,0:T(8,128)(2,1)S(1)}, u32[]{:S(2)}) copy-start(bf16[4,64,512]{2,1,0:T(8,128)(2,1)S(1)} %get-tuple-element.69) | copy-start | bytes 786436
  106.5 4.2 %copy-start.9 = (bf16[4,2,256,512]{3,2,1,0:T(8,128)(2,1)S(1)}, bf16[4,2,256,512]{3,2,1,0:T(8,128)(2,1)}, u32[]{:S(2)}) copy-start(bf16[4,2,256,512]{3,2,1,0:T(8,128)(2,1)} %copy-done.8) | copy-start | bytes 6291460
  110.7 5.3 %copy-start.16 = (bf16[4,64,512]{2,1,0:T(8,128)(2,1)}, bf16[4,64,512]{2,1,0:T(8,128)(2,1)S(1)}, u32[]{:S(2)}) copy-start(bf16[4,64,512]{2,1,0:T(8,128)(2,1)S(1)} %get-tuple-element.76) | copy-start | bytes 786436
  116.0 8.6 %collective-permute-start.14 = (bf16[4,64,512]{2,1,0:T(8,128)(2,1)}, bf16[4,64,512]{2,1,0:T(8,128)(2,1)}, u32[]{:S(2)}, u32[]{:S(2)}) collective-permute-start(bf16[4,64,512]{2,1,0:T(8,128)(2,1)} %get-tuple-element.75), channel_id=1, source_target_pairs={{0,16},{16,0},{1,17},{17,1},{2,18},{18,2},{3,19},{19,3},{4,20},{20... | collective-permute-start | bytes 786440 | tf_op jit(solution)/shard_map/ppermute | solution.py:24
  118.6 6.1 %copy-start.19 = (bf16[4,64,512]{2,1,0:T(8,128)(2,1)S(1)}, bf16[4,64,512]{2,1,0:T(8,128)(2,1)}, u32[]{:S(2)}) copy-start(bf16[4,64,512]{2,1,0:T(8,128)(2,1)} %copy-done.18) | copy-start | bytes 786436
  118.6 7.2 %copy-start.3 = (bf16[512,1024]{1,0:T(8,128)(2,1)S(1)}, bf16[512,1024]{1,0:T(8,128)(2,1)}, u32[]{:S(2)}) copy-start(bf16[512,1024]{1,0:T(8,128)(2,1)} %copy-done.2) | copy-start | bytes 3145732
  118.6 7.2 %copy-start.5 = (bf16[512,1024]{1,0:T(8,128)(2,1)S(1)}, bf16[512,1024]{1,0:T(8,128)(2,1)}, u32[]{:S(2)}) copy-start(bf16[512,1024]{1,0:T(8,128)(2,1)} %copy-done.4) | copy-start | bytes 3145732
  123.9 8.2 %collective-permute-start.17 = (bf16[4,64,512]{2,1,0:T(8,128)(2,1)S(1)}, bf16[4,64,512]{2,1,0:T(8,128)(2,1)S(1)}, u32[]{:S(2)}, u32[]{:S(2)}) collective-permute-start(bf16[4,64,512]{2,1,0:T(8,128)(2,1)S(1)} %get-tuple-element.79), channel_id=1, source_target_pairs={{0,16},{16,0},{1,17},{17,1},{2,18},{18,2},{3,19},{19,3},{4,20},{20... | collective-permute-start | bytes 786440 | tf_op jit(solution)/shard_map/ppermute | solution.py:24
  125.7 1.6 collective-permute-start.15
  126.3 5.8 %copy-start.22 = (bf16[4,512,1024]{2,1,0:T(8,128)(2,1)}, bf16[4,512,1024]{2,1,0:T(8,128)(2,1)S(1)}, u32[]{:S(2)}) copy-start(bf16[4,512,1024]{2,1,0:T(8,128)(2,1)S(1)} %pad_maximum_fusion) | copy-start | bytes 12582916
  126.3 5.7 %copy-start.17 = (bf16[4,64,512]{2,1,0:T(8,128)(2,1)S(1)}, bf16[4,64,512]{2,1,0:T(8,128)(2,1)}, u32[]{:S(2)}) copy-start(bf16[4,64,512]{2,1,0:T(8,128)(2,1)} %copy-done.16) | copy-start | bytes 786436
  127.3 4.9 %copy-start.27 = (bf16[256,512]{1,0:T(8,128)(2,1)}, bf16[256,512]{1,0:T(8,128)(2,1)S(1)}, u32[]{:S(2)}) copy-start(bf16[256,512]{1,0:T(8,128)(2,1)S(1)} %collective-permute-done.15) | copy-start | bytes 786436
  132.2 3.6 %collective-permute-start.18 = (bf16[256,512]{1,0:T(8,128)(2,1)S(1)}, bf16[256,512]{1,0:T(8,128)(2,1)S(1)}, u32[]{:S(2)}, u32[]{:S(2)}) collective-permute-start(bf16[256,512]{1,0:T(8,128)(2,1)S(1)} %bitcast_add_fusion), channel_id=1, source_target_pairs={{0,1},{1,0},{2,3},{3,2},{4,5},{5,4},{6,7},{7,6},{8,9},{9,8},{10,11... | collective-permute-start | bytes 786440 | tf_op jit(solution)/shard_map/ppermute | solution.py:28
  132.3 3.4 %copy-start.28 = (bf16[256,512]{1,0:T(8,128)(2,1)S(1)}, bf16[256,512]{1,0:T(8,128)(2,1)}, u32[]{:S(2)}) copy-start(bf16[256,512]{1,0:T(8,128)(2,1)} %copy-done.27) | copy-start | bytes 786436
  134.2 25.5 %collective-permute-start.21 = (bf16[1024,512]{1,0:T(8,128)(2,1)S(1)}, bf16[1024,512]{1,0:T(8,128)(2,1)S(1)}, u32[]{:S(2)}, u32[]{:S(2)}) collective-permute-start(bf16[1024,512]{1,0:T(8,128)(2,1)S(1)} %convolution_convert_fusion.5), channel_id=1, source_target_pairs={{0,2},{1,3},{2,0},{3,1},{4,6},{5,7},{6,4},{7,5},{8,10},{9,11},{10,... | collective-permute-start | bytes 3145736 | tf_op jit(solution)/shard_map/ppermute | solution.py:24
  138.7 25.2 %collective-permute-start.22 = (bf16[1024,512]{1,0:T(8,128)(2,1)S(1)}, bf16[1024,512]{1,0:T(8,128)(2,1)S(1)}, u32[]{:S(2)}, u32[]{:S(2)}) collective-permute-start(bf16[1024,512]{1,0:T(8,128)(2,1)S(1)} %convolution_convert_fusion.4), channel_id=1, source_target_pairs={{0,16},{16,0},{1,17},{17,1},{2,18},{18,2},{3,19},{19,3},{4,20},{20... | collective-permute-start | bytes 3145736 | tf_op jit(solution)/shard_map/ppermute | solution.py:24
  139.2 24.7 %collective-permute-start.19 = (bf16[256,1024]{1,0:T(8,128)(2,1)S(1)}, bf16[256,1024]{1,0:T(8,128)(2,1)S(1)}, u32[]{:S(2)}, u32[]{:S(2)}) collective-permute-start(bf16[256,1024]{1,0:T(8,128)(2,1)S(1)} %get-tuple-element.104), channel_id=1, source_target_pairs={{0,4},{4,8},{8,12},{12,0},{1,5},{5,9},{9,13},{13,1},{2,6},{6,10},{... | collective-permute-start | bytes 1572872 | tf_op jit(solution)/shard_map/ppermute | solution.py:24
  139.5 24.7 %collective-permute-start.20 = (bf16[256,1024]{1,0:T(8,128)(2,1)S(1)}, bf16[256,1024]{1,0:T(8,128)(2,1)S(1)}, u32[]{:S(2)}, u32[]{:S(2)}) collective-permute-start(bf16[256,1024]{1,0:T(8,128)(2,1)S(1)} %get-tuple-element.103), channel_id=1, source_target_pairs={{0,12},{4,0},{8,4},{12,8},{1,13},{5,1},{9,5},{13,9},{2,14},{6,2},{... | collective-permute-start | bytes 1572872 | tf_op jit(solution)/shard_map/ppermute | solution.py:24
  164.5 25.9 %collective-permute-start.26 = (bf16[512,1024]{1,0:T(8,128)(2,1)S(1)}, bf16[512,1024]{1,0:T(8,128)(2,1)S(1)}, u32[]{:S(2)}, u32[]{:S(2)}) collective-permute-start(bf16[512,1024]{1,0:T(8,128)(2,1)S(1)} %fusion.31), channel_id=1, source_target_pairs={{0,12},{4,0},{8,4},{12,8},{1,13},{5,1},{9,5},{13,9},{2,14},{6,2},{... | collective-permute-start | bytes 3145736 | tf_op jit(solution)/shard_map/ppermute | solution.py:24
  167.4 46.4 %collective-permute-start.24 = (bf16[1024,1024]{1,0:T(8,128)(2,1)S(1)}, bf16[1024,1024]{1,0:T(8,128)(2,1)S(1)}, u32[]{:S(2)}, u32[]{:S(2)}) collective-permute-start(bf16[1024,1024]{1,0:T(8,128)(2,1)S(1)} %fusion.19), channel_id=1, source_target_pairs={{0,2},{1,3},{2,0},{3,1},{4,6},{5,7},{6,4},{7,5},{8,10},{9,11},{10,... | collective-permute-start | bytes 6291464 | tf_op jit(solution)/shard_map/ppermute | solution.py:24
  168.7 46.0 %collective-permute-start.23 = (bf16[1024,1024]{1,0:T(8,128)(2,1)S(1)}, bf16[1024,1024]{1,0:T(8,128)(2,1)S(1)}, u32[]{:S(2)}, u32[]{:S(2)}) collective-permute-start(bf16[1024,1024]{1,0:T(8,128)(2,1)S(1)} %fusion.18), channel_id=1, source_target_pairs={{0,16},{16,0},{1,17},{17,1},{2,18},{18,2},{3,19},{19,3},{4,20},{20... | collective-permute-start | bytes 6291464 | tf_op jit(solution)/shard_map/ppermute | solution.py:24
  170.6 42.1 %collective-permute-start.25 = (bf16[512,1024]{1,0:T(8,128)(2,1)S(1)}, bf16[512,1024]{1,0:T(8,128)(2,1)S(1)}, u32[]{:S(2)}, u32[]{:S(2)}) collective-permute-start(bf16[512,1024]{1,0:T(8,128)(2,1)S(1)} %fusion.30), channel_id=1, source_target_pairs={{0,4},{4,8},{8,12},{12,0},{1,5},{5,9},{9,13},{13,1},{2,6},{6,10},{... | collective-permute-start | bytes 3145736 | tf_op jit(solution)/shard_map/ppermute | solution.py:24
  213.0 3.9 %collective-permute-start.27 = (bf16[256,1024]{1,0:T(8,128)(2,1)S(1)}, bf16[256,1024]{1,0:T(8,128)(2,1)S(1)}, u32[]{:S(2)}, u32[]{:S(2)}) collective-permute-start(bf16[256,1024]{1,0:T(8,128)(2,1)S(1)} %add_convert_fusion.2), channel_id=1, source_target_pairs={{0,1},{1,0},{2,3},{3,2},{4,5},{5,4},{6,7},{7,6},{8,9},{9,8},{10,11... | collective-permute-start | bytes 1572872 | tf_op jit(solution)/shard_map/ppermute | solution.py:28
  (11 other events, 21.8 us)

commit v15 on v14

--- a/solution.py
+++ b/solution.py
@@ -353,8 +353,20 @@
     left_from = [block[:, :cut] for block in along_seq[1:]]
     right_from = [block[:, cut:] for block in along_dp[1:]]
     grads = [[to_owner(out_grad[:, :half], step) for step in range(seq_count)]]
-    left_from, right_from, found, staged, grads = lax.optimization_barrier(
-        (left_from, right_from, [acts[k] for k in near], staged, grads)
+
+    def block_at(i, j):
+        block = ((seq_at - i) % seq_count) * dp_count + ((dp_at // 2 - j) % couples) * 2
+        return block // (2 * per), (block % (2 * per)) // 2
+
+    def placed(weights, piece, i, j, start):
+        at, inner = block_at(i, j)
+        return lax.dynamic_update_slice(weights, piece[None], (at, inner * depth, start))
+
+    places = [(i, j) for i in range(seq_count) for j in range(couples)]
+    weights = jnp.zeros((tensor_count, per * depth, width), BF16)
+    weights = placed(weights, q_weight, 0, 0, 0)
+    left_from, right_from, found, staged, grads, weights = lax.optimization_barrier(
+        (left_from, right_from, [acts[k] for k in near], staged, grads, weights)
     )
     acts = found[:opposite] + [None] + found[opposite:]
 
@@ -368,14 +380,7 @@
     depth_blocks = [(tensor_at - k) % tensor_count for k in range(tensor_count)]
     table = jnp.stack(depth_blocks).astype(jnp.int32)
 
-    def block_at(i, j):
-        block = ((seq_at - i) % seq_count) * dp_count + ((dp_at // 2 - j) % couples) * 2
-        return block // (2 * per), (block % (2 * per)) // 2
-
-    places = [(i, j) for i in range(seq_count) for j in range(couples)]
-    weights = jnp.zeros((tensor_count, per * depth, width), BF16)
-    for i, j in places:
-        at, inner = block_at(i, j)
+    for i, j in places[1:]:
         if j == 0:
             pieces = [(along_seq[i], 0)]
         elif i == 0:
@@ -383,7 +388,7 @@
         else:
             pieces = [(corner_left[i - 1][j], 0), (corner_right[j - 1][i], cut)]
         for piece, start in pieces:
-            weights = lax.dynamic_update_slice(weights, piece[None], (at, inner * depth, start))
+            weights = placed(weights, piece, i, j, start)
 
     def from_owner(value, step):
         value = shift(value, "seq", -step) if step else value

time: 220 us -> 221 us (level)
  transfers between devices with their start and end apart: 28 -> 28, of which waited for: 15 -> 16; matrix products, arithmetic and copies ran while one was open for 13% -> 13% of each run, Pallas kernels for 13% -> 13%
where the time goes in v15:
time: 221 us; the launch traced here: 220 us
  waiting for transfers between devices  114 us (52%)
  Pallas kernels  30.4 us (14%)
  starting transfers between devices  30.2 us (14%)
  local copies, waits for them, and re-layouts  28.1 us (13%)
  matrix products  10.7 us (5%)
  other arithmetic  4.52 us (2%)
    ppermute x22, waiting for transfers between devices, shift(): lax.ppermute(value, axis, [(i, (i + step * stride) % size) for i in range...  111 us
    ppermute x22, starting transfers between devices, shift(): lax.ppermute(value, axis, [(i, (i + step * stride) % size) for i in range...  28.7 us
    pallas_call x4, Pallas kernels, attend(): pl.pallas_call(attend_kernel, grid_spec=pltpu.PrefetchScalarGridSpec(num_...  20.1 us
    unnamed x63, local copies, waits for them, and re-layouts  13.4 us
    dot_general x9, matrix products, dot(): lax.dot_general(a, b, (contract, ((), ())), preferred_element_type=F32)  10.7 us
    dynamic_update_slice x5, local copies, waits for them, and re-layouts, placed(): lax.dynamic_update_slice(weights, piece[None], (at, inner * depth, start))  6.06 us
    pallas_call x2, Pallas kernels, product(): pl.pallas_call(functools.partial(product_kernel, count, start), out_shape...  5.79 us
  transfers between devices with their start and end apart: 28, of which 16 were waited for; matrix products, arithmetic and copies ran while one was open for 13% of the time, Pallas kernels for 13%

profile of v15, /device:TPU:0, one launch (start us, length us, event | category | flops | bytes accessed | tf_op | source)
XLA Modules:
  0.0 219.5 jit_solution(8629333628287959398)
XLA Ops:
  0.7 1.3 constant_dynamic-slice_fusion.2
  2.5 1.5 collective-permute-done
  4.1 2.9 %collective-permute-start.1 = (bf16[1024,1024]{1,0:T(8,128)(2,1)}, bf16[1024,1024]{1,0:T(8,128)(2,1)}, u32[]{:S(2)}, u32[]{:S(2)}) collective-permute-start(bf16[1024,1024]{1,0:T(8,128)(2,1)} %param.7), channel_id=1, source_target_pairs={{0,16},{16,0},{1,17},{17,1},{2,18},{18,2},{3,19},{19,3},{4,20},{20... | collective-permute-start | bytes 6291464 | tf_op jit(solution)/shard_map/ppermute | solution.py:24
  7.0 1.5 collective-permute-start.2
  8.6 1.6 collective-permute-start.3
  10.1 2.2 %collective-permute-start.4 = (bf16[512,1024]{1,0:T(8,128)(2,1)S(1)}, bf16[512,1024]{1,0:T(8,128)(2,1)S(1)}, u32[]{:S(2)}, u32[]{:S(2)}) collective-permute-start(bf16[512,1024]{1,0:T(8,128)(2,1)S(1)} %pad_maximum_fusion.1.refs_0_), channel_id=1, source_target_pairs={{0,12},{4,0},{8,4},{12,8},{1,13},{5,1},{9,5},{13,9},{2,14},{6,2},{... | collective-permute-start | bytes 3145736 | tf_op jit(solution)/shard_map/ppermute | solution.py:24
  13.7 3.4 %copy-done.1 = bf16[8,2,256,1024]{3,2,1,0:T(8,128)(2,1)S(1)} copy-done((bf16[8,2,256,1024]{3,2,1,0:T(8,128)(2,1)S(1)}, bf16[8,2,256,1024]{3,2,1,0:T(8,128)(2,1)}, u32[]{:S(2)}) %copy-start.1) | copy-done | bytes 8388632
  18.7 1.3 copy-done.8
  20.4 1.4 copy-done.10
  24.7 1.9 bitcast_dynamic-update-slice_fusion.2
  26.5 10.0 %collective-permute-done.3.refs_1_ = bf16[512,1024]{1,0:T(8,128)(2,1)S(1)} collective-permute-done((bf16[512,1024]{1,0:T(8,128)(2,1)S(1)}, bf16[512,1024]{1,0:T(8,128)(2,1)S(1)}, u32[]{:S(2)}, u32[]{:S(2)}) %collective-permute-start.3) | collective-permute-done | bytes 1048608 | tf_op jit(solution)/shard_map/ppermute | solution.py:24
  36.5 20.5 %collective-permute-done.4.refs_3_ = bf16[512,1024]{1,0:T(8,128)(2,1)S(1)} collective-permute-done((bf16[512,1024]{1,0:T(8,128)(2,1)S(1)}, bf16[512,1024]{1,0:T(8,128)(2,1)S(1)}, u32[]{:S(2)}, u32[]{:S(2)}) %collective-permute-start.4) | collective-permute-done | bytes 1048608 | tf_op jit(solution)/shard_map/ppermute | solution.py:24
  57.0 1.8 slice.77
  61.0 1.6 collective-permute-start.6
  62.7 2.5 %collective-permute-start.7 = (bf16[256,1024]{1,0:T(8,128)(2,1)S(1)}, bf16[256,1024]{1,0:T(8,128)(2,1)S(1)}, u32[]{:S(2)}, u32[]{:S(2)}) collective-permute-start(bf16[256,1024]{1,0:T(8,128)(2,1)S(1)} %slice.62), channel_id=1, source_target_pairs={{0,12},{4,0},{8,4},{12,8},{1,13},{5,1},{9,5},{13,9},{2,14},{6,2},{... | collective-permute-start | bytes 1572872 | tf_op jit(solution)/shard_map/ppermute | solution.py:24
  65.1 1.5 collective-permute-start.9
  66.6 1.9 bitcast_dynamic-update-slice_fusion.1
  68.5 1.9 bitcast_dynamic-update-slice_fusion
  70.4 7.4 %collective-permute-done.6 = bf16[256,1024]{1,0:T(8,128)(2,1)S(1)} collective-permute-done((bf16[256,1024]{1,0:T(8,128)(2,1)S(1)}, bf16[256,1024]{1,0:T(8,128)(2,1)S(1)}, u32[]{:S(2)}, u32[]{:S(2)}) %collective-permute-start.6) | collective-permute-done | bytes 524320 | tf_op jit(solution)/shard_map/ppermute | solution.py:24
  77.8 9.2 %collective-permute-done.7 = bf16[256,1024]{1,0:T(8,128)(2,1)S(1)} collective-permute-done((bf16[256,1024]{1,0:T(8,128)(2,1)S(1)}, bf16[256,1024]{1,0:T(8,128)(2,1)S(1)}, u32[]{:S(2)}, u32[]{:S(2)}) %collective-permute-start.7) | collective-permute-done | bytes 524320 | tf_op jit(solution)/shard_map/ppermute | solution.py:24
  88.3 1.9 collective-permute-done.8
  90.8 2.9 %shard_map.87 = f32[512,512]{1,0:T(8,128)S(1)} custom-call(s32[4]{0:T(128)S(1)} %pad_add_fusion.1.table_ref, bf16[512,1024]{1,0:T(8,128)(2,1)S(1)} %pad_maximum_fusion.1.refs_0_, bf16[512,1024]{1,0:T(8,128)(2,1)S(1)} %collective-permute-done.3.refs_1_, bf16[512,1024]{1,0:T(8,128)(2,1)S(1)} %constant_dynamic-update-slice_fusion.refs_2_, ...), custom_call_target="tpu_custom_call" | custom-call | flops 2147483648 | bytes 9437184 | tf_op jit(solution)/shard_map/pallas_call | solution.py:90
  94.1 2.9 %shard_map.88 = f32[512,512]{1,0:T(8,128)S(1)} custom-call(s32[4]{0:T(128)S(1)} %pad_add_fusion.1.table_ref, bf16[512,1024]{1,0:T(8,128)(2,1)S(1)} %pad_maximum_fusion.1.refs_0_, bf16[512,1024]{1,0:T(8,128)(2,1)S(1)} %collective-permute-done.3.refs_1_, bf16[512,1024]{1,0:T(8,128)(2,1)S(1)} %constant_dynamic-update-slice_fusion.refs_2_, ...), custom_call_target="tpu_custom_call" | custom-call | flops 2147483648 | bytes 9437184 | tf_op jit(solution)/shard_map/pallas_call | solution.py:90
  100.2 5.3 %shard_map.89 = (bf16[4,64,512]{2,1,0:T(8,128)(2,1)S(1)}, bf16[8,2,256,1024]{3,2,1,0:T(8,128)(2,1)}) custom-call(s32[12]{0:T(128)S(1)} %pad_add_fusion.table_ref, bf16[4,64,512]{2,1,0:T(8,128)(2,1)S(1)} %bitcast.79, bf16[4,64,512]{2,1,0:T(8,128)(2,1)} %bitcast.7.g_ref, f32[8,256,128]{2,1,0:T(8,128)S(1)} %broadcast_in_dim.20.live_ref, ...), custom_call_target="tpu_custom_call" | custom-call | flops 1342177280 | bytes 4194304 | tf_op jit(solution)/shard_map/pallas_call | solution.py:178
  105.5 4.1 %shard_map.90 = (bf16[4,64,512]{2,1,0:T(8,128)(2,1)S(1)}, bf16[8,2,256,1024]{3,2,1,0:T(8,128)(2,1)}) custom-call(s32[12]{0:T(128)S(1)} %pad_add_fusion.table_ref, bf16[4,64,512]{2,1,0:T(8,128)(2,1)S(1)} %bitcast.75, bf16[4,64,512]{2,1,0:T(8,128)(2,1)S(1)} %bitcast.77, f32[8,256,128]{2,1,0:T(8,128)S(1)} %broadcast_in_dim.20.live_ref, ...), custom_call_target="tpu_custom_call", output_to_operand_aliasing={{1}: (5, {})} | custom-call | flops 1342177280 | bytes 4194304 | tf_op jit(solution)/shard_map/pallas_call | solution.py:178
  109.7 5.3 %shard_map.91 = (bf16[4,64,512]{2,1,0:T(8,128)(2,1)}, bf16[8,2,256,1024]{3,2,1,0:T(8,128)(2,1)}) custom-call(s32[12]{0:T(128)S(1)} %pad_add_fusion.2.table_ref, bf16[4,64,512]{2,1,0:T(8,128)(2,1)S(1)} %collective-permute-done.13.q_ref, bf16[4,64,512]{2,1,0:T(8,128)(2,1)} %collective-permute-done.5.g_ref, ...), custom_call_target="tpu_custom_call", output_to_operand_aliasing={{1}: (5, {})} | custom-call | flops 1342177280 | bytes 4194304 | tf_op jit(solution)/shard_map/pallas_call | solution.py:178
  115.0 1.6 copy-done.7
  117.6 5.3 %shard_map.92 = (bf16[4,64,512]{2,1,0:T(8,128)(2,1)S(1)}, bf16[8,2,256,1024]{3,2,1,0:T(8,128)(2,1)}) custom-call(s32[12]{0:T(128)S(1)} %pad_add_fusion.2.table_ref, bf16[4,64,512]{2,1,0:T(8,128)(2,1)} %collective-permute-done.16.q_ref, bf16[4,64,512]{2,1,0:T(8,128)(2,1)S(1)} %copy-done.15, ...), custom_call_target="tpu_custom_call", output_to_operand_aliasing={{1}: (5, {})} | custom-call | flops 1342177280 | bytes 4194304 | tf_op jit(solution)/shard_map/pallas_call | solution.py:178
  127.0 3.9 %collective-permute-done.17 = bf16[4,64,512]{2,1,0:T(8,128)(2,1)S(1)} collective-permute-done((bf16[4,64,512]{2,1,0:T(8,128)(2,1)S(1)}, bf16[4,64,512]{2,1,0:T(8,128)(2,1)S(1)}, u32[]{:S(2)}, u32[]{:S(2)}) %collective-permute-start.17) | collective-permute-done | bytes 262176 | tf_op jit(solution)/shard_map/ppermute | solution.py:24
  131.1 1.8 dynamic-slice_bitcast_fusion
  132.9 1.6 collective-permute-start.21
  134.5 1.3 convolution_convert_fusion.3
  138.0 1.6 collective-permute-start.19
  139.5 2.2 %collective-permute-start.20 = (bf16[256,1024]{1,0:T(8,128)(2,1)S(1)}, bf16[256,1024]{1,0:T(8,128)(2,1)S(1)}, u32[]{:S(2)}, u32[]{:S(2)}) collective-permute-start(bf16[256,1024]{1,0:T(8,128)(2,1)S(1)} %get-tuple-element.105), channel_id=1, source_target_pairs={{0,12},{4,0},{8,4},{12,8},{1,13},{5,1},{9,5},{13,9},{2,14},{6,2},{... | collective-permute-start | bytes 1572872 | tf_op jit(solution)/shard_map/ppermute | solution.py:24
  145.5 1.3 fusion.15
  148.2 1.3 fusion.12
  149.5 1.3 fusion.9.own_ref
  150.8 7.6 %collective-permute-done.21 = bf16[1024,512]{1,0:T(8,128)(2,1)S(1)} collective-permute-done((bf16[1024,512]{1,0:T(8,128)(2,1)S(1)}, bf16[1024,512]{1,0:T(8,128)(2,1)S(1)}, u32[]{:S(2)}, u32[]{:S(2)}) %collective-permute-start.21) | collective-permute-done | bytes 1048608 | tf_op jit(solution)/shard_map/ppermute | solution.py:24
  158.5 4.2 %collective-permute-done.22 = bf16[1024,512]{1,0:T(8,128)(2,1)S(1)} collective-permute-done((bf16[1024,512]{1,0:T(8,128)(2,1)S(1)}, bf16[1024,512]{1,0:T(8,128)(2,1)S(1)}, u32[]{:S(2)}, u32[]{:S(2)}) %collective-permute-start.22) | collective-permute-done | bytes 1048608 | tf_op jit(solution)/shard_map/ppermute | solution.py:24
  162.7 1.6 collective-permute-done.20
  164.5 2.2 collective-permute-start.26
  167.3 1.7 collective-permute-start.24
  170.5 20.5 %collective-permute-done.26.down_ref = bf16[512,1024]{1,0:T(8,128)(2,1)S(1)} collective-permute-done((bf16[512,1024]{1,0:T(8,128)(2,1)S(1)}, bf16[512,1024]{1,0:T(8,128)(2,1)S(1)}, u32[]{:S(2)}, u32[]{:S(2)}) %collective-permute-start.26) | collective-permute-done | bytes 1048608 | tf_op jit(solution)/shard_map/ppermute | solution.py:24
  191.0 20.9 %collective-permute-done.25.up_ref = bf16[512,1024]{1,0:T(8,128)(2,1)S(1)} collective-permute-done((bf16[512,1024]{1,0:T(8,128)(2,1)S(1)}, bf16[512,1024]{1,0:T(8,128)(2,1)S(1)}, u32[]{:S(2)}, u32[]{:S(2)}) %collective-permute-start.25) | collective-permute-done | bytes 1048608 | tf_op jit(solution)/shard_map/ppermute | solution.py:24
  212.2 1.5 collective-permute-done.24.refs_2_
  213.8 1.9 collective-permute-done.23.refs_1_
  215.7 2.2 shard_map.93
  217.9 1.6 shard_map.94
  (133 shorter events, 29.0 us)
Async XLA Ops:
  0.7 11.7 %copy-start.24 = (bf16[256,1024]{1,0:T(8,128)(2,1)S(1)}, bf16[256,1024]{1,0:T(8,128)(2,1)}, u32[]{:S(2)}) copy-start(bf16[256,1024]{1,0:T(8,128)(2,1)} %param.8) | copy-start | bytes 1572868
  2.0 2.1 collective-permute-start
  4.1 52.9 %collective-permute-start.1 = (bf16[1024,1024]{1,0:T(8,128)(2,1)}, bf16[1024,1024]{1,0:T(8,128)(2,1)}, u32[]{:S(2)}, u32[]{:S(2)}) collective-permute-start(bf16[1024,1024]{1,0:T(8,128)(2,1)} %param.7), channel_id=1, source_target_pairs={{0,16},{16,0},{1,17},{17,1},{2,18},{18,2},{3,19},{19,3},{4,20},{20... | collective-permute-start | bytes 6291464 | tf_op jit(solution)/shard_map/ppermute | solution.py:24
  7.0 51.7 %collective-permute-start.2 = (bf16[1024,1024]{1,0:T(8,128)(2,1)}, bf16[1024,1024]{1,0:T(8,128)(2,1)}, u32[]{:S(2)}, u32[]{:S(2)}) collective-permute-start(bf16[1024,1024]{1,0:T(8,128)(2,1)} %param.7), channel_id=1, source_target_pairs={{0,2},{1,3},{2,0},{3,1},{4,6},{5,7},{6,4},{7,5},{8,10},{9,11},{10,... | collective-permute-start | bytes 6291464 | tf_op jit(solution)/shard_map/ppermute | solution.py:24
  8.6 27.9 %collective-permute-start.3 = (bf16[512,1024]{1,0:T(8,128)(2,1)S(1)}, bf16[512,1024]{1,0:T(8,128)(2,1)S(1)}, u32[]{:S(2)}, u32[]{:S(2)}) collective-permute-start(bf16[512,1024]{1,0:T(8,128)(2,1)S(1)} %pad_maximum_fusion.1.refs_0_), channel_id=1, source_target_pairs={{0,4},{4,8},{8,12},{12,0},{1,5},{5,9},{9,13},{13,1},{2,6},{6,10},{... | collective-permute-start | bytes 3145736 | tf_op jit(solution)/shard_map/ppermute | solution.py:24
  10.1 46.8 %collective-permute-start.4 = (bf16[512,1024]{1,0:T(8,128)(2,1)S(1)}, bf16[512,1024]{1,0:T(8,128)(2,1)S(1)}, u32[]{:S(2)}, u32[]{:S(2)}) collective-permute-start(bf16[512,1024]{1,0:T(8,128)(2,1)S(1)} %pad_maximum_fusion.1.refs_0_), channel_id=1, source_target_pairs={{0,12},{4,0},{8,4},{12,8},{1,13},{5,1},{9,5},{13,9},{2,14},{6,2},{... | collective-permute-start | bytes 3145736 | tf_op jit(solution)/shard_map/ppermute | solution.py:24
  13.2 73.9 %copy-start.12 = (bf16[256,512]{1,0:T(8,128)(2,1)}, bf16[256,512]{1,0:T(8,128)(2,1)S(1)}, u32[]{:S(2)}) copy-start(bf16[256,512]{1,0:T(8,128)(2,1)S(1)} %get-tuple-element.66) | copy-start | bytes 786436
  13.2 46.9 %collective-permute-start.5 = (bf16[4,64,512]{2,1,0:T(8,128)(2,1)}, bf16[4,64,512]{2,1,0:T(8,128)(2,1)}, u32[]{:S(2)}, u32[]{:S(2)}) collective-permute-start(bf16[4,64,512]{2,1,0:T(8,128)(2,1)} %bitcast.7.g_ref), channel_id=1, source_target_pairs={{0,16},{16,0},{1,17},{17,1},{2,18},{18,2},{3,19},{19,3},{4,20},{20... | collective-permute-start | bytes 786440 | tf_op jit(solution)/shard_map/ppermute | solution.py:24
  13.7 3.4 %copy-start.1 = (bf16[8,2,256,1024]{3,2,1,0:T(8,128)(2,1)S(1)}, bf16[8,2,256,1024]{3,2,1,0:T(8,128)(2,1)}, u32[]{:S(2)}) copy-start(bf16[8,2,256,1024]{3,2,1,0:T(8,128)(2,1)} %kv_ref.3) | copy-start | bytes 25165828
  57.0 36.8 %copy-start.2 = (bf16[512,1024]{1,0:T(8,128)(2,1)}, bf16[512,1024]{1,0:T(8,128)(2,1)S(1)}, u32[]{:S(2)}) copy-start(bf16[512,1024]{1,0:T(8,128)(2,1)S(1)} %collective-permute-done.4.refs_3_) | copy-start | bytes 3145732
  60.0 30.2 %collective-permute-start.8 = (bf16[1024,640]{1,0:T(8,128)(2,1)S(1)}, bf16[1024,640]{1,0:T(8,128)(2,1)S(1)}, u32[]{:S(2)}, u32[]{:S(2)}) collective-permute-start(bf16[1024,640]{1,0:T(8,128)(2,1)S(1)} %slice.77), channel_id=1, source_target_pairs={{0,2},{1,3},{2,0},{3,1},{4,6},{5,7},{6,4},{7,5},{8,10},{9,11},{10,... | collective-permute-start | bytes 3932168 | tf_op jit(solution)/shard_map/ppermute | solution.py:24
  61.0 16.8 %collective-permute-start.6 = (bf16[256,1024]{1,0:T(8,128)(2,1)S(1)}, bf16[256,1024]{1,0:T(8,128)(2,1)S(1)}, u32[]{:S(2)}, u32[]{:S(2)}) collective-permute-start(bf16[256,1024]{1,0:T(8,128)(2,1)S(1)} %slice.61), channel_id=1, source_target_pairs={{0,4},{4,8},{8,12},{12,0},{1,5},{5,9},{9,13},{13,1},{2,6},{6,10},{... | collective-permute-start | bytes 1572872 | tf_op jit(solution)/shard_map/ppermute | solution.py:24
  62.7 24.3 %collective-permute-start.7 = (bf16[256,1024]{1,0:T(8,128)(2,1)S(1)}, bf16[256,1024]{1,0:T(8,128)(2,1)S(1)}, u32[]{:S(2)}, u32[]{:S(2)}) collective-permute-start(bf16[256,1024]{1,0:T(8,128)(2,1)S(1)} %slice.62), channel_id=1, source_target_pairs={{0,12},{4,0},{8,4},{12,8},{1,13},{5,1},{9,5},{13,9},{2,14},{6,2},{... | collective-permute-start | bytes 1572872 | tf_op jit(solution)/shard_map/ppermute | solution.py:24
  65.1 21.9 %collective-permute-start.9 = (bf16[1024,384]{1,0:T(8,128)(2,1)S(1)}, bf16[1024,384]{1,0:T(8,128)(2,1)S(1)}, u32[]{:S(2)}, u32[]{:S(2)}) collective-permute-start(bf16[1024,384]{1,0:T(8,128)(2,1)S(1)} %slice.78), channel_id=1, source_target_pairs={{0,16},{16,0},{1,17},{17,1},{2,18},{18,2},{3,19},{19,3},{4,20},{20... | collective-permute-start | bytes 2359304 | tf_op jit(solution)/shard_map/ppermute | solution.py:24
  87.0 6.8 %copy-start.4 = (bf16[512,1024]{1,0:T(8,128)(2,1)}, bf16[512,1024]{1,0:T(8,128)(2,1)S(1)}, u32[]{:S(2)}) copy-start(bf16[512,1024]{1,0:T(8,128)(2,1)S(1)} %constant_dynamic-update-slice_fusion.refs_2_) | copy-start | bytes 3145732
  87.1 10.4 %collective-permute-start.11 = (bf16[4,64,512]{2,1,0:T(8,128)(2,1)S(1)}, bf16[4,64,512]{2,1,0:T(8,128)(2,1)S(1)}, u32[]{:S(2)}, u32[]{:S(2)}) collective-permute-start(bf16[4,64,512]{2,1,0:T(8,128)(2,1)S(1)} %bitcast.76), channel_id=1, source_target_pairs={{0,16},{16,0},{1,17},{17,1},{2,18},{18,2},{3,19},{19,3},{4,20},{20... | collective-permute-start | bytes 786440 | tf_op jit(solution)/shard_map/ppermute | solution.py:24
  90.8 3.3 %copy-start = (bf16[4,1024,1024]{2,1,0:T(8,128)(2,1)}, bf16[4,1024,1024]{2,1,0:T(8,128)(2,1)S(1)}, u32[]{:S(2)}) copy-start(bf16[4,1024,1024]{2,1,0:T(8,128)(2,1)S(1)} %bitcast_dynamic-update-slice_fusion.4.refs_4_) | copy-start | bytes 25165828
  93.7 3.7 %copy-start.25 = (s32[8,256]{1,0:T(8,128)S(1)}, s32[8,256]{1,0:T(8,128)}, u32[]{:S(2)}) copy-start(s32[8,256]{1,0:T(8,128)} %param.10) | copy-start | bytes 24580
  93.7 3.7 %collective-permute-start.10 = (f32[256,512]{1,0:T(8,128)S(1)}, f32[256,512]{1,0:T(8,128)S(1)}, u32[]{:S(2)}, u32[]{:S(2)}) collective-permute-start(f32[256,512]{1,0:T(8,128)S(1)} %slice.80), channel_id=1, source_target_pairs={{0,1},{1,0},{2,3},{3,2},{4,5},{5,4},{6,7},{7,6},{8,9},{9,8},{10,11... | collective-permute-start | bytes 1572872 | tf_op jit(solution)/shard_map/ppermute | solution.py:28
  97.0 2.0 collective-permute-start.12
  97.4 8.1 %copy-start.14 = (bf16[4,64,512]{2,1,0:T(8,128)(2,1)}, bf16[4,64,512]{2,1,0:T(8,128)(2,1)S(1)}, u32[]{:S(2)}) copy-start(bf16[4,64,512]{2,1,0:T(8,128)(2,1)S(1)} %collective-permute-done.11.g_ref) | copy-start | bytes 786436
  97.5 12.1 %collective-permute-start.13 = (bf16[4,64,512]{2,1,0:T(8,128)(2,1)S(1)}, bf16[4,64,512]{2,1,0:T(8,128)(2,1)S(1)}, u32[]{:S(2)}, u32[]{:S(2)}) collective-permute-start(bf16[4,64,512]{2,1,0:T(8,128)(2,1)S(1)} %bitcast.78), channel_id=1, source_target_pairs={{0,16},{16,0},{1,17},{17,1},{2,18},{18,2},{3,19},{19,3},{4,20},{20... | collective-permute-start | bytes 786440 | tf_op jit(solution)/shard_map/ppermute | solution.py:24
  99.1 15.9 %collective-permute-start.16 = (bf16[4,64,512]{2,1,0:T(8,128)(2,1)S(1)}, bf16[4,64,512]{2,1,0:T(8,128)(2,1)}, u32[]{:S(2)}, u32[]{:S(2)}) collective-permute-start(bf16[4,64,512]{2,1,0:T(8,128)(2,1)S(1)} %bitcast.74), channel_id=1, source_target_pairs={{0,16},{16,0},{1,17},{17,1},{2,18},{18,2},{3,19},{19,3},{4,20},{20... | collective-permute-start | bytes 786440 | tf_op jit(solution)/shard_map/ppermute | solution.py:24
  100.1 5.4 %copy-start.11 = (bf16[4,2,256,512]{3,2,1,0:T(8,128)(2,1)S(1)}, bf16[4,2,256,512]{3,2,1,0:T(8,128)(2,1)}, u32[]{:S(2)}) copy-start(bf16[4,2,256,512]{3,2,1,0:T(8,128)(2,1)} %copy-done.10) | copy-start | bytes 6291460
  100.1 5.4 %copy-start.13 = (bf16[256,512]{1,0:T(8,128)(2,1)S(1)}, bf16[256,512]{1,0:T(8,128)(2,1)}, u32[]{:S(2)}) copy-start(bf16[256,512]{1,0:T(8,128)(2,1)} %copy-done.12) | copy-start | bytes 786436
  105.5 4.2 %copy-start.18 = (bf16[4,64,512]{2,1,0:T(8,128)(2,1)}, bf16[4,64,512]{2,1,0:T(8,128)(2,1)S(1)}, u32[]{:S(2)}) copy-start(bf16[4,64,512]{2,1,0:T(8,128)(2,1)S(1)} %get-tuple-element.71) | copy-start | bytes 786436
  105.5 4.2 %copy-start.9 = (bf16[4,2,256,512]{3,2,1,0:T(8,128)(2,1)S(1)}, bf16[4,2,256,512]{3,2,1,0:T(8,128)(2,1)}, u32[]{:S(2)}) copy-start(bf16[4,2,256,512]{3,2,1,0:T(8,128)(2,1)} %copy-done.8) | copy-start | bytes 6291460
  109.7 5.3 %copy-start.16 = (bf16[4,64,512]{2,1,0:T(8,128)(2,1)}, bf16[4,64,512]{2,1,0:T(8,128)(2,1)S(1)}, u32[]{:S(2)}) copy-start(bf16[4,64,512]{2,1,0:T(8,128)(2,1)S(1)} %get-tuple-element.78) | copy-start | bytes 786436
  115.0 8.6 %collective-permute-start.14 = (bf16[4,64,512]{2,1,0:T(8,128)(2,1)}, bf16[4,64,512]{2,1,0:T(8,128)(2,1)}, u32[]{:S(2)}, u32[]{:S(2)}) collective-permute-start(bf16[4,64,512]{2,1,0:T(8,128)(2,1)} %get-tuple-element.77), channel_id=1, source_target_pairs={{0,16},{16,0},{1,17},{17,1},{2,18},{18,2},{3,19},{19,3},{4,20},{20... | collective-permute-start | bytes 786440 | tf_op jit(solution)/shard_map/ppermute | solution.py:24
  117.6 6.1 %copy-start.19 = (bf16[4,64,512]{2,1,0:T(8,128)(2,1)S(1)}, bf16[4,64,512]{2,1,0:T(8,128)(2,1)}, u32[]{:S(2)}) copy-start(bf16[4,64,512]{2,1,0:T(8,128)(2,1)} %copy-done.18) | copy-start | bytes 786436
  117.6 7.5 %copy-start.3 = (bf16[512,1024]{1,0:T(8,128)(2,1)S(1)}, bf16[512,1024]{1,0:T(8,128)(2,1)}, u32[]{:S(2)}) copy-start(bf16[512,1024]{1,0:T(8,128)(2,1)} %copy-done.2) | copy-start | bytes 3145732
  117.6 7.5 %copy-start.5 = (bf16[512,1024]{1,0:T(8,128)(2,1)S(1)}, bf16[512,1024]{1,0:T(8,128)(2,1)}, u32[]{:S(2)}) copy-start(bf16[512,1024]{1,0:T(8,128)(2,1)} %copy-done.4) | copy-start | bytes 3145732
  122.9 8.0 %collective-permute-start.17 = (bf16[4,64,512]{2,1,0:T(8,128)(2,1)S(1)}, bf16[4,64,512]{2,1,0:T(8,128)(2,1)S(1)}, u32[]{:S(2)}, u32[]{:S(2)}) collective-permute-start(bf16[4,64,512]{2,1,0:T(8,128)(2,1)S(1)} %get-tuple-element.81), channel_id=1, source_target_pairs={{0,16},{16,0},{1,17},{17,1},{2,18},{18,2},{3,19},{19,3},{4,20},{20... | collective-permute-start | bytes 786440 | tf_op jit(solution)/shard_map/ppermute | solution.py:24
  124.6 1.6 collective-permute-start.15
  125.6 5.3 %copy-start.22 = (bf16[4,512,1024]{2,1,0:T(8,128)(2,1)}, bf16[4,512,1024]{2,1,0:T(8,128)(2,1)S(1)}, u32[]{:S(2)}) copy-start(bf16[4,512,1024]{2,1,0:T(8,128)(2,1)S(1)} %pad_maximum_fusion) | copy-start | bytes 12582916
  125.6 5.2 %copy-start.17 = (bf16[4,64,512]{2,1,0:T(8,128)(2,1)S(1)}, bf16[4,64,512]{2,1,0:T(8,128)(2,1)}, u32[]{:S(2)}) copy-start(bf16[4,64,512]{2,1,0:T(8,128)(2,1)} %copy-done.16) | copy-start | bytes 786436
  126.2 4.7 %copy-start.27 = (bf16[256,512]{1,0:T(8,128)(2,1)}, bf16[256,512]{1,0:T(8,128)(2,1)S(1)}, u32[]{:S(2)}) copy-start(bf16[256,512]{1,0:T(8,128)(2,1)S(1)} %collective-permute-done.15) | copy-start | bytes 786436
  130.9 3.6 %collective-permute-start.18 = (bf16[256,512]{1,0:T(8,128)(2,1)S(1)}, bf16[256,512]{1,0:T(8,128)(2,1)S(1)}, u32[]{:S(2)}, u32[]{:S(2)}) collective-permute-start(bf16[256,512]{1,0:T(8,128)(2,1)S(1)} %bitcast_add_fusion), channel_id=1, source_target_pairs={{0,1},{1,0},{2,3},{3,2},{4,5},{5,4},{6,7},{7,6},{8,9},{9,8},{10,11... | collective-permute-start | bytes 786440 | tf_op jit(solution)/shard_map/ppermute | solution.py:28
  131.1 3.4 %copy-start.28 = (bf16[256,512]{1,0:T(8,128)(2,1)S(1)}, bf16[256,512]{1,0:T(8,128)(2,1)}, u32[]{:S(2)}) copy-start(bf16[256,512]{1,0:T(8,128)(2,1)} %copy-done.27) | copy-start | bytes 786436
  132.9 25.5 %collective-permute-start.21 = (bf16[1024,512]{1,0:T(8,128)(2,1)S(1)}, bf16[1024,512]{1,0:T(8,128)(2,1)S(1)}, u32[]{:S(2)}, u32[]{:S(2)}) collective-permute-start(bf16[1024,512]{1,0:T(8,128)(2,1)S(1)} %convolution_convert_fusion.5), channel_id=1, source_target_pairs={{0,2},{1,3},{2,0},{3,1},{4,6},{5,7},{6,4},{7,5},{8,10},{9,11},{10,... | collective-permute-start | bytes 3145736 | tf_op jit(solution)/shard_map/ppermute | solution.py:24
  137.5 25.2 %collective-permute-start.22 = (bf16[1024,512]{1,0:T(8,128)(2,1)S(1)}, bf16[1024,512]{1,0:T(8,128)(2,1)S(1)}, u32[]{:S(2)}, u32[]{:S(2)}) collective-permute-start(bf16[1024,512]{1,0:T(8,128)(2,1)S(1)} %convolution_convert_fusion.4), channel_id=1, source_target_pairs={{0,16},{16,0},{1,17},{17,1},{2,18},{18,2},{3,19},{19,3},{4,20},{20... | collective-permute-start | bytes 3145736 | tf_op jit(solution)/shard_map/ppermute | solution.py:24
  138.0 24.7 %collective-permute-start.19 = (bf16[256,1024]{1,0:T(8,128)(2,1)S(1)}, bf16[256,1024]{1,0:T(8,128)(2,1)S(1)}, u32[]{:S(2)}, u32[]{:S(2)}) collective-permute-start(bf16[256,1024]{1,0:T(8,128)(2,1)S(1)} %get-tuple-element.106), channel_id=1, source_target_pairs={{0,4},{4,8},{8,12},{12,0},{1,5},{5,9},{9,13},{13,1},{2,6},{6,10},{... | collective-permute-start | bytes 1572872 | tf_op jit(solution)/shard_map/ppermute | solution.py:24
  139.5 24.8 %collective-permute-start.20 = (bf16[256,1024]{1,0:T(8,128)(2,1)S(1)}, bf16[256,1024]{1,0:T(8,128)(2,1)S(1)}, u32[]{:S(2)}, u32[]{:S(2)}) collective-permute-start(bf16[256,1024]{1,0:T(8,128)(2,1)S(1)} %get-tuple-element.105), channel_id=1, source_target_pairs={{0,12},{4,0},{8,4},{12,8},{1,13},{5,1},{9,5},{13,9},{2,14},{6,2},{... | collective-permute-start | bytes 1572872 | tf_op jit(solution)/shard_map/ppermute | solution.py:24
  164.5 26.5 %collective-permute-start.26 = (bf16[512,1024]{1,0:T(8,128)(2,1)S(1)}, bf16[512,1024]{1,0:T(8,128)(2,1)S(1)}, u32[]{:S(2)}, u32[]{:S(2)}) collective-permute-start(bf16[512,1024]{1,0:T(8,128)(2,1)S(1)} %fusion.31), channel_id=1, source_target_pairs={{0,12},{4,0},{8,4},{12,8},{1,13},{5,1},{9,5},{13,9},{2,14},{6,2},{... | collective-permute-start | bytes 3145736 | tf_op jit(solution)/shard_map/ppermute | solution.py:24
  167.3 46.4 %collective-permute-start.24 = (bf16[1024,1024]{1,0:T(8,128)(2,1)S(1)}, bf16[1024,1024]{1,0:T(8,128)(2,1)S(1)}, u32[]{:S(2)}, u32[]{:S(2)}) collective-permute-start(bf16[1024,1024]{1,0:T(8,128)(2,1)S(1)} %fusion.19), channel_id=1, source_target_pairs={{0,2},{1,3},{2,0},{3,1},{4,6},{5,7},{6,4},{7,5},{8,10},{9,11},{10,... | collective-permute-start | bytes 6291464 | tf_op jit(solution)/shard_map/ppermute | solution.py:24
  169.7 46.0 %collective-permute-start.23 = (bf16[1024,1024]{1,0:T(8,128)(2,1)S(1)}, bf16[1024,1024]{1,0:T(8,128)(2,1)S(1)}, u32[]{:S(2)}, u32[]{:S(2)}) collective-permute-start(bf16[1024,1024]{1,0:T(8,128)(2,1)S(1)} %fusion.18), channel_id=1, source_target_pairs={{0,16},{16,0},{1,17},{17,1},{2,18},{18,2},{3,19},{19,3},{4,20},{20... | collective-permute-start | bytes 6291464 | tf_op jit(solution)/shard_map/ppermute | solution.py:24
  170.5 41.4 %collective-permute-start.25 = (bf16[512,1024]{1,0:T(8,128)(2,1)S(1)}, bf16[512,1024]{1,0:T(8,128)(2,1)S(1)}, u32[]{:S(2)}, u32[]{:S(2)}) collective-permute-start(bf16[512,1024]{1,0:T(8,128)(2,1)S(1)} %fusion.30), channel_id=1, source_target_pairs={{0,4},{4,8},{8,12},{12,0},{1,5},{5,9},{9,13},{13,1},{2,6},{6,10},{... | collective-permute-start | bytes 3145736 | tf_op jit(solution)/shard_map/ppermute | solution.py:24
  212.1 5.8 %collective-permute-start.27 = (bf16[256,1024]{1,0:T(8,128)(2,1)S(1)}, bf16[256,1024]{1,0:T(8,128)(2,1)S(1)}, u32[]{:S(2)}, u32[]{:S(2)}) collective-permute-start(bf16[256,1024]{1,0:T(8,128)(2,1)S(1)} %add_convert_fusion.2), channel_id=1, source_target_pairs={{0,1},{1,0},{2,3},{3,2},{4,5},{5,4},{6,7},{7,6},{8,9},{9,8},{10,11... | collective-permute-start | bytes 1572872 | tf_op jit(solution)/shard_map/ppermute | solution.py:28
  (11 other events, 21.4 us)

commit v16 on v15

--- a/solution.py
+++ b/solution.py
@@ -105,7 +105,7 @@
 def attend_block(q_ref, g_ref, kv_ref, live_ref, dq_ref, grad_ref):
     pairs = q_ref.shape[-1] // HD // 2
     scale = HD ** (-0.5)
-    live = live_ref[...] > 0.5
+    live = live_ref[...].astype(F32) > 0.5
     zero = jnp.zeros((SPAN, HD), BF16)
 
     def diagonal(ref, start):
@@ -407,7 +407,7 @@
             names = (place < jnp.sum(names)).astype(jnp.int32)
         return place, names, sources[step]
 
-    live = jnp.broadcast_to((neighbour_ids != 0).astype(F32)[:, :, None], (capacity, KEYS, HD))
+    live = jnp.broadcast_to((neighbour_ids != 0).astype(BF16)[:, :, None], (capacity, KEYS, HD))
     slots = [slots_of(step) for step in range(seq_count)]
 
     queries = []

time: 221 us -> 221 us (level)
    unnamed x63 -> x67, local copies, waits for them, and re-layouts: 13.4 us -> 14.5 us
where the time goes in v16:
time: 221 us; the launch traced here: 220 us
  waiting for transfers between devices  113 us (51%)
  starting transfers between devices  31.1 us (14%)
  Pallas kernels  30.4 us (14%)
  local copies, waits for them, and re-layouts  28.9 us (13%)
  matrix products  10.6 us (5%)
  other arithmetic  4.56 us (2%)
    ppermute x22, waiting for transfers between devices, shift(): lax.ppermute(value, axis, [(i, (i + step * stride) % size) for i in range...  110 us
    ppermute x22, starting transfers between devices, shift(): lax.ppermute(value, axis, [(i, (i + step * stride) % size) for i in range...  29.9 us
    pallas_call x4, Pallas kernels, attend(): pl.pallas_call(attend_kernel, grid_spec=pltpu.PrefetchScalarGridSpec(num_...  20.1 us
    unnamed x67, local copies, waits for them, and re-layouts  14.5 us
    dot_general x9, matrix products, dot(): lax.dot_general(a, b, (contract, ((), ())), preferred_element_type=F32)  10.6 us
    dynamic_update_slice x5, local copies, waits for them, and re-layouts, placed(): lax.dynamic_update_slice(weights, piece[None], (at, inner * depth, start))  6.06 us
    pallas_call x2, Pallas kernels, product(): pl.pallas_call(functools.partial(product_kernel, count, start), out_shape...  5.79 us
  transfers between devices with their start and end apart: 28, of which 16 were waited for; matrix products, arithmetic and copies ran while one was open for 13% of the time, Pallas kernels for 13%

profile of v16, /device:TPU:0, one launch (start us, length us, event | category | flops | bytes accessed | tf_op | source)
XLA Modules:
  0.0 219.7 jit_solution(2621083866645846198)
XLA Ops:
  0.7 1.3 constant_dynamic-slice_fusion.2
  2.5 1.5 collective-permute-done
  4.1 2.9 %collective-permute-start.1 = (bf16[1024,1024]{1,0:T(8,128)(2,1)}, bf16[1024,1024]{1,0:T(8,128)(2,1)}, u32[]{:S(2)}, u32[]{:S(2)}) collective-permute-start(bf16[1024,1024]{1,0:T(8,128)(2,1)} %param.7), channel_id=1, source_target_pairs={{0,16},{16,0},{1,17},{17,1},{2,18},{18,2},{3,19},{19,3},{4,20},{20... | collective-permute-start | bytes 6291464 | tf_op jit(solution)/shard_map/ppermute | solution.py:24
  7.0 1.5 collective-permute-start.2
  8.6 1.6 collective-permute-start.3
  10.1 2.2 %collective-permute-start.4 = (bf16[512,1024]{1,0:T(8,128)(2,1)S(1)}, bf16[512,1024]{1,0:T(8,128)(2,1)S(1)}, u32[]{:S(2)}, u32[]{:S(2)}) collective-permute-start(bf16[512,1024]{1,0:T(8,128)(2,1)S(1)} %pad_maximum_fusion.1.refs_0_), channel_id=1, source_target_pairs={{0,12},{4,0},{8,4},{12,8},{1,13},{5,1},{9,5},{13,9},{2,14},{6,2},{... | collective-permute-start | bytes 3145736 | tf_op jit(solution)/shard_map/ppermute | solution.py:24
  13.7 3.4 %copy-done.1 = bf16[8,2,256,1024]{3,2,1,0:T(8,128)(2,1)S(1)} copy-done((bf16[8,2,256,1024]{3,2,1,0:T(8,128)(2,1)S(1)}, bf16[8,2,256,1024]{3,2,1,0:T(8,128)(2,1)}, u32[]{:S(2)}) %copy-start.1) | copy-done | bytes 8388632
  17.4 1.3 copy-done.6
  20.4 1.4 copy-done.10
  21.8 1.3 copy-done.20
  24.6 1.9 bitcast_dynamic-update-slice_fusion.2
  26.5 10.0 %collective-permute-done.3.refs_1_ = bf16[512,1024]{1,0:T(8,128)(2,1)S(1)} collective-permute-done((bf16[512,1024]{1,0:T(8,128)(2,1)S(1)}, bf16[512,1024]{1,0:T(8,128)(2,1)S(1)}, u32[]{:S(2)}, u32[]{:S(2)}) %collective-permute-start.3) | collective-permute-done | bytes 1048608 | tf_op jit(solution)/shard_map/ppermute | solution.py:24
  36.5 20.5 %collective-permute-done.4.refs_3_ = bf16[512,1024]{1,0:T(8,128)(2,1)S(1)} collective-permute-done((bf16[512,1024]{1,0:T(8,128)(2,1)S(1)}, bf16[512,1024]{1,0:T(8,128)(2,1)S(1)}, u32[]{:S(2)}, u32[]{:S(2)}) %collective-permute-start.4) | collective-permute-done | bytes 1048608 | tf_op jit(solution)/shard_map/ppermute | solution.py:24
  57.0 1.4 slice.77
  61.0 1.6 collective-permute-start.6
  62.7 2.5 %collective-permute-start.7 = (bf16[256,1024]{1,0:T(8,128)(2,1)S(1)}, bf16[256,1024]{1,0:T(8,128)(2,1)S(1)}, u32[]{:S(2)}, u32[]{:S(2)}) collective-permute-start(bf16[256,1024]{1,0:T(8,128)(2,1)S(1)} %slice.62), channel_id=1, source_target_pairs={{0,12},{4,0},{8,4},{12,8},{1,13},{5,1},{9,5},{13,9},{2,14},{6,2},{... | collective-permute-start | bytes 1572872 | tf_op jit(solution)/shard_map/ppermute | solution.py:24
  65.1 1.5 collective-permute-start.9
  66.6 1.9 bitcast_dynamic-update-slice_fusion.1
  68.5 1.9 bitcast_dynamic-update-slice_fusion
  70.4 7.4 %collective-permute-done.6 = bf16[256,1024]{1,0:T(8,128)(2,1)S(1)} collective-permute-done((bf16[256,1024]{1,0:T(8,128)(2,1)S(1)}, bf16[256,1024]{1,0:T(8,128)(2,1)S(1)}, u32[]{:S(2)}, u32[]{:S(2)}) %collective-permute-start.6) | collective-permute-done | bytes 524320 | tf_op jit(solution)/shard_map/ppermute | solution.py:24
  77.8 8.9 %collective-permute-done.7 = bf16[256,1024]{1,0:T(8,128)(2,1)S(1)} collective-permute-done((bf16[256,1024]{1,0:T(8,128)(2,1)S(1)}, bf16[256,1024]{1,0:T(8,128)(2,1)S(1)}, u32[]{:S(2)}, u32[]{:S(2)}) %collective-permute-start.7) | collective-permute-done | bytes 524320 | tf_op jit(solution)/shard_map/ppermute | solution.py:24
  86.8 1.6 collective-permute-start.11
  88.3 1.5 collective-permute-done.8
  90.4 2.9 %shard_map.87 = f32[512,512]{1,0:T(8,128)S(1)} custom-call(s32[4]{0:T(128)S(1)} %pad_add_fusion.1.table_ref, bf16[512,1024]{1,0:T(8,128)(2,1)S(1)} %pad_maximum_fusion.1.refs_0_, bf16[512,1024]{1,0:T(8,128)(2,1)S(1)} %collective-permute-done.3.refs_1_, bf16[512,1024]{1,0:T(8,128)(2,1)S(1)} %constant_dynamic-update-slice_fusion.refs_2_, ...), custom_call_target="tpu_custom_call" | custom-call | flops 2147483648 | bytes 9437184 | tf_op jit(solution)/shard_map/pallas_call | solution.py:90
  93.7 2.9 %shard_map.88 = f32[512,512]{1,0:T(8,128)S(1)} custom-call(s32[4]{0:T(128)S(1)} %pad_add_fusion.1.table_ref, bf16[512,1024]{1,0:T(8,128)(2,1)S(1)} %pad_maximum_fusion.1.refs_0_, bf16[512,1024]{1,0:T(8,128)(2,1)S(1)} %collective-permute-done.3.refs_1_, bf16[512,1024]{1,0:T(8,128)(2,1)S(1)} %constant_dynamic-update-slice_fusion.refs_2_, ...), custom_call_target="tpu_custom_call" | custom-call | flops 2147483648 | bytes 9437184 | tf_op jit(solution)/shard_map/pallas_call | solution.py:90
  99.9 5.5 %shard_map.89 = (bf16[4,64,512]{2,1,0:T(8,128)(2,1)S(1)}, bf16[8,2,256,1024]{3,2,1,0:T(8,128)(2,1)}) custom-call(s32[12]{0:T(128)S(1)} %pad_add_fusion.table_ref, bf16[4,64,512]{2,1,0:T(8,128)(2,1)S(1)} %bitcast.79, bf16[4,64,512]{2,1,0:T(8,128)(2,1)} %bitcast.7.g_ref, bf16[8,256,128]{2,1,0:T(8,128)(2,1)S(1)} %broadcast_in_dim.20.live_ref, ...), custom_call_target="tpu_custom_call" | custom-call | flops 1342177280 | bytes 4194304 | tf_op jit(solution)/shard_map/pallas_call | solution.py:178
  105.5 4.2 %shard_map.90 = (bf16[4,64,512]{2,1,0:T(8,128)(2,1)S(1)}, bf16[8,2,256,1024]{3,2,1,0:T(8,128)(2,1)}) custom-call(s32[12]{0:T(128)S(1)} %pad_add_fusion.table_ref, bf16[4,64,512]{2,1,0:T(8,128)(2,1)S(1)} %bitcast.75, bf16[4,64,512]{2,1,0:T(8,128)(2,1)S(1)} %bitcast.77, ...), custom_call_target="tpu_custom_call", output_to_operand_aliasing={{1}: (5, {})} | custom-call | flops 1342177280 | bytes 4194304 | tf_op jit(solution)/shard_map/pallas_call | solution.py:178
  109.7 5.3 %shard_map.91 = (bf16[4,64,512]{2,1,0:T(8,128)(2,1)}, bf16[8,2,256,1024]{3,2,1,0:T(8,128)(2,1)}) custom-call(s32[12]{0:T(128)S(1)} %pad_add_fusion.2.table_ref, bf16[4,64,512]{2,1,0:T(8,128)(2,1)S(1)} %collective-permute-done.13.q_ref, bf16[4,64,512]{2,1,0:T(8,128)(2,1)} %collective-permute-done.5.g_ref, ...), custom_call_target="tpu_custom_call", output_to_operand_aliasing={{1}: (5, {})} | custom-call | flops 1342177280 | bytes 4194304 | tf_op jit(solution)/shard_map/pallas_call | solution.py:178
  116.0 1.6 copy-done.7
  118.6 5.2 %shard_map.92 = (bf16[4,64,512]{2,1,0:T(8,128)(2,1)S(1)}, bf16[8,2,256,1024]{3,2,1,0:T(8,128)(2,1)}) custom-call(s32[12]{0:T(128)S(1)} %pad_add_fusion.2.table_ref, bf16[4,64,512]{2,1,0:T(8,128)(2,1)} %collective-permute-done.16.q_ref, bf16[4,64,512]{2,1,0:T(8,128)(2,1)S(1)} %copy-done.15, ...), custom_call_target="tpu_custom_call", output_to_operand_aliasing={{1}: (5, {})} | custom-call | flops 1342177280 | bytes 4194304 | tf_op jit(solution)/shard_map/pallas_call | solution.py:178
  127.9 4.1 %collective-permute-done.17 = bf16[4,64,512]{2,1,0:T(8,128)(2,1)S(1)} collective-permute-done((bf16[4,64,512]{2,1,0:T(8,128)(2,1)S(1)}, bf16[4,64,512]{2,1,0:T(8,128)(2,1)S(1)}, u32[]{:S(2)}, u32[]{:S(2)}) %collective-permute-start.17) | collective-permute-done | bytes 262176 | tf_op jit(solution)/shard_map/ppermute | solution.py:24
  132.2 1.8 dynamic-slice_bitcast_fusion
  134.0 1.6 collective-permute-start.21
  139.1 1.6 collective-permute-start.19
  140.7 2.2 %collective-permute-start.20 = (bf16[256,1024]{1,0:T(8,128)(2,1)S(1)}, bf16[256,1024]{1,0:T(8,128)(2,1)S(1)}, u32[]{:S(2)}, u32[]{:S(2)}) collective-permute-start(bf16[256,1024]{1,0:T(8,128)(2,1)S(1)} %get-tuple-element.105), channel_id=1, source_target_pairs={{0,12},{4,0},{8,4},{12,8},{1,13},{5,1},{9,5},{13,9},{2,14},{6,2},{... | collective-permute-start | bytes 1572872 | tf_op jit(solution)/shard_map/ppermute | solution.py:24
  146.6 1.3 fusion.15
  149.3 1.3 fusion.12
  150.6 1.3 fusion.9.own_ref
  151.9 7.6 %collective-permute-done.21 = bf16[1024,512]{1,0:T(8,128)(2,1)S(1)} collective-permute-done((bf16[1024,512]{1,0:T(8,128)(2,1)S(1)}, bf16[1024,512]{1,0:T(8,128)(2,1)S(1)}, u32[]{:S(2)}, u32[]{:S(2)}) %collective-permute-start.21) | collective-permute-done | bytes 1048608 | tf_op jit(solution)/shard_map/ppermute | solution.py:24
  159.5 4.3 %collective-permute-done.22 = bf16[1024,512]{1,0:T(8,128)(2,1)S(1)} collective-permute-done((bf16[1024,512]{1,0:T(8,128)(2,1)S(1)}, bf16[1024,512]{1,0:T(8,128)(2,1)S(1)}, u32[]{:S(2)}, u32[]{:S(2)}) %collective-permute-start.22) | collective-permute-done | bytes 1048608 | tf_op jit(solution)/shard_map/ppermute | solution.py:24
  163.8 1.5 collective-permute-done.20
  165.5 2.4 %collective-permute-start.26 = (bf16[512,1024]{1,0:T(8,128)(2,1)S(1)}, bf16[512,1024]{1,0:T(8,128)(2,1)S(1)}, u32[]{:S(2)}, u32[]{:S(2)}) collective-permute-start(bf16[512,1024]{1,0:T(8,128)(2,1)S(1)} %fusion.31), channel_id=1, source_target_pairs={{0,12},{4,0},{8,4},{12,8},{1,13},{5,1},{9,5},{13,9},{2,14},{6,2},{... | collective-permute-start | bytes 3145736 | tf_op jit(solution)/shard_map/ppermute | solution.py:24
  169.7 1.7 collective-permute-start.23
  171.7 19.9 %collective-permute-done.26.down_ref = bf16[512,1024]{1,0:T(8,128)(2,1)S(1)} collective-permute-done((bf16[512,1024]{1,0:T(8,128)(2,1)S(1)}, bf16[512,1024]{1,0:T(8,128)(2,1)S(1)}, u32[]{:S(2)}, u32[]{:S(2)}) %collective-permute-start.26) | collective-permute-done | bytes 1048608 | tf_op jit(solution)/shard_map/ppermute | solution.py:24
  191.5 21.5 %collective-permute-done.25.up_ref = bf16[512,1024]{1,0:T(8,128)(2,1)S(1)} collective-permute-done((bf16[512,1024]{1,0:T(8,128)(2,1)S(1)}, bf16[512,1024]{1,0:T(8,128)(2,1)S(1)}, u32[]{:S(2)}, u32[]{:S(2)}) %collective-permute-start.25) | collective-permute-done | bytes 1048608 | tf_op jit(solution)/shard_map/ppermute | solution.py:24
  213.4 1.6 collective-permute-done.24.refs_2_
  215.9 2.2 shard_map.93
  218.1 1.6 shard_map.94
  (137 shorter events, 30.3 us)
Async XLA Ops:
  0.7 11.7 %copy-start.24 = (bf16[256,1024]{1,0:T(8,128)(2,1)S(1)}, bf16[256,1024]{1,0:T(8,128)(2,1)}, u32[]{:S(2)}) copy-start(bf16[256,1024]{1,0:T(8,128)(2,1)} %param.8) | copy-start | bytes 1572868
  2.0 2.1 collective-permute-start
  4.1 52.9 %collective-permute-start.1 = (bf16[1024,1024]{1,0:T(8,128)(2,1)}, bf16[1024,1024]{1,0:T(8,128)(2,1)}, u32[]{:S(2)}, u32[]{:S(2)}) collective-permute-start(bf16[1024,1024]{1,0:T(8,128)(2,1)} %param.7), channel_id=1, source_target_pairs={{0,16},{16,0},{1,17},{17,1},{2,18},{18,2},{3,19},{19,3},{4,20},{20... | collective-permute-start | bytes 6291464 | tf_op jit(solution)/shard_map/ppermute | solution.py:24
  7.0 51.4 %collective-permute-start.2 = (bf16[1024,1024]{1,0:T(8,128)(2,1)}, bf16[1024,1024]{1,0:T(8,128)(2,1)}, u32[]{:S(2)}, u32[]{:S(2)}) collective-permute-start(bf16[1024,1024]{1,0:T(8,128)(2,1)} %param.7), channel_id=1, source_target_pairs={{0,2},{1,3},{2,0},{3,1},{4,6},{5,7},{6,4},{7,5},{8,10},{9,11},{10,... | collective-permute-start | bytes 6291464 | tf_op jit(solution)/shard_map/ppermute | solution.py:24
  8.6 27.9 %collective-permute-start.3 = (bf16[512,1024]{1,0:T(8,128)(2,1)S(1)}, bf16[512,1024]{1,0:T(8,128)(2,1)S(1)}, u32[]{:S(2)}, u32[]{:S(2)}) collective-permute-start(bf16[512,1024]{1,0:T(8,128)(2,1)S(1)} %pad_maximum_fusion.1.refs_0_), channel_id=1, source_target_pairs={{0,4},{4,8},{8,12},{12,0},{1,5},{5,9},{9,13},{13,1},{2,6},{6,10},{... | collective-permute-start | bytes 3145736 | tf_op jit(solution)/shard_map/ppermute | solution.py:24
  10.1 46.8 %collective-permute-start.4 = (bf16[512,1024]{1,0:T(8,128)(2,1)S(1)}, bf16[512,1024]{1,0:T(8,128)(2,1)S(1)}, u32[]{:S(2)}, u32[]{:S(2)}) collective-permute-start(bf16[512,1024]{1,0:T(8,128)(2,1)S(1)} %pad_maximum_fusion.1.refs_0_), channel_id=1, source_target_pairs={{0,12},{4,0},{8,4},{12,8},{1,13},{5,1},{9,5},{13,9},{2,14},{6,2},{... | collective-permute-start | bytes 3145736 | tf_op jit(solution)/shard_map/ppermute | solution.py:24
  13.1 73.6 %copy-start.12 = (bf16[256,512]{1,0:T(8,128)(2,1)}, bf16[256,512]{1,0:T(8,128)(2,1)S(1)}, u32[]{:S(2)}) copy-start(bf16[256,512]{1,0:T(8,128)(2,1)S(1)} %get-tuple-element.66) | copy-start | bytes 786436
  13.1 46.5 %collective-permute-start.5 = (bf16[4,64,512]{2,1,0:T(8,128)(2,1)}, bf16[4,64,512]{2,1,0:T(8,128)(2,1)}, u32[]{:S(2)}, u32[]{:S(2)}) collective-permute-start(bf16[4,64,512]{2,1,0:T(8,128)(2,1)} %bitcast.7.g_ref), channel_id=1, source_target_pairs={{0,16},{16,0},{1,17},{17,1},{2,18},{18,2},{3,19},{19,3},{4,20},{20... | collective-permute-start | bytes 786440 | tf_op jit(solution)/shard_map/ppermute | solution.py:24
  13.7 3.4 %copy-start.1 = (bf16[8,2,256,1024]{3,2,1,0:T(8,128)(2,1)S(1)}, bf16[8,2,256,1024]{3,2,1,0:T(8,128)(2,1)}, u32[]{:S(2)}) copy-start(bf16[8,2,256,1024]{3,2,1,0:T(8,128)(2,1)} %kv_ref.3) | copy-start | bytes 25165828
  59.7 30.2 %collective-permute-start.8 = (bf16[1024,640]{1,0:T(8,128)(2,1)S(1)}, bf16[1024,640]{1,0:T(8,128)(2,1)S(1)}, u32[]{:S(2)}, u32[]{:S(2)}) collective-permute-start(bf16[1024,640]{1,0:T(8,128)(2,1)S(1)} %slice.77), channel_id=1, source_target_pairs={{0,2},{1,3},{2,0},{3,1},{4,6},{5,7},{6,4},{7,5},{8,10},{9,11},{10,... | collective-permute-start | bytes 3932168 | tf_op jit(solution)/shard_map/ppermute | solution.py:24
  61.0 16.8 %collective-permute-start.6 = (bf16[256,1024]{1,0:T(8,128)(2,1)S(1)}, bf16[256,1024]{1,0:T(8,128)(2,1)S(1)}, u32[]{:S(2)}, u32[]{:S(2)}) collective-permute-start(bf16[256,1024]{1,0:T(8,128)(2,1)S(1)} %slice.61), channel_id=1, source_target_pairs={{0,4},{4,8},{8,12},{12,0},{1,5},{5,9},{9,13},{13,1},{2,6},{6,10},{... | collective-permute-start | bytes 1572872 | tf_op jit(solution)/shard_map/ppermute | solution.py:24
  62.7 24.0 %collective-permute-start.7 = (bf16[256,1024]{1,0:T(8,128)(2,1)S(1)}, bf16[256,1024]{1,0:T(8,128)(2,1)S(1)}, u32[]{:S(2)}, u32[]{:S(2)}) collective-permute-start(bf16[256,1024]{1,0:T(8,128)(2,1)S(1)} %slice.62), channel_id=1, source_target_pairs={{0,12},{4,0},{8,4},{12,8},{1,13},{5,1},{9,5},{13,9},{2,14},{6,2},{... | collective-permute-start | bytes 1572872 | tf_op jit(solution)/shard_map/ppermute | solution.py:24
  65.1 21.6 %collective-permute-start.9 = (bf16[1024,384]{1,0:T(8,128)(2,1)S(1)}, bf16[1024,384]{1,0:T(8,128)(2,1)S(1)}, u32[]{:S(2)}, u32[]{:S(2)}) collective-permute-start(bf16[1024,384]{1,0:T(8,128)(2,1)S(1)} %slice.78), channel_id=1, source_target_pairs={{0,16},{16,0},{1,17},{17,1},{2,18},{18,2},{3,19},{19,3},{4,20},{20... | collective-permute-start | bytes 2359304 | tf_op jit(solution)/shard_map/ppermute | solution.py:24
  86.7 6.7 %copy-start.2 = (bf16[512,1024]{1,0:T(8,128)(2,1)}, bf16[512,1024]{1,0:T(8,128)(2,1)S(1)}, u32[]{:S(2)}) copy-start(bf16[512,1024]{1,0:T(8,128)(2,1)S(1)} %constant_dynamic-update-slice_fusion.refs_2_) | copy-start | bytes 3145732
  86.8 10.3 %collective-permute-start.11 = (bf16[4,64,512]{2,1,0:T(8,128)(2,1)S(1)}, bf16[4,64,512]{2,1,0:T(8,128)(2,1)S(1)}, u32[]{:S(2)}, u32[]{:S(2)}) collective-permute-start(bf16[4,64,512]{2,1,0:T(8,128)(2,1)S(1)} %bitcast.76), channel_id=1, source_target_pairs={{0,16},{16,0},{1,17},{17,1},{2,18},{18,2},{3,19},{19,3},{4,20},{20... | collective-permute-start | bytes 786440 | tf_op jit(solution)/shard_map/ppermute | solution.py:24
  90.4 3.3 %copy-start = (bf16[4,1024,1024]{2,1,0:T(8,128)(2,1)}, bf16[4,1024,1024]{2,1,0:T(8,128)(2,1)S(1)}, u32[]{:S(2)}) copy-start(bf16[4,1024,1024]{2,1,0:T(8,128)(2,1)S(1)} %bitcast_dynamic-update-slice_fusion.4.refs_4_) | copy-start | bytes 25165828
  93.3 3.7 %copy-start.27 = (s32[8,256]{1,0:T(8,128)S(1)}, s32[8,256]{1,0:T(8,128)}, u32[]{:S(2)}) copy-start(s32[8,256]{1,0:T(8,128)} %param.10) | copy-start | bytes 24580
  93.3 3.7 %collective-permute-start.10 = (f32[256,512]{1,0:T(8,128)S(1)}, f32[256,512]{1,0:T(8,128)S(1)}, u32[]{:S(2)}, u32[]{:S(2)}) collective-permute-start(f32[256,512]{1,0:T(8,128)S(1)} %slice.80), channel_id=1, source_target_pairs={{0,1},{1,0},{2,3},{3,2},{4,5},{5,4},{6,7},{7,6},{8,9},{9,8},{10,11... | collective-permute-start | bytes 1572872 | tf_op jit(solution)/shard_map/ppermute | solution.py:28
  96.6 2.0 collective-permute-start.12
  97.0 8.4 %copy-start.14 = (bf16[4,64,512]{2,1,0:T(8,128)(2,1)}, bf16[4,64,512]{2,1,0:T(8,128)(2,1)S(1)}, u32[]{:S(2)}) copy-start(bf16[4,64,512]{2,1,0:T(8,128)(2,1)S(1)} %collective-permute-done.11.g_ref) | copy-start | bytes 786436
  97.2 12.5 %collective-permute-start.13 = (bf16[4,64,512]{2,1,0:T(8,128)(2,1)S(1)}, bf16[4,64,512]{2,1,0:T(8,128)(2,1)S(1)}, u32[]{:S(2)}, u32[]{:S(2)}) collective-permute-start(bf16[4,64,512]{2,1,0:T(8,128)(2,1)S(1)} %bitcast.78), channel_id=1, source_target_pairs={{0,16},{16,0},{1,17},{17,1},{2,18},{18,2},{3,19},{19,3},{4,20},{20... | collective-permute-start | bytes 786440 | tf_op jit(solution)/shard_map/ppermute | solution.py:24
  98.7 16.3 %collective-permute-start.16 = (bf16[4,64,512]{2,1,0:T(8,128)(2,1)S(1)}, bf16[4,64,512]{2,1,0:T(8,128)(2,1)}, u32[]{:S(2)}, u32[]{:S(2)}) collective-permute-start(bf16[4,64,512]{2,1,0:T(8,128)(2,1)S(1)} %bitcast.74), channel_id=1, source_target_pairs={{0,16},{16,0},{1,17},{17,1},{2,18},{18,2},{3,19},{19,3},{4,20},{20... | collective-permute-start | bytes 786440 | tf_op jit(solution)/shard_map/ppermute | solution.py:24
  99.9 9.8 %copy-start.4 = (bf16[8,256,128]{2,1,0:T(8,128)(2,1)}, bf16[8,256,128]{2,1,0:T(8,128)(2,1)S(1)}, u32[]{:S(2)}) copy-start(bf16[8,256,128]{2,1,0:T(8,128)(2,1)S(1)} %broadcast_in_dim.20.live_ref) | copy-start | bytes 1572868
  99.9 5.6 %copy-start.11 = (bf16[4,2,256,512]{3,2,1,0:T(8,128)(2,1)S(1)}, bf16[4,2,256,512]{3,2,1,0:T(8,128)(2,1)}, u32[]{:S(2)}) copy-start(bf16[4,2,256,512]{3,2,1,0:T(8,128)(2,1)} %copy-done.10) | copy-start | bytes 6291460
  99.9 5.6 %copy-start.13 = (bf16[256,512]{1,0:T(8,128)(2,1)S(1)}, bf16[256,512]{1,0:T(8,128)(2,1)}, u32[]{:S(2)}) copy-start(bf16[256,512]{1,0:T(8,128)(2,1)} %copy-done.12) | copy-start | bytes 786436
  105.5 4.2 %copy-start.18 = (bf16[4,64,512]{2,1,0:T(8,128)(2,1)}, bf16[4,64,512]{2,1,0:T(8,128)(2,1)S(1)}, u32[]{:S(2)}) copy-start(bf16[4,64,512]{2,1,0:T(8,128)(2,1)S(1)} %get-tuple-element.71) | copy-start | bytes 786436
  105.5 4.2 %copy-start.9 = (bf16[4,2,256,512]{3,2,1,0:T(8,128)(2,1)S(1)}, bf16[4,2,256,512]{3,2,1,0:T(8,128)(2,1)}, u32[]{:S(2)}) copy-start(bf16[4,2,256,512]{3,2,1,0:T(8,128)(2,1)} %copy-done.8) | copy-start | bytes 6291460
  109.6 5.3 %copy-start.16 = (bf16[4,64,512]{2,1,0:T(8,128)(2,1)}, bf16[4,64,512]{2,1,0:T(8,128)(2,1)S(1)}, u32[]{:S(2)}) copy-start(bf16[4,64,512]{2,1,0:T(8,128)(2,1)S(1)} %get-tuple-element.78) | copy-start | bytes 786436
  114.9 9.5 %collective-permute-start.14 = (bf16[4,64,512]{2,1,0:T(8,128)(2,1)}, bf16[4,64,512]{2,1,0:T(8,128)(2,1)}, u32[]{:S(2)}, u32[]{:S(2)}) collective-permute-start(bf16[4,64,512]{2,1,0:T(8,128)(2,1)} %get-tuple-element.77), channel_id=1, source_target_pairs={{0,16},{16,0},{1,17},{17,1},{2,18},{18,2},{3,19},{19,3},{4,20},{20... | collective-permute-start | bytes 786440 | tf_op jit(solution)/shard_map/ppermute | solution.py:24
  118.6 5.9 %copy-start.19 = (bf16[4,64,512]{2,1,0:T(8,128)(2,1)S(1)}, bf16[4,64,512]{2,1,0:T(8,128)(2,1)}, u32[]{:S(2)}) copy-start(bf16[4,64,512]{2,1,0:T(8,128)(2,1)} %copy-done.18) | copy-start | bytes 786436
  118.6 7.0 %copy-start.3 = (bf16[512,1024]{1,0:T(8,128)(2,1)S(1)}, bf16[512,1024]{1,0:T(8,128)(2,1)}, u32[]{:S(2)}) copy-start(bf16[512,1024]{1,0:T(8,128)(2,1)} %copy-done.2) | copy-start | bytes 3145732
  123.8 8.2 %collective-permute-start.17 = (bf16[4,64,512]{2,1,0:T(8,128)(2,1)S(1)}, bf16[4,64,512]{2,1,0:T(8,128)(2,1)S(1)}, u32[]{:S(2)}, u32[]{:S(2)}) collective-permute-start(bf16[4,64,512]{2,1,0:T(8,128)(2,1)S(1)} %get-tuple-element.81), channel_id=1, source_target_pairs={{0,16},{16,0},{1,17},{17,1},{2,18},{18,2},{3,19},{19,3},{4,20},{20... | collective-permute-start | bytes 786440 | tf_op jit(solution)/shard_map/ppermute | solution.py:24
  125.5 1.6 collective-permute-start.15
  126.2 5.8 %copy-start.22 = (bf16[4,512,1024]{2,1,0:T(8,128)(2,1)}, bf16[4,512,1024]{2,1,0:T(8,128)(2,1)S(1)}, u32[]{:S(2)}) copy-start(bf16[4,512,1024]{2,1,0:T(8,128)(2,1)S(1)} %pad_maximum_fusion) | copy-start | bytes 12582916
  126.2 5.7 %copy-start.17 = (bf16[4,64,512]{2,1,0:T(8,128)(2,1)S(1)}, bf16[4,64,512]{2,1,0:T(8,128)(2,1)}, u32[]{:S(2)}) copy-start(bf16[4,64,512]{2,1,0:T(8,128)(2,1)} %copy-done.16) | copy-start | bytes 786436
  127.1 4.9 %copy-start.29 = (bf16[256,512]{1,0:T(8,128)(2,1)}, bf16[256,512]{1,0:T(8,128)(2,1)S(1)}, u32[]{:S(2)}) copy-start(bf16[256,512]{1,0:T(8,128)(2,1)S(1)} %collective-permute-done.15) | copy-start | bytes 786436
  132.0 3.6 %collective-permute-start.18 = (bf16[256,512]{1,0:T(8,128)(2,1)S(1)}, bf16[256,512]{1,0:T(8,128)(2,1)S(1)}, u32[]{:S(2)}, u32[]{:S(2)}) collective-permute-start(bf16[256,512]{1,0:T(8,128)(2,1)S(1)} %bitcast_add_fusion), channel_id=1, source_target_pairs={{0,1},{1,0},{2,3},{3,2},{4,5},{5,4},{6,7},{7,6},{8,9},{9,8},{10,11... | collective-permute-start | bytes 786440 | tf_op jit(solution)/shard_map/ppermute | solution.py:28
  132.2 3.5 %copy-start.26 = (bf16[4,64,512]{2,1,0:T(8,128)(2,1)S(1)}, bf16[4,64,512]{2,1,0:T(8,128)(2,1)}, u32[]{:S(2)}) copy-start(bf16[4,64,512]{2,1,0:T(8,128)(2,1)} %copy-done.25) | copy-start | bytes 786436
  132.2 3.4 %copy-start.30 = (bf16[256,512]{1,0:T(8,128)(2,1)S(1)}, bf16[256,512]{1,0:T(8,128)(2,1)}, u32[]{:S(2)}) copy-start(bf16[256,512]{1,0:T(8,128)(2,1)} %copy-done.29) | copy-start | bytes 786436
  134.0 25.5 %collective-permute-start.21 = (bf16[1024,512]{1,0:T(8,128)(2,1)S(1)}, bf16[1024,512]{1,0:T(8,128)(2,1)S(1)}, u32[]{:S(2)}, u32[]{:S(2)}) collective-permute-start(bf16[1024,512]{1,0:T(8,128)(2,1)S(1)} %convolution_convert_fusion.5), channel_id=1, source_target_pairs={{0,2},{1,3},{2,0},{3,1},{4,6},{5,7},{6,4},{7,5},{8,10},{9,11},{10,... | collective-permute-start | bytes 3145736 | tf_op jit(solution)/shard_map/ppermute | solution.py:24
  138.6 25.2 %collective-permute-start.22 = (bf16[1024,512]{1,0:T(8,128)(2,1)S(1)}, bf16[1024,512]{1,0:T(8,128)(2,1)S(1)}, u32[]{:S(2)}, u32[]{:S(2)}) collective-permute-start(bf16[1024,512]{1,0:T(8,128)(2,1)S(1)} %convolution_convert_fusion.4), channel_id=1, source_target_pairs={{0,16},{16,0},{1,17},{17,1},{2,18},{18,2},{3,19},{19,3},{4,20},{20... | collective-permute-start | bytes 3145736 | tf_op jit(solution)/shard_map/ppermute | solution.py:24
  139.1 24.7 %collective-permute-start.19 = (bf16[256,1024]{1,0:T(8,128)(2,1)S(1)}, bf16[256,1024]{1,0:T(8,128)(2,1)S(1)}, u32[]{:S(2)}, u32[]{:S(2)}) collective-permute-start(bf16[256,1024]{1,0:T(8,128)(2,1)S(1)} %get-tuple-element.106), channel_id=1, source_target_pairs={{0,4},{4,8},{8,12},{12,0},{1,5},{5,9},{9,13},{13,1},{2,6},{6,10},{... | collective-permute-start | bytes 1572872 | tf_op jit(solution)/shard_map/ppermute | solution.py:24
  140.7 24.6 %collective-permute-start.20 = (bf16[256,1024]{1,0:T(8,128)(2,1)S(1)}, bf16[256,1024]{1,0:T(8,128)(2,1)S(1)}, u32[]{:S(2)}, u32[]{:S(2)}) collective-permute-start(bf16[256,1024]{1,0:T(8,128)(2,1)S(1)} %get-tuple-element.105), channel_id=1, source_target_pairs={{0,12},{4,0},{8,4},{12,8},{1,13},{5,1},{9,5},{13,9},{2,14},{6,2},{... | collective-permute-start | bytes 1572872 | tf_op jit(solution)/shard_map/ppermute | solution.py:24
  165.5 26.0 %collective-permute-start.26 = (bf16[512,1024]{1,0:T(8,128)(2,1)S(1)}, bf16[512,1024]{1,0:T(8,128)(2,1)S(1)}, u32[]{:S(2)}, u32[]{:S(2)}) collective-permute-start(bf16[512,1024]{1,0:T(8,128)(2,1)S(1)} %fusion.31), channel_id=1, source_target_pairs={{0,12},{4,0},{8,4},{12,8},{1,13},{5,1},{9,5},{13,9},{2,14},{6,2},{... | collective-permute-start | bytes 3145736 | tf_op jit(solution)/shard_map/ppermute | solution.py:24
  168.5 46.4 %collective-permute-start.24 = (bf16[1024,1024]{1,0:T(8,128)(2,1)S(1)}, bf16[1024,1024]{1,0:T(8,128)(2,1)S(1)}, u32[]{:S(2)}, u32[]{:S(2)}) collective-permute-start(bf16[1024,1024]{1,0:T(8,128)(2,1)S(1)} %fusion.19), channel_id=1, source_target_pairs={{0,2},{1,3},{2,0},{3,1},{4,6},{5,7},{6,4},{7,5},{8,10},{9,11},{10,... | collective-permute-start | bytes 6291464 | tf_op jit(solution)/shard_map/ppermute | solution.py:24
  169.7 46.1 %collective-permute-start.23 = (bf16[1024,1024]{1,0:T(8,128)(2,1)S(1)}, bf16[1024,1024]{1,0:T(8,128)(2,1)S(1)}, u32[]{:S(2)}, u32[]{:S(2)}) collective-permute-start(bf16[1024,1024]{1,0:T(8,128)(2,1)S(1)} %fusion.18), channel_id=1, source_target_pairs={{0,16},{16,0},{1,17},{17,1},{2,18},{18,2},{3,19},{19,3},{4,20},{20... | collective-permute-start | bytes 6291464 | tf_op jit(solution)/shard_map/ppermute | solution.py:24
  171.6 41.4 %collective-permute-start.25 = (bf16[512,1024]{1,0:T(8,128)(2,1)S(1)}, bf16[512,1024]{1,0:T(8,128)(2,1)S(1)}, u32[]{:S(2)}, u32[]{:S(2)}) collective-permute-start(bf16[512,1024]{1,0:T(8,128)(2,1)S(1)} %fusion.30), channel_id=1, source_target_pairs={{0,4},{4,8},{8,12},{12,0},{1,5},{5,9},{9,13},{13,1},{2,6},{6,10},{... | collective-permute-start | bytes 3145736 | tf_op jit(solution)/shard_map/ppermute | solution.py:24
  213.3 4.8 %collective-permute-start.27 = (bf16[256,1024]{1,0:T(8,128)(2,1)S(1)}, bf16[256,1024]{1,0:T(8,128)(2,1)S(1)}, u32[]{:S(2)}, u32[]{:S(2)}) collective-permute-start(bf16[256,1024]{1,0:T(8,128)(2,1)S(1)} %add_convert_fusion.2), channel_id=1, source_target_pairs={{0,1},{1,0},{2,3},{3,2},{4,5},{5,4},{6,7},{7,6},{8,9},{9,8},{10,11... | collective-permute-start | bytes 1572872 | tf_op jit(solution)/shard_map/ppermute | solution.py:28
  (13 other events, 24.2 us)
